TPU v7x, 32 devices: a whole 2x2x4 slice. The times are simulated.
32 devices in a mesh: section: 2 (over x), dp: 16 (over z, y, core).
Axes of the slice: x: 2, y: 2, z: 4, core: 2. Of those that a mesh axis runs over, the one named last changes fastest.
Arguments:
- saved: bfloat16 [2, 2, 2048, 4096], P('section', None, 'dp'), may hold values from -6 to 6
- top_grad: bfloat16 [2, 2048, 4096], P(None, 'dp'), may hold values from -0.4375 to 0.4375
- gains: float32 [2, 2, 4096], P('section'), may hold values from 0.1 to 1.9
- adapter_in: bfloat16 [2, 2, 4096, 32], P('section'), may hold values from -0.09375 to 0.09375
- adapter_out: bfloat16 [2, 2, 32, 4096], P('section'), may hold values from -1 to 1
Outputs:
- grad_in: float32 [2, 4096, 32], P('section', 'dp')
- grad_out: float32 [2, 32, 4096], P('section', None, 'dp')
All inputs are finite; a program needn't handle non-finite values.
Results may differ from a plain program's by a relative error of at most 0.014.
Values may be sent and summed in bfloat16 or wider, within the bound.
No kernel may reach another device: no remote copies, remote signals or barrier semaphores. Data moves between devices by JAX's collectives and lax.ppermute only.
A program may use at most 64 MiB of HBM per device.

v0:
```python
from functools import partial

import jax
import jax.numpy as jnp
from jax import lax
from jax.sharding import PartitionSpec as P

EPS = 1e-05


def for_sending(shard):
    return jax.tree.map(lambda a: a.astype(jnp.bfloat16) if a.dtype == jnp.float32 else a, shard)


def passed_along(shard, axis, by):
    count = lax.axis_size(axis)
    pairs = [(i, i + by) for i in range(count) if 0 <= i + by < count]
    return lax.ppermute(shard, axis, pairs)


def from_partner(block, axis, distance):
    count = lax.axis_size(axis)
    route = []
    for low in range(count):
        high = low | 1 << distance
        if high != low and high < count:
            route += [(low, high), (high, low)]
    return lax.ppermute(block, axis, route)


def forward_part(x, gain, weight_in):
    xf = x.astype(jnp.float32)
    scale = lax.rsqrt(jnp.mean(xf * xf, axis=-1, keepdims=True) + EPS)
    normed = xf * scale
    hidden = (normed * gain).astype(jnp.bfloat16)
    pre = jnp.dot(hidden, weight_in, preferred_element_type=jnp.float32)
    return (normed, scale, hidden, pre)


def front_pass(x, gain, weight_in, weight_out, upstream):
    normed, scale, hidden, pre = forward_part(x, gain, weight_in)
    sig = jax.nn.sigmoid(pre)
    active = (pre * sig).astype(jnp.bfloat16)
    delta_act = jnp.dot(upstream, weight_out.T, preferred_element_type=jnp.float32)
    delta_pre = (delta_act * sig * (1.0 + pre * (1.0 - sig))).astype(jnp.bfloat16)
    delta_hidden = jnp.dot(delta_pre, weight_in.T, preferred_element_type=jnp.float32)
    delta_norm = delta_hidden * gain
    inner = jnp.mean(delta_norm * normed, axis=-1, keepdims=True)
    result = (upstream.astype(jnp.float32) + scale * (delta_norm - normed * inner)).astype(
        jnp.bfloat16
    )
    return (result, hidden, active, delta_pre)


def weight_terms(hidden, active, delta_pre, upstream):
    term_in = jnp.dot(hidden.T, delta_pre, preferred_element_type=jnp.float32)
    term_out = jnp.dot(active.T, upstream, preferred_element_type=jnp.float32)
    return (term_in, term_out)


def full_pass(x, gain, weight_in, weight_out, upstream):
    result, hidden, active, delta_pre = front_pass(x, gain, weight_in, weight_out, upstream)
    term_in, term_out = weight_terms(hidden, active, delta_pre, upstream)
    return (result, term_in, term_out)


def on_device(saved, top_grad, gains, adapter_in, adapter_out):
    sections = lax.axis_size("section")
    place = lax.axis_index("section")
    width = top_grad.shape[2]
    rank = adapter_in.shape[3]
    zero_in = jnp.zeros((width, rank), jnp.float32)
    zero_out = jnp.zeros((rank, width), jnp.float32)

    def pieces(replica):
        return (
            saved[0, replica],
            gains[0, replica],
            adapter_in[0, replica],
            adapter_out[0, replica],
        )

    def serves(replica, turn):
        if replica == 0:
            return place == sections - 1 - turn
        return place == turn

    def pass_on(first, second):
        moved_first = jax.tree.map(
            lambda part, own: part.astype(own.dtype),
            passed_along(for_sending(first), "section", -1),
            first,
        )
        moved_second = jax.tree.map(
            lambda part, own: part.astype(own.dtype),
            passed_along(for_sending(second), "section", 1),
            second,
        )
        return (moved_first, moved_second)

    def skip_full(upstream):
        return (upstream, zero_in, zero_out)

    def advance(turn, carry, send):
        flows = carry[0:2]
        sums = list(carry[2:])
        leaving = []
        for replica in (0, 1):
            result, term_in, term_out = lax.cond(
                serves(replica, turn),
                partial(full_pass, *pieces(replica)),
                skip_full,
                flows[replica],
            )
            leaving.append(result)
            sums[2 * replica] = sums[2 * replica] + term_in
            sums[2 * replica + 1] = sums[2 * replica + 1] + term_out
        if send:
            leaving = list(pass_on(leaving[0], leaving[1]))
        return (leaving[0], leaving[1], sums[0], sums[1], sums[2], sums[3])

    start = (top_grad[0], top_grad[1], zero_in, zero_out, zero_in, zero_out)
    carry = lax.fori_loop(0, sections - 1, lambda turn, state: advance(turn, state, True), start)
    carry = advance(sections - 1, carry, False)
    mine_in, mine_out, mirror_in, mirror_out = (carry[2], carry[3], carry[4], carry[5])
    levels = sections.bit_length() - 1
    shares = (
        lax.psum_scatter(mine_in, "dp", scatter_dimension=0, tiled=True),
        lax.psum_scatter(mine_out, "dp", scatter_dimension=1, tiled=True),
        lax.psum_scatter(mirror_in, "dp", scatter_dimension=0, tiled=True),
        lax.psum_scatter(mirror_out, "dp", scatter_dimension=1, tiled=True),
    )
    moved = (shares[2], shares[3])
    for level in range(levels):
        moved = from_partner((moved[0], moved[1]), "section", level)
    total_in = shares[0] + moved[0]
    total_out = shares[1] + moved[1]
    return (total_in[None], total_out[None])


def solution(mesh):
    in_specs = (
        P("section", None, "dp", None),
        P(None, "dp", None),
        P("section", None, None),
        P("section", None, None, None),
        P("section", None, None, None),
    )
    out_specs = (P("section", "dp", None), P("section", None, "dp"))
    return jax.shard_map(
        on_device, mesh=mesh, in_specs=in_specs, out_specs=out_specs, check_vma=False
    )
```

profile of v0, /device:TPU:0, one launch (start us, length us, event | category | flops | bytes accessed | tf_op | source)
XLA Modules:
  0.0 299.1 jit_solution(3955548002418082869)
XLA Ops:
  7.2 0.0 reduce-scatter.11.cloned.1.call-start
  7.2 1.9 slice_bitcast_fusion
  9.1 0.3 copy-done.5
  9.4 1.2 slice_bitcast_fusion.1
  10.6 0.7 fusion.72
  11.3 1.3 copy.10
  12.7 1.8 slice_bitcast_fusion.4
  14.4 7.5 %conditional.6 = (bf16[128,4096]{1,0:T(8,128)(2,1)}, f32[4096,32]{0,1:T(8,128)}, f32[32,4096]{1,0:T(8,128)}) conditional(s32[]{:T(128)} %convert_element_type.71, bf16[128,4096]{1,0:T(8,128)(2,1)} %get-tuple-element.129, (bf16[128,4096]{1,0:T(8,128)(2,1)}, bf16[128,4096]{1,0:T(8,128)(2,1)S(1)}, bf16[32,4096]{1,0:T(8,128)(2,1)}, ...), branch_computations={%region_8.9_spmd, %region_9.12_spmd} | conditional | flops 180412544 | bytes 21886572 | solution.py:109
  14.5 0.3 fusion.45
  14.8 1.9 fusion.50
  16.8 0.5 fusion.47
  17.2 0.7 fusion.40
  17.9 1.6 fusion.44
  19.6 1.3 fusion.48
  20.9 1.1 fusion.52
  21.9 2.3 collective-permute-start.1
  24.3 22.6 %collective-permute-done.1 = bf16[128,4096]{1,0:T(8,128)(2,1)} collective-permute-done((bf16[128,4096]{1,0:T(8,128)(2,1)}, bf16[128,4096]{1,0:T(8,128)(2,1)}, u32[]{:S(2)}, u32[]{:S(2)}) %collective-permute-start.1) | collective-permute-done | bytes 1048608 | tf_op jit(solution)/shard_map/while/body/eval_jaxpr/ppermute | solution.py:18
  46.8 1.7 conditional.7
  46.8 0.8 broadcast_in_dim.30
  47.7 0.8 broadcast_in_dim.31
  48.5 2.1 add.104
  50.6 0.0 reduce-scatter.11.cloned.1.call-update
  50.6 0.0 reduce-scatter.7.cloned.1.call-start
  50.7 1.4 copy.9
  52.1 1.9 conditional.4
  52.1 1.0 copy.11
  53.1 0.8 broadcast_in_dim.1
  53.9 0.8 copy-done.3
  54.7 1.3 collective-permute-start
  56.0 2.0 add.101
  58.1 0.0 reduce-scatter.9.cloned.1.call-start
  58.2 32.8 %collective-permute-done = bf16[128,4096]{1,0:T(8,128)(2,1)S(1)} collective-permute-done((bf16[128,4096]{1,0:T(8,128)(2,1)}, bf16[128,4096]{1,0:T(8,128)(2,1)S(1)}, u32[]{:S(2)}, u32[]{:S(2)}) %collective-permute-start) | collective-permute-done | bytes 1048608 | tf_op jit(solution)/shard_map/while/body/eval_jaxpr/ppermute | solution.py:18
  91.0 3.6 %conditional.5 = (f32[4096,32]{0,1:T(8,128)}, f32[32,4096]{1,0:T(8,128)}) conditional(s32[]{:T(128)} %convert_element_type.71, () %tuple.45, (bf16[128,4096]{1,0:T(8,128)(2,1)S(1)}, f32[1,1,4096]{2,1,0:T(1,128)S(1)}, bf16[128,4096]{1,0:T(8,128)(2,1)S(1)}, bf16[32,4096]{1,0:T(8,128)(2,1)S(1)}, bf16[4096,32]{1,0:T(8,128)(2,1)S(1)}) %tuple.77), branch_computations={%region_4.5_spmd, %region_5.7_spmd} | conditional | flops 140042368 | bytes 6900240 | solution.py:109
  91.0 0.3 fusion.19
  91.3 0.5 fusion.26
  91.8 1.7 fusion.24
  93.6 1.1 fusion.31
  94.6 2.1 add.103
  96.8 0.0 reduce-scatter.5.cloned.1.call-start
  96.8 1.9 add.100
  98.7 16.6 %reduce-scatter.11.cloned.1.call-done = f32[32,256]{1,0:T(8,128)} async-done(((f32[32,4096]{1,0:T(8,128)}), f32[32,256]{1,0:T(8,128)}) %reduce-scatter.11.cloned.1.call-update) | async-done | bytes 32784 | tf_op jit(solution)/shard_map/reduce_scatter | solution.py:131
  115.4 1.4 collective-permute-start.3
  116.8 57.3 %reduce-scatter.7.cloned.1.call-done = f32[256,32]{0,1:T(8,128)} async-done(((f32[4096,32]{0,1:T(8,128)}), f32[256,32]{0,1:T(8,128)}) %reduce-scatter.7.cloned.1.call-update) | async-done | bytes 32784 | tf_op jit(solution)/shard_map/reduce_scatter | solution.py:130
  174.1 1.5 collective-permute-start.2
  175.6 56.9 %reduce-scatter.9.cloned.1.call-done = f32[32,256]{1,0:T(8,128)} async-done(((f32[32,4096]{1,0:T(8,128)}), f32[32,256]{1,0:T(8,128)}) %reduce-scatter.9.cloned.1.call-update) | async-done | bytes 32784 | tf_op jit(solution)/shard_map/reduce_scatter | solution.py:129
  232.6 1.4 add_bitcast_fusion
  233.9 57.3 %reduce-scatter.5.cloned.1.call-done = f32[256,32]{0,1:T(8,128)} async-done(((f32[4096,32]{0,1:T(8,128)}), f32[256,32]{0,1:T(8,128)}) %reduce-scatter.5.cloned.1.call-update) | async-done | bytes 32784 | tf_op jit(solution)/shard_map/reduce_scatter | solution.py:128
  291.2 1.4 add_bitcast_fusion.1
  (24 shorter events, 0.2 us)
Async XLA Ops:
  7.2 108.2 %reduce-scatter.11.cloned.1.call-start = ((), (), s32[]{:S(2)}) async-start(), calls=%async_computation.7 | async-start | bytes 557056 | tf_op jit(solution)/shard_map/reduce_scatter | solution.py:131
  7.2 2.2 copy-start.5
  9.4 1.2 copy-start.6
  10.6 3.8 %copy-start.7 = (f32[1,2,4096]{2,1,0:T(2,128)S(1)}, f32[1,2,4096]{2,1,0:T(2,128)}, u32[]{:S(2)}) copy-start(f32[1,2,4096]{2,1,0:T(2,128)} %param.15) | copy-start | bytes 98308
  14.5 2.2 copy-start
  14.5 2.3 copy-start.2
  14.5 2.7 copy-start.1
  21.9 24.9 %collective-permute-start.1 = (bf16[128,4096]{1,0:T(8,128)(2,1)}, bf16[128,4096]{1,0:T(8,128)(2,1)}, u32[]{:S(2)}, u32[]{:S(2)}) collective-permute-start(bf16[128,4096]{1,0:T(8,128)(2,1)} %get-tuple-element.117), channel_id=1, source_target_pairs={{0,16},{1,17},{2,18},{3,19},{4,20},{5,21},{6,22},{7,23},{8,24},{9,... | collective-permute-start | bytes 3145736 | tf_op jit(solution)/shard_map/while/body/eval_jaxpr/ppermute | solution.py:18
  50.6 123.5 %reduce-scatter.7.cloned.1.call-start = ((), (), s32[]{:S(2)}) async-start(), calls=%async_computation.5 | async-start | bytes 557056 | tf_op jit(solution)/shard_map/reduce_scatter | solution.py:130
  53.9 0.8 copy-start.3
  54.7 36.2 %collective-permute-start = (bf16[128,4096]{1,0:T(8,128)(2,1)}, bf16[128,4096]{1,0:T(8,128)(2,1)S(1)}, u32[]{:S(2)}, u32[]{:S(2)}) collective-permute-start(bf16[128,4096]{1,0:T(8,128)(2,1)} %get-tuple-element.114), channel_id=1, source_target_pairs={{16,0},{17,1},{18,2},{19,3},{20,4},{21,5},{22,6},{23,7},{24,8},{25... | collective-permute-start | bytes 3145736 | tf_op jit(solution)/shard_map/while/body/eval_jaxpr/ppermute | solution.py:18
  58.1 174.5 %reduce-scatter.9.cloned.1.call-start = ((), (), s32[]{:S(2)}) async-start(), calls=%async_computation.6 | async-start | bytes 557056 | tf_op jit(solution)/shard_map/reduce_scatter | solution.py:129
  94.6 2.2 copy-start.4
  96.8 194.4 %reduce-scatter.5.cloned.1.call-start = ((), (), s32[]{:S(2)}) async-start(), calls=%async_computation.4 | async-start | bytes 557056 | tf_op jit(solution)/shard_map/reduce_scatter | solution.py:128
  115.4 117.2 %collective-permute-start.3 = (f32[32,256]{1,0:T(8,128)}, f32[32,256]{1,0:T(8,128)S(1)}, u32[]{:S(2)}, u32[]{:S(2)}) collective-permute-start(f32[32,256]{1,0:T(8,128)} %reduce-scatter.11.cloned.1.call-done), channel_id=1, source_target_pairs={{0,16},{16,0},{1,17},{17,1},{2,18},{18,2},{3,19},{19,3},{4,20},{20... | collective-permute-start | bytes 98312 | tf_op jit(solution)/shard_map/ppermute | solution.py:28
  174.1 117.1 %collective-permute-start.2 = (f32[256,32]{0,1:T(8,128)}, f32[256,32]{0,1:T(8,128)S(1)}, u32[]{:S(2)}, u32[]{:S(2)}) collective-permute-start(f32[256,32]{0,1:T(8,128)} %reduce-scatter.7.cloned.1.call-done), channel_id=1, source_target_pairs={{0,16},{16,0},{1,17},{17,1},{2,18},{18,2},{3,19},{19,3},{4,20},{20... | collective-permute-start | bytes 98312 | tf_op jit(solution)/shard_map/ppermute | solution.py:28
Sparse Core Ops, SparseCore 0:
  50.7 64.5 reduce-scatter.10
  119.3 54.7 reduce-scatter.6
  177.7 54.8 reduce-scatter.8
  236.4 54.7 reduce-scatter.4
where the time goes:
time: 300 us; the launch traced here: 299 us
  waiting for transfers between devices  244 us (81%)
  between operations  13.8 us (5%)
  other arithmetic  13.1 us (4%)
  local copies, waits for them, and re-layouts  13 us (4%)
  matrix products  8.74 us (3%)
  starting transfers between devices  6.71 us (2%)
    reduce_scatter x1, waiting for transfers between devices, on_device(): lax.psum_scatter(mirror_in, 'dp', scatter_dimension=0, tiled=True)  57.3 us
    reduce_scatter x1, waiting for transfers between devices, on_device(): lax.psum_scatter(mine_in, 'dp', scatter_dimension=0, tiled=True)  57.3 us
    reduce_scatter x1, waiting for transfers between devices, on_device(): lax.psum_scatter(mine_out, 'dp', scatter_dimension=1, tiled=True)  56.9 us
    ppermute x2, waiting for transfers between devices, passed_along(): return lax.ppermute(shard, axis, pairs)  55.4 us
    reduce_scatter x1, waiting for transfers between devices, on_device(): lax.psum_scatter(mirror_out, 'dp', scatter_dimension=1, tiled=True)  16.6 us
  transfers between devices with their start and end apart: 8, of which 6 were waited for; matrix products, arithmetic and copies ran while one was open for 5% of the time, Pallas kernels for 0%

commit v1 on v0

v1 whole, which is shorter than its diff:
```python
from functools import partial

import jax
import jax.numpy as jnp
from jax import lax
from jax.experimental import pallas as pl
from jax.experimental.pallas import tpu as pltpu
from jax.sharding import PartitionSpec as P

EPS = 1e-05
VMEM_BYTES = 48 * 1024 * 1024
F32 = jnp.float32
BF16 = jnp.bfloat16


def nn(a, b):
    return lax.dot_general(a, b, (((1,), (0,)), ((), ())), preferred_element_type=F32)


def nt(a, b):
    return lax.dot_general(a, b, (((1,), (1,)), ((), ())), preferred_element_type=F32)


def tn(a, b):
    return lax.dot_general(a, b, (((0,), (0,)), ((), ())), preferred_element_type=F32)


def as_row(column):
    count = column.shape[0]
    return jnp.transpose(jnp.broadcast_to(column, (count, count)))[0:1, :]


def silu_slope(pre):
    sig = jax.nn.sigmoid(pre)
    return sig, sig * (1.0 + pre * (1.0 - sig))


def project(x_ref, gain_ref, w_ref, xg_ref, step):
    tokens, width = x_ref.shape
    squares = jnp.zeros((tokens, 128), F32)
    pre = jnp.zeros((w_ref.shape[0], tokens), F32)
    for c in range(0, width, step):
        x = x_ref[:, c : c + step].astype(F32)
        for k in range(0, step, 128):
            part = x[:, k : k + 128]
            squares += part * part
        xg = (x * gain_ref[:, c : c + step]).astype(BF16)
        xg_ref[:, c : c + step] = xg
        pre += nt(w_ref[:, c : c + step], xg)
    mean = jnp.sum(squares, axis=1, keepdims=True) * (1.0 / width)
    scale = lax.rsqrt(mean + EPS)
    return scale, pre


def upper_kernel(
    share, place_ref, saved, top, gains, w_in, w_out,
    out_ref, flow_ref, xg0_ref, low_ref,
    x1, x0, g, gain1, gain0, wi1, wi0, wo1, xg1, sems,
):
    place = place_ref[0]
    upper, lower = 1 - place, place
    copies = [
        (gains.at[0, pl.ds(upper, 1)], gain1),
        (w_in.at[0, upper], wi1),
        (saved.at[0, upper], x1),
        (w_out.at[0, upper], wo1),
        (top.at[upper], g),
        (gains.at[0, pl.ds(lower, 1)], gain0),
        (w_in.at[0, lower], wi0),
        (saved.at[0, lower], x0),
    ]
    copies = [pltpu.make_async_copy(a, b, sems.at[i]) for i, (a, b) in enumerate(copies)]
    for copy in copies:
        copy.start()
    width = x1.shape[1]
    rank = wi1.shape[0]
    step = share
    for copy in copies[0:3]:
        copy.wait()
    scale1, raw1 = project(x1, gain1, wi1, xg1, step)
    for copy in copies[3:5]:
        copy.wait()
    delta = jnp.zeros(raw1.shape, F32)
    for c in range(0, width, step):
        delta += nt(wo1[:, c : c + step], g[:, c : c + step])
    row1 = as_row(scale1)
    pre1 = raw1 * row1
    sig, slope = silu_slope(pre1)
    act1 = (pre1 * sig).astype(BF16)
    da1 = (delta * slope).astype(BF16)
    da1f = da1.astype(F32)
    inner = jnp.sum(da1f * pre1, axis=0, keepdims=True) * (1.0 / width)
    das1 = (da1f * row1).astype(BF16)
    pull = jnp.transpose(jnp.broadcast_to(inner * row1 * row1, (x1.shape[0],) * 2))[:, 0:1]
    for copy in copies[5:8]:
        copy.wait()
    scale0, raw0 = project(x0, gain0, wi0, xg0_ref, step)
    row0 = as_row(scale0)
    pre0 = raw0 * row0
    sig0, slope0 = silu_slope(pre0)
    low_ref[0] = (pre0 * sig0).astype(BF16).astype(F32)
    low_ref[1] = slope0
    low_ref[2] = jnp.broadcast_to(row0, raw0.shape)
    for i, c in enumerate(range(0, width, step)):
        cols = slice(c, c + step)
        dn = tn(da1, wi1[:, cols]) * gain1[:, cols]
        flow = g[:, cols].astype(F32) + scale1 * dn - pull * x1[:, cols].astype(F32)
        flow_ref[:, cols] = flow.astype(BF16)
        out_ref[i, 0:rank] = nn(das1, xg1[:, cols]).astype(BF16)
        out_ref[i, rank : 2 * rank] = nn(act1, g[:, cols]).astype(BF16)


def flow_kernel(share, flow_ref, w_ref, low_ref, send_ref):
    width = flow_ref.shape[1]
    rank = w_ref.shape[0]
    delta = jnp.zeros((rank, flow_ref.shape[0]), F32)
    for c in range(0, width, share):
        delta += nt(w_ref[:, c : c + share], flow_ref[:, c : c + share])
    send_ref[0] = low_ref[0]
    send_ref[1] = delta


def lower_kernel(share, _, flow_ref, xg0_ref, low_ref, got_ref, out_ref):
    width = flow_ref.shape[1]
    rank = got_ref.shape[1]
    act0 = got_ref[0].astype(BF16)
    da0 = (got_ref[1] * low_ref[1]).astype(BF16)
    das0 = (da0.astype(F32) * low_ref[2]).astype(BF16)
    for i, c in enumerate(range(0, width, share)):
        cols = slice(c, c + share)
        out_ref[i, 0:rank] = nn(das0, xg0_ref[:, cols]).astype(BF16)
        out_ref[i, rank : 2 * rank] = nn(act0, flow_ref[:, cols]).astype(BF16)


def sum_kernel(got_ref, in_ref, out_ref):
    rank = in_ref.shape[1]
    total = got_ref[0].astype(F32)
    for i in range(1, got_ref.shape[0]):
        total += got_ref[i].astype(F32)
    in_ref[0] = total[0:rank]
    out_ref[0] = total[rank : 2 * rank]


def params():
    return pltpu.CompilerParams(vmem_limit_bytes=VMEM_BYTES)


def whole():
    return pl.BlockSpec(memory_space=pltpu.VMEM)


def pair_on_device(saved, top_grad, gains, adapter_in, adapter_out):
    place = lax.axis_index("section")
    count = lax.axis_size("dp")
    tokens, width = saved.shape[2:]
    rank = adapter_in.shape[3]
    share = width // count
    swap = [(0, 1), (1, 0)]
    adapter_in = jnp.swapaxes(adapter_in, 2, 3)
    any_space = pl.BlockSpec(memory_space=pl.ANY)
    partner_out = lax.ppermute(
        lax.dynamic_index_in_dim(adapter_out[0], place, 0, keepdims=False), "section", swap
    )
    blocks = jax.ShapeDtypeStruct((2 * count, 2 * rank, share), BF16)
    wide = jax.ShapeDtypeStruct((tokens, width), BF16)
    out, flow, xg0, low = pl.pallas_call(
        partial(upper_kernel, share),
        grid=(1,),
        in_specs=[pl.BlockSpec(memory_space=pltpu.SMEM)] + [any_space] * 5,
        out_specs=[
            pl.BlockSpec((count, 2 * rank, share), lambda i: (1, 0, 0)),
            whole(),
            whole(),
            whole(),
        ],
        out_shape=[blocks, wide, wide, jax.ShapeDtypeStruct((3, rank, tokens), F32)],
        scratch_shapes=[pltpu.VMEM((tokens, width), BF16)] * 3
        + [pltpu.VMEM((1, width), F32)] * 2
        + [pltpu.VMEM((rank, width), BF16)] * 3
        + [pltpu.VMEM((tokens, width), BF16), pltpu.SemaphoreType.DMA((8,))],
        compiler_params=params(),
        cost_estimate=pl.CostEstimate(
            flops=12 * tokens * width * rank, bytes_accessed=12 * tokens * width, transcendentals=0
        ),
        name="upper",
    )(place.astype(jnp.int32)[None], saved, top_grad, gains, adapter_in, adapter_out)
    send = pl.pallas_call(
        partial(flow_kernel, share),
        in_specs=[whole()] * 3,
        out_specs=whole(),
        out_shape=jax.ShapeDtypeStruct((2, rank, tokens), F32),
        compiler_params=params(),
        name="flow",
    )(flow, partner_out, low)
    got = lax.ppermute(send, "section", swap)
    out = pl.pallas_call(
        partial(lower_kernel, share),
        grid=(1,),
        in_specs=[any_space] + [whole()] * 4,
        out_specs=pl.BlockSpec((count, 2 * rank, share), lambda i: (0, 0, 0)),
        out_shape=blocks,
        input_output_aliases={0: 0},
        compiler_params=params(),
        name="lower",
    )(out, flow, xg0, low, got)
    got = lax.all_to_all(out, ("section", "dp"), 0, 0, tiled=True)
    total_in, total_out = pl.pallas_call(
        sum_kernel,
        in_specs=[whole()],
        out_specs=[whole()] * 2,
        out_shape=[jax.ShapeDtypeStruct((1, rank, share), F32)] * 2,
        compiler_params=params(),
        name="total",
    )(got)
    return (jnp.swapaxes(total_in, 1, 2), total_out)


def section_back(x, gain, weight_in, weight_out, upstream):
    xf = x.astype(F32)
    scale = lax.rsqrt(jnp.mean(xf * xf, axis=-1, keepdims=True) + EPS)
    normed = xf * scale
    hidden = (normed * gain).astype(BF16)
    pre = jnp.dot(hidden, weight_in, preferred_element_type=F32)
    sig, slope = silu_slope(pre)
    active = (pre * sig).astype(BF16)
    delta_act = jnp.dot(upstream, weight_out.T, preferred_element_type=F32)
    delta_pre = (delta_act * slope).astype(BF16)
    delta_norm = jnp.dot(delta_pre, weight_in.T, preferred_element_type=F32) * gain
    inner = jnp.mean(delta_norm * normed, axis=-1, keepdims=True)
    result = (upstream.astype(F32) + scale * (delta_norm - normed * inner)).astype(BF16)
    term_in = jnp.dot(hidden.T, delta_pre, preferred_element_type=F32)
    term_out = jnp.dot(active.T, upstream, preferred_element_type=F32)
    return (result, term_in, term_out)


def relay_on_device(saved, top_grad, gains, adapter_in, adapter_out):
    sections = lax.axis_size("section")
    place = lax.axis_index("section")
    width = top_grad.shape[2]
    rank = adapter_in.shape[3]
    zero_in = jnp.zeros((width, rank), F32)
    zero_out = jnp.zeros((rank, width), F32)

    def step(turn, flows, sums):
        leaving, added = [], []
        for replica in (0, 1):
            serves = place == (sections - 1 - turn if replica == 0 else turn)
            result, term_in, term_out = lax.cond(
                serves,
                partial(
                    section_back,
                    saved[0, replica],
                    gains[0, replica],
                    adapter_in[0, replica],
                    adapter_out[0, replica],
                ),
                lambda flow: (flow, zero_in, zero_out),
                flows[replica],
            )
            leaving.append(result)
            added += [sums[2 * replica] + term_in, sums[2 * replica + 1] + term_out]
        return leaving, added

    down = [(i, i - 1) for i in range(1, sections)]
    up = [(i, i + 1) for i in range(sections - 1)]

    def turn_and_pass(turn, carry):
        leaving, sums = step(turn, carry[0], carry[1])
        return (
            [lax.ppermute(leaving[0], "section", down), lax.ppermute(leaving[1], "section", up)],
            sums,
        )

    start = ([top_grad[0], top_grad[1]], [zero_in, zero_out, zero_in, zero_out])
    flows, sums = lax.fori_loop(0, sections - 1, turn_and_pass, start)
    _, sums = step(sections - 1, flows, sums)
    shares = [
        lax.psum_scatter(term, "dp", scatter_dimension=i % 2, tiled=True)
        for i, term in enumerate(sums)
    ]
    mirror = [(i, sections - 1 - i) for i in range(sections)]
    total_in = shares[0] + lax.ppermute(shares[2], "section", mirror)
    total_out = shares[1] + lax.ppermute(shares[3], "section", mirror)
    return (total_in[None], total_out[None])


def solution(mesh):
    in_specs = (
        P("section", None, "dp", None),
        P(None, "dp", None),
        P("section", None, None),
        P("section", None, None, None),
        P("section", None, None, None),
    )
    out_specs = (P("section", "dp", None), P("section", None, "dp"))

    def run(saved, *others):
        share = saved.shape[3] // mesh.shape["dp"]
        pair = mesh.shape["section"] == 2 and share % 128 == 0
        on_device = pair_on_device if pair else relay_on_device
        return jax.shard_map(
            on_device, mesh=mesh, in_specs=in_specs, out_specs=out_specs, check_vma=False
        )(saved, *others)

    return run
```

time: 300 us -> 49.9 us (0.17)
  waiting for transfers between devices: 244 us -> 2.55 us
  blocking collectives: 0 us -> 32.7 us
  between operations: 13.8 us -> 0.67 us
  other arithmetic: 13.1 us -> 0 us
  local copies, waits for them, and re-layouts: 13 us -> 3.81 us
  matrix products: 8.74 us -> 0 us
  Pallas kernels: 0 us -> 5.42 us
    reduce_scatter x4 -> x0, waiting for transfers between devices: 188 us -> none  [the longest x1 57.3 us: on_device(): lax.psum_scatter(mirror_in, 'dp', scatter_dimension=0, tiled=True)]
    ppermute x4 -> x2, waiting for transfers between devices: 55.4 us -> 2.55 us  [the longest x1 2.54 us: pair_on_device(): got = lax.ppermute(send, 'section', swap)]
    all_to_all x0 -> x1, blocking collectives: none -> 32.7 us  [pair_on_device(): got = lax.all_to_all(out, ('section', 'dp'), 0, 0, tiled=True)]
    dot_general x8 -> x0, matrix products: 8.74 us -> none  [the longest x2 3.04 us: weight_terms(): term_in = jnp.dot(hidden.T, delta_pre, preferred_element_type=jnp.float32)]
    add x4 -> x0, other arithmetic: 8.11 us -> none  [the longest x2 4.19 us: advance(): sums[2 * replica + 1] = sums[2 * replica + 1] + term_out]
    pallas_call x0 -> x4, Pallas kernels: none -> 5.42 us  [the longest x1 3.81 us: pair_on_device(): pl.pallas_call(partial(upper_kernel, share), grid=(1,), in_specs=[pl.Bloc...]
    squeeze x3 -> x1, local copies, waits for them, and re-layouts: 4.78 us -> 0.97 us  [pair_on_device(): lax.dynamic_index_in_dim(adapter_out[0], place, 0, keepdims=False)]
    ppermute x4 -> x2, starting transfers between devices: 6.54 us -> 4.41 us  [the longest x1 3 us: pair_on_device(): lax.ppermute(lax.dynamic_index_in_dim(adapter_out[0], place, 0, keepdims=...]
  transfers between devices with their start and end apart: 8 -> 2, of which waited for: 6 -> 1; matrix products, arithmetic and copies ran while one was open for 5% -> 0% of each run, Pallas kernels for 0% -> 8%
where the time goes in v1:
time: 49.9 us; the launch traced here: 49.6 us
  blocking collectives  32.7 us (66%)
  Pallas kernels  5.42 us (11%)
  starting transfers between devices  4.41 us (9%)
  local copies, waits for them, and re-layouts  3.81 us (8%)
  waiting for transfers between devices  2.55 us (5%)
  between operations  0.67 us (1%)
    all_to_all x1, blocking collectives, pair_on_device(): got = lax.all_to_all(out, ('section', 'dp'), 0, 0, tiled=True)  32.7 us
    pallas_call x1, Pallas kernels, pair_on_device(): pl.pallas_call(partial(upper_kernel, share), grid=(1,), in_specs=[pl.Bloc...  3.81 us
    ppermute x1, starting transfers between devices, pair_on_device(): lax.ppermute(lax.dynamic_index_in_dim(adapter_out[0], place, 0, keepdims=...  3 us
    unnamed x6, local copies, waits for them, and re-layouts  2.84 us
    ppermute x1, waiting for transfers between devices, pair_on_device(): got = lax.ppermute(send, 'section', swap)  2.54 us
    ppermute x1, starting transfers between devices, pair_on_device(): got = lax.ppermute(send, 'section', swap)  1.41 us
  transfers between devices with their start and end apart: 2, of which 1 were waited for; matrix products, arithmetic and copies ran while one was open for 0% of the time, Pallas kernels for 8%

profile of v1, /device:TPU:0, one launch (start us, length us, event | category | flops | bytes accessed | tf_op | source)
XLA Modules:
  0.0 49.6 jit_solution(2392759535321748234)
XLA Ops:
  0.6 1.0 %dynamic-slice_bitcast_fusion = bf16[32,4096]{1,0:T(8,128)(2,1)S(1)} fusion(bf16[1,2,32,4096]{3,2,1,0:T(8,128)(2,1)} %w_out.1, s32[]{:T(128)S(6)} %select_n.4), kind=kLoop, calls=%fused_computation | loop fusion | bytes 524292 | tf_op jit(solution)/shard_map/jit(dynamic_index_in_dim)/squeeze | solution.py:162
  1.6 3.0 %collective-permute-start = (bf16[32,4096]{1,0:T(8,128)(2,1)S(1)}, bf16[32,4096]{1,0:T(8,128)(2,1)S(1)}, u32[]{:S(2)}, u32[]{:S(2)}) collective-permute-start(bf16[32,4096]{1,0:T(8,128)(2,1)S(1)} %dynamic-slice_bitcast_fusion), channel_id=1, source_target_pairs={{0,16},{16,0},{1,17},{17,1},{2,18},{18,2},{3,19},{19,3},{4,20},{20... | collective-permute-start | bytes 786440 | tf_op jit(solution)/shard_map/ppermute | solution.py:161
  4.6 0.0 copy-start
  4.6 1.0 %copy-done = bf16[1,2,32,4096]{3,2,1,0:T(8,128)(2,1)S(1)} copy-done((bf16[1,2,32,4096]{3,2,1,0:T(8,128)(2,1)S(1)}, bf16[1,2,32,4096]{3,2,1,0:T(8,128)(2,1)}, u32[]{:S(2)}) %copy-start) | copy-done | bytes 524312
  5.7 0.0 copy-start.1
  5.7 1.0 %copy-done.1 = bf16[1,2,4096,32]{2,3,1,0:T(8,128)(2,1)S(1)} copy-done((bf16[1,2,4096,32]{2,3,1,0:T(8,128)(2,1)S(1)}, bf16[1,2,4096,32]{2,3,1,0:T(8,128)(2,1)}, u32[]{:S(2)}) %copy-start.1) | copy-done | bytes 524312
  6.7 0.0 copy-start.2
  6.7 0.8 %copy-done.2 = f32[1,2,4096]{2,1,0:T(2,128)S(1)} copy-done((f32[1,2,4096]{2,1,0:T(2,128)S(1)}, f32[1,2,4096]{2,1,0:T(2,128)}, u32[]{:S(2)}) %copy-start.2) | copy-done | bytes 32792
  7.5 3.8 %upper.1 = (bf16[32,64,256]{2,1,0:T(8,128)(2,1)S(1)}, bf16[128,4096]{1,0:T(8,128)(2,1)S(1)}, bf16[128,4096]{1,0:T(8,128)(2,1)S(1)}, f32[3,32,128]{2,1,0:T(8,128)S(1)}) custom-call(s32[1]{0:T(128)} %bitcast.place_ref, bf16[1,2,128,4096]{3,2,1,0:T(8,128)(2,1)} %saved.1, bf16[2,128,4096]{2,1,0:T(8,128)(2,1)} %top.1, f32[1,2,4096]{2,1,0:T(2,128)S(1)} %copy-done.2, ...), custom_call_target="tpu_custom_call" | custom-call | flops 201326592 | bytes 6291456 | tf_op jit(solution)/shard_map/upper/pallas_call | solution.py:166
  11.3 0.0 collective-permute-done.w_ref
  11.3 0.4 flow.1
  11.7 1.4 %collective-permute-start.1 = (f32[2,32,128]{2,1,0:T(8,128)S(1)}, f32[2,32,128]{2,1,0:T(8,128)S(1)}, u32[]{:S(2)}, u32[]{:S(2)}) collective-permute-start(f32[2,32,128]{2,1,0:T(8,128)S(1)} %flow.1), channel_id=1, source_target_pairs={{0,16},{16,0},{1,17},{17,1},{2,18},{18,2},{3,19},{19,3},{4,20},{20... | collective-permute-start | bytes 98312 | tf_op jit(solution)/shard_map/ppermute | solution.py:195
  13.1 2.5 %collective-permute-done.1.got_ref = f32[2,32,128]{2,1,0:T(8,128)S(1)} collective-permute-done((f32[2,32,128]{2,1,0:T(8,128)S(1)}, f32[2,32,128]{2,1,0:T(8,128)S(1)}, u32[]{:S(2)}, u32[]{:S(2)}) %collective-permute-start.1) | collective-permute-done | bytes 32800 | tf_op jit(solution)/shard_map/ppermute | solution.py:195
  15.7 0.4 lower.1
  16.1 32.7 %all_to_all.5.got_ref = bf16[32,64,256]{2,1,0:T(8,128)(2,1)S(1)} all-to-all(bf16[32,64,256]{2,1,0:T(8,128)(2,1)S(1)} %lower.1), channel_id=1, replica_groups=mesh['section'=2,'dp'=16] {'section','dp'}, dimensions={0} | all-to-all | bytes 2097152 | tf_op jit(solution)/shard_map/all_to_all | solution.py:206
  48.8 0.8 %total.1 = (f32[1,32,256]{2,1,0:T(8,128)}, f32[1,32,256]{2,1,0:T(8,128)}) custom-call(bf16[32,64,256]{2,1,0:T(8,128)(2,1)S(1)} %all_to_all.5.got_ref), custom_call_target="tpu_custom_call" | custom-call | tf_op jit(solution)/shard_map/total/pallas_call | solution.py:207
Async XLA Ops:
  1.6 9.7 %collective-permute-start = (bf16[32,4096]{1,0:T(8,128)(2,1)S(1)}, bf16[32,4096]{1,0:T(8,128)(2,1)S(1)}, u32[]{:S(2)}, u32[]{:S(2)}) collective-permute-start(bf16[32,4096]{1,0:T(8,128)(2,1)S(1)} %dynamic-slice_bitcast_fusion), channel_id=1, source_target_pairs={{0,16},{16,0},{1,17},{17,1},{2,18},{18,2},{3,19},{19,3},{4,20},{20... | collective-permute-start | bytes 786440 | tf_op jit(solution)/shard_map/ppermute | solution.py:161
  4.6 1.0 %copy-start = (bf16[1,2,32,4096]{3,2,1,0:T(8,128)(2,1)S(1)}, bf16[1,2,32,4096]{3,2,1,0:T(8,128)(2,1)}, u32[]{:S(2)}) copy-start(bf16[1,2,32,4096]{3,2,1,0:T(8,128)(2,1)} %w_out.1) | copy-start | bytes 1572868
  5.7 1.0 %copy-start.1 = (bf16[1,2,4096,32]{2,3,1,0:T(8,128)(2,1)S(1)}, bf16[1,2,4096,32]{2,3,1,0:T(8,128)(2,1)}, u32[]{:S(2)}) copy-start(bf16[1,2,4096,32]{2,3,1,0:T(8,128)(2,1)} %param.8) | copy-start | bytes 1572868
  6.7 0.8 %copy-start.2 = (f32[1,2,4096]{2,1,0:T(2,128)S(1)}, f32[1,2,4096]{2,1,0:T(2,128)}, u32[]{:S(2)}) copy-start(f32[1,2,4096]{2,1,0:T(2,128)} %gains.1) | copy-start | bytes 98308
  11.7 4.0 %collective-permute-start.1 = (f32[2,32,128]{2,1,0:T(8,128)S(1)}, f32[2,32,128]{2,1,0:T(8,128)S(1)}, u32[]{:S(2)}, u32[]{:S(2)}) collective-permute-start(f32[2,32,128]{2,1,0:T(8,128)S(1)} %flow.1), channel_id=1, source_target_pairs={{0,16},{16,0},{1,17},{17,1},{2,18},{18,2},{3,19},{19,3},{4,20},{20... | collective-permute-start | bytes 98312 | tf_op jit(solution)/shard_map/ppermute | solution.py:195

commit v2 on v1

--- a/solution.py
+++ b/solution.py
@@ -8,7 +8,7 @@
 from jax.sharding import PartitionSpec as P
 
 EPS = 1e-05
-VMEM_BYTES = 48 * 1024 * 1024
+VMEM_BYTES = 24 * 1024 * 1024
 F32 = jnp.float32
 BF16 = jnp.bfloat16
 
@@ -52,9 +52,19 @@
     return scale, pre
 
 
+def split_terms(share, index, das, xg_ref, act, flow_ref, keep_ref, send_ref):
+    rank = das.shape[0]
+    core = index % 2
+    for i in range(keep_ref.shape[0]):
+        for to_ref, number in ((keep_ref, core), (send_ref, 1 - core)):
+            cols = pl.ds(pl.multiple_of((2 * i + number) * share, share), share)
+            to_ref[i, 0:rank] = nn(das, xg_ref[:, cols]).astype(BF16)
+            to_ref[i, rank : 2 * rank] = nn(act, flow_ref[:, cols]).astype(BF16)
+
+
 def upper_kernel(
-    share, place_ref, saved, top, gains, w_in, w_out,
-    out_ref, flow_ref, xg0_ref, low_ref,
+    share, place_ref, index_ref, saved, top, gains, w_in, w_out,
+    keep_ref, send_ref, flow_ref, xg0_ref, low_ref,
     x1, x0, g, gain1, gain0, wi1, wi0, wo1, xg1, sems,
 ):
     place = place_ref[0]
@@ -101,13 +111,12 @@
     low_ref[0] = (pre0 * sig0).astype(BF16).astype(F32)
     low_ref[1] = slope0
     low_ref[2] = jnp.broadcast_to(row0, raw0.shape)
-    for i, c in enumerate(range(0, width, step)):
+    for c in range(0, width, step):
         cols = slice(c, c + step)
         dn = tn(da1, wi1[:, cols]) * gain1[:, cols]
         flow = g[:, cols].astype(F32) + scale1 * dn - pull * x1[:, cols].astype(F32)
         flow_ref[:, cols] = flow.astype(BF16)
-        out_ref[i, 0:rank] = nn(das1, xg1[:, cols]).astype(BF16)
-        out_ref[i, rank : 2 * rank] = nn(act1, g[:, cols]).astype(BF16)
+    split_terms(share, index_ref[0], das1, xg1, act1, g, keep_ref, send_ref)
 
 
 def flow_kernel(share, flow_ref, w_ref, low_ref, send_ref):
@@ -120,23 +129,25 @@
     send_ref[1] = delta
 
 
-def lower_kernel(share, _, flow_ref, xg0_ref, low_ref, got_ref, out_ref):
-    width = flow_ref.shape[1]
-    rank = got_ref.shape[1]
+def lower_kernel(share, index_ref, flow_ref, xg0_ref, low_ref, got_ref, keep_ref, send_ref):
     act0 = got_ref[0].astype(BF16)
     da0 = (got_ref[1] * low_ref[1]).astype(BF16)
     das0 = (da0.astype(F32) * low_ref[2]).astype(BF16)
-    for i, c in enumerate(range(0, width, share)):
-        cols = slice(c, c + share)
-        out_ref[i, 0:rank] = nn(das0, xg0_ref[:, cols]).astype(BF16)
-        out_ref[i, rank : 2 * rank] = nn(act0, flow_ref[:, cols]).astype(BF16)
-
-
-def sum_kernel(got_ref, in_ref, out_ref):
+    split_terms(share, index_ref[0], das0, xg0_ref, act0, flow_ref, keep_ref, send_ref)
+
+
+def chip_kernel(keep1, got1, keep0, got0, out_ref):
+    chips = keep1.shape[0]
+    for i in range(chips):
+        out_ref[i] = (keep0[i].astype(F32) + got0[i].astype(F32)).astype(BF16)
+        out_ref[chips + i] = (keep1[i].astype(F32) + got1[i].astype(F32)).astype(BF16)
+
+
+def total_kernel(got, in_ref, out_ref):
     rank = in_ref.shape[1]
-    total = got_ref[0].astype(F32)
-    for i in range(1, got_ref.shape[0]):
-        total += got_ref[i].astype(F32)
+    total = got[0].astype(F32)
+    for i in range(1, got.shape[0]):
+        total += got[i].astype(F32)
     in_ref[0] = total[0:rank]
     out_ref[0] = total[rank : 2 * rank]
 
@@ -157,23 +168,34 @@
     share = width // count
     swap = [(0, 1), (1, 0)]
     adapter_in = jnp.swapaxes(adapter_in, 2, 3)
-    any_space = pl.BlockSpec(memory_space=pl.ANY)
     partner_out = lax.ppermute(
         lax.dynamic_index_in_dim(adapter_out[0], place, 0, keepdims=False), "section", swap
     )
-    blocks = jax.ShapeDtypeStruct((2 * count, 2 * rank, share), BF16)
+    index = lax.axis_index("dp")
+    saved, top_grad, gains, adapter_in, adapter_out = [
+        pltpu.with_memory_space_constraint(a, pltpu.HBM)
+        for a in (saved, top_grad, gains, adapter_in, adapter_out)
+    ]
+    place_ref = place.astype(jnp.int32)[None]
+    index_ref = index.astype(jnp.int32)[None]
+    scalar = pl.BlockSpec(memory_space=pltpu.SMEM)
+    chips = count // 2
+    blocks = jax.ShapeDtypeStruct((chips, 2 * rank, share), BF16)
     wide = jax.ShapeDtypeStruct((tokens, width), BF16)
-    out, flow, xg0, low = pl.pallas_call(
+
+    def swapped(array, over_section, bits):
+        pairs = [
+            (s * count + d, (s ^ over_section) * count + (d ^ bits))
+            for s in range(2)
+            for d in range(count)
+        ]
+        return lax.ppermute(array, ("section", "dp"), pairs)
+
+    keep1, send1, flow, xg0, low = pl.pallas_call(
         partial(upper_kernel, share),
-        grid=(1,),
-        in_specs=[pl.BlockSpec(memory_space=pltpu.SMEM)] + [any_space] * 5,
-        out_specs=[
-            pl.BlockSpec((count, 2 * rank, share), lambda i: (1, 0, 0)),
-            whole(),
-            whole(),
-            whole(),
-        ],
-        out_shape=[blocks, wide, wide, jax.ShapeDtypeStruct((3, rank, tokens), F32)],
+        in_specs=[scalar] * 2 + [pl.BlockSpec(memory_space=pltpu.HBM)] * 5,
+        out_specs=[whole()] * 5,
+        out_shape=[blocks, blocks, wide, wide, jax.ShapeDtypeStruct((3, rank, tokens), F32)],
         scratch_shapes=[pltpu.VMEM((tokens, width), BF16)] * 3
         + [pltpu.VMEM((1, width), F32)] * 2
         + [pltpu.VMEM((rank, width), BF16)] * 3
@@ -183,7 +205,8 @@
             flops=12 * tokens * width * rank, bytes_accessed=12 * tokens * width, transcendentals=0
         ),
         name="upper",
-    )(place.astype(jnp.int32)[None], saved, top_grad, gains, adapter_in, adapter_out)
+    )(place_ref, index_ref, saved, top_grad, gains, adapter_in, adapter_out)
+    got1 = swapped(send1, 0, 1)
     send = pl.pallas_call(
         partial(flow_kernel, share),
         in_specs=[whole()] * 3,
@@ -193,25 +216,35 @@
         name="flow",
     )(flow, partner_out, low)
     got = lax.ppermute(send, "section", swap)
-    out = pl.pallas_call(
+    keep0, send0 = pl.pallas_call(
         partial(lower_kernel, share),
-        grid=(1,),
-        in_specs=[any_space] + [whole()] * 4,
-        out_specs=pl.BlockSpec((count, 2 * rank, share), lambda i: (0, 0, 0)),
-        out_shape=blocks,
-        input_output_aliases={0: 0},
+        in_specs=[scalar] + [whole()] * 4,
+        out_specs=[whole()] * 2,
+        out_shape=[blocks] * 2,
         compiler_params=params(),
         name="lower",
-    )(out, flow, xg0, low, got)
-    got = lax.all_to_all(out, ("section", "dp"), 0, 0, tiled=True)
+    )(index_ref, flow, xg0, low, got)
+    got0 = swapped(send0, 0, 1)
+    sums = pl.pallas_call(
+        chip_kernel,
+        in_specs=[whole()] * 4,
+        out_specs=whole(),
+        out_shape=jax.ShapeDtypeStruct((2 * chips, 2 * rank, share), BF16),
+        compiler_params=params(),
+        name="chip",
+    )(keep1, got1, keep0, got0)
+    groups = [[s * count + 2 * i + core for s in range(2) for i in range(chips)] for core in range(2)]
+    sums = lax.all_to_all(
+        sums, ("section", "dp"), 0, 0, axis_index_groups=groups, tiled=True
+    )
     total_in, total_out = pl.pallas_call(
-        sum_kernel,
+        total_kernel,
         in_specs=[whole()],
         out_specs=[whole()] * 2,
         out_shape=[jax.ShapeDtypeStruct((1, rank, share), F32)] * 2,
         compiler_params=params(),
         name="total",
-    )(got)
+    )(sums)
     return (jnp.swapaxes(total_in, 1, 2), total_out)
 
 
@@ -296,7 +329,9 @@
 
     def run(saved, *others):
         share = saved.shape[3] // mesh.shape["dp"]
+        count = mesh.shape["dp"]
         pair = mesh.shape["section"] == 2 and share % 128 == 0
+        pair = pair and count % 2 == 0
         on_device = pair_on_device if pair else relay_on_device
         return jax.shard_map(
             on_device, mesh=mesh, in_specs=in_specs, out_specs=out_specs, check_vma=False

time: 49.9 us -> 40.7 us (0.82)
  blocking collectives: 32.7 us -> 22.4 us
  waiting for transfers between devices: 2.55 us -> 5.79 us
  local copies, waits for them, and re-layouts: 3.81 us -> 0.97 us
    all_to_all x1, blocking collectives: 32.7 us -> 22.4 us  [pair_on_device(): lax.all_to_all(sums, ('section', 'dp'), 0, 0, axis_index_groups=groups, t...]
    unnamed x6 -> x0, local copies, waits for them, and re-layouts: 2.84 us -> none
    ppermute x1, waiting for transfers between devices: 0.01 us -> 2.11 us  [pair_on_device(): lax.ppermute(lax.dynamic_index_in_dim(adapter_out[0], place, 0, keepdims=...]
    ppermute x0 -> x2, waiting for transfers between devices: none -> 1.51 us  [swapped(): return lax.ppermute(array, ('section', 'dp'), pairs)]
    pallas_call x3 -> x4, Pallas kernels: 5 us -> 5.41 us  [the longest x1 4.19 us: pair_on_device(): pl.pallas_call(partial(upper_kernel, share), in_specs=[scalar] * 2 + [pl....]
  transfers between devices with their start and end apart: 2 -> 4, of which waited for: 1 -> 3; matrix products, arithmetic and copies ran while one was open for 0% -> 0% of each run, Pallas kernels for 8% -> 11%
where the time goes in v2:
time: 40.7 us; the launch traced here: 40.5 us
  blocking collectives  22.4 us (55%)
  Pallas kernels  5.82 us (14%)
  waiting for transfers between devices  5.79 us (14%)
  starting transfers between devices  4.86 us (12%)
  local copies, waits for them, and re-layouts  0.97 us (2%)
  between operations  0.68 us (2%)
    all_to_all x1, blocking collectives, pair_on_device(): lax.all_to_all(sums, ('section', 'dp'), 0, 0, axis_index_groups=groups, t...  22.4 us
    pallas_call x1, Pallas kernels, pair_on_device(): pl.pallas_call(partial(upper_kernel, share), in_specs=[scalar] * 2 + [pl....  4.19 us
    ppermute x1, starting transfers between devices, pair_on_device(): lax.ppermute(lax.dynamic_index_in_dim(adapter_out[0], place, 0, keepdims=...  3 us
    ppermute x1, waiting for transfers between devices, pair_on_device(): got = lax.ppermute(send, 'section', swap)  2.17 us
    ppermute x1, waiting for transfers between devices, pair_on_device(): lax.ppermute(lax.dynamic_index_in_dim(adapter_out[0], place, 0, keepdims=...  2.11 us
    ppermute x1, starting transfers between devices, pair_on_device(): got = lax.ppermute(send, 'section', swap)  1.78 us
    ppermute x2, waiting for transfers between devices, swapped(): return lax.ppermute(array, ('section', 'dp'), pairs)  1.51 us
    squeeze x1, local copies, waits for them, and re-layouts, pair_on_device(): lax.dynamic_index_in_dim(adapter_out[0], place, 0, keepdims=False)  0.97 us
  transfers between devices with their start and end apart: 4, of which 3 were waited for; matrix products, arithmetic and copies ran while one was open for 0% of the time, Pallas kernels for 11%

profile of v2, /device:TPU:0, one launch (start us, length us, event | category | flops | bytes accessed | tf_op | source)
XLA Modules:
  0.0 40.5 jit_solution(11314260661214938887)
XLA Ops:
  0.6 1.0 %dynamic-slice_bitcast_fusion = bf16[32,4096]{1,0:T(8,128)(2,1)S(1)} fusion(bf16[1,2,32,4096]{3,2,1,0:T(8,128)(2,1)} %w_out.1, s32[]{:T(128)S(6)} %select_n.4), kind=kLoop, calls=%fused_computation | loop fusion | bytes 524292 | tf_op jit(solution)/shard_map/jit(dynamic_index_in_dim)/squeeze | solution.py:172
  1.6 3.0 %collective-permute-start.1 = (bf16[32,4096]{1,0:T(8,128)(2,1)S(1)}, bf16[32,4096]{1,0:T(8,128)(2,1)S(1)}, u32[]{:S(2)}, u32[]{:S(2)}) collective-permute-start(bf16[32,4096]{1,0:T(8,128)(2,1)S(1)} %dynamic-slice_bitcast_fusion), channel_id=1, source_target_pairs={{0,16},{16,0},{1,17},{17,1},{2,18},{18,2},{3,19},{19,3},{4,20},{20... | collective-permute-start | bytes 786440 | tf_op jit(solution)/shard_map/ppermute | solution.py:171
  4.6 4.2 %upper.1 = (bf16[8,64,256]{2,1,0:T(8,128)(2,1)S(1)}, bf16[8,64,256]{2,1,0:T(8,128)(2,1)S(1)}, bf16[128,4096]{1,0:T(8,128)(2,1)S(1)}, bf16[128,4096]{1,0:T(8,128)(2,1)S(1)}, f32[3,32,128]{2,1,0:T(8,128)S(1)}) custom-call(s32[1]{0:T(128)} %bitcast.place_ref, s32[1]{0:T(128)} %bitcast.1.index_ref, bf16[1,2,128,4096]{3,2,1,0:T(8,128)(2,1)} %saved.1, ...), custom_call_target="tpu_custom_call" | custom-call | flops 201326592 | bytes 6291456 | tf_op jit(solution)/shard_map/upper/pallas_call | solution.py:194
  8.8 2.1 %collective-permute-done.1.w_ref = bf16[32,4096]{1,0:T(8,128)(2,1)S(1)} collective-permute-done((bf16[32,4096]{1,0:T(8,128)(2,1)S(1)}, bf16[32,4096]{1,0:T(8,128)(2,1)S(1)}, u32[]{:S(2)}, u32[]{:S(2)}) %collective-permute-start.1) | collective-permute-done | bytes 262176 | tf_op jit(solution)/shard_map/ppermute | solution.py:171
  10.9 0.4 %flow.1 = f32[2,32,128]{2,1,0:T(8,128)S(1)} custom-call(bf16[128,4096]{1,0:T(8,128)(2,1)S(1)} %get-tuple-element.13.flow_ref, bf16[32,4096]{1,0:T(8,128)(2,1)S(1)} %collective-permute-done.1.w_ref, f32[3,32,128]{2,1,0:T(8,128)S(1)} %get-tuple-element.15.low_ref), custom_call_target="tpu_custom_call" | custom-call | tf_op jit(solution)/shard_map/flow/pallas_call | solution.py:210
  11.3 1.8 %collective-permute-start.2 = (f32[2,32,128]{2,1,0:T(8,128)S(1)}, f32[2,32,128]{2,1,0:T(8,128)S(1)}, u32[]{:S(2)}, u32[]{:S(2)}) collective-permute-start(f32[2,32,128]{2,1,0:T(8,128)S(1)} %flow.1), channel_id=1, source_target_pairs={{0,16},{16,0},{1,17},{17,1},{2,18},{18,2},{3,19},{19,3},{4,20},{20... | collective-permute-start | bytes 98312 | tf_op jit(solution)/shard_map/ppermute | solution.py:218
  13.1 0.0 collective-permute-start
  13.1 2.2 %collective-permute-done.2.got_ref = f32[2,32,128]{2,1,0:T(8,128)S(1)} collective-permute-done((f32[2,32,128]{2,1,0:T(8,128)S(1)}, f32[2,32,128]{2,1,0:T(8,128)S(1)}, u32[]{:S(2)}, u32[]{:S(2)}) %collective-permute-start.2) | collective-permute-done | bytes 32800 | tf_op jit(solution)/shard_map/ppermute | solution.py:218
  15.3 0.4 lower.1
  15.7 0.1 collective-permute-start.3
  15.8 0.0 collective-permute-done.got1
  15.8 1.5 %collective-permute-done.3.got0 = bf16[8,64,256]{2,1,0:T(8,128)(2,1)S(1)} collective-permute-done((bf16[8,64,256]{2,1,0:T(8,128)(2,1)S(1)}, bf16[8,64,256]{2,1,0:T(8,128)(2,1)S(1)}, u32[]{:S(2)}, u32[]{:S(2)}) %collective-permute-start.3) | collective-permute-done | bytes 262176 | tf_op jit(solution)/shard_map/ppermute | solution.py:192
  17.3 0.1 chip.1
  17.4 22.4 %all_to_all.5.got = bf16[16,64,256]{2,1,0:T(8,128)(2,1)S(1)} all-to-all(bf16[16,64,256]{2,1,0:T(8,128)(2,1)S(1)} %chip.1), channel_id=1, replica_groups={{0,2,4,6,8,10,12,14,16,18,20,22,24,26,28,30},{1,3,5,7,9,11,13,15,17,19,..., dimensions={0} | all-to-all | bytes 1048576 | tf_op jit(solution)/shard_map/all_to_all | solution.py:237
  39.8 0.7 %total.1 = (f32[1,32,256]{2,1,0:T(8,128)}, f32[1,32,256]{2,1,0:T(8,128)}) custom-call(bf16[16,64,256]{2,1,0:T(8,128)(2,1)S(1)} %all_to_all.5.got), custom_call_target="tpu_custom_call" | custom-call | tf_op jit(solution)/shard_map/total/pallas_call | solution.py:240
Async XLA Ops:
  1.6 9.3 %collective-permute-start.1 = (bf16[32,4096]{1,0:T(8,128)(2,1)S(1)}, bf16[32,4096]{1,0:T(8,128)(2,1)S(1)}, u32[]{:S(2)}, u32[]{:S(2)}) collective-permute-start(bf16[32,4096]{1,0:T(8,128)(2,1)S(1)} %dynamic-slice_bitcast_fusion), channel_id=1, source_target_pairs={{0,16},{16,0},{1,17},{17,1},{2,18},{18,2},{3,19},{19,3},{4,20},{20... | collective-permute-start | bytes 786440 | tf_op jit(solution)/shard_map/ppermute | solution.py:171
  11.3 4.0 %collective-permute-start.2 = (f32[2,32,128]{2,1,0:T(8,128)S(1)}, f32[2,32,128]{2,1,0:T(8,128)S(1)}, u32[]{:S(2)}, u32[]{:S(2)}) collective-permute-start(f32[2,32,128]{2,1,0:T(8,128)S(1)} %flow.1), channel_id=1, source_target_pairs={{0,16},{16,0},{1,17},{17,1},{2,18},{18,2},{3,19},{19,3},{4,20},{20... | collective-permute-start | bytes 98312 | tf_op jit(solution)/shard_map/ppermute | solution.py:218
  13.1 2.7 %collective-permute-start = (bf16[8,64,256]{2,1,0:T(8,128)(2,1)S(1)}, bf16[8,64,256]{2,1,0:T(8,128)(2,1)S(1)}, u32[]{:S(2)}, u32[]{:S(2)}) collective-permute-start(bf16[8,64,256]{2,1,0:T(8,128)(2,1)S(1)} %get-tuple-element.12), channel_id=1, source_target_pairs={{0,1},{1,0},{2,3},{3,2},{4,5},{5,4},{6,7},{7,6},{8,9},{9,8},{10,11... | collective-permute-start | bytes 786440 | tf_op jit(solution)/shard_map/ppermute | solution.py:192
  15.7 1.6 %collective-permute-start.3 = (bf16[8,64,256]{2,1,0:T(8,128)(2,1)S(1)}, bf16[8,64,256]{2,1,0:T(8,128)(2,1)S(1)}, u32[]{:S(2)}, u32[]{:S(2)}) collective-permute-start(bf16[8,64,256]{2,1,0:T(8,128)(2,1)S(1)} %get-tuple-element.17), channel_id=1, source_target_pairs={{0,1},{1,0},{2,3},{3,2},{4,5},{5,4},{6,7},{7,6},{8,9},{9,8},{10,11... | collective-permute-start | bytes 786440 | tf_op jit(solution)/shard_map/ppermute | solution.py:192

commit v3 on v2

v3 whole, which is shorter than its diff:
```python
from functools import partial

import jax
import jax.numpy as jnp
from jax import lax
from jax.experimental import pallas as pl
from jax.experimental.pallas import tpu as pltpu
from jax.sharding import PartitionSpec as P

EPS = 1e-05
VMEM_BYTES = 24 * 1024 * 1024
F32 = jnp.float32
BF16 = jnp.bfloat16


def nn(a, b):
    return lax.dot_general(a, b, (((1,), (0,)), ((), ())), preferred_element_type=F32)


def nt(a, b):
    return lax.dot_general(a, b, (((1,), (1,)), ((), ())), preferred_element_type=F32)


def tn(a, b):
    return lax.dot_general(a, b, (((0,), (0,)), ((), ())), preferred_element_type=F32)


def as_row(column):
    count = column.shape[0]
    return jnp.transpose(jnp.broadcast_to(column, (count, count)))[0:1, :]


def silu_slope(pre):
    sig = jax.nn.sigmoid(pre)
    return sig, sig * (1.0 + pre * (1.0 - sig))


def project(x_ref, gain_ref, w_ref, xg_ref, step):
    tokens, width = x_ref.shape
    squares = jnp.zeros((tokens, 128), F32)
    pre = jnp.zeros((w_ref.shape[0], tokens), F32)
    for c in range(0, width, step):
        x = x_ref[:, c : c + step].astype(F32)
        for k in range(0, step, 128):
            part = x[:, k : k + 128]
            squares += part * part
        xg = (x * gain_ref[:, c : c + step]).astype(BF16)
        xg_ref[:, c : c + step] = xg
        pre += nt(w_ref[:, c : c + step], xg)
    mean = jnp.sum(squares, axis=1, keepdims=True) * (1.0 / width)
    scale = lax.rsqrt(mean + EPS)
    return scale, pre


def fill(index, matrix, wide_ref, keep_ref, send_ref, first):
    count, _, share = keep_ref.shape[0] // 2, *keep_ref.shape[1:]
    core = index % 2
    for i in range(count):
        for to_ref, number in ((keep_ref, core), (send_ref, 1 - core)):
            cols = pl.ds(pl.multiple_of((2 * i + number) * share, share), share)
            to_ref[first + i] = nn(matrix, wide_ref[:, cols]).astype(BF16)


def start_all(sems, *pairs):
    copies = [pltpu.make_async_copy(a, b, sems.at[i]) for i, (a, b) in enumerate(pairs)]
    for copy in copies:
        copy.start()
    return copies


def front_kernel(step, place_ref, saved, gains, w_in, act_ref, low_ref, xg_ref, x, gain, wi, sems):
    lower = place_ref[0]
    copies = start_all(
        sems,
        (gains.at[0, pl.ds(lower, 1)], gain),
        (w_in.at[0, lower], wi),
        (saved.at[0, lower], x),
    )
    for copy in copies:
        copy.wait()
    scale, raw = project(x, gain, wi, xg_ref, step)
    row = as_row(scale)
    pre = raw * row
    sig, slope = silu_slope(pre)
    act_ref[...] = (pre * sig).astype(BF16)
    low_ref[0] = slope
    low_ref[1] = jnp.broadcast_to(row, raw.shape)


def upper_kernel(
    step, place_ref, saved, top, gains, w_in, w_out,
    flow_ref, xg_ref, das_ref, act_ref,
    x, g, gain, wi, wo, sems,
):
    upper = 1 - place_ref[0]
    copies = start_all(
        sems,
        (gains.at[0, pl.ds(upper, 1)], gain),
        (w_in.at[0, upper], wi),
        (saved.at[0, upper], x),
        (w_out.at[0, upper], wo),
        (top.at[upper], g),
    )
    width = x.shape[1]
    for copy in copies[0:3]:
        copy.wait()
    scale, raw = project(x, gain, wi, xg_ref, step)
    for copy in copies[3:5]:
        copy.wait()
    delta = jnp.zeros(raw.shape, F32)
    for c in range(0, width, step):
        delta += nt(wo[:, c : c + step], g[:, c : c + step])
    row = as_row(scale)
    pre = raw * row
    sig, slope = silu_slope(pre)
    da = (delta * slope).astype(BF16)
    daf = da.astype(F32)
    inner = jnp.sum(daf * pre, axis=0, keepdims=True) * (1.0 / width)
    act_ref[...] = (pre * sig).astype(BF16)
    das_ref[...] = (daf * row).astype(BF16)
    pull = jnp.transpose(jnp.broadcast_to(inner * row * row, (x.shape[0],) * 2))[:, 0:1]
    for c in range(0, width, step):
        cols = slice(c, c + step)
        dn = tn(da, wi[:, cols]) * gain[:, cols]
        flow = g[:, cols].astype(F32) + scale * dn - pull * x[:, cols].astype(F32)
        flow_ref[:, cols] = flow.astype(BF16)


def terms_kernel(
    place_ref, index_ref, flow_ref, xg1_ref, das1_ref, act1_ref, act0_ref, top,
    keep_out, send_out, keep_in, send_in,
    g, sems,
):
    index = index_ref[0]
    copy = pltpu.make_async_copy(top.at[1 - place_ref[0]], g, sems.at[0])
    copy.start()
    fill(index, act0_ref[...], flow_ref, keep_out, send_out, 0)
    chips = keep_out.shape[0] // 2
    copy.wait()
    fill(index, act1_ref[...], g, keep_out, send_out, chips)
    core = index % 2
    share = keep_in.shape[2]
    for i in range(chips):
        for to_ref, number in ((keep_in, core), (send_in, 1 - core)):
            cols = pl.ds(pl.multiple_of((2 * i + number) * share, share), share)
            to_ref[i] = nn(das1_ref[...], xg1_ref[:, cols]).astype(BF16)


def flow_kernel(step, flow_ref, w_ref, send_ref):
    width = flow_ref.shape[1]
    delta = jnp.zeros(send_ref.shape, F32)
    for c in range(0, width, step):
        delta += nt(w_ref[:, c : c + step], flow_ref[:, c : c + step])
    send_ref[...] = delta


def lower_kernel(index_ref, xg0_ref, low_ref, got_ref, keep1, send1, keep_ref, send_ref):
    da = (got_ref[...] * low_ref[0]).astype(BF16)
    das = (da.astype(F32) * low_ref[1]).astype(BF16)
    fill(index_ref[0], das, xg0_ref, keep_ref, send_ref, 0)
    chips = keep1.shape[0]
    keep_ref[chips : 2 * chips] = keep1[...]
    send_ref[chips : 2 * chips] = send1[...]


def halves_kernel(place_ref, keep, got, own_ref, send_ref):
    half = own_ref.shape[2]
    first = place_ref[0] == 0
    for i in range(keep.shape[0]):
        total = (keep[i].astype(F32) + got[i].astype(F32)).astype(BF16)
        left, right = total[:, 0:half], total[:, half : 2 * half]
        own_ref[i] = jnp.where(first, left, right)
        send_ref[i] = jnp.where(first, right, left)


def gather_kernel(keep, got, own, partner, out_ref):
    rank, half = own.shape[1:]
    for i in range(keep.shape[0]):
        total = (keep[i].astype(F32) + got[i].astype(F32)).astype(BF16)
        out_ref[i, 0:rank] = total[:, 0:half]
        out_ref[i, rank : 2 * rank] = total[:, half : 2 * half]
        out_ref[i, 2 * rank : 3 * rank] = (own[i].astype(F32) + partner[i].astype(F32)).astype(BF16)


def total_kernel(got, in_ref, out_ref):
    rank = in_ref.shape[1]
    half = in_ref.shape[2] // 2
    count = got.shape[0]

    def summed(numbers, first):
        return sum(got[i, first : first + rank].astype(F32) for i in numbers)

    in_ref[0, :, 0:half] = summed(range(count), 0)
    in_ref[0, :, half : 2 * half] = summed(range(count), rank)
    out_ref[0, :, 0:half] = summed(range(count // 2), 2 * rank)
    out_ref[0, :, half : 2 * half] = summed(range(count // 2, count), 2 * rank)


def params():
    return pltpu.CompilerParams(vmem_limit_bytes=VMEM_BYTES)


def whole():
    return pl.BlockSpec(memory_space=pltpu.VMEM)


def local(kernel, name, out_shapes, *operands, scratch=()):
    spaces = {"scalar": pltpu.SMEM, "far": pltpu.HBM, "near": pltpu.VMEM}
    out = pl.pallas_call(
        kernel,
        in_specs=[pl.BlockSpec(memory_space=spaces[kind]) for kind, _ in operands],
        out_specs=[pl.BlockSpec(memory_space=pltpu.VMEM)] * len(out_shapes),
        out_shape=[jax.ShapeDtypeStruct(shape, dtype) for shape, dtype in out_shapes],
        scratch_shapes=list(scratch),
        compiler_params=pltpu.CompilerParams(vmem_limit_bytes=VMEM_BYTES),
        name=name,
    )(*[array for _, array in operands])
    return out if len(out) > 1 else out[0]


def near(*arrays):
    return [("near", array) for array in arrays]


def pair_on_device(saved, top_grad, gains, adapter_in, adapter_out):
    count = lax.axis_size("dp")
    tokens, width = saved.shape[2:]
    rank = adapter_in.shape[3]
    share = width // count
    half = share // 2
    chips = count // 2
    place = ("scalar", lax.axis_index("section").astype(jnp.int32)[None])
    index = ("scalar", lax.axis_index("dp").astype(jnp.int32)[None])
    saved, top, gains, w_in, w_out = [
        ("far", pltpu.with_memory_space_constraint(a, pltpu.HBM))
        for a in (saved, top_grad, gains, jnp.swapaxes(adapter_in, 2, 3), adapter_out)
    ]

    def swapped(array, over_section, bits):
        pairs = [
            (s * count + d, (s ^ over_section) * count + (d ^ bits))
            for s in range(2)
            for d in range(count)
        ]
        return lax.ppermute(array, ("section", "dp"), pairs)

    wide = pltpu.VMEM((tokens, width), BF16)
    thin = pltpu.VMEM((rank, width), BF16)
    gain = pltpu.VMEM((1, width), F32)
    sems = pltpu.SemaphoreType.DMA
    wide_out = ((tokens, width), BF16)
    thin_out = ((rank, tokens), BF16)

    mine = lax.dynamic_index_in_dim(
        adapter_out[0], lax.axis_index("section"), 0, keepdims=False
    )
    partner_out = swapped(mine, 1, 0)
    act0, low, xg0 = local(
        partial(front_kernel, share), "front",
        [thin_out, ((2, rank, tokens), F32), wide_out],
        place, saved, gains, w_in, scratch=[wide, gain, thin, sems((3,))],
    )
    partner_act0 = swapped(act0, 1, 0)
    flow, xg1, das1, act1 = local(
        partial(upper_kernel, share), "upper",
        [wide_out, wide_out, thin_out, thin_out],
        place, saved, top, gains, w_in, w_out,
        scratch=[wide, wide, gain, thin, thin, sems((5,))],
    )
    both = ((2 * chips, rank, share), BF16)
    one = ((chips, rank, share), BF16)
    core = lax.axis_index("dp") % 2

    def parts(m, w):
        t = nn(m, w).astype(BF16).reshape(rank, chips, 2, share).transpose(2, 1, 0, 3)
        k = lax.dynamic_index_in_dim(t, core, 0, keepdims=False)
        return k, lax.dynamic_index_in_dim(t, 1 - core, 0, keepdims=False)

    k0, s0 = parts(partner_act0, flow)
    g1 = lax.dynamic_index_in_dim(top_grad, 1 - lax.axis_index("section"), 0, keepdims=False)
    k1, s1 = parts(act1, g1)
    keep1, send1 = parts(das1, xg1)
    keep_out = jnp.concatenate([k0, k1])
    send_out = jnp.concatenate([s0, s1])
    got_out = swapped(send_out, 0, 1)
    delta = nt(partner_out, flow)
    partner_delta = swapped(delta, 1, 0)
    halves = ((2 * chips, rank, half), BF16)
    total_out = (keep_out.astype(F32) + got_out.astype(F32)).astype(BF16)
    first = lax.axis_index("section") == 0
    left, right = total_out[:, :, 0:half], total_out[:, :, half:]
    own_half = jnp.where(first, left, right)
    send_half = jnp.where(first, right, left)
    partner_half = swapped(send_half, 1, 0)
    da = (partner_delta * low[0]).astype(BF16)
    das = (da.astype(F32) * low[1]).astype(BF16)
    t0 = nn(das, xg0).astype(BF16).reshape(rank, chips, 2, share).transpose(2, 1, 0, 3)
    core = lax.axis_index("dp") % 2
    k0 = lax.dynamic_index_in_dim(t0, core, 0, keepdims=False)
    s0 = lax.dynamic_index_in_dim(t0, 1 - core, 0, keepdims=False)
    keep_in = jnp.concatenate([k0, keep1])
    send_in = jnp.concatenate([s0, send1])
    got_in = swapped(send_in, 0, 1)
    total_in = (keep_in.astype(F32) + got_in.astype(F32)).astype(BF16)
    sums = jnp.concatenate(
        [
            total_in[:, :, 0:half],
            total_in[:, :, half:],
            (own_half.astype(F32) + partner_half.astype(F32)).astype(BF16),
        ],
        1,
    )
    groups = [
        [s * count + 2 * i + core for s in range(2) for i in range(chips)] for core in range(2)
    ]
    sums = lax.all_to_all(sums, ("section", "dp"), 0, 0, axis_index_groups=groups, tiled=True)
    sums = sums.astype(F32)
    total_in = jnp.concatenate([sums[:, 0:rank].sum(0), sums[:, rank:2*rank].sum(0)], 1)[None]
    total_out = jnp.concatenate([sums[:chips, 2*rank:].sum(0), sums[chips:, 2*rank:].sum(0)], 1)[None]
    return (jnp.swapaxes(total_in, 1, 2), total_out)


def section_back(x, gain, weight_in, weight_out, upstream):
    xf = x.astype(F32)
    scale = lax.rsqrt(jnp.mean(xf * xf, axis=-1, keepdims=True) + EPS)
    normed = xf * scale
    hidden = (normed * gain).astype(BF16)
    pre = jnp.dot(hidden, weight_in, preferred_element_type=F32)
    sig, slope = silu_slope(pre)
    active = (pre * sig).astype(BF16)
    delta_act = jnp.dot(upstream, weight_out.T, preferred_element_type=F32)
    delta_pre = (delta_act * slope).astype(BF16)
    delta_norm = jnp.dot(delta_pre, weight_in.T, preferred_element_type=F32) * gain
    inner = jnp.mean(delta_norm * normed, axis=-1, keepdims=True)
    result = (upstream.astype(F32) + scale * (delta_norm - normed * inner)).astype(BF16)
    term_in = jnp.dot(hidden.T, delta_pre, preferred_element_type=F32)
    term_out = jnp.dot(active.T, upstream, preferred_element_type=F32)
    return (result, term_in, term_out)


def relay_on_device(saved, top_grad, gains, adapter_in, adapter_out):
    sections = lax.axis_size("section")
    place = lax.axis_index("section")
    width = top_grad.shape[2]
    rank = adapter_in.shape[3]
    zero_in = jnp.zeros((width, rank), F32)
    zero_out = jnp.zeros((rank, width), F32)

    def step(turn, flows, sums):
        leaving, added = [], []
        for replica in (0, 1):
            serves = place == (sections - 1 - turn if replica == 0 else turn)
            result, term_in, term_out = lax.cond(
                serves,
                partial(
                    section_back,
                    saved[0, replica],
                    gains[0, replica],
                    adapter_in[0, replica],
                    adapter_out[0, replica],
                ),
                lambda flow: (flow, zero_in, zero_out),
                flows[replica],
            )
            leaving.append(result)
            added += [sums[2 * replica] + term_in, sums[2 * replica + 1] + term_out]
        return leaving, added

    down = [(i, i - 1) for i in range(1, sections)]
    up = [(i, i + 1) for i in range(sections - 1)]

    def turn_and_pass(turn, carry):
        leaving, sums = step(turn, carry[0], carry[1])
        return (
            [lax.ppermute(leaving[0], "section", down), lax.ppermute(leaving[1], "section", up)],
            sums,
        )

    start = ([top_grad[0], top_grad[1]], [zero_in, zero_out, zero_in, zero_out])
    flows, sums = lax.fori_loop(0, sections - 1, turn_and_pass, start)
    _, sums = step(sections - 1, flows, sums)
    shares = [
        lax.psum_scatter(term, "dp", scatter_dimension=i % 2, tiled=True)
        for i, term in enumerate(sums)
    ]
    mirror = [(i, sections - 1 - i) for i in range(sections)]
    total_in = shares[0] + lax.ppermute(shares[2], "section", mirror)
    total_out = shares[1] + lax.ppermute(shares[3], "section", mirror)
    return (total_in[None], total_out[None])


def solution(mesh):
    in_specs = (
        P("section", None, "dp", None),
        P(None, "dp", None),
        P("section", None, None),
        P("section", None, None, None),
        P("section", None, None, None),
    )
    out_specs = (P("section", "dp", None), P("section", None, "dp"))

    def run(saved, *others):
        share = saved.shape[3] // mesh.shape["dp"]
        count = mesh.shape["dp"]
        pair = mesh.shape["section"] == 2 and share % 256 == 0
        pair = pair and count % 2 == 0
        on_device = pair_on_device if pair else relay_on_device
        return jax.shard_map(
            on_device, mesh=mesh, in_specs=in_specs, out_specs=out_specs, check_vma=False
        )(saved, *others)

    return run
```

time: 40.7 us -> 53.8 us (1.32)
  local copies, waits for them, and re-layouts: 0.97 us -> 11.6 us
  matrix products: 0 us -> 5.1 us
  blocking collectives: 22.4 us -> 18.4 us
  other arithmetic: 0 us -> 3.3 us
  waiting for transfers between devices: 5.79 us -> 3.6 us
    ppermute x2 -> x6, starting transfers between devices: 0.07 us -> 5.2 us  [swapped(): return lax.ppermute(array, ('section', 'dp'), pairs)]
    dot_general x0 -> x5, matrix products: none -> 5.1 us  [the longest x4 3.7 us: nn(): lax.dot_general(a, b, (((1,), (0,)), ((), ())), preferred_element_type=F32)]
    ppermute x2 -> x0, starting transfers between devices: 4.78 us -> none  [the longest x1 3 us: pair_on_device(): lax.ppermute(lax.dynamic_index_in_dim(adapter_out[0], place, 0, keepdims=...]
    ppermute x2 -> x0, waiting for transfers between devices: 4.28 us -> none  [the longest x1 2.17 us: pair_on_device(): got = lax.ppermute(send, 'section', swap)]
    all_to_all x1, blocking collectives: 22.4 us -> 18.4 us  [pair_on_device(): lax.all_to_all(sums, ('section', 'dp'), 0, 0, axis_index_groups=groups, t...]
    another operation x0 -> x2, local copies, waits for them, and re-layouts: none -> 4.01 us  [run(): jax.shard_map(on_device, mesh=mesh, in_specs=in_specs, out_specs=out_spec...]
    reshape x0 -> x4, local copies, waits for them, and re-layouts: none -> 3.34 us  [the longest x3 3.15 us: parts(): nn(m, w).astype(BF16).reshape(rank, chips, 2, share).transpose(2, 1, 0, 3)]
    unnamed x0 -> x8, local copies, waits for them, and re-layouts: none -> 2.52 us
  transfers between devices with their start and end apart: 4 -> 6, of which waited for: 3 -> 2; matrix products, arithmetic and copies ran while one was open for 0% -> 32% of each run, Pallas kernels for 11% -> 10%
where the time goes in v3:
time: 53.8 us; the launch traced here: 53.3 us
  blocking collectives  18.4 us (34%)
  local copies, waits for them, and re-layouts  11.6 us (22%)
  Pallas kernels  5.32 us (10%)
  starting transfers between devices  5.2 us (10%)
  matrix products  5.1 us (9%)
  waiting for transfers between devices  3.6 us (7%)
  other arithmetic  3.3 us (6%)
  between operations  0.87 us (2%)
    all_to_all x1, blocking collectives, pair_on_device(): lax.all_to_all(sums, ('section', 'dp'), 0, 0, axis_index_groups=groups, t...  18.4 us
    pallas_call x2, Pallas kernels, local(): pl.pallas_call(kernel, in_specs=[pl.BlockSpec(memory_space=spaces[kind])...  5.32 us
    ppermute x6, starting transfers between devices, swapped(): return lax.ppermute(array, ('section', 'dp'), pairs)  5.2 us
    another operation x2, local copies, waits for them, and re-layouts, run(): jax.shard_map(on_device, mesh=mesh, in_specs=in_specs, out_specs=out_spec...  4.01 us
    dot_general x4, matrix products, nn(): lax.dot_general(a, b, (((1,), (0,)), ((), ())), preferred_element_type=F32)  3.7 us
    ppermute x6, waiting for transfers between devices, swapped(): return lax.ppermute(array, ('section', 'dp'), pairs)  3.6 us
    reshape x3, local copies, waits for them, and re-layouts, parts(): nn(m, w).astype(BF16).reshape(rank, chips, 2, share).transpose(2, 1, 0, 3)  3.15 us
    unnamed x8, local copies, waits for them, and re-layouts  2.52 us
  transfers between devices with their start and end apart: 6, of which 2 were waited for; matrix products, arithmetic and copies ran while one was open for 32% of the time, Pallas kernels for 10%

profile of v3, /device:TPU:0, one launch (start us, length us, event | category | flops | bytes accessed | tf_op | source)
XLA Modules:
  0.0 53.3 jit_solution(17712783134317734767)
XLA Ops:
  0.6 1.7 %dynamic-slice_bitcast_fusion = bf16[32,4096]{1,0:T(8,128)(2,1)} fusion(bf16[1,2,32,4096]{3,2,1,0:T(8,128)(2,1)} %w_out.1, s32[]{:T(128)S(6)} %select_n.42), kind=kLoop, calls=%fused_computation.14 | loop fusion | bytes 524292 | tf_op jit(solution)/shard_map/jit(dynamic_index_in_dim)/squeeze | solution.py:254
  2.3 2.9 %collective-permute-start = (bf16[32,4096]{1,0:T(8,128)(2,1)}, bf16[32,4096]{1,0:T(8,128)(2,1)}, u32[]{:S(2)}, u32[]{:S(2)}) collective-permute-start(bf16[32,4096]{1,0:T(8,128)(2,1)} %dynamic-slice_bitcast_fusion), channel_id=1, source_target_pairs={{0,16},{1,17},{2,18},{3,19},{4,20},{5,21},{6,22},{7,23},{8,24},{9,... | collective-permute-start | bytes 786440 | tf_op jit(solution)/shard_map/ppermute | solution.py:245
  5.2 1.9 %front.1 = (bf16[32,128]{1,0:T(8,128)(2,1)S(1)}, f32[2,32,128]{2,1,0:T(8,128)S(1)}, bf16[128,4096]{1,0:T(8,128)(2,1)S(1)}) custom-call(s32[1]{0:T(128)} %bitcast.1.place_ref, bf16[1,2,128,4096]{3,2,1,0:T(8,128)(2,1)} %saved.3, f32[1,2,4096]{2,1,0:T(2,128)} %gains.3, bf16[1,2,32,4096]{3,2,1,0:T(8,128)(2,1)} %bitcast.73), custom_call_target="tpu_custom_call" | custom-call | tf_op jit(solution)/shard_map/front/pallas_call | solution.py:209
  7.1 0.1 collective-permute-start.3
  7.2 3.4 %upper.1 = (bf16[128,4096]{1,0:T(8,128)(2,1)S(1)}, bf16[128,4096]{1,0:T(8,128)(2,1)S(1)}, bf16[32,128]{1,0:T(8,128)(2,1)S(1)}, bf16[32,128]{1,0:T(8,128)(2,1)S(1)}) custom-call(s32[1]{0:T(128)} %bitcast.1.place_ref, bf16[1,2,128,4096]{3,2,1,0:T(8,128)(2,1)} %saved.3, bf16[2,128,4096]{2,1,0:T(8,128)(2,1)} %top.1, f32[1,2,4096]{2,1,0:T(2,128)} %gains.3, ...), custom_call_target="tpu_custom_call" | custom-call | tf_op jit(solution)/shard_map/upper/pallas_call | solution.py:209
  10.6 2.2 %convolution_convert_fusion = bf16[32,4096]{1,0:T(8,128)(2,1)} fusion(bf16[32,128]{1,0:T(8,128)(2,1)S(1)} %get-tuple-element.15, bf16[2,128,4096]{2,1,0:T(8,128)(2,1)} %top.1, s32[]{:T(128)S(6)} %select_n.47), kind=kOutput, calls=%fused_computation | convolution fusion | flops 33685504 | bytes 1318916 | tf_op jit(solution)/shard_map/dot_general | solution.py:17
  12.8 1.1 %reshape.21 = bf16[32,8,2,256]{3,2,1,0:T(2,128)(2,1)S(1)} reshape(bf16[32,4096]{1,0:T(8,128)(2,1)} %convolution_convert_fusion) | data formatting | bytes 524288 | tf_op jit(solution)/shard_map/reshape | solution.py:275
  14.0 0.0 collective-permute-done.3
  14.0 1.0 %convolution_convert_fusion.1 = bf16[32,4096]{1,0:T(8,128)(2,1)} fusion(bf16[32,128]{1,0:T(8,128)(2,1)S(1)} %collective-permute-done.3, bf16[128,4096]{1,0:T(8,128)(2,1)S(1)} %get-tuple-element.9), kind=kOutput, calls=%fused_computation.1 | convolution fusion | flops 33685504 | bytes 1318912 | tf_op jit(solution)/shard_map/dot_general | solution.py:17
  15.0 1.8 %reshape.20 = bf16[32,8,2,256]{3,2,1,0:T(2,128)(2,1)} reshape(bf16[32,4096]{1,0:T(8,128)(2,1)} %convolution_convert_fusion.1) | data formatting | bytes 524288 | tf_op jit(solution)/shard_map/reshape | solution.py:275
  16.8 2.9 %constant_dynamic-slice_fusion.2 = (bf16[32,8,1,256]{3,2,1,0:T(2,128)(2,1)}, bf16[32,8,1,256]{3,2,1,0:T(2,128)(2,1)S(1)}, bf16[32,8,1,256]{3,2,1,0:T(2,128)(2,1)S(1)}, bf16[32,8,1,256]{3,2,1,0:T(2,128)(2,1)}) fusion(bf16[32,8,2,256]{3,2,1,0:T(2,128)(2,1)S(1)} %reshape.21, s32[]{:T(128)S(6)} %select_n.44, s32[]{:T(128)S(6)} %select_n.45, ...), kind=kLoop, calls=%fused_computation.34 | loop fusion | bytes 1048584 | tf_op jit(solution)/shard_map/dynamic-slice.6 | solution.py:408
  19.7 0.1 copy.38
  19.8 0.1 copy.39
  19.9 0.7 %pad_maximum_fusion.2 = bf16[16,32,256]{2,1,0:T(8,128)(2,1)} fusion(bf16[8,32,256]{2,1,0:T(8,128)(2,1)S(1)} %bitcast.79, bf16[8,32,256]{2,1,0:T(8,128)(2,1)S(1)} %bitcast.81), kind=kLoop, calls=%fused_computation.12 | loop fusion | flops 131072 | bytes 524288 | tf_op jit(solution)/shard_map/concatenate | solution.py:284
  20.6 0.0 collective-permute-start.4
  20.6 0.3 convolution_convert_fusion.2
  20.9 0.2 reshape.19
  21.1 1.0 %copy.40 = bf16[32,8,1,256]{3,0,1,2:T(8,128)(2,1)S(1)} copy(bf16[32,8,1,256]{3,2,1,0:T(2,128)(2,1)} %get-tuple-element.28) | data formatting | bytes 262144
  22.1 1.0 %copy.41 = bf16[32,8,1,256]{3,0,1,2:T(8,128)(2,1)S(1)} copy(bf16[32,8,1,256]{3,2,1,0:T(2,128)(2,1)} %get-tuple-element.31) | data formatting | bytes 262144
  23.1 0.0 collective-permute-done
  23.2 1.4 %fusion.7 = f32[32,128]{1,0:T(8,128)S(1)} fusion(bf16[32,4096]{1,0:T(8,128)(2,1)} %collective-permute-done, bf16[128,4096]{1,0:T(8,128)(2,1)S(1)} %get-tuple-element.9), kind=kOutput, calls=%fused_computation.42 | convolution fusion | flops 33554432 | bytes 1327104 | tf_op jit(solution)/shard_map/dot_general | solution.py:21
  24.6 2.0 %collective-permute-start.1 = (f32[32,128]{1,0:T(8,128)S(1)}, f32[32,128]{1,0:T(8,128)S(1)}, u32[]{:S(2)}, u32[]{:S(2)}) collective-permute-start(f32[32,128]{1,0:T(8,128)S(1)} %fusion.7), channel_id=1, source_target_pairs={{0,16},{1,17},{2,18},{3,19},{4,20},{5,21},{6,22},{7,23},{8,24},{9,... | collective-permute-start | bytes 49160 | tf_op jit(solution)/shard_map/ppermute | solution.py:245
  26.6 0.0 collective-permute-done.4
  26.6 1.0 %add_convert_fusion = bf16[16,32,256]{2,1,0:T(8,128)(2,1)S(1)} fusion(bf16[16,32,256]{2,1,0:T(8,128)(2,1)} %collective-permute-done.4, bf16[8,32,256]{2,1,0:T(8,128)(2,1)S(1)} %bitcast.75, bf16[8,32,256]{2,1,0:T(8,128)(2,1)S(1)} %bitcast.76), kind=kLoop, calls=%fused_computation.6 | loop fusion | flops 655360 | bytes 786432 | tf_op jit(solution)/shard_map/convert_element_type | solution.py:289
  27.6 0.1 collective-permute-start.5
  27.7 0.6 %collective-permute-done.1 = f32[32,128]{1,0:T(8,128)S(1)} collective-permute-done((f32[32,128]{1,0:T(8,128)S(1)}, f32[32,128]{1,0:T(8,128)S(1)}, u32[]{:S(2)}, u32[]{:S(2)}) %collective-permute-start.1) | collective-permute-done | bytes 16416 | tf_op jit(solution)/shard_map/ppermute | solution.py:245
  28.3 0.3 convolution_convert_fusion.3
  28.6 0.2 reshape.18
  28.8 1.1 %constant_dynamic-slice_fusion.6 = (bf16[32,8,1,256]{3,2,1,0:T(2,128)(2,1)S(1)}, bf16[32,8,1,256]{3,2,1,0:T(2,128)(2,1)S(1)}, bf16[32,8,1,256]{3,2,1,0:T(2,128)(2,1)S(1)}, bf16[32,8,1,256]{3,2,1,0:T(2,128)(2,1)S(1)}) fusion(bf16[32,8,2,256]{3,2,1,0:T(2,128)(2,1)S(1)} %reshape.19, s32[]{:T(128)S(6)} %select_n.44, s32[]{:T(128)S(6)} %select_n.45, ...), kind=kLoop, calls=%fused_computation.39 | loop fusion | bytes 1048584 | tf_op jit(solution)/shard_map/dynamic-slice.2 | solution.py:408
  29.9 0.1 copy.42
  30.0 0.1 copy.43
  30.1 0.1 collective-permute-start.2
  30.2 0.1 copy.44
  30.2 0.1 copy.45
  30.3 3.0 %collective-permute-done.5 = bf16[16,32,128]{2,1,0:T(8,128)(2,1)S(1)} collective-permute-done((bf16[16,32,128]{2,1,0:T(8,128)(2,1)S(1)}, bf16[16,32,128]{2,1,0:T(8,128)(2,1)S(1)}, u32[]{:S(2)}, u32[]{:S(2)}) %collective-permute-start.5) | collective-permute-done | bytes 131104 | tf_op jit(solution)/shard_map/ppermute | solution.py:245
  33.3 0.1 add_convert_fusion.2
  33.4 0.0 collective-permute-done.2
  33.4 0.1 add_convert_fusion.1
  33.6 18.4 %all_to_all.5 = bf16[16,96,128]{2,1,0:T(8,128)(2,1)S(1)} all-to-all(bf16[16,96,128]{2,1,0:T(8,128)(2,1)S(1)} %pad_maximum_fusion), channel_id=1, replica_groups={{0,2,4,6,8,10,12,14,16,18,20,22,24,26,28,30},{1,3,5,7,9,11,13,15,17,19,..., dimensions={0} | all-to-all | bytes 786432 | tf_op jit(solution)/shard_map/all_to_all | solution.py:316
  51.9 0.1 convert_element_type.67
  52.1 0.6 %maximum_bitcast_fusion.1 = f32[1,32,256]{2,1,0:T(8,128)} fusion(f32[32,128]{1,0:T(8,128)S(1)} %get-tuple-element.17, f32[32,128]{1,0:T(8,128)S(1)} %get-tuple-element.16), kind=kLoop, calls=%fused_computation.27 | loop fusion | flops 8192 | bytes 65536 | tf_op jit(solution)/shard_map/broadcast_in_dim | solution.py:319
  52.7 0.6 %maximum_bitcast_fusion = f32[1,256,32]{1,2,0:T(8,128)} fusion(f32[32,128]{1,0:T(8,128)S(1)} %get-tuple-element.19, f32[32,128]{1,0:T(8,128)S(1)} %get-tuple-element.18), kind=kLoop, calls=%fused_computation.26 | loop fusion | flops 8192 | bytes 65536 | tf_op jit(solution)/shard_map/transpose | solution.py:320
  (6 shorter events, 0.2 us)
Async XLA Ops:
  2.3 20.9 %collective-permute-start = (bf16[32,4096]{1,0:T(8,128)(2,1)}, bf16[32,4096]{1,0:T(8,128)(2,1)}, u32[]{:S(2)}, u32[]{:S(2)}) collective-permute-start(bf16[32,4096]{1,0:T(8,128)(2,1)} %dynamic-slice_bitcast_fusion), channel_id=1, source_target_pairs={{0,16},{1,17},{2,18},{3,19},{4,20},{5,21},{6,22},{7,23},{8,24},{9,... | collective-permute-start | bytes 786440 | tf_op jit(solution)/shard_map/ppermute | solution.py:245
  7.1 6.9 %collective-permute-start.3 = (bf16[32,128]{1,0:T(8,128)(2,1)S(1)}, bf16[32,128]{1,0:T(8,128)(2,1)S(1)}, u32[]{:S(2)}, u32[]{:S(2)}) collective-permute-start(bf16[32,128]{1,0:T(8,128)(2,1)S(1)} %get-tuple-element.14), channel_id=1, source_target_pairs={{0,16},{1,17},{2,18},{3,19},{4,20},{5,21},{6,22},{7,23},{8,24},{9,... | collective-permute-start | bytes 24584 | tf_op jit(solution)/shard_map/ppermute | solution.py:245
  20.6 6.0 %collective-permute-start.4 = (bf16[16,32,256]{2,1,0:T(8,128)(2,1)}, bf16[16,32,256]{2,1,0:T(8,128)(2,1)}, u32[]{:S(2)}, u32[]{:S(2)}) collective-permute-start(bf16[16,32,256]{2,1,0:T(8,128)(2,1)} %pad_maximum_fusion.2), channel_id=1, source_target_pairs={{0,1},{1,0},{2,3},{3,2},{4,5},{5,4},{6,7},{7,6},{8,9},{9,8},{10,11... | collective-permute-start | bytes 786440 | tf_op jit(solution)/shard_map/ppermute | solution.py:245
  24.6 3.8 %collective-permute-start.1 = (f32[32,128]{1,0:T(8,128)S(1)}, f32[32,128]{1,0:T(8,128)S(1)}, u32[]{:S(2)}, u32[]{:S(2)}) collective-permute-start(f32[32,128]{1,0:T(8,128)S(1)} %fusion.7), channel_id=1, source_target_pairs={{0,16},{1,17},{2,18},{3,19},{4,20},{5,21},{6,22},{7,23},{8,24},{9,... | collective-permute-start | bytes 49160 | tf_op jit(solution)/shard_map/ppermute | solution.py:245
  27.6 5.7 %collective-permute-start.5 = (bf16[16,32,128]{2,1,0:T(8,128)(2,1)S(1)}, bf16[16,32,128]{2,1,0:T(8,128)(2,1)S(1)}, u32[]{:S(2)}, u32[]{:S(2)}) collective-permute-start(bf16[16,32,128]{2,1,0:T(8,128)(2,1)S(1)} %broadcast_select_fusion), channel_id=1, source_target_pairs={{0,16},{1,17},{2,18},{3,19},{4,20},{5,21},{6,22},{7,23},{8,24},{9,... | collective-permute-start | bytes 393224 | tf_op jit(solution)/shard_map/ppermute | solution.py:245
  30.1 3.3 %collective-permute-start.2 = (bf16[16,32,256]{2,1,0:T(8,128)(2,1)S(1)}, bf16[16,32,256]{2,1,0:T(8,128)(2,1)S(1)}, u32[]{:S(2)}, u32[]{:S(2)}) collective-permute-start(bf16[16,32,256]{2,1,0:T(8,128)(2,1)S(1)} %pad_maximum_fusion.1), channel_id=1, source_target_pairs={{0,1},{1,0},{2,3},{3,2},{4,5},{5,4},{6,7},{7,6},{8,9},{9,8},{10,11... | collective-permute-start | bytes 786440 | tf_op jit(solution)/shard_map/ppermute | solution.py:245

commit v4 on v2

--- a/solution.py
+++ b/solution.py
@@ -64,7 +64,7 @@
 
 def upper_kernel(
     share, place_ref, index_ref, saved, top, gains, w_in, w_out,
-    keep_ref, send_ref, flow_ref, xg0_ref, low_ref,
+    keep_ref, send_ref, flow_ref, xg0_ref, act0_ref, low_ref,
     x1, x0, g, gain1, gain0, wi1, wi0, wo1, xg1, sems,
 ):
     place = place_ref[0]
@@ -108,9 +108,9 @@
     row0 = as_row(scale0)
     pre0 = raw0 * row0
     sig0, slope0 = silu_slope(pre0)
-    low_ref[0] = (pre0 * sig0).astype(BF16).astype(F32)
-    low_ref[1] = slope0
-    low_ref[2] = jnp.broadcast_to(row0, raw0.shape)
+    act0_ref[...] = (pre0 * sig0).astype(BF16)
+    low_ref[0] = slope0
+    low_ref[1] = jnp.broadcast_to(row0, raw0.shape)
     for c in range(0, width, step):
         cols = slice(c, c + step)
         dn = tn(da1, wi1[:, cols]) * gain1[:, cols]
@@ -119,35 +119,73 @@
     split_terms(share, index_ref[0], das1, xg1, act1, g, keep_ref, send_ref)
 
 
-def flow_kernel(share, flow_ref, w_ref, low_ref, send_ref):
-    width = flow_ref.shape[1]
-    rank = w_ref.shape[0]
-    delta = jnp.zeros((rank, flow_ref.shape[0]), F32)
-    for c in range(0, width, share):
-        delta += nt(w_ref[:, c : c + share], flow_ref[:, c : c + share])
-    send_ref[0] = low_ref[0]
-    send_ref[1] = delta
+def pick_kernel(place_ref, index_ref, w_out, out_ref, sems):
+    half = out_ref.shape[1]
+    cols = pl.ds(pl.multiple_of((index_ref[0] % 2) * half, half), half)
+    copy = pltpu.make_async_copy(w_out.at[0, place_ref[0], :, cols], out_ref, sems.at[0])
+    copy.start()
+    copy.wait()
+
+
+def flow_kernel(share, index_ref, flow_ref, own_ref, other_ref, act0_ref, send_ref):
+    half = own_ref.shape[1]
+    core = index_ref[0] % 2
+    delta = jnp.zeros(act0_ref.shape, F32)
+    for w_ref, number in ((own_ref, core), (other_ref, 1 - core)):
+        for c in range(0, half, share):
+            cols = pl.ds(pl.multiple_of(number * half + c, share), share)
+            delta += nt(w_ref[:, c : c + share], flow_ref[:, cols])
+    send_ref[0] = act0_ref[...]
+    send_ref[1] = delta.astype(BF16)
 
 
 def lower_kernel(share, index_ref, flow_ref, xg0_ref, low_ref, got_ref, keep_ref, send_ref):
-    act0 = got_ref[0].astype(BF16)
-    da0 = (got_ref[1] * low_ref[1]).astype(BF16)
-    das0 = (da0.astype(F32) * low_ref[2]).astype(BF16)
-    split_terms(share, index_ref[0], das0, xg0_ref, act0, flow_ref, keep_ref, send_ref)
-
-
-def chip_kernel(keep1, got1, keep0, got0, out_ref):
-    chips = keep1.shape[0]
-    for i in range(chips):
-        out_ref[i] = (keep0[i].astype(F32) + got0[i].astype(F32)).astype(BF16)
-        out_ref[chips + i] = (keep1[i].astype(F32) + got1[i].astype(F32)).astype(BF16)
-
-
-def total_kernel(got, in_ref, out_ref):
+    da0 = (got_ref[1].astype(F32) * low_ref[0]).astype(BF16)
+    das0 = (da0.astype(F32) * low_ref[1]).astype(BF16)
+    split_terms(share, index_ref[0], das0, xg0_ref, got_ref[0], flow_ref, keep_ref, send_ref)
+
+
+def plane_kernel(
+    place_ref, index_ref, keep1, got1, keep0, got0, own_ref, first_ref, second_ref, across
+):
+    row = (index_ref[0] // 2) % 2
+
+    def order(near, far, along_x, along_y):
+        for i in range(own_ref.shape[0]):
+            for to_ref, (keep, got), number in (
+                (across, far, 1 - row),
+                (along_x, far, row),
+                (along_y, near, 1 - row),
+                (own_ref, near, row),
+            ):
+                block = 2 * i + number
+                to_ref[i] = (keep[block].astype(F32) + got[block].astype(F32)).astype(BF16)
+
+    for place, near, far in (
+        (1, (keep1, got1), (keep0, got0)),
+        (0, (keep0, got0), (keep1, got1)),
+    ):
+        for core, ways in ((0, (second_ref, first_ref)), (1, (first_ref, second_ref))):
+            pl.when((place_ref[0] == place) & (index_ref[0] % 2 == core))(
+                partial(order, near, far, *ways)
+            )
+
+
+def layer_kernel(index_ref, own, got_a, got_b, got_c, *out_refs):
+    layer = index_ref[0] // 4
+    for k, out_ref in enumerate(out_refs):
+        block = layer ^ k
+        total = own[block].astype(F32) + got_a[block].astype(F32)
+        total += got_b[block].astype(F32) + got_c[block].astype(F32)
+        out_ref[...] = total.astype(BF16)
+
+
+def total_kernel(*refs):
+    *got, in_ref, out_ref = refs
     rank = in_ref.shape[1]
-    total = got[0].astype(F32)
-    for i in range(1, got.shape[0]):
-        total += got[i].astype(F32)
+    total = got[0][...].astype(F32)
+    for ref in got[1:]:
+        total += ref[...].astype(F32)
     in_ref[0] = total[0:rank]
     out_ref[0] = total[rank : 2 * rank]
 
@@ -166,36 +204,47 @@
     tokens, width = saved.shape[2:]
     rank = adapter_in.shape[3]
     share = width // count
-    swap = [(0, 1), (1, 0)]
     adapter_in = jnp.swapaxes(adapter_in, 2, 3)
-    partner_out = lax.ppermute(
-        lax.dynamic_index_in_dim(adapter_out[0], place, 0, keepdims=False), "section", swap
-    )
-    index = lax.axis_index("dp")
     saved, top_grad, gains, adapter_in, adapter_out = [
         pltpu.with_memory_space_constraint(a, pltpu.HBM)
         for a in (saved, top_grad, gains, adapter_in, adapter_out)
     ]
     place_ref = place.astype(jnp.int32)[None]
-    index_ref = index.astype(jnp.int32)[None]
+    index_ref = lax.axis_index("dp").astype(jnp.int32)[None]
     scalar = pl.BlockSpec(memory_space=pltpu.SMEM)
-    chips = count // 2
+    chips, layers = count // 2, count // 4
     blocks = jax.ShapeDtypeStruct((chips, 2 * rank, share), BF16)
+    fourth = jax.ShapeDtypeStruct((layers, 2 * rank, share), BF16)
+    block = jax.ShapeDtypeStruct((2 * rank, share), BF16)
     wide = jax.ShapeDtypeStruct((tokens, width), BF16)
 
-    def swapped(array, over_section, bits):
-        pairs = [
-            (s * count + d, (s ^ over_section) * count + (d ^ bits))
-            for s in range(2)
-            for d in range(count)
-        ]
+    def swapped(array, *ways):
+        pairs = []
+        for s in range(2):
+            for d in range(count):
+                over_section, bits = ways[d % len(ways)]
+                pairs.append((s * count + d, (s ^ over_section) * count + (d ^ bits)))
         return lax.ppermute(array, ("section", "dp"), pairs)
 
-    keep1, send1, flow, xg0, low = pl.pallas_call(
+    mine = pl.pallas_call(
+        pick_kernel,
+        in_specs=[scalar] * 2 + [pl.BlockSpec(memory_space=pltpu.HBM)],
+        out_specs=whole(),
+        out_shape=jax.ShapeDtypeStruct((rank, width // 2), BF16),
+        scratch_shapes=[pltpu.SemaphoreType.DMA((1,))],
+        compiler_params=params(),
+        name="pick",
+    )(place_ref, index_ref, adapter_out)
+    partner_half = swapped(mine, (1, 0))
+    keep1, send1, flow, xg0, act0, low = pl.pallas_call(
         partial(upper_kernel, share),
         in_specs=[scalar] * 2 + [pl.BlockSpec(memory_space=pltpu.HBM)] * 5,
-        out_specs=[whole()] * 5,
-        out_shape=[blocks, blocks, wide, wide, jax.ShapeDtypeStruct((3, rank, tokens), F32)],
+        out_specs=[whole()] * 6,
+        out_shape=[
+            blocks, blocks, wide, wide,
+            jax.ShapeDtypeStruct((rank, tokens), BF16),
+            jax.ShapeDtypeStruct((2, rank, tokens), F32),
+        ],
         scratch_shapes=[pltpu.VMEM((tokens, width), BF16)] * 3
         + [pltpu.VMEM((1, width), F32)] * 2
         + [pltpu.VMEM((rank, width), BF16)] * 3
@@ -206,16 +255,18 @@
         ),
         name="upper",
     )(place_ref, index_ref, saved, top_grad, gains, adapter_in, adapter_out)
-    got1 = swapped(send1, 0, 1)
+    partner_half, flow = lax.optimization_barrier((partner_half, flow))
+    partner_other = swapped(partner_half, (0, 1))
+    got1 = swapped(send1, (0, 1))
     send = pl.pallas_call(
         partial(flow_kernel, share),
-        in_specs=[whole()] * 3,
+        in_specs=[scalar] + [whole()] * 4,
         out_specs=whole(),
-        out_shape=jax.ShapeDtypeStruct((2, rank, tokens), F32),
+        out_shape=jax.ShapeDtypeStruct((2, rank, tokens), BF16),
         compiler_params=params(),
         name="flow",
-    )(flow, partner_out, low)
-    got = lax.ppermute(send, "section", swap)
+    )(index_ref, flow, partner_half, partner_other, act0)
+    got = swapped(send, (1, 0))
     keep0, send0 = pl.pallas_call(
         partial(lower_kernel, share),
         in_specs=[scalar] + [whole()] * 4,
@@ -224,27 +275,35 @@
         compiler_params=params(),
         name="lower",
     )(index_ref, flow, xg0, low, got)
-    got0 = swapped(send0, 0, 1)
-    sums = pl.pallas_call(
-        chip_kernel,
-        in_specs=[whole()] * 4,
-        out_specs=whole(),
-        out_shape=jax.ShapeDtypeStruct((2 * chips, 2 * rank, share), BF16),
-        compiler_params=params(),
-        name="chip",
-    )(keep1, got1, keep0, got0)
-    groups = [[s * count + 2 * i + core for s in range(2) for i in range(chips)] for core in range(2)]
-    sums = lax.all_to_all(
-        sums, ("section", "dp"), 0, 0, axis_index_groups=groups, tiled=True
-    )
+    got0 = swapped(send0, (0, 1))
+    own, first, second, across = pl.pallas_call(
+        plane_kernel,
+        in_specs=[scalar] * 2 + [whole()] * 4,
+        out_specs=[whole()] * 4,
+        out_shape=[fourth] * 4,
+        compiler_params=params(),
+        name="plane",
+    )(place_ref, index_ref, keep1, got1, keep0, got0)
+    first = swapped(first, (0, 2), (1, 0))
+    second = swapped(second, (1, 0), (0, 2))
+    across = swapped(across, (1, 2))
+    mine, *others = pl.pallas_call(
+        layer_kernel,
+        in_specs=[scalar] + [whole()] * 4,
+        out_specs=[whole()] * layers,
+        out_shape=[block] * layers,
+        compiler_params=params(),
+        name="layer",
+    )(index_ref, own, first, second, across)
+    others = [swapped(other, (0, 4 * k)) for k, other in enumerate(others, 1)]
     total_in, total_out = pl.pallas_call(
         total_kernel,
-        in_specs=[whole()],
+        in_specs=[whole()] * layers,
         out_specs=[whole()] * 2,
         out_shape=[jax.ShapeDtypeStruct((1, rank, share), F32)] * 2,
         compiler_params=params(),
         name="total",
-    )(sums)
+    )(mine, *others[::-1])
     return (jnp.swapaxes(total_in, 1, 2), total_out)
 
 
@@ -331,7 +390,7 @@
         share = saved.shape[3] // mesh.shape["dp"]
         count = mesh.shape["dp"]
         pair = mesh.shape["section"] == 2 and share % 128 == 0
-        pair = pair and count % 2 == 0
+        pair = pair and count >= 4 and count & (count - 1) == 0
         on_device = pair_on_device if pair else relay_on_device
         return jax.shard_map(
             on_device, mesh=mesh, in_specs=in_specs, out_specs=out_specs, check_vma=False

time: 40.7 us -> 35.3 us (0.87)
  blocking collectives: 22.4 us -> 0 us
  waiting for transfers between devices: 5.79 us -> 15.5 us
  starting transfers between devices: 4.86 us -> 12.1 us
  Pallas kernels: 5.82 us -> 6.81 us
  local copies, waits for them, and re-layouts: 0.97 us -> 0 us
    all_to_all x1 -> x0, blocking collectives: 22.4 us -> none  [pair_on_device(): lax.all_to_all(sums, ('section', 'dp'), 0, 0, axis_index_groups=groups, t...]
    ppermute x2 -> x11, waiting for transfers between devices: 1.51 us -> 15.5 us  [swapped(): return lax.ppermute(array, ('section', 'dp'), pairs)]
    ppermute x2 -> x11, starting transfers between devices: 0.07 us -> 12.1 us  [swapped(): return lax.ppermute(array, ('section', 'dp'), pairs)]
    ppermute x2 -> x0, starting transfers between devices: 4.78 us -> none  [the longest x1 3 us: pair_on_device(): lax.ppermute(lax.dynamic_index_in_dim(adapter_out[0], place, 0, keepdims=...]
    ppermute x2 -> x0, waiting for transfers between devices: 4.28 us -> none  [the longest x1 2.17 us: pair_on_device(): got = lax.ppermute(send, 'section', swap)]
    pallas_call x3 -> x5, Pallas kernels: 1.22 us -> 2.21 us  [the longest x1 0.92 us: pair_on_device(): pl.pallas_call(pick_kernel, in_specs=[scalar] * 2 + [pl.BlockSpec(memory_...]
    squeeze x1 -> x0, local copies, waits for them, and re-layouts: 0.97 us -> none  [pair_on_device(): lax.dynamic_index_in_dim(adapter_out[0], place, 0, keepdims=False)]
  transfers between devices with their start and end apart: 4 -> 11, of which waited for: 3 -> 7; matrix products, arithmetic and copies ran while one was open for 0% -> 0% of each run, Pallas kernels for 11% -> 13%
where the time goes in v4:
time: 35.3 us; the launch traced here: 35.1 us
  waiting for transfers between devices  15.5 us (44%)
  starting transfers between devices  12.1 us (34%)
  Pallas kernels  6.81 us (19%)
  between operations  0.71 us (2%)
    ppermute x11, waiting for transfers between devices, swapped(): return lax.ppermute(array, ('section', 'dp'), pairs)  15.5 us
    ppermute x11, starting transfers between devices, swapped(): return lax.ppermute(array, ('section', 'dp'), pairs)  12.1 us
    pallas_call x1, Pallas kernels, pair_on_device(): pl.pallas_call(partial(upper_kernel, share), in_specs=[scalar] * 2 + [pl....  4.19 us
    pallas_call x1, Pallas kernels, pair_on_device(): pl.pallas_call(pick_kernel, in_specs=[scalar] * 2 + [pl.BlockSpec(memory_...  0.92 us
  transfers between devices with their start and end apart: 11, of which 7 were waited for; matrix products, arithmetic and copies ran while one was open for 0% of the time, Pallas kernels for 13%

profile of v4, /device:TPU:0, one launch (start us, length us, event | category | flops | bytes accessed | tf_op | source)
XLA Modules:
  0.0 35.1 jit_solution(802213437889513539)
XLA Ops:
  0.6 0.9 %pick.1 = bf16[32,2048]{1,0:T(8,128)(2,1)S(1)} custom-call(s32[1]{0:T(128)} %bitcast.1.place_ref, s32[1]{0:T(128)} %bitcast.index_ref, bf16[1,2,32,4096]{3,2,1,0:T(8,128)(2,1)} %w_out.3), custom_call_target="tpu_custom_call" | custom-call | tf_op jit(solution)/shard_map/pick/pallas_call | solution.py:229
  1.6 3.0 %collective-permute-start.1 = (bf16[32,2048]{1,0:T(8,128)(2,1)S(1)}, bf16[32,2048]{1,0:T(8,128)(2,1)S(1)}, u32[]{:S(2)}, u32[]{:S(2)}) collective-permute-start(bf16[32,2048]{1,0:T(8,128)(2,1)S(1)} %pick.1), channel_id=1, source_target_pairs={{0,16},{1,17},{2,18},{3,19},{4,20},{5,21},{6,22},{7,23},{8,24},{9,... | collective-permute-start | bytes 393224 | tf_op jit(solution)/shard_map/ppermute | solution.py:227
  4.6 4.2 %upper.1 = (bf16[8,64,256]{2,1,0:T(8,128)(2,1)S(1)}, bf16[8,64,256]{2,1,0:T(8,128)(2,1)S(1)}, bf16[128,4096]{1,0:T(8,128)(2,1)S(1)}, bf16[128,4096]{1,0:T(8,128)...) custom-call(s32[1]{0:T(128)} %bitcast.1.place_ref, s32[1]{0:T(128)} %bitcast.index_ref, ...), custom_call_target="tpu_custom_call" | custom-call | flops 201326592 | bytes 6291456 | tf_op jit(solution)/shard_map/upper/pallas_call | solution.py:239
  8.8 0.0 collective-permute-done.1.own_ref
  8.8 0.1 collective-permute-start.2
  8.9 1.3 %collective-permute-done.2.other_ref = bf16[32,2048]{1,0:T(8,128)(2,1)S(1)} collective-permute-done((bf16[32,2048]{1,0:T(8,128)(2,1)S(1)}, bf16[32,2048]{1,0:T(8,128)(2,1)S(1)}, u32[]{:S(2)}, u32[]{:S(2)}) %collective-permute-start.2) | collective-permute-done | bytes 131104 | tf_op jit(solution)/shard_map/ppermute | solution.py:227
  10.2 0.4 %flow.1 = bf16[2,32,128]{2,1,0:T(8,128)(2,1)S(1)} custom-call(s32[1]{0:T(128)} %bitcast.index_ref, bf16[128,4096]{1,0:T(8,128)(2,1)S(1)} %get-tuple-element.25.flow_ref, bf16[32,2048]{1,0:T(8,128)(2,1)S(1)} %collective-permute-done.1.own_ref, bf16[32,2048]{1,0:T(8,128)(2,1)S(1)} %collective-permute-done.2.other_ref, ...), custom_call_target="tpu_custom_call" | custom-call | tf_op jit(solution)/shard_map/flow/pallas_call | solution.py:261
  10.6 1.0 %collective-permute-start.3 = (bf16[2,32,128]{2,1,0:T(8,128)(2,1)S(1)}, bf16[2,32,128]{2,1,0:T(8,128)(2,1)S(1)}, u32[]{:S(2)}, u32[]{:S(2)}) collective-permute-start(bf16[2,32,128]{2,1,0:T(8,128)(2,1)S(1)} %flow.1), channel_id=1, source_target_pairs={{0,16},{1,17},{2,18},{3,19},{4,20},{5,21},{6,22},{7,23},{8,24},{9,... | collective-permute-start | bytes 49160 | tf_op jit(solution)/shard_map/ppermute | solution.py:227
  11.6 0.0 collective-permute-start
  11.6 2.8 %collective-permute-done.3.got_ref = bf16[2,32,128]{2,1,0:T(8,128)(2,1)S(1)} collective-permute-done((bf16[2,32,128]{2,1,0:T(8,128)(2,1)S(1)}, bf16[2,32,128]{2,1,0:T(8,128)(2,1)S(1)}, u32[]{:S(2)}, u32[]{:S(2)}) %collective-permute-start.3) | collective-permute-done | bytes 16416 | tf_op jit(solution)/shard_map/ppermute | solution.py:227
  14.4 0.4 %lower.1 = (bf16[8,64,256]{2,1,0:T(8,128)(2,1)S(1)}, bf16[8,64,256]{2,1,0:T(8,128)(2,1)S(1)}) custom-call(s32[1]{0:T(128)} %bitcast.index_ref, bf16[128,4096]{1,0:T(8,128)(2,1)S(1)} %get-tuple-element.25.flow_ref, bf16[128,4096]{1,0:T(8,128)(2,1)S(1)} %get-tuple-element.26.xg0_ref, f32[2,32,128]{2,1,0:T(8,128)S(1)} %get-tuple-element.27.low_ref, ...), custom_call_target="tpu_custom_call" | custom-call | tf_op jit(solution)/shard_map/lower/pallas_call | solution.py:270
  14.8 0.1 collective-permute-start.4
  14.9 0.0 collective-permute-done.got1
  14.9 1.5 %collective-permute-done.4.got0 = bf16[8,64,256]{2,1,0:T(8,128)(2,1)S(1)} collective-permute-done((bf16[8,64,256]{2,1,0:T(8,128)(2,1)S(1)}, bf16[8,64,256]{2,1,0:T(8,128)(2,1)S(1)}, u32[]{:S(2)}, u32[]{:S(2)}) %collective-permute-start.4) | collective-permute-done | bytes 262176 | tf_op jit(solution)/shard_map/ppermute | solution.py:227
  16.4 0.1 plane.1
  16.6 1.6 %collective-permute-start.5 = (bf16[4,64,256]{2,1,0:T(8,128)(2,1)S(1)}, bf16[4,64,256]{2,1,0:T(8,128)(2,1)S(1)}, u32[]{:S(2)}, u32[]{:S(2)}) collective-permute-start(bf16[4,64,256]{2,1,0:T(8,128)(2,1)S(1)} %get-tuple-element.33), channel_id=1, source_target_pairs={{0,2},{1,17},{2,0},{3,19},{4,6},{5,21},{6,4},{7,23},{8,10},{9,25},... | collective-permute-start | bytes 393224 | tf_op jit(solution)/shard_map/ppermute | solution.py:227
  18.1 1.0 %collective-permute-start.6 = (bf16[4,64,256]{2,1,0:T(8,128)(2,1)S(1)}, bf16[4,64,256]{2,1,0:T(8,128)(2,1)S(1)}, u32[]{:S(2)}, u32[]{:S(2)}) collective-permute-start(bf16[4,64,256]{2,1,0:T(8,128)(2,1)S(1)} %get-tuple-element.34), channel_id=1, source_target_pairs={{0,16},{1,3},{2,18},{3,1},{4,20},{5,7},{6,22},{7,5},{8,24},{9,11},... | collective-permute-start | bytes 393224 | tf_op jit(solution)/shard_map/ppermute | solution.py:227
  19.1 1.0 %collective-permute-start.7 = (bf16[4,64,256]{2,1,0:T(8,128)(2,1)S(1)}, bf16[4,64,256]{2,1,0:T(8,128)(2,1)S(1)}, u32[]{:S(2)}, u32[]{:S(2)}) collective-permute-start(bf16[4,64,256]{2,1,0:T(8,128)(2,1)S(1)} %get-tuple-element.35), channel_id=1, source_target_pairs={{0,18},{1,19},{2,16},{3,17},{4,22},{5,23},{6,20},{7,21},{8,26},{9,... | collective-permute-start | bytes 393224 | tf_op jit(solution)/shard_map/ppermute | solution.py:227
  20.1 4.6 %collective-permute-done.5.got_a = bf16[4,64,256]{2,1,0:T(8,128)(2,1)S(1)} collective-permute-done((bf16[4,64,256]{2,1,0:T(8,128)(2,1)S(1)}, bf16[4,64,256]{2,1,0:T(8,128)(2,1)S(1)}, u32[]{:S(2)}, u32[]{:S(2)}) %collective-permute-start.5) | collective-permute-done | bytes 131104 | tf_op jit(solution)/shard_map/ppermute | solution.py:227
  24.7 0.0 collective-permute-done.6.got_b
  24.8 1.2 %collective-permute-done.7.got_c = bf16[4,64,256]{2,1,0:T(8,128)(2,1)S(1)} collective-permute-done((bf16[4,64,256]{2,1,0:T(8,128)(2,1)S(1)}, bf16[4,64,256]{2,1,0:T(8,128)(2,1)S(1)}, u32[]{:S(2)}, u32[]{:S(2)}) %collective-permute-start.7) | collective-permute-done | bytes 131104 | tf_op jit(solution)/shard_map/ppermute | solution.py:227
  25.9 0.1 layer.1
  26.0 3.7 %collective-permute-start.8 = (bf16[64,256]{1,0:T(8,128)(2,1)S(1)}, bf16[64,256]{1,0:T(8,128)(2,1)S(1)}, u32[]{:S(2)}, u32[]{:S(2)}) collective-permute-start(bf16[64,256]{1,0:T(8,128)(2,1)S(1)} %get-tuple-element.37), channel_id=1, source_target_pairs={{0,12},{1,13},{2,14},{3,15},{4,8},{5,9},{6,10},{7,11},{8,4},{9,5},... | collective-permute-start | bytes 98312 | tf_op jit(solution)/shard_map/ppermute | solution.py:227
  29.7 0.0 collective-permute-start.9
  29.7 0.8 %collective-permute-start.10 = (bf16[64,256]{1,0:T(8,128)(2,1)S(1)}, bf16[64,256]{1,0:T(8,128)(2,1)S(1)}, u32[]{:S(2)}, u32[]{:S(2)}) collective-permute-start(bf16[64,256]{1,0:T(8,128)(2,1)S(1)} %get-tuple-element.39), channel_id=1, source_target_pairs={{0,4},{1,5},{2,6},{3,7},{4,0},{5,1},{6,2},{7,3},{8,12},{9,13},{10,... | collective-permute-start | bytes 98312 | tf_op jit(solution)/shard_map/ppermute | solution.py:227
  30.4 1.4 %collective-permute-done.8.refs_1_ = bf16[64,256]{1,0:T(8,128)(2,1)S(1)} collective-permute-done((bf16[64,256]{1,0:T(8,128)(2,1)S(1)}, bf16[64,256]{1,0:T(8,128)(2,1)S(1)}, u32[]{:S(2)}, u32[]{:S(2)}) %collective-permute-start.8) | collective-permute-done | bytes 32800 | tf_op jit(solution)/shard_map/ppermute | solution.py:227
  31.8 2.7 %collective-permute-done.9.refs_2_ = bf16[64,256]{1,0:T(8,128)(2,1)S(1)} collective-permute-done((bf16[64,256]{1,0:T(8,128)(2,1)S(1)}, bf16[64,256]{1,0:T(8,128)(2,1)S(1)}, u32[]{:S(2)}, u32[]{:S(2)}) %collective-permute-start.9) | collective-permute-done | bytes 32800 | tf_op jit(solution)/shard_map/ppermute | solution.py:227
  34.5 0.0 collective-permute-done.10.refs_3_
  34.5 0.6 %total.1 = (f32[1,32,256]{2,1,0:T(8,128)}, f32[1,32,256]{2,1,0:T(8,128)}) custom-call(bf16[64,256]{1,0:T(8,128)(2,1)S(1)} %get-tuple-element.36.refs_0_, bf16[64,256]{1,0:T(8,128)(2,1)S(1)} %collective-permute-done.8.refs_1_, bf16[64,256]{1,0:T(8,128)(2,1)S(1)} %collective-permute-done.9.refs_2_, bf16[64,256]{1,0:T(8,128)(2,1)S(1)} %collective-permute-done.10.refs_3_), custom_call_target="tpu_custom_call" | custom-call | tf_op jit(solution)/shard_map/total/pallas_call | solution.py:299
Async XLA Ops:
  1.6 7.2 %collective-permute-start.1 = (bf16[32,2048]{1,0:T(8,128)(2,1)S(1)}, bf16[32,2048]{1,0:T(8,128)(2,1)S(1)}, u32[]{:S(2)}, u32[]{:S(2)}) collective-permute-start(bf16[32,2048]{1,0:T(8,128)(2,1)S(1)} %pick.1), channel_id=1, source_target_pairs={{0,16},{1,17},{2,18},{3,19},{4,20},{5,21},{6,22},{7,23},{8,24},{9,... | collective-permute-start | bytes 393224 | tf_op jit(solution)/shard_map/ppermute | solution.py:227
  8.8 1.4 %collective-permute-start.2 = (bf16[32,2048]{1,0:T(8,128)(2,1)S(1)}, bf16[32,2048]{1,0:T(8,128)(2,1)S(1)}, u32[]{:S(2)}, u32[]{:S(2)}) collective-permute-start(bf16[32,2048]{1,0:T(8,128)(2,1)S(1)} %collective-permute-done.1.own_ref), channel_id=1, source_target_pairs={{0,1},{1,0},{2,3},{3,2},{4,5},{5,4},{6,7},{7,6},{8,9},{9,8},{10,11... | collective-permute-start | bytes 393224 | tf_op jit(solution)/shard_map/ppermute | solution.py:227
  10.6 3.8 %collective-permute-start.3 = (bf16[2,32,128]{2,1,0:T(8,128)(2,1)S(1)}, bf16[2,32,128]{2,1,0:T(8,128)(2,1)S(1)}, u32[]{:S(2)}, u32[]{:S(2)}) collective-permute-start(bf16[2,32,128]{2,1,0:T(8,128)(2,1)S(1)} %flow.1), channel_id=1, source_target_pairs={{0,16},{1,17},{2,18},{3,19},{4,20},{5,21},{6,22},{7,23},{8,24},{9,... | collective-permute-start | bytes 49160 | tf_op jit(solution)/shard_map/ppermute | solution.py:227
  11.6 3.3 %collective-permute-start = (bf16[8,64,256]{2,1,0:T(8,128)(2,1)S(1)}, bf16[8,64,256]{2,1,0:T(8,128)(2,1)S(1)}, u32[]{:S(2)}, u32[]{:S(2)}) collective-permute-start(bf16[8,64,256]{2,1,0:T(8,128)(2,1)S(1)} %get-tuple-element.23), channel_id=1, source_target_pairs={{0,1},{1,0},{2,3},{3,2},{4,5},{5,4},{6,7},{7,6},{8,9},{9,8},{10,11... | collective-permute-start | bytes 786440 | tf_op jit(solution)/shard_map/ppermute | solution.py:227
  14.8 1.6 %collective-permute-start.4 = (bf16[8,64,256]{2,1,0:T(8,128)(2,1)S(1)}, bf16[8,64,256]{2,1,0:T(8,128)(2,1)S(1)}, u32[]{:S(2)}, u32[]{:S(2)}) collective-permute-start(bf16[8,64,256]{2,1,0:T(8,128)(2,1)S(1)} %get-tuple-element.31), channel_id=1, source_target_pairs={{0,1},{1,0},{2,3},{3,2},{4,5},{5,4},{6,7},{7,6},{8,9},{9,8},{10,11... | collective-permute-start | bytes 786440 | tf_op jit(solution)/shard_map/ppermute | solution.py:227
  16.6 8.2 %collective-permute-start.5 = (bf16[4,64,256]{2,1,0:T(8,128)(2,1)S(1)}, bf16[4,64,256]{2,1,0:T(8,128)(2,1)S(1)}, u32[]{:S(2)}, u32[]{:S(2)}) collective-permute-start(bf16[4,64,256]{2,1,0:T(8,128)(2,1)S(1)} %get-tuple-element.33), channel_id=1, source_target_pairs={{0,2},{1,17},{2,0},{3,19},{4,6},{5,21},{6,4},{7,23},{8,10},{9,25},... | collective-permute-start | bytes 393224 | tf_op jit(solution)/shard_map/ppermute | solution.py:227
  18.1 6.6 %collective-permute-start.6 = (bf16[4,64,256]{2,1,0:T(8,128)(2,1)S(1)}, bf16[4,64,256]{2,1,0:T(8,128)(2,1)S(1)}, u32[]{:S(2)}, u32[]{:S(2)}) collective-permute-start(bf16[4,64,256]{2,1,0:T(8,128)(2,1)S(1)} %get-tuple-element.34), channel_id=1, source_target_pairs={{0,16},{1,3},{2,18},{3,1},{4,20},{5,7},{6,22},{7,5},{8,24},{9,11},... | collective-permute-start | bytes 393224 | tf_op jit(solution)/shard_map/ppermute | solution.py:227
  19.1 6.8 %collective-permute-start.7 = (bf16[4,64,256]{2,1,0:T(8,128)(2,1)S(1)}, bf16[4,64,256]{2,1,0:T(8,128)(2,1)S(1)}, u32[]{:S(2)}, u32[]{:S(2)}) collective-permute-start(bf16[4,64,256]{2,1,0:T(8,128)(2,1)S(1)} %get-tuple-element.35), channel_id=1, source_target_pairs={{0,18},{1,19},{2,16},{3,17},{4,22},{5,23},{6,20},{7,21},{8,26},{9,... | collective-permute-start | bytes 393224 | tf_op jit(solution)/shard_map/ppermute | solution.py:227
  26.0 5.8 %collective-permute-start.8 = (bf16[64,256]{1,0:T(8,128)(2,1)S(1)}, bf16[64,256]{1,0:T(8,128)(2,1)S(1)}, u32[]{:S(2)}, u32[]{:S(2)}) collective-permute-start(bf16[64,256]{1,0:T(8,128)(2,1)S(1)} %get-tuple-element.37), channel_id=1, source_target_pairs={{0,12},{1,13},{2,14},{3,15},{4,8},{5,9},{6,10},{7,11},{8,4},{9,5},... | collective-permute-start | bytes 98312 | tf_op jit(solution)/shard_map/ppermute | solution.py:227
  29.7 4.8 %collective-permute-start.9 = (bf16[64,256]{1,0:T(8,128)(2,1)S(1)}, bf16[64,256]{1,0:T(8,128)(2,1)S(1)}, u32[]{:S(2)}, u32[]{:S(2)}) collective-permute-start(bf16[64,256]{1,0:T(8,128)(2,1)S(1)} %get-tuple-element.38), channel_id=1, source_target_pairs={{0,8},{1,9},{2,10},{3,11},{4,12},{5,13},{6,14},{7,15},{8,0},{9,1},... | collective-permute-start | bytes 98312 | tf_op jit(solution)/shard_map/ppermute | solution.py:227
  29.7 4.8 %collective-permute-start.10 = (bf16[64,256]{1,0:T(8,128)(2,1)S(1)}, bf16[64,256]{1,0:T(8,128)(2,1)S(1)}, u32[]{:S(2)}, u32[]{:S(2)}) collective-permute-start(bf16[64,256]{1,0:T(8,128)(2,1)S(1)} %get-tuple-element.39), channel_id=1, source_target_pairs={{0,4},{1,5},{2,6},{3,7},{4,0},{5,1},{6,2},{7,3},{8,12},{9,13},{10,... | collective-permute-start | bytes 98312 | tf_op jit(solution)/shard_map/ppermute | solution.py:227

commit v5 on v4

--- a/solution.py
+++ b/solution.py
@@ -139,53 +139,33 @@
     send_ref[1] = delta.astype(BF16)
 
 
-def lower_kernel(share, index_ref, flow_ref, xg0_ref, low_ref, got_ref, keep_ref, send_ref):
+def lower_kernel(
+    share, index_ref, flow_ref, xg0_ref, low_ref, got_ref, keep1, got1, keep_ref, send_ref, sum_ref
+):
     da0 = (got_ref[1].astype(F32) * low_ref[0]).astype(BF16)
     das0 = (da0.astype(F32) * low_ref[1]).astype(BF16)
     split_terms(share, index_ref[0], das0, xg0_ref, got_ref[0], flow_ref, keep_ref, send_ref)
-
-
-def plane_kernel(
-    place_ref, index_ref, keep1, got1, keep0, got0, own_ref, first_ref, second_ref, across
-):
-    row = (index_ref[0] // 2) % 2
-
-    def order(near, far, along_x, along_y):
-        for i in range(own_ref.shape[0]):
-            for to_ref, (keep, got), number in (
-                (across, far, 1 - row),
-                (along_x, far, row),
-                (along_y, near, 1 - row),
-                (own_ref, near, row),
-            ):
-                block = 2 * i + number
-                to_ref[i] = (keep[block].astype(F32) + got[block].astype(F32)).astype(BF16)
-
-    for place, near, far in (
-        (1, (keep1, got1), (keep0, got0)),
-        (0, (keep0, got0), (keep1, got1)),
-    ):
-        for core, ways in ((0, (second_ref, first_ref)), (1, (first_ref, second_ref))):
-            pl.when((place_ref[0] == place) & (index_ref[0] % 2 == core))(
-                partial(order, near, far, *ways)
-            )
-
-
-def layer_kernel(index_ref, own, got_a, got_b, got_c, *out_refs):
-    layer = index_ref[0] // 4
-    for k, out_ref in enumerate(out_refs):
-        block = layer ^ k
-        total = own[block].astype(F32) + got_a[block].astype(F32)
-        total += got_b[block].astype(F32) + got_c[block].astype(F32)
-        out_ref[...] = total.astype(BF16)
-
-
-def total_kernel(*refs):
-    *got, in_ref, out_ref = refs
+    for i in range(sum_ref.shape[0]):
+        sum_ref[i] = (keep1[i].astype(F32) + got1[i].astype(F32)).astype(BF16)
+
+
+def plane_kernel(sum1, keep0, got0, out_ref):
+    layers = out_ref.shape[1]
+    for row in range(2):
+        for i in range(layers):
+            block = 2 * i + row
+            out_ref[row, i] = (keep0[block].astype(F32) + got0[block].astype(F32)).astype(BF16)
+            out_ref[2 + row, i] = sum1[block]
+
+
+def layer_kernel(got, out_ref):
+    for i in range(out_ref.shape[0]):
+        out_ref[i] = sum(got[k, i].astype(F32) for k in range(got.shape[0])).astype(BF16)
+
+
+def total_kernel(got, in_ref, out_ref):
     rank = in_ref.shape[1]
-    total = got[0][...].astype(F32)
-    for ref in got[1:]:
-        total += ref[...].astype(F32)
+    total = sum(got[i].astype(F32) for i in range(got.shape[0]))
     in_ref[0] = total[0:rank]
     out_ref[0] = total[rank : 2 * rank]
 
@@ -214,8 +194,6 @@
     scalar = pl.BlockSpec(memory_space=pltpu.SMEM)
     chips, layers = count // 2, count // 4
     blocks = jax.ShapeDtypeStruct((chips, 2 * rank, share), BF16)
-    fourth = jax.ShapeDtypeStruct((layers, 2 * rank, share), BF16)
-    block = jax.ShapeDtypeStruct((2 * rank, share), BF16)
     wide = jax.ShapeDtypeStruct((tokens, width), BF16)
 
     def swapped(array, *ways):
@@ -267,43 +245,57 @@
         name="flow",
     )(index_ref, flow, partner_half, partner_other, act0)
     got = swapped(send, (1, 0))
-    keep0, send0 = pl.pallas_call(
+    keep0, send0, sum1 = pl.pallas_call(
         partial(lower_kernel, share),
-        in_specs=[scalar] + [whole()] * 4,
-        out_specs=[whole()] * 2,
-        out_shape=[blocks] * 2,
+        in_specs=[scalar] + [whole()] * 6,
+        out_specs=[whole()] * 3,
+        out_shape=[blocks] * 3,
         compiler_params=params(),
         name="lower",
-    )(index_ref, flow, xg0, low, got)
+    )(index_ref, flow, xg0, low, got, keep1, got1)
     got0 = swapped(send0, (0, 1))
-    own, first, second, across = pl.pallas_call(
+    number = lambda s, z, y, core: s * count + 4 * z + 2 * y + core
+    planes = [
+        [number(s, z, y, core) for s in range(2) for y in range(2)]
+        for z in range(layers)
+        for core in range(2)
+    ]
+    columns = [
+        [number(s, z, y, core) for z in range(layers)]
+        for s in range(2)
+        for y in range(2)
+        for core in range(2)
+    ]
+
+    def dealt(blocks, groups):
+        return lax.all_to_all(
+            blocks, ("section", "dp"), 0, 0, axis_index_groups=groups, tiled=True
+        )
+
+    sums = pl.pallas_call(
         plane_kernel,
-        in_specs=[scalar] * 2 + [whole()] * 4,
-        out_specs=[whole()] * 4,
-        out_shape=[fourth] * 4,
+        in_specs=[whole()] * 3,
+        out_specs=whole(),
+        out_shape=jax.ShapeDtypeStruct((4, layers, 2 * rank, share), BF16),
         compiler_params=params(),
         name="plane",
-    )(place_ref, index_ref, keep1, got1, keep0, got0)
-    first = swapped(first, (0, 2), (1, 0))
-    second = swapped(second, (1, 0), (0, 2))
-    across = swapped(across, (1, 2))
-    mine, *others = pl.pallas_call(
+    )(sum1, keep0, got0)
+    sums = pl.pallas_call(
         layer_kernel,
-        in_specs=[scalar] + [whole()] * 4,
-        out_specs=[whole()] * layers,
-        out_shape=[block] * layers,
+        in_specs=[whole()],
+        out_specs=whole(),
+        out_shape=jax.ShapeDtypeStruct((layers, 2 * rank, share), BF16),
         compiler_params=params(),
         name="layer",
-    )(index_ref, own, first, second, across)
-    others = [swapped(other, (0, 4 * k)) for k, other in enumerate(others, 1)]
+    )(dealt(sums, planes))
     total_in, total_out = pl.pallas_call(
         total_kernel,
-        in_specs=[whole()] * layers,
+        in_specs=[whole()],
         out_specs=[whole()] * 2,
         out_shape=[jax.ShapeDtypeStruct((1, rank, share), F32)] * 2,
         compiler_params=params(),
         name="total",
-    )(mine, *others[::-1])
+    )(dealt(sums, columns))
     return (jnp.swapaxes(total_in, 1, 2), total_out)
 
 

time: 35.3 us -> 39.9 us (1.13)
  blocking collectives: 0 us -> 22.1 us
  waiting for transfers between devices: 15.5 us -> 5.87 us
  starting transfers between devices: 12.1 us -> 4.26 us
    all_to_all x0 -> x2, blocking collectives: none -> 22.1 us  [dealt(): lax.all_to_all(blocks, ('section', 'dp'), 0, 0, axis_index_groups=groups,...]
    ppermute x11 -> x5, waiting for transfers between devices: 15.5 us -> 5.87 us  [swapped(): return lax.ppermute(array, ('section', 'dp'), pairs)]
    ppermute x11 -> x5, starting transfers between devices: 12.1 us -> 4.26 us  [swapped(): return lax.ppermute(array, ('section', 'dp'), pairs)]
  transfers between devices with their start and end apart: 11 -> 5, of which waited for: 7 -> 3; matrix products, arithmetic and copies ran while one was open for 0% -> 0% of each run, Pallas kernels for 13% -> 12%
where the time goes in v5:
time: 39.9 us; the launch traced here: 39.7 us
  blocking collectives  22.1 us (55%)
  Pallas kernels  6.74 us (17%)
  waiting for transfers between devices  5.87 us (15%)
  starting transfers between devices  4.26 us (11%)
  between operations  0.69 us (2%)
    all_to_all x2, blocking collectives, dealt(): lax.all_to_all(blocks, ('section', 'dp'), 0, 0, axis_index_groups=groups,...  22.1 us
    ppermute x5, waiting for transfers between devices, swapped(): return lax.ppermute(array, ('section', 'dp'), pairs)  5.87 us
    ppermute x5, starting transfers between devices, swapped(): return lax.ppermute(array, ('section', 'dp'), pairs)  4.26 us
    pallas_call x1, Pallas kernels, pair_on_device(): pl.pallas_call(partial(upper_kernel, share), in_specs=[scalar] * 2 + [pl....  4.19 us
    pallas_call x1, Pallas kernels, pair_on_device(): pl.pallas_call(pick_kernel, in_specs=[scalar] * 2 + [pl.BlockSpec(memory_...  0.92 us
  transfers between devices with their start and end apart: 5, of which 3 were waited for; matrix products, arithmetic and copies ran while one was open for 0% of the time, Pallas kernels for 12%

profile of v5, /device:TPU:0, one launch (start us, length us, event | category | flops | bytes accessed | tf_op | source)
XLA Modules:
  0.0 39.7 jit_solution(14910388440071675770)
XLA Ops:
  0.6 0.9 %pick.1 = bf16[32,2048]{1,0:T(8,128)(2,1)S(1)} custom-call(s32[1]{0:T(128)} %bitcast.1.place_ref, s32[1]{0:T(128)} %bitcast.index_ref, bf16[1,2,32,4096]{3,2,1,0:T(8,128)(2,1)} %w_out.3), custom_call_target="tpu_custom_call" | custom-call | tf_op jit(solution)/shard_map/pick/pallas_call | solution.py:207
  1.6 3.0 %collective-permute-start = (bf16[32,2048]{1,0:T(8,128)(2,1)S(1)}, bf16[32,2048]{1,0:T(8,128)(2,1)S(1)}, u32[]{:S(2)}, u32[]{:S(2)}) collective-permute-start(bf16[32,2048]{1,0:T(8,128)(2,1)S(1)} %pick.1), channel_id=1, source_target_pairs={{0,16},{1,17},{2,18},{3,19},{4,20},{5,21},{6,22},{7,23},{8,24},{9,... | collective-permute-start | bytes 393224 | tf_op jit(solution)/shard_map/ppermute | solution.py:205
  4.6 4.2 %upper.1 = (bf16[8,64,256]{2,1,0:T(8,128)(2,1)S(1)}, bf16[8,64,256]{2,1,0:T(8,128)(2,1)S(1)}, bf16[128,4096]{1,0:T(8,128)(2,1)S(1)}, bf16[128,4096]{1,0:T(8,128)...) custom-call(s32[1]{0:T(128)} %bitcast.1.place_ref, s32[1]{0:T(128)} %bitcast.index_ref, ...), custom_call_target="tpu_custom_call" | custom-call | flops 201326592 | bytes 6291456 | tf_op jit(solution)/shard_map/upper/pallas_call | solution.py:217
  8.8 0.1 collective-permute-start.3
  8.8 0.0 collective-permute-done.own_ref
  8.9 0.5 %collective-permute-start.1 = (bf16[32,2048]{1,0:T(8,128)(2,1)S(1)}, bf16[32,2048]{1,0:T(8,128)(2,1)S(1)}, u32[]{:S(2)}, u32[]{:S(2)}) collective-permute-start(bf16[32,2048]{1,0:T(8,128)(2,1)S(1)} %collective-permute-done.own_ref), channel_id=1, source_target_pairs={{0,1},{1,0},{2,3},{3,2},{4,5},{5,4},{6,7},{7,6},{8,9},{9,8},{10,11... | collective-permute-start | bytes 393224 | tf_op jit(solution)/shard_map/ppermute | solution.py:205
  9.3 1.2 %collective-permute-done.1.other_ref = bf16[32,2048]{1,0:T(8,128)(2,1)S(1)} collective-permute-done((bf16[32,2048]{1,0:T(8,128)(2,1)S(1)}, bf16[32,2048]{1,0:T(8,128)(2,1)S(1)}, u32[]{:S(2)}, u32[]{:S(2)}) %collective-permute-start.1) | collective-permute-done | bytes 131104 | tf_op jit(solution)/shard_map/ppermute | solution.py:205
  10.6 0.4 %flow.1 = bf16[2,32,128]{2,1,0:T(8,128)(2,1)S(1)} custom-call(s32[1]{0:T(128)} %bitcast.index_ref, bf16[128,4096]{1,0:T(8,128)(2,1)S(1)} %get-tuple-element.16.flow_ref, bf16[32,2048]{1,0:T(8,128)(2,1)S(1)} %collective-permute-done.own_ref, bf16[32,2048]{1,0:T(8,128)(2,1)S(1)} %collective-permute-done.1.other_ref, bf16[32,128]{1,0:T(8,128)(2,1)S(1)} %get-tuple-element.20.act0_ref), custom_call_target="tpu_custom_call" | custom-call | tf_op jit(solution)/shard_map/flow/pallas_call | solution.py:239
  11.0 0.6 %collective-permute-start.2 = (bf16[2,32,128]{2,1,0:T(8,128)(2,1)S(1)}, bf16[2,32,128]{2,1,0:T(8,128)(2,1)S(1)}, u32[]{:S(2)}, u32[]{:S(2)}) collective-permute-start(bf16[2,32,128]{2,1,0:T(8,128)(2,1)S(1)} %flow.1), channel_id=1, source_target_pairs={{0,16},{1,17},{2,18},{3,19},{4,20},{5,21},{6,22},{7,23},{8,24},{9,... | collective-permute-start | bytes 49160 | tf_op jit(solution)/shard_map/ppermute | solution.py:205
  11.6 0.0 collective-permute-done.3.got1
  11.6 3.1 %collective-permute-done.2.got_ref = bf16[2,32,128]{2,1,0:T(8,128)(2,1)S(1)} collective-permute-done((bf16[2,32,128]{2,1,0:T(8,128)(2,1)S(1)}, bf16[2,32,128]{2,1,0:T(8,128)(2,1)S(1)}, u32[]{:S(2)}, u32[]{:S(2)}) %collective-permute-start.2) | collective-permute-done | bytes 16416 | tf_op jit(solution)/shard_map/ppermute | solution.py:205
  14.8 0.4 %lower.1 = (bf16[8,64,256]{2,1,0:T(8,128)(2,1)S(1)}, bf16[8,64,256]{2,1,0:T(8,128)(2,1)S(1)}, bf16[8,64,256]{2,1,0:T(8,128)(2,1)S(1)}) custom-call(s32[1]{0:T(128)} %bitcast.index_ref, bf16[128,4096]{1,0:T(8,128)(2,1)S(1)} %get-tuple-element.16.flow_ref, bf16[128,4096]{1,0:T(8,128)(2,1)S(1)} %get-tuple-element.17.xg0_ref, ...), custom_call_target="tpu_custom_call" | custom-call | tf_op jit(solution)/shard_map/lower/pallas_call | solution.py:248
  15.2 0.1 collective-permute-start.4
  15.3 1.5 %collective-permute-done.4.got0 = bf16[8,64,256]{2,1,0:T(8,128)(2,1)S(1)} collective-permute-done((bf16[8,64,256]{2,1,0:T(8,128)(2,1)S(1)}, bf16[8,64,256]{2,1,0:T(8,128)(2,1)S(1)}, u32[]{:S(2)}, u32[]{:S(2)}) %collective-permute-start.4) | collective-permute-done | bytes 262176 | tf_op jit(solution)/shard_map/ppermute | solution.py:205
  16.8 0.1 plane.1
  16.9 11.5 %all_to_all.10.got = bf16[4,4,64,256]{3,2,1,0:T(8,128)(2,1)S(1)} all-to-all(bf16[4,4,64,256]{3,2,1,0:T(8,128)(2,1)S(1)} %plane.1), channel_id=1, replica_groups={{0,2,16,18},{1,3,17,19},{4,6,20,22},{5,7,21,23},{8,10,24,26},{9,11,25,2..., dimensions={0} | all-to-all | bytes 1048576 | tf_op jit(solution)/shard_map/all_to_all | solution.py:271
  28.4 0.1 layer.1
  28.4 10.6 %all_to_all.11.got = bf16[4,64,256]{2,1,0:T(8,128)(2,1)S(1)} all-to-all(bf16[4,64,256]{2,1,0:T(8,128)(2,1)S(1)} %layer.1), channel_id=1, replica_groups={{0,4,8,12},{1,5,9,13},{2,6,10,14},{3,7,11,15},{16,20,24,28},{17,21,25,2..., dimensions={0} | all-to-all | bytes 262144 | tf_op jit(solution)/shard_map/all_to_all | solution.py:271
  39.0 0.6 %total.1 = (f32[1,32,256]{2,1,0:T(8,128)}, f32[1,32,256]{2,1,0:T(8,128)}) custom-call(bf16[4,64,256]{2,1,0:T(8,128)(2,1)S(1)} %all_to_all.11.got), custom_call_target="tpu_custom_call" | custom-call | tf_op jit(solution)/shard_map/total/pallas_call | solution.py:291
Async XLA Ops:
  1.6 7.3 %collective-permute-start = (bf16[32,2048]{1,0:T(8,128)(2,1)S(1)}, bf16[32,2048]{1,0:T(8,128)(2,1)S(1)}, u32[]{:S(2)}, u32[]{:S(2)}) collective-permute-start(bf16[32,2048]{1,0:T(8,128)(2,1)S(1)} %pick.1), channel_id=1, source_target_pairs={{0,16},{1,17},{2,18},{3,19},{4,20},{5,21},{6,22},{7,23},{8,24},{9,... | collective-permute-start | bytes 393224 | tf_op jit(solution)/shard_map/ppermute | solution.py:205
  8.8 2.9 %collective-permute-start.3 = (bf16[8,64,256]{2,1,0:T(8,128)(2,1)S(1)}, bf16[8,64,256]{2,1,0:T(8,128)(2,1)S(1)}, u32[]{:S(2)}, u32[]{:S(2)}) collective-permute-start(bf16[8,64,256]{2,1,0:T(8,128)(2,1)S(1)} %get-tuple-element.22), channel_id=1, source_target_pairs={{0,1},{1,0},{2,3},{3,2},{4,5},{5,4},{6,7},{7,6},{8,9},{9,8},{10,11... | collective-permute-start | bytes 786440 | tf_op jit(solution)/shard_map/ppermute | solution.py:205
  8.9 1.7 %collective-permute-start.1 = (bf16[32,2048]{1,0:T(8,128)(2,1)S(1)}, bf16[32,2048]{1,0:T(8,128)(2,1)S(1)}, u32[]{:S(2)}, u32[]{:S(2)}) collective-permute-start(bf16[32,2048]{1,0:T(8,128)(2,1)S(1)} %collective-permute-done.own_ref), channel_id=1, source_target_pairs={{0,1},{1,0},{2,3},{3,2},{4,5},{5,4},{6,7},{7,6},{8,9},{9,8},{10,11... | collective-permute-start | bytes 393224 | tf_op jit(solution)/shard_map/ppermute | solution.py:205
  11.0 3.8 %collective-permute-start.2 = (bf16[2,32,128]{2,1,0:T(8,128)(2,1)S(1)}, bf16[2,32,128]{2,1,0:T(8,128)(2,1)S(1)}, u32[]{:S(2)}, u32[]{:S(2)}) collective-permute-start(bf16[2,32,128]{2,1,0:T(8,128)(2,1)S(1)} %flow.1), channel_id=1, source_target_pairs={{0,16},{1,17},{2,18},{3,19},{4,20},{5,21},{6,22},{7,23},{8,24},{9,... | collective-permute-start | bytes 49160 | tf_op jit(solution)/shard_map/ppermute | solution.py:205
  15.2 1.6 %collective-permute-start.4 = (bf16[8,64,256]{2,1,0:T(8,128)(2,1)S(1)}, bf16[8,64,256]{2,1,0:T(8,128)(2,1)S(1)}, u32[]{:S(2)}, u32[]{:S(2)}) collective-permute-start(bf16[8,64,256]{2,1,0:T(8,128)(2,1)S(1)} %get-tuple-element.25), channel_id=1, source_target_pairs={{0,1},{1,0},{2,3},{3,2},{4,5},{5,4},{6,7},{7,6},{8,9},{9,8},{10,11... | collective-permute-start | bytes 786440 | tf_op jit(solution)/shard_map/ppermute | solution.py:205

commit v6 on v4

--- a/solution.py
+++ b/solution.py
@@ -294,8 +294,9 @@
         out_shape=[block] * layers,
         compiler_params=params(),
         name="layer",
-    )(index_ref, own, first, second, across)
+    )(index_ref, own, first, across, second)
     others = [swapped(other, (0, 4 * k)) for k, other in enumerate(others, 1)]
+    others = others[1:] + others[:1]
     total_in, total_out = pl.pallas_call(
         total_kernel,
         in_specs=[whole()] * layers,
@@ -303,7 +304,7 @@
         out_shape=[jax.ShapeDtypeStruct((1, rank, share), F32)] * 2,
         compiler_params=params(),
         name="total",
-    )(mine, *others[::-1])
+    )(mine, *others)
     return (jnp.swapaxes(total_in, 1, 2), total_out)
 
 

time: 35.3 us -> 34.5 us (0.977)
  waiting for transfers between devices: 15.5 us -> 14.9 us
    ppermute x11, waiting for transfers between devices: 15.5 us -> 14.9 us  [swapped(): return lax.ppermute(array, ('section', 'dp'), pairs)]
  transfers between devices with their start and end apart: 11 -> 11, of which waited for: 7 -> 8; matrix products, arithmetic and copies ran while one was open for 0% -> 0% of each run, Pallas kernels for 13% -> 13%
where the time goes in v6:
time: 34.5 us; the launch traced here: 34.4 us
  waiting for transfers between devices  14.9 us (43%)
  starting transfers between devices  11.9 us (34%)
  Pallas kernels  6.81 us (20%)
  between operations  0.71 us (2%)
    ppermute x11, waiting for transfers between devices, swapped(): return lax.ppermute(array, ('section', 'dp'), pairs)  14.9 us
    ppermute x11, starting transfers between devices, swapped(): return lax.ppermute(array, ('section', 'dp'), pairs)  11.9 us
    pallas_call x1, Pallas kernels, pair_on_device(): pl.pallas_call(partial(upper_kernel, share), in_specs=[scalar] * 2 + [pl....  4.19 us
    pallas_call x1, Pallas kernels, pair_on_device(): pl.pallas_call(pick_kernel, in_specs=[scalar] * 2 + [pl.BlockSpec(memory_...  0.92 us
  transfers between devices with their start and end apart: 11, of which 8 were waited for; matrix products, arithmetic and copies ran while one was open for 0% of the time, Pallas kernels for 13%

profile of v6, /device:TPU:0, one launch (start us, length us, event | category | flops | bytes accessed | tf_op | source)
XLA Modules:
  0.0 34.4 jit_solution(1726124828865948513)
XLA Ops:
  0.6 0.9 %pick.1 = bf16[32,2048]{1,0:T(8,128)(2,1)S(1)} custom-call(s32[1]{0:T(128)} %bitcast.1.place_ref, s32[1]{0:T(128)} %bitcast.index_ref, bf16[1,2,32,4096]{3,2,1,0:T(8,128)(2,1)} %w_out.3), custom_call_target="tpu_custom_call" | custom-call | tf_op jit(solution)/shard_map/pick/pallas_call | solution.py:229
  1.6 3.0 %collective-permute-start.1 = (bf16[32,2048]{1,0:T(8,128)(2,1)S(1)}, bf16[32,2048]{1,0:T(8,128)(2,1)S(1)}, u32[]{:S(2)}, u32[]{:S(2)}) collective-permute-start(bf16[32,2048]{1,0:T(8,128)(2,1)S(1)} %pick.1), channel_id=1, source_target_pairs={{0,16},{1,17},{2,18},{3,19},{4,20},{5,21},{6,22},{7,23},{8,24},{9,... | collective-permute-start | bytes 393224 | tf_op jit(solution)/shard_map/ppermute | solution.py:227
  4.6 4.2 %upper.1 = (bf16[8,64,256]{2,1,0:T(8,128)(2,1)S(1)}, bf16[8,64,256]{2,1,0:T(8,128)(2,1)S(1)}, bf16[128,4096]{1,0:T(8,128)(2,1)S(1)}, bf16[128,4096]{1,0:T(8,128)...) custom-call(s32[1]{0:T(128)} %bitcast.1.place_ref, s32[1]{0:T(128)} %bitcast.index_ref, ...), custom_call_target="tpu_custom_call" | custom-call | flops 201326592 | bytes 6291456 | tf_op jit(solution)/shard_map/upper/pallas_call | solution.py:239
  8.8 0.0 collective-permute-done.1.own_ref
  8.8 0.1 collective-permute-start.2
  8.9 1.3 %collective-permute-done.2.other_ref = bf16[32,2048]{1,0:T(8,128)(2,1)S(1)} collective-permute-done((bf16[32,2048]{1,0:T(8,128)(2,1)S(1)}, bf16[32,2048]{1,0:T(8,128)(2,1)S(1)}, u32[]{:S(2)}, u32[]{:S(2)}) %collective-permute-start.2) | collective-permute-done | bytes 131104 | tf_op jit(solution)/shard_map/ppermute | solution.py:227
  10.2 0.4 %flow.1 = bf16[2,32,128]{2,1,0:T(8,128)(2,1)S(1)} custom-call(s32[1]{0:T(128)} %bitcast.index_ref, bf16[128,4096]{1,0:T(8,128)(2,1)S(1)} %get-tuple-element.25.flow_ref, bf16[32,2048]{1,0:T(8,128)(2,1)S(1)} %collective-permute-done.1.own_ref, bf16[32,2048]{1,0:T(8,128)(2,1)S(1)} %collective-permute-done.2.other_ref, ...), custom_call_target="tpu_custom_call" | custom-call | tf_op jit(solution)/shard_map/flow/pallas_call | solution.py:261
  10.6 1.0 %collective-permute-start.3 = (bf16[2,32,128]{2,1,0:T(8,128)(2,1)S(1)}, bf16[2,32,128]{2,1,0:T(8,128)(2,1)S(1)}, u32[]{:S(2)}, u32[]{:S(2)}) collective-permute-start(bf16[2,32,128]{2,1,0:T(8,128)(2,1)S(1)} %flow.1), channel_id=1, source_target_pairs={{0,16},{1,17},{2,18},{3,19},{4,20},{5,21},{6,22},{7,23},{8,24},{9,... | collective-permute-start | bytes 49160 | tf_op jit(solution)/shard_map/ppermute | solution.py:227
  11.6 0.0 collective-permute-start
  11.6 2.8 %collective-permute-done.3.got_ref = bf16[2,32,128]{2,1,0:T(8,128)(2,1)S(1)} collective-permute-done((bf16[2,32,128]{2,1,0:T(8,128)(2,1)S(1)}, bf16[2,32,128]{2,1,0:T(8,128)(2,1)S(1)}, u32[]{:S(2)}, u32[]{:S(2)}) %collective-permute-start.3) | collective-permute-done | bytes 16416 | tf_op jit(solution)/shard_map/ppermute | solution.py:227
  14.4 0.4 %lower.1 = (bf16[8,64,256]{2,1,0:T(8,128)(2,1)S(1)}, bf16[8,64,256]{2,1,0:T(8,128)(2,1)S(1)}) custom-call(s32[1]{0:T(128)} %bitcast.index_ref, bf16[128,4096]{1,0:T(8,128)(2,1)S(1)} %get-tuple-element.25.flow_ref, bf16[128,4096]{1,0:T(8,128)(2,1)S(1)} %get-tuple-element.26.xg0_ref, f32[2,32,128]{2,1,0:T(8,128)S(1)} %get-tuple-element.27.low_ref, ...), custom_call_target="tpu_custom_call" | custom-call | tf_op jit(solution)/shard_map/lower/pallas_call | solution.py:270
  14.8 0.1 collective-permute-start.4
  14.9 0.0 collective-permute-done.got1
  14.9 1.5 %collective-permute-done.4.got0 = bf16[8,64,256]{2,1,0:T(8,128)(2,1)S(1)} collective-permute-done((bf16[8,64,256]{2,1,0:T(8,128)(2,1)S(1)}, bf16[8,64,256]{2,1,0:T(8,128)(2,1)S(1)}, u32[]{:S(2)}, u32[]{:S(2)}) %collective-permute-start.4) | collective-permute-done | bytes 262176 | tf_op jit(solution)/shard_map/ppermute | solution.py:227
  16.4 0.1 plane.1
  16.6 1.6 %collective-permute-start.5 = (bf16[4,64,256]{2,1,0:T(8,128)(2,1)S(1)}, bf16[4,64,256]{2,1,0:T(8,128)(2,1)S(1)}, u32[]{:S(2)}, u32[]{:S(2)}) collective-permute-start(bf16[4,64,256]{2,1,0:T(8,128)(2,1)S(1)} %get-tuple-element.33), channel_id=1, source_target_pairs={{0,2},{1,17},{2,0},{3,19},{4,6},{5,21},{6,4},{7,23},{8,10},{9,25},... | collective-permute-start | bytes 393224 | tf_op jit(solution)/shard_map/ppermute | solution.py:227
  18.1 0.9 %collective-permute-start.6 = (bf16[4,64,256]{2,1,0:T(8,128)(2,1)S(1)}, bf16[4,64,256]{2,1,0:T(8,128)(2,1)S(1)}, u32[]{:S(2)}, u32[]{:S(2)}) collective-permute-start(bf16[4,64,256]{2,1,0:T(8,128)(2,1)S(1)} %get-tuple-element.34), channel_id=1, source_target_pairs={{0,18},{1,19},{2,16},{3,17},{4,22},{5,23},{6,20},{7,21},{8,26},{9,... | collective-permute-start | bytes 393224 | tf_op jit(solution)/shard_map/ppermute | solution.py:227
  19.1 1.0 %collective-permute-start.7 = (bf16[4,64,256]{2,1,0:T(8,128)(2,1)S(1)}, bf16[4,64,256]{2,1,0:T(8,128)(2,1)S(1)}, u32[]{:S(2)}, u32[]{:S(2)}) collective-permute-start(bf16[4,64,256]{2,1,0:T(8,128)(2,1)S(1)} %get-tuple-element.35), channel_id=1, source_target_pairs={{0,16},{1,3},{2,18},{3,1},{4,20},{5,7},{6,22},{7,5},{8,24},{9,11},... | collective-permute-start | bytes 393224 | tf_op jit(solution)/shard_map/ppermute | solution.py:227
  20.1 4.2 %collective-permute-done.5.got_a = bf16[4,64,256]{2,1,0:T(8,128)(2,1)S(1)} collective-permute-done((bf16[4,64,256]{2,1,0:T(8,128)(2,1)S(1)}, bf16[4,64,256]{2,1,0:T(8,128)(2,1)S(1)}, u32[]{:S(2)}, u32[]{:S(2)}) %collective-permute-start.5) | collective-permute-done | bytes 131104 | tf_op jit(solution)/shard_map/ppermute | solution.py:227
  24.3 0.3 collective-permute-done.6.got_b
  24.6 0.7 %collective-permute-done.7.got_c = bf16[4,64,256]{2,1,0:T(8,128)(2,1)S(1)} collective-permute-done((bf16[4,64,256]{2,1,0:T(8,128)(2,1)S(1)}, bf16[4,64,256]{2,1,0:T(8,128)(2,1)S(1)}, u32[]{:S(2)}, u32[]{:S(2)}) %collective-permute-start.7) | collective-permute-done | bytes 131104 | tf_op jit(solution)/shard_map/ppermute | solution.py:227
  25.3 0.1 layer.1
  25.3 2.7 %collective-permute-start.8 = (bf16[64,256]{1,0:T(8,128)(2,1)S(1)}, bf16[64,256]{1,0:T(8,128)(2,1)S(1)}, u32[]{:S(2)}, u32[]{:S(2)}) collective-permute-start(bf16[64,256]{1,0:T(8,128)(2,1)S(1)} %get-tuple-element.37), channel_id=1, source_target_pairs={{0,8},{1,9},{2,10},{3,11},{4,12},{5,13},{6,14},{7,15},{8,0},{9,1},... | collective-permute-start | bytes 98312 | tf_op jit(solution)/shard_map/ppermute | solution.py:227
  28.0 1.3 %collective-permute-start.9 = (bf16[64,256]{1,0:T(8,128)(2,1)S(1)}, bf16[64,256]{1,0:T(8,128)(2,1)S(1)}, u32[]{:S(2)}, u32[]{:S(2)}) collective-permute-start(bf16[64,256]{1,0:T(8,128)(2,1)S(1)} %get-tuple-element.38), channel_id=1, source_target_pairs={{0,12},{1,13},{2,14},{3,15},{4,8},{5,9},{6,10},{7,11},{8,4},{9,5},... | collective-permute-start | bytes 98312 | tf_op jit(solution)/shard_map/ppermute | solution.py:227
  29.3 0.2 collective-permute-start.10
  29.6 0.6 %collective-permute-done.8.refs_1_ = bf16[64,256]{1,0:T(8,128)(2,1)S(1)} collective-permute-done((bf16[64,256]{1,0:T(8,128)(2,1)S(1)}, bf16[64,256]{1,0:T(8,128)(2,1)S(1)}, u32[]{:S(2)}, u32[]{:S(2)}) %collective-permute-start.8) | collective-permute-done | bytes 32800 | tf_op jit(solution)/shard_map/ppermute | solution.py:227
  30.2 3.5 %collective-permute-done.9.refs_2_ = bf16[64,256]{1,0:T(8,128)(2,1)S(1)} collective-permute-done((bf16[64,256]{1,0:T(8,128)(2,1)S(1)}, bf16[64,256]{1,0:T(8,128)(2,1)S(1)}, u32[]{:S(2)}, u32[]{:S(2)}) %collective-permute-start.9) | collective-permute-done | bytes 32800 | tf_op jit(solution)/shard_map/ppermute | solution.py:227
  33.7 0.0 collective-permute-done.10.refs_3_
  33.7 0.6 %total.1 = (f32[1,32,256]{2,1,0:T(8,128)}, f32[1,32,256]{2,1,0:T(8,128)}) custom-call(bf16[64,256]{1,0:T(8,128)(2,1)S(1)} %get-tuple-element.36.refs_0_, bf16[64,256]{1,0:T(8,128)(2,1)S(1)} %collective-permute-done.8.refs_1_, bf16[64,256]{1,0:T(8,128)(2,1)S(1)} %collective-permute-done.9.refs_2_, bf16[64,256]{1,0:T(8,128)(2,1)S(1)} %collective-permute-done.10.refs_3_), custom_call_target="tpu_custom_call" | custom-call | tf_op jit(solution)/shard_map/total/pallas_call | solution.py:300
Async XLA Ops:
  1.6 7.2 %collective-permute-start.1 = (bf16[32,2048]{1,0:T(8,128)(2,1)S(1)}, bf16[32,2048]{1,0:T(8,128)(2,1)S(1)}, u32[]{:S(2)}, u32[]{:S(2)}) collective-permute-start(bf16[32,2048]{1,0:T(8,128)(2,1)S(1)} %pick.1), channel_id=1, source_target_pairs={{0,16},{1,17},{2,18},{3,19},{4,20},{5,21},{6,22},{7,23},{8,24},{9,... | collective-permute-start | bytes 393224 | tf_op jit(solution)/shard_map/ppermute | solution.py:227
  8.8 1.4 %collective-permute-start.2 = (bf16[32,2048]{1,0:T(8,128)(2,1)S(1)}, bf16[32,2048]{1,0:T(8,128)(2,1)S(1)}, u32[]{:S(2)}, u32[]{:S(2)}) collective-permute-start(bf16[32,2048]{1,0:T(8,128)(2,1)S(1)} %collective-permute-done.1.own_ref), channel_id=1, source_target_pairs={{0,1},{1,0},{2,3},{3,2},{4,5},{5,4},{6,7},{7,6},{8,9},{9,8},{10,11... | collective-permute-start | bytes 393224 | tf_op jit(solution)/shard_map/ppermute | solution.py:227
  10.6 3.8 %collective-permute-start.3 = (bf16[2,32,128]{2,1,0:T(8,128)(2,1)S(1)}, bf16[2,32,128]{2,1,0:T(8,128)(2,1)S(1)}, u32[]{:S(2)}, u32[]{:S(2)}) collective-permute-start(bf16[2,32,128]{2,1,0:T(8,128)(2,1)S(1)} %flow.1), channel_id=1, source_target_pairs={{0,16},{1,17},{2,18},{3,19},{4,20},{5,21},{6,22},{7,23},{8,24},{9,... | collective-permute-start | bytes 49160 | tf_op jit(solution)/shard_map/ppermute | solution.py:227
  11.6 3.3 %collective-permute-start = (bf16[8,64,256]{2,1,0:T(8,128)(2,1)S(1)}, bf16[8,64,256]{2,1,0:T(8,128)(2,1)S(1)}, u32[]{:S(2)}, u32[]{:S(2)}) collective-permute-start(bf16[8,64,256]{2,1,0:T(8,128)(2,1)S(1)} %get-tuple-element.23), channel_id=1, source_target_pairs={{0,1},{1,0},{2,3},{3,2},{4,5},{5,4},{6,7},{7,6},{8,9},{9,8},{10,11... | collective-permute-start | bytes 786440 | tf_op jit(solution)/shard_map/ppermute | solution.py:227
  14.8 1.6 %collective-permute-start.4 = (bf16[8,64,256]{2,1,0:T(8,128)(2,1)S(1)}, bf16[8,64,256]{2,1,0:T(8,128)(2,1)S(1)}, u32[]{:S(2)}, u32[]{:S(2)}) collective-permute-start(bf16[8,64,256]{2,1,0:T(8,128)(2,1)S(1)} %get-tuple-element.31), channel_id=1, source_target_pairs={{0,1},{1,0},{2,3},{3,2},{4,5},{5,4},{6,7},{7,6},{8,9},{9,8},{10,11... | collective-permute-start | bytes 786440 | tf_op jit(solution)/shard_map/ppermute | solution.py:227
  16.6 7.8 %collective-permute-start.5 = (bf16[4,64,256]{2,1,0:T(8,128)(2,1)S(1)}, bf16[4,64,256]{2,1,0:T(8,128)(2,1)S(1)}, u32[]{:S(2)}, u32[]{:S(2)}) collective-permute-start(bf16[4,64,256]{2,1,0:T(8,128)(2,1)S(1)} %get-tuple-element.33), channel_id=1, source_target_pairs={{0,2},{1,17},{2,0},{3,19},{4,6},{5,21},{6,4},{7,23},{8,10},{9,25},... | collective-permute-start | bytes 393224 | tf_op jit(solution)/shard_map/ppermute | solution.py:227
  18.1 6.5 %collective-permute-start.6 = (bf16[4,64,256]{2,1,0:T(8,128)(2,1)S(1)}, bf16[4,64,256]{2,1,0:T(8,128)(2,1)S(1)}, u32[]{:S(2)}, u32[]{:S(2)}) collective-permute-start(bf16[4,64,256]{2,1,0:T(8,128)(2,1)S(1)} %get-tuple-element.34), channel_id=1, source_target_pairs={{0,18},{1,19},{2,16},{3,17},{4,22},{5,23},{6,20},{7,21},{8,26},{9,... | collective-permute-start | bytes 393224 | tf_op jit(solution)/shard_map/ppermute | solution.py:227
  19.1 6.2 %collective-permute-start.7 = (bf16[4,64,256]{2,1,0:T(8,128)(2,1)S(1)}, bf16[4,64,256]{2,1,0:T(8,128)(2,1)S(1)}, u32[]{:S(2)}, u32[]{:S(2)}) collective-permute-start(bf16[4,64,256]{2,1,0:T(8,128)(2,1)S(1)} %get-tuple-element.35), channel_id=1, source_target_pairs={{0,16},{1,3},{2,18},{3,1},{4,20},{5,7},{6,22},{7,5},{8,24},{9,11},... | collective-permute-start | bytes 393224 | tf_op jit(solution)/shard_map/ppermute | solution.py:227
  25.3 4.9 %collective-permute-start.8 = (bf16[64,256]{1,0:T(8,128)(2,1)S(1)}, bf16[64,256]{1,0:T(8,128)(2,1)S(1)}, u32[]{:S(2)}, u32[]{:S(2)}) collective-permute-start(bf16[64,256]{1,0:T(8,128)(2,1)S(1)} %get-tuple-element.37), channel_id=1, source_target_pairs={{0,8},{1,9},{2,10},{3,11},{4,12},{5,13},{6,14},{7,15},{8,0},{9,1},... | collective-permute-start | bytes 98312 | tf_op jit(solution)/shard_map/ppermute | solution.py:227
  28.0 5.7 %collective-permute-start.9 = (bf16[64,256]{1,0:T(8,128)(2,1)S(1)}, bf16[64,256]{1,0:T(8,128)(2,1)S(1)}, u32[]{:S(2)}, u32[]{:S(2)}) collective-permute-start(bf16[64,256]{1,0:T(8,128)(2,1)S(1)} %get-tuple-element.38), channel_id=1, source_target_pairs={{0,12},{1,13},{2,14},{3,15},{4,8},{5,9},{6,10},{7,11},{8,4},{9,5},... | collective-permute-start | bytes 98312 | tf_op jit(solution)/shard_map/ppermute | solution.py:227
  29.3 4.4 %collective-permute-start.10 = (bf16[64,256]{1,0:T(8,128)(2,1)S(1)}, bf16[64,256]{1,0:T(8,128)(2,1)S(1)}, u32[]{:S(2)}, u32[]{:S(2)}) collective-permute-start(bf16[64,256]{1,0:T(8,128)(2,1)S(1)} %get-tuple-element.39), channel_id=1, source_target_pairs={{0,4},{1,5},{2,6},{3,7},{4,0},{5,1},{6,2},{7,3},{8,12},{9,13},{10,... | collective-permute-start | bytes 98312 | tf_op jit(solution)/shard_map/ppermute | solution.py:227

commit v7 on v6

--- a/solution.py
+++ b/solution.py
@@ -11,6 +11,9 @@
 VMEM_BYTES = 24 * 1024 * 1024
 F32 = jnp.float32
 BF16 = jnp.bfloat16
+
+
+LONG = pl.CostEstimate(flops=2 * 10**10, bytes_accessed=2**20, transcendentals=0)
 
 
 def nn(a, b):
@@ -62,61 +65,74 @@
             to_ref[i, rank : 2 * rank] = nn(act, flow_ref[:, cols]).astype(BF16)
 
 
-def upper_kernel(
-    share, place_ref, index_ref, saved, top, gains, w_in, w_out,
-    keep_ref, send_ref, flow_ref, xg0_ref, act0_ref, low_ref,
-    x1, x0, g, gain1, gain0, wi1, wi0, wo1, xg1, sems,
+def front_kernel(
+    step, place_ref, saved, top, gains, w_in, w_out,
+    act0_ref, low_ref, xg0_ref, x1, g, gain1, wi1, wo1,
+    x0, gain0, wi0, sems,
 ):
-    place = place_ref[0]
-    upper, lower = 1 - place, place
+    lower = place_ref[0]
+    upper = 1 - lower
     copies = [
+        (gains.at[0, pl.ds(lower, 1)], gain0),
+        (w_in.at[0, lower], wi0),
+        (saved.at[0, lower], x0),
         (gains.at[0, pl.ds(upper, 1)], gain1),
         (w_in.at[0, upper], wi1),
         (saved.at[0, upper], x1),
         (w_out.at[0, upper], wo1),
         (top.at[upper], g),
-        (gains.at[0, pl.ds(lower, 1)], gain0),
-        (w_in.at[0, lower], wi0),
-        (saved.at[0, lower], x0),
     ]
     copies = [pltpu.make_async_copy(a, b, sems.at[i]) for i, (a, b) in enumerate(copies)]
     for copy in copies:
         copy.start()
-    width = x1.shape[1]
-    rank = wi1.shape[0]
-    step = share
     for copy in copies[0:3]:
         copy.wait()
-    scale1, raw1 = project(x1, gain1, wi1, xg1, step)
-    for copy in copies[3:5]:
+    scale, raw = project(x0, gain0, wi0, xg0_ref, step)
+    row = as_row(scale)
+    pre = raw * row
+    sig, slope = silu_slope(pre)
+    act0_ref[...] = (pre * sig).astype(BF16)
+    low_ref[0] = slope
+    low_ref[1] = jnp.broadcast_to(row, raw.shape)
+    for copy in copies[3:8]:
         copy.wait()
-    delta = jnp.zeros(raw1.shape, F32)
+
+
+def upper_kernel(step, x, g, gain, wi, wo, xg_ref, act_ref, das_ref, da_ref, columns_ref):
+    width = x.shape[1]
+    scale, raw = project(x, gain, wi, xg_ref, step)
+    delta = jnp.zeros(raw.shape, F32)
     for c in range(0, width, step):
-        delta += nt(wo1[:, c : c + step], g[:, c : c + step])
-    row1 = as_row(scale1)
-    pre1 = raw1 * row1
-    sig, slope = silu_slope(pre1)
-    act1 = (pre1 * sig).astype(BF16)
-    da1 = (delta * slope).astype(BF16)
-    da1f = da1.astype(F32)
-    inner = jnp.sum(da1f * pre1, axis=0, keepdims=True) * (1.0 / width)
-    das1 = (da1f * row1).astype(BF16)
-    pull = jnp.transpose(jnp.broadcast_to(inner * row1 * row1, (x1.shape[0],) * 2))[:, 0:1]
-    for copy in copies[5:8]:
-        copy.wait()
-    scale0, raw0 = project(x0, gain0, wi0, xg0_ref, step)
-    row0 = as_row(scale0)
-    pre0 = raw0 * row0
-    sig0, slope0 = silu_slope(pre0)
-    act0_ref[...] = (pre0 * sig0).astype(BF16)
-    low_ref[0] = slope0
-    low_ref[1] = jnp.broadcast_to(row0, raw0.shape)
-    for c in range(0, width, step):
+        delta += nt(wo[:, c : c + step], g[:, c : c + step])
+    row = as_row(scale)
+    pre = raw * row
+    sig, slope = silu_slope(pre)
+    da = (delta * slope).astype(BF16)
+    daf = da.astype(F32)
+    inner = jnp.sum(daf * pre, axis=0, keepdims=True) * (1.0 / width)
+    act_ref[...] = (pre * sig).astype(BF16)
+    das_ref[...] = (daf * row).astype(BF16)
+    da_ref[...] = da
+    square = columns_ref.shape[1:]
+    columns_ref[0] = jnp.broadcast_to(scale, square)
+    columns_ref[1] = jnp.transpose(jnp.broadcast_to(inner * row * row, square))
+
+
+def outgoing_kernel(step, x, g, gain, wi, da_ref, columns_ref, flow_ref):
+    da = da_ref[...]
+    scale = columns_ref[0][:, 0:1]
+    pull = columns_ref[1][:, 0:1]
+    for c in range(0, x.shape[1], step):
         cols = slice(c, c + step)
-        dn = tn(da1, wi1[:, cols]) * gain1[:, cols]
-        flow = g[:, cols].astype(F32) + scale1 * dn - pull * x1[:, cols].astype(F32)
+        dn = tn(da, wi[:, cols]) * gain[:, cols]
+        flow = g[:, cols].astype(F32) + scale * dn - pull * x[:, cols].astype(F32)
         flow_ref[:, cols] = flow.astype(BF16)
-    split_terms(share, index_ref[0], das1, xg1, act1, g, keep_ref, send_ref)
+
+
+def terms_kernel(share, index_ref, g, xg_ref, act_ref, das_ref, _, keep_ref, send_ref):
+    split_terms(
+        share, index_ref[0], das_ref[...], xg_ref, act_ref[...], g, keep_ref, send_ref
+    )
 
 
 def pick_kernel(place_ref, index_ref, w_out, out_ref, sems):
@@ -190,33 +206,37 @@
     out_ref[0] = total[rank : 2 * rank]
 
 
-def params():
-    return pltpu.CompilerParams(vmem_limit_bytes=VMEM_BYTES)
-
-
-def whole():
-    return pl.BlockSpec(memory_space=pltpu.VMEM)
+def local(kernel, name, out_shapes, *operands, scratch=(), cost=None):
+    spaces = {"scalar": pltpu.SMEM, "far": pltpu.HBM, "near": pltpu.VMEM}
+    out = pl.pallas_call(
+        kernel,
+        in_specs=[pl.BlockSpec(memory_space=spaces[kind]) for kind, _ in operands],
+        out_specs=[pl.BlockSpec(memory_space=pltpu.VMEM)] * len(out_shapes),
+        out_shape=[jax.ShapeDtypeStruct(shape, dtype) for shape, dtype in out_shapes],
+        scratch_shapes=list(scratch),
+        compiler_params=pltpu.CompilerParams(vmem_limit_bytes=VMEM_BYTES),
+        cost_estimate=cost,
+        name=name,
+    )(*[array for _, array in operands])
+    return out if len(out) > 1 else out[0]
+
+
+def near(*arrays):
+    return [("near", array) for array in arrays]
 
 
 def pair_on_device(saved, top_grad, gains, adapter_in, adapter_out):
-    place = lax.axis_index("section")
     count = lax.axis_size("dp")
     tokens, width = saved.shape[2:]
     rank = adapter_in.shape[3]
     share = width // count
-    adapter_in = jnp.swapaxes(adapter_in, 2, 3)
-    saved, top_grad, gains, adapter_in, adapter_out = [
-        pltpu.with_memory_space_constraint(a, pltpu.HBM)
-        for a in (saved, top_grad, gains, adapter_in, adapter_out)
+    chips, layers = count // 2, count // 4
+    place = ("scalar", lax.axis_index("section").astype(jnp.int32)[None])
+    index = ("scalar", lax.axis_index("dp").astype(jnp.int32)[None])
+    saved, top, gains, w_in, w_out = [
+        ("far", pltpu.with_memory_space_constraint(a, pltpu.HBM))
+        for a in (saved, top_grad, gains, jnp.swapaxes(adapter_in, 2, 3), adapter_out)
     ]
-    place_ref = place.astype(jnp.int32)[None]
-    index_ref = lax.axis_index("dp").astype(jnp.int32)[None]
-    scalar = pl.BlockSpec(memory_space=pltpu.SMEM)
-    chips, layers = count // 2, count // 4
-    blocks = jax.ShapeDtypeStruct((chips, 2 * rank, share), BF16)
-    fourth = jax.ShapeDtypeStruct((layers, 2 * rank, share), BF16)
-    block = jax.ShapeDtypeStruct((2 * rank, share), BF16)
-    wide = jax.ShapeDtypeStruct((tokens, width), BF16)
 
     def swapped(array, *ways):
         pairs = []
@@ -226,85 +246,64 @@
                 pairs.append((s * count + d, (s ^ over_section) * count + (d ^ bits)))
         return lax.ppermute(array, ("section", "dp"), pairs)
 
-    mine = pl.pallas_call(
-        pick_kernel,
-        in_specs=[scalar] * 2 + [pl.BlockSpec(memory_space=pltpu.HBM)],
-        out_specs=whole(),
-        out_shape=jax.ShapeDtypeStruct((rank, width // 2), BF16),
-        scratch_shapes=[pltpu.SemaphoreType.DMA((1,))],
-        compiler_params=params(),
-        name="pick",
-    )(place_ref, index_ref, adapter_out)
-    partner_half = swapped(mine, (1, 0))
-    keep1, send1, flow, xg0, act0, low = pl.pallas_call(
-        partial(upper_kernel, share),
-        in_specs=[scalar] * 2 + [pl.BlockSpec(memory_space=pltpu.HBM)] * 5,
-        out_specs=[whole()] * 6,
-        out_shape=[
-            blocks, blocks, wide, wide,
-            jax.ShapeDtypeStruct((rank, tokens), BF16),
-            jax.ShapeDtypeStruct((2, rank, tokens), F32),
-        ],
-        scratch_shapes=[pltpu.VMEM((tokens, width), BF16)] * 3
-        + [pltpu.VMEM((1, width), F32)] * 2
-        + [pltpu.VMEM((rank, width), BF16)] * 3
-        + [pltpu.VMEM((tokens, width), BF16), pltpu.SemaphoreType.DMA((8,))],
-        compiler_params=params(),
-        cost_estimate=pl.CostEstimate(
-            flops=12 * tokens * width * rank, bytes_accessed=12 * tokens * width, transcendentals=0
-        ),
-        name="upper",
-    )(place_ref, index_ref, saved, top_grad, gains, adapter_in, adapter_out)
-    partner_half, flow = lax.optimization_barrier((partner_half, flow))
-    partner_other = swapped(partner_half, (0, 1))
-    got1 = swapped(send1, (0, 1))
-    send = pl.pallas_call(
-        partial(flow_kernel, share),
-        in_specs=[scalar] + [whole()] * 4,
-        out_specs=whole(),
-        out_shape=jax.ShapeDtypeStruct((2, rank, tokens), BF16),
-        compiler_params=params(),
-        name="flow",
-    )(index_ref, flow, partner_half, partner_other, act0)
-    got = swapped(send, (1, 0))
-    keep0, send0 = pl.pallas_call(
-        partial(lower_kernel, share),
-        in_specs=[scalar] + [whole()] * 4,
-        out_specs=[whole()] * 2,
-        out_shape=[blocks] * 2,
-        compiler_params=params(),
-        name="lower",
-    )(index_ref, flow, xg0, low, got)
-    got0 = swapped(send0, (0, 1))
-    own, first, second, across = pl.pallas_call(
-        plane_kernel,
-        in_specs=[scalar] * 2 + [whole()] * 4,
-        out_specs=[whole()] * 4,
-        out_shape=[fourth] * 4,
-        compiler_params=params(),
-        name="plane",
-    )(place_ref, index_ref, keep1, got1, keep0, got0)
+    sems = pltpu.SemaphoreType.DMA
+    wide = ((tokens, width), BF16)
+    thin = ((rank, width), BF16)
+    gain = ((1, width), F32)
+    small = ((rank, tokens), BF16)
+    blocks = ((chips, 2 * rank, share), BF16)
+    quarter = ((layers, 2 * rank, share), BF16)
+    along_x, other_core = (1, 0), (0, 1)
+
+    mine = local(
+        pick_kernel, "pick", [((rank, width // 2), BF16)], place, index, w_out, scratch=[sems((1,))]
+    )
+    own_half = swapped(mine, along_x)
+    act0, low, xg0, x1, g, gain1, wi1, wo1 = local(
+        partial(front_kernel, share), "front",
+        [small, ((2, rank, tokens), F32), wide, wide, wide, gain, thin, thin],
+        place, saved, top, gains, w_in, w_out,
+        scratch=[pltpu.VMEM(*wide), pltpu.VMEM(*gain), pltpu.VMEM(*thin), sems((8,))],
+    )
+    xg1, act1, das1, da1, columns = local(
+        partial(upper_kernel, share), "upper",
+        [wide, small, small, small, ((2, tokens, tokens), F32)],
+        *near(x1, g, gain1, wi1, wo1),
+    )
+    own_half, da1 = lax.optimization_barrier((own_half, da1))
+    other_half = swapped(own_half, other_core)
+    flow = local(
+        partial(outgoing_kernel, share), "outgoing", [wide], *near(x1, g, gain1, wi1, da1, columns)
+    )
+    send = local(
+        partial(flow_kernel, share), "flow", [((2, rank, tokens), BF16)],
+        index, *near(flow, own_half, other_half, act0), cost=LONG,
+    )
+    got = swapped(send, along_x)
+    keep1, send1 = local(
+        partial(terms_kernel, share), "terms", [blocks, blocks],
+        index, *near(g, xg1, act1, das1, send),
+    )
+    got1 = swapped(send1, other_core)
+    keep0, send0 = local(
+        partial(lower_kernel, share), "lower", [blocks, blocks],
+        index, *near(flow, xg0, low, got), cost=LONG,
+    )
+    got0 = swapped(send0, other_core)
+    own, first, second, across = local(
+        plane_kernel, "plane", [quarter] * 4, place, index, *near(keep1, got1, keep0, got0)
+    )
     first = swapped(first, (0, 2), (1, 0))
     second = swapped(second, (1, 0), (0, 2))
     across = swapped(across, (1, 2))
-    mine, *others = pl.pallas_call(
-        layer_kernel,
-        in_specs=[scalar] + [whole()] * 4,
-        out_specs=[whole()] * layers,
-        out_shape=[block] * layers,
-        compiler_params=params(),
-        name="layer",
-    )(index_ref, own, first, across, second)
+    mine, *others = local(
+        layer_kernel, "layer", [((2 * rank, share), BF16)] * layers,
+        index, *near(own, first, across, second),
+    )
     others = [swapped(other, (0, 4 * k)) for k, other in enumerate(others, 1)]
     others = others[1:] + others[:1]
-    total_in, total_out = pl.pallas_call(
-        total_kernel,
-        in_specs=[whole()] * layers,
-        out_specs=[whole()] * 2,
-        out_shape=[jax.ShapeDtypeStruct((1, rank, share), F32)] * 2,
-        compiler_params=params(),
-        name="total",
-    )(mine, *others)
+    block = ((1, rank, share), F32)
+    total_in, total_out = local(total_kernel, "total", [block, block], *near(mine, *others))
     return (jnp.swapaxes(total_in, 1, 2), total_out)
 
 

time: 34.5 us -> 34.5 us (level)
  waiting for transfers between devices: 14.9 us -> 13.9 us
  starting transfers between devices: 11.9 us -> 12.8 us
    ppermute x11, waiting for transfers between devices: 14.9 us -> 13.9 us  [swapped(): return lax.ppermute(array, ('section', 'dp'), pairs)]
    ppermute x11, starting transfers between devices: 11.9 us -> 12.8 us  [swapped(): return lax.ppermute(array, ('section', 'dp'), pairs)]
    pallas_call x7 -> x10, Pallas kernels: 6.81 us -> 6.9 us  [local(): pl.pallas_call(kernel, in_specs=[pl.BlockSpec(memory_space=spaces[kind])...]
  transfers between devices with their start and end apart: 11 -> 11, of which waited for: 8 -> 9; matrix products, arithmetic and copies ran while one was open for 0% -> 0% of each run, Pallas kernels for 13% -> 14%
where the time goes in v7:
time: 34.5 us; the launch traced here: 34.4 us
  waiting for transfers between devices  13.9 us (40%)
  starting transfers between devices  12.8 us (37%)
  Pallas kernels  6.9 us (20%)
  between operations  0.72 us (2%)
    ppermute x11, waiting for transfers between devices, swapped(): return lax.ppermute(array, ('section', 'dp'), pairs)  13.9 us
    ppermute x11, starting transfers between devices, swapped(): return lax.ppermute(array, ('section', 'dp'), pairs)  12.8 us
    pallas_call x10, Pallas kernels, local(): pl.pallas_call(kernel, in_specs=[pl.BlockSpec(memory_space=spaces[kind])...  6.9 us
  transfers between devices with their start and end apart: 11, of which 9 were waited for; matrix products, arithmetic and copies ran while one was open for 0% of the time, Pallas kernels for 14%

profile of v7, /device:TPU:0, one launch (start us, length us, event | category | flops | bytes accessed | tf_op | source)
XLA Modules:
  0.0 34.4 jit_solution(9609325934059051171)
XLA Ops:
  0.6 0.9 %pick.1 = bf16[32,2048]{1,0:T(8,128)(2,1)S(1)} custom-call(s32[1]{0:T(128)} %bitcast.1.place_ref, s32[1]{0:T(128)} %bitcast.index_ref, bf16[1,2,32,4096]{3,2,1,0:T(8,128)(2,1)} %w_out.3), custom_call_target="tpu_custom_call" | custom-call | tf_op jit(solution)/shard_map/pick/pallas_call | solution.py:211
  1.6 3.0 %collective-permute-start = (bf16[32,2048]{1,0:T(8,128)(2,1)S(1)}, bf16[32,2048]{1,0:T(8,128)(2,1)S(1)}, u32[]{:S(2)}, u32[]{:S(2)}) collective-permute-start(bf16[32,2048]{1,0:T(8,128)(2,1)S(1)} %pick.1), channel_id=1, source_target_pairs={{0,16},{1,17},{2,18},{3,19},{4,20},{5,21},{6,22},{7,23},{8,24},{9,... | collective-permute-start | bytes 393224 | tf_op jit(solution)/shard_map/ppermute | solution.py:247
  4.6 2.2 %front.1 = (bf16[32,128]{1,0:T(8,128)(2,1)S(1)}, f32[2,32,128]{2,1,0:T(8,128)S(1)}, bf16[128,4096]{1,0:T(8,128)(2,1)S(1)}, bf16[128,4096]{1,0:T(8,128)(2,1)S(1)}...) custom-call(s32[1]{0:T(128)} %bitcast.1.place_ref, ...), custom_call_target="tpu_custom_call" | custom-call | tf_op jit(solution)/shard_map/front/pallas_call | solution.py:211
  6.8 0.9 %upper.1 = (bf16[128,4096]{1,0:T(8,128)(2,1)S(1)}, bf16[32,128]{1,0:T(8,128)(2,1)S(1)}, bf16[32,128]{1,0:T(8,128)(2,1)S(1)}, bf16[32,128]{1,0:T(8,128)(2,1)S(1)}, f32[2,128,128]{2,1,0:T(8,128)S(1)}) custom-call(bf16[128,4096]{1,0:T(8,128)(2,1)S(1)} %get-tuple-element.32.x, bf16[128,4096]{1,0:T(8,128)(2,1)S(1)} %get-tuple-element.31.g, ...), custom_call_target="tpu_custom_call" | custom-call | tf_op jit(solution)/shard_map/upper/pallas_call | solution.py:211
  7.7 0.3 %collective-permute-done.own_ref = bf16[32,2048]{1,0:T(8,128)(2,1)S(1)} collective-permute-done((bf16[32,2048]{1,0:T(8,128)(2,1)S(1)}, bf16[32,2048]{1,0:T(8,128)(2,1)S(1)}, u32[]{:S(2)}, u32[]{:S(2)}) %collective-permute-start) | collective-permute-done | bytes 131104 | tf_op jit(solution)/shard_map/ppermute | solution.py:247
  8.1 0.0 collective-permute-start.1
  8.1 0.7 %outgoing.1.flow_ref = bf16[128,4096]{1,0:T(8,128)(2,1)S(1)} custom-call(bf16[128,4096]{1,0:T(8,128)(2,1)S(1)} %get-tuple-element.32.x, bf16[128,4096]{1,0:T(8,128)(2,1)S(1)} %get-tuple-element.31.g, f32[1,4096]{1,0:T(1,128)S(1)} %get-tuple-element.33.gain, bf16[32,4096]{1,0:T(8,128)(2,1)S(1)} %get-tuple-element.34.wi, ...), custom_call_target="tpu_custom_call" | custom-call | tf_op jit(solution)/shard_map/outgoing/pallas_call | solution.py:211
  8.8 0.6 %collective-permute-done.1.other_ref = bf16[32,2048]{1,0:T(8,128)(2,1)S(1)} collective-permute-done((bf16[32,2048]{1,0:T(8,128)(2,1)S(1)}, bf16[32,2048]{1,0:T(8,128)(2,1)S(1)}, u32[]{:S(2)}, u32[]{:S(2)}) %collective-permute-start.1) | collective-permute-done | bytes 131104 | tf_op jit(solution)/shard_map/ppermute | solution.py:247
  9.4 0.4 %flow.1._ = bf16[2,32,128]{2,1,0:T(8,128)(2,1)S(1)} custom-call(s32[1]{0:T(128)} %bitcast.index_ref, bf16[128,4096]{1,0:T(8,128)(2,1)S(1)} %outgoing.1.flow_ref, bf16[32,2048]{1,0:T(8,128)(2,1)S(1)} %collective-permute-done.own_ref, bf16[32,2048]{1,0:T(8,128)(2,1)S(1)} %collective-permute-done.1.other_ref, bf16[32,128]{1,0:T(8,128)(2,1)S(1)} %get-tuple-element.43.act0_ref), custom_call_target="tpu_custom_call" | custom-call | flops 20000000000 | bytes 1048576 | tf_op jit(solution)/shard_map/flow/pallas_call | solution.py:211
  9.9 1.8 %collective-permute-start.3 = (bf16[2,32,128]{2,1,0:T(8,128)(2,1)S(1)}, bf16[2,32,128]{2,1,0:T(8,128)(2,1)S(1)}, u32[]{:S(2)}, u32[]{:S(2)}) collective-permute-start(bf16[2,32,128]{2,1,0:T(8,128)(2,1)S(1)} %flow.1._), channel_id=1, source_target_pairs={{0,16},{1,17},{2,18},{3,19},{4,20},{5,21},{6,22},{7,23},{8,24},{9,... | collective-permute-start | bytes 49160 | tf_op jit(solution)/shard_map/ppermute | solution.py:247
  11.6 0.4 %terms.1 = (bf16[8,64,256]{2,1,0:T(8,128)(2,1)S(1)}, bf16[8,64,256]{2,1,0:T(8,128)(2,1)S(1)}) custom-call(s32[1]{0:T(128)} %bitcast.index_ref, bf16[128,4096]{1,0:T(8,128)(2,1)S(1)} %get-tuple-element.31.g, bf16[128,4096]{1,0:T(8,128)(2,1)S(1)} %get-tuple-element.36.xg_ref, bf16[32,128]{1,0:T(8,128)(2,1)S(1)} %get-tuple-element.37.act_ref, ...), custom_call_target="tpu_custom_call" | custom-call | tf_op jit(solution)/shard_map/terms/pallas_call | solution.py:211
  12.0 0.1 collective-permute-start.2
  12.1 1.5 %collective-permute-done.3.got_ref = bf16[2,32,128]{2,1,0:T(8,128)(2,1)S(1)} collective-permute-done((bf16[2,32,128]{2,1,0:T(8,128)(2,1)S(1)}, bf16[2,32,128]{2,1,0:T(8,128)(2,1)S(1)}, u32[]{:S(2)}, u32[]{:S(2)}) %collective-permute-start.3) | collective-permute-done | bytes 16416 | tf_op jit(solution)/shard_map/ppermute | solution.py:247
  13.6 0.4 %lower.1 = (bf16[8,64,256]{2,1,0:T(8,128)(2,1)S(1)}, bf16[8,64,256]{2,1,0:T(8,128)(2,1)S(1)}) custom-call(s32[1]{0:T(128)} %bitcast.index_ref, bf16[128,4096]{1,0:T(8,128)(2,1)S(1)} %outgoing.1.flow_ref, bf16[128,4096]{1,0:T(8,128)(2,1)S(1)} %get-tuple-element.46.xg0_ref, f32[2,32,128]{2,1,0:T(8,128)S(1)} %get-tuple-element.47.low_ref, ...), custom_call_target="tpu_custom_call" | custom-call | flops 20000000000 | bytes 1048576 | tf_op jit(solution)/shard_map/lower/pallas_call | solution.py:211
  14.0 0.1 collective-permute-start.4
  14.1 0.0 collective-permute-done.2.got1
  14.1 1.5 %collective-permute-done.4.got0 = bf16[8,64,256]{2,1,0:T(8,128)(2,1)S(1)} collective-permute-done((bf16[8,64,256]{2,1,0:T(8,128)(2,1)S(1)}, bf16[8,64,256]{2,1,0:T(8,128)(2,1)S(1)}, u32[]{:S(2)}, u32[]{:S(2)}) %collective-permute-start.4) | collective-permute-done | bytes 262176 | tf_op jit(solution)/shard_map/ppermute | solution.py:247
  15.6 0.1 plane.1
  15.8 1.8 %collective-permute-start.5 = (bf16[4,64,256]{2,1,0:T(8,128)(2,1)S(1)}, bf16[4,64,256]{2,1,0:T(8,128)(2,1)S(1)}, u32[]{:S(2)}, u32[]{:S(2)}) collective-permute-start(bf16[4,64,256]{2,1,0:T(8,128)(2,1)S(1)} %get-tuple-element.51), channel_id=1, source_target_pairs={{0,2},{1,17},{2,0},{3,19},{4,6},{5,21},{6,4},{7,23},{8,10},{9,25},... | collective-permute-start | bytes 393224 | tf_op jit(solution)/shard_map/ppermute | solution.py:247
  17.6 1.5 %collective-permute-start.6 = (bf16[4,64,256]{2,1,0:T(8,128)(2,1)S(1)}, bf16[4,64,256]{2,1,0:T(8,128)(2,1)S(1)}, u32[]{:S(2)}, u32[]{:S(2)}) collective-permute-start(bf16[4,64,256]{2,1,0:T(8,128)(2,1)S(1)} %get-tuple-element.52), channel_id=1, source_target_pairs={{0,18},{1,19},{2,16},{3,17},{4,22},{5,23},{6,20},{7,21},{8,26},{9,... | collective-permute-start | bytes 393224 | tf_op jit(solution)/shard_map/ppermute | solution.py:247
  19.1 0.3 collective-permute-start.7
  19.3 4.6 %collective-permute-done.5.got_a = bf16[4,64,256]{2,1,0:T(8,128)(2,1)S(1)} collective-permute-done((bf16[4,64,256]{2,1,0:T(8,128)(2,1)S(1)}, bf16[4,64,256]{2,1,0:T(8,128)(2,1)S(1)}, u32[]{:S(2)}, u32[]{:S(2)}) %collective-permute-start.5) | collective-permute-done | bytes 131104 | tf_op jit(solution)/shard_map/ppermute | solution.py:247
  24.0 0.1 collective-permute-done.6.got_b
  24.1 1.0 %collective-permute-done.7.got_c = bf16[4,64,256]{2,1,0:T(8,128)(2,1)S(1)} collective-permute-done((bf16[4,64,256]{2,1,0:T(8,128)(2,1)S(1)}, bf16[4,64,256]{2,1,0:T(8,128)(2,1)S(1)}, u32[]{:S(2)}, u32[]{:S(2)}) %collective-permute-start.7) | collective-permute-done | bytes 131104 | tf_op jit(solution)/shard_map/ppermute | solution.py:247
  25.1 0.1 layer.1
  25.2 2.8 %collective-permute-start.8 = (bf16[64,256]{1,0:T(8,128)(2,1)S(1)}, bf16[64,256]{1,0:T(8,128)(2,1)S(1)}, u32[]{:S(2)}, u32[]{:S(2)}) collective-permute-start(bf16[64,256]{1,0:T(8,128)(2,1)S(1)} %get-tuple-element.55), channel_id=1, source_target_pairs={{0,8},{1,9},{2,10},{3,11},{4,12},{5,13},{6,14},{7,15},{8,0},{9,1},... | collective-permute-start | bytes 98312 | tf_op jit(solution)/shard_map/ppermute | solution.py:247
  28.0 1.3 %collective-permute-start.9 = (bf16[64,256]{1,0:T(8,128)(2,1)S(1)}, bf16[64,256]{1,0:T(8,128)(2,1)S(1)}, u32[]{:S(2)}, u32[]{:S(2)}) collective-permute-start(bf16[64,256]{1,0:T(8,128)(2,1)S(1)} %get-tuple-element.56), channel_id=1, source_target_pairs={{0,12},{1,13},{2,14},{3,15},{4,8},{5,9},{6,10},{7,11},{8,4},{9,5},... | collective-permute-start | bytes 98312 | tf_op jit(solution)/shard_map/ppermute | solution.py:247
  29.3 0.2 collective-permute-start.10
  29.6 0.5 %collective-permute-done.8.refs_1_ = bf16[64,256]{1,0:T(8,128)(2,1)S(1)} collective-permute-done((bf16[64,256]{1,0:T(8,128)(2,1)S(1)}, bf16[64,256]{1,0:T(8,128)(2,1)S(1)}, u32[]{:S(2)}, u32[]{:S(2)}) %collective-permute-start.8) | collective-permute-done | bytes 32800 | tf_op jit(solution)/shard_map/ppermute | solution.py:247
  30.1 3.6 %collective-permute-done.9.refs_2_ = bf16[64,256]{1,0:T(8,128)(2,1)S(1)} collective-permute-done((bf16[64,256]{1,0:T(8,128)(2,1)S(1)}, bf16[64,256]{1,0:T(8,128)(2,1)S(1)}, u32[]{:S(2)}, u32[]{:S(2)}) %collective-permute-start.9) | collective-permute-done | bytes 32800 | tf_op jit(solution)/shard_map/ppermute | solution.py:247
  33.7 0.0 collective-permute-done.10.refs_3_
  33.7 0.6 %total.1 = (f32[1,32,256]{2,1,0:T(8,128)}, f32[1,32,256]{2,1,0:T(8,128)}) custom-call(bf16[64,256]{1,0:T(8,128)(2,1)S(1)} %get-tuple-element.54.refs_0_, bf16[64,256]{1,0:T(8,128)(2,1)S(1)} %collective-permute-done.8.refs_1_, bf16[64,256]{1,0:T(8,128)(2,1)S(1)} %collective-permute-done.9.refs_2_, bf16[64,256]{1,0:T(8,128)(2,1)S(1)} %collective-permute-done.10.refs_3_), custom_call_target="tpu_custom_call" | custom-call | tf_op jit(solution)/shard_map/total/pallas_call | solution.py:211
Async XLA Ops:
  1.6 6.5 %collective-permute-start = (bf16[32,2048]{1,0:T(8,128)(2,1)S(1)}, bf16[32,2048]{1,0:T(8,128)(2,1)S(1)}, u32[]{:S(2)}, u32[]{:S(2)}) collective-permute-start(bf16[32,2048]{1,0:T(8,128)(2,1)S(1)} %pick.1), channel_id=1, source_target_pairs={{0,16},{1,17},{2,18},{3,19},{4,20},{5,21},{6,22},{7,23},{8,24},{9,... | collective-permute-start | bytes 393224 | tf_op jit(solution)/shard_map/ppermute | solution.py:247
  8.1 1.3 %collective-permute-start.1 = (bf16[32,2048]{1,0:T(8,128)(2,1)S(1)}, bf16[32,2048]{1,0:T(8,128)(2,1)S(1)}, u32[]{:S(2)}, u32[]{:S(2)}) collective-permute-start(bf16[32,2048]{1,0:T(8,128)(2,1)S(1)} %collective-permute-done.own_ref), channel_id=1, source_target_pairs={{0,1},{1,0},{2,3},{3,2},{4,5},{5,4},{6,7},{7,6},{8,9},{9,8},{10,11... | collective-permute-start | bytes 393224 | tf_op jit(solution)/shard_map/ppermute | solution.py:247
  9.9 3.8 %collective-permute-start.3 = (bf16[2,32,128]{2,1,0:T(8,128)(2,1)S(1)}, bf16[2,32,128]{2,1,0:T(8,128)(2,1)S(1)}, u32[]{:S(2)}, u32[]{:S(2)}) collective-permute-start(bf16[2,32,128]{2,1,0:T(8,128)(2,1)S(1)} %flow.1._), channel_id=1, source_target_pairs={{0,16},{1,17},{2,18},{3,19},{4,20},{5,21},{6,22},{7,23},{8,24},{9,... | collective-permute-start | bytes 49160 | tf_op jit(solution)/shard_map/ppermute | solution.py:247
  12.0 2.1 %collective-permute-start.2 = (bf16[8,64,256]{2,1,0:T(8,128)(2,1)S(1)}, bf16[8,64,256]{2,1,0:T(8,128)(2,1)S(1)}, u32[]{:S(2)}, u32[]{:S(2)}) collective-permute-start(bf16[8,64,256]{2,1,0:T(8,128)(2,1)S(1)} %get-tuple-element.45), channel_id=1, source_target_pairs={{0,1},{1,0},{2,3},{3,2},{4,5},{5,4},{6,7},{7,6},{8,9},{9,8},{10,11... | collective-permute-start | bytes 786440 | tf_op jit(solution)/shard_map/ppermute | solution.py:247
  14.0 1.6 %collective-permute-start.4 = (bf16[8,64,256]{2,1,0:T(8,128)(2,1)S(1)}, bf16[8,64,256]{2,1,0:T(8,128)(2,1)S(1)}, u32[]{:S(2)}, u32[]{:S(2)}) collective-permute-start(bf16[8,64,256]{2,1,0:T(8,128)(2,1)S(1)} %get-tuple-element.49), channel_id=1, source_target_pairs={{0,1},{1,0},{2,3},{3,2},{4,5},{5,4},{6,7},{7,6},{8,9},{9,8},{10,11... | collective-permute-start | bytes 786440 | tf_op jit(solution)/shard_map/ppermute | solution.py:247
  15.8 8.2 %collective-permute-start.5 = (bf16[4,64,256]{2,1,0:T(8,128)(2,1)S(1)}, bf16[4,64,256]{2,1,0:T(8,128)(2,1)S(1)}, u32[]{:S(2)}, u32[]{:S(2)}) collective-permute-start(bf16[4,64,256]{2,1,0:T(8,128)(2,1)S(1)} %get-tuple-element.51), channel_id=1, source_target_pairs={{0,2},{1,17},{2,0},{3,19},{4,6},{5,21},{6,4},{7,23},{8,10},{9,25},... | collective-permute-start | bytes 393224 | tf_op jit(solution)/shard_map/ppermute | solution.py:247
  17.6 6.5 %collective-permute-start.6 = (bf16[4,64,256]{2,1,0:T(8,128)(2,1)S(1)}, bf16[4,64,256]{2,1,0:T(8,128)(2,1)S(1)}, u32[]{:S(2)}, u32[]{:S(2)}) collective-permute-start(bf16[4,64,256]{2,1,0:T(8,128)(2,1)S(1)} %get-tuple-element.52), channel_id=1, source_target_pairs={{0,18},{1,19},{2,16},{3,17},{4,22},{5,23},{6,20},{7,21},{8,26},{9,... | collective-permute-start | bytes 393224 | tf_op jit(solution)/shard_map/ppermute | solution.py:247
  19.1 6.1 %collective-permute-start.7 = (bf16[4,64,256]{2,1,0:T(8,128)(2,1)S(1)}, bf16[4,64,256]{2,1,0:T(8,128)(2,1)S(1)}, u32[]{:S(2)}, u32[]{:S(2)}) collective-permute-start(bf16[4,64,256]{2,1,0:T(8,128)(2,1)S(1)} %get-tuple-element.53), channel_id=1, source_target_pairs={{0,16},{1,3},{2,18},{3,1},{4,20},{5,7},{6,22},{7,5},{8,24},{9,11},... | collective-permute-start | bytes 393224 | tf_op jit(solution)/shard_map/ppermute | solution.py:247
  25.2 4.9 %collective-permute-start.8 = (bf16[64,256]{1,0:T(8,128)(2,1)S(1)}, bf16[64,256]{1,0:T(8,128)(2,1)S(1)}, u32[]{:S(2)}, u32[]{:S(2)}) collective-permute-start(bf16[64,256]{1,0:T(8,128)(2,1)S(1)} %get-tuple-element.55), channel_id=1, source_target_pairs={{0,8},{1,9},{2,10},{3,11},{4,12},{5,13},{6,14},{7,15},{8,0},{9,1},... | collective-permute-start | bytes 98312 | tf_op jit(solution)/shard_map/ppermute | solution.py:247
  28.0 5.7 %collective-permute-start.9 = (bf16[64,256]{1,0:T(8,128)(2,1)S(1)}, bf16[64,256]{1,0:T(8,128)(2,1)S(1)}, u32[]{:S(2)}, u32[]{:S(2)}) collective-permute-start(bf16[64,256]{1,0:T(8,128)(2,1)S(1)} %get-tuple-element.56), channel_id=1, source_target_pairs={{0,12},{1,13},{2,14},{3,15},{4,8},{5,9},{6,10},{7,11},{8,4},{9,5},... | collective-permute-start | bytes 98312 | tf_op jit(solution)/shard_map/ppermute | solution.py:247
  29.3 4.4 %collective-permute-start.10 = (bf16[64,256]{1,0:T(8,128)(2,1)S(1)}, bf16[64,256]{1,0:T(8,128)(2,1)S(1)}, u32[]{:S(2)}, u32[]{:S(2)}) collective-permute-start(bf16[64,256]{1,0:T(8,128)(2,1)S(1)} %get-tuple-element.57), channel_id=1, source_target_pairs={{0,4},{1,5},{2,6},{3,7},{4,0},{5,1},{6,2},{7,3},{8,12},{9,13},{10,... | collective-permute-start | bytes 98312 | tf_op jit(solution)/shard_map/ppermute | solution.py:247

commit v8 on v7

--- a/solution.py
+++ b/solution.py
@@ -55,14 +55,13 @@
     return scale, pre
 
 
-def split_terms(share, index, das, xg_ref, act, flow_ref, keep_ref, send_ref):
-    rank = das.shape[0]
+def fill(index, matrix, wide_ref, keep_ref, send_ref):
+    share = keep_ref.shape[2]
     core = index % 2
-    for i in range(keep_ref.shape[0]):
+    for i in range(wide_ref.shape[1] // share // 2):
         for to_ref, number in ((keep_ref, core), (send_ref, 1 - core)):
             cols = pl.ds(pl.multiple_of((2 * i + number) * share, share), share)
-            to_ref[i, 0:rank] = nn(das, xg_ref[:, cols]).astype(BF16)
-            to_ref[i, rank : 2 * rank] = nn(act, flow_ref[:, cols]).astype(BF16)
+            to_ref[i] = nn(matrix, wide_ref[:, cols]).astype(BF16)
 
 
 def front_kernel(
@@ -129,10 +128,20 @@
         flow_ref[:, cols] = flow.astype(BF16)
 
 
-def terms_kernel(share, index_ref, g, xg_ref, act_ref, das_ref, _, keep_ref, send_ref):
-    split_terms(
-        share, index_ref[0], das_ref[...], xg_ref, act_ref[...], g, keep_ref, send_ref
-    )
+def terms1_kernel(index_ref, g, xg_ref, act_ref, das_ref, _, keep_out, send_out, keep_in, send_in):
+    fill(index_ref[0], act_ref[...], g, keep_out, send_out)
+    fill(index_ref[0], das_ref[...], xg_ref, keep_in, send_in)
+
+
+def terms_kernel(
+    index_ref, flow_ref, act0_ref, keep_out1, send_out1, keep_in1, send_in1, keep_ref, send_ref
+):
+    fill(index_ref[0], act0_ref[...], flow_ref, keep_ref, send_ref)
+    chips = keep_in1.shape[0]
+    keep_ref[chips : 2 * chips] = keep_out1[...]
+    send_ref[chips : 2 * chips] = send_out1[...]
+    keep_ref[2 * chips : 3 * chips] = keep_in1[...]
+    send_ref[2 * chips : 3 * chips] = send_in1[...]
 
 
 def pick_kernel(place_ref, index_ref, w_out, out_ref, sems):
@@ -143,57 +152,80 @@
     copy.wait()
 
 
-def flow_kernel(share, index_ref, flow_ref, own_ref, other_ref, act0_ref, send_ref):
+def flow_kernel(share, index_ref, flow_ref, own_ref, other_ref, send_ref):
     half = own_ref.shape[1]
     core = index_ref[0] % 2
-    delta = jnp.zeros(act0_ref.shape, F32)
+    delta = jnp.zeros(send_ref.shape, F32)
     for w_ref, number in ((own_ref, core), (other_ref, 1 - core)):
         for c in range(0, half, share):
             cols = pl.ds(pl.multiple_of(number * half + c, share), share)
             delta += nt(w_ref[:, c : c + share], flow_ref[:, cols])
-    send_ref[0] = act0_ref[...]
-    send_ref[1] = delta.astype(BF16)
-
-
-def lower_kernel(share, index_ref, flow_ref, xg0_ref, low_ref, got_ref, keep_ref, send_ref):
-    da0 = (got_ref[1].astype(F32) * low_ref[0]).astype(BF16)
-    das0 = (da0.astype(F32) * low_ref[1]).astype(BF16)
-    split_terms(share, index_ref[0], das0, xg0_ref, got_ref[0], flow_ref, keep_ref, send_ref)
+    send_ref[...] = delta.astype(BF16)
+
+
+def lower_kernel(index_ref, xg0_ref, low_ref, got_ref, keep_ref, send_ref):
+    da = (got_ref[...].astype(F32) * low_ref[0]).astype(BF16)
+    das = (da.astype(F32) * low_ref[1]).astype(BF16)
+    fill(index_ref[0], das, xg0_ref, keep_ref, send_ref)
+
+
+def chip_kernel(place_ref, index_ref, keep, got, _, sum_ref, across):
+    for i in range(keep.shape[0]):
+        sum_ref[i] = (keep[i].astype(F32) + got[i].astype(F32)).astype(BF16)
+    row = (index_ref[0] // 2) % 2
+    first = (1 - place_ref[0]) * (2 * across.shape[0]) + 1 - row
+    for i in range(across.shape[0]):
+        across[i] = sum_ref[first + 2 * i]
 
 
 def plane_kernel(
-    place_ref, index_ref, keep1, got1, keep0, got0, own_ref, first_ref, second_ref, across
+    place_ref, index_ref, sums, keep0, got0, own_ref, first_ref, second_ref, across
 ):
+    rank = keep0.shape[1]
+    chips = keep0.shape[0]
     row = (index_ref[0] // 2) % 2
 
-    def order(near, far, along_x, along_y):
+    def terms_in(section, block):
+        if section == 0:
+            return (keep0[block].astype(F32) + got0[block].astype(F32)).astype(BF16)
+        return sums[2 * chips + block]
+
+    def order(near, along_x, along_y):
+        far = 1 - near
         for i in range(own_ref.shape[0]):
-            for to_ref, (keep, got), number in (
-                (across, far, 1 - row),
+            across[i] = terms_in(far, 2 * i + 1 - row)
+            for to_ref, section, number in (
                 (along_x, far, row),
                 (along_y, near, 1 - row),
                 (own_ref, near, row),
             ):
                 block = 2 * i + number
-                to_ref[i] = (keep[block].astype(F32) + got[block].astype(F32)).astype(BF16)
-
-    for place, near, far in (
-        (1, (keep1, got1), (keep0, got0)),
-        (0, (keep0, got0), (keep1, got1)),
-    ):
+                to_ref[i, 0:rank] = terms_in(section, block)
+                to_ref[i, rank : 2 * rank] = sums[section * chips + block]
+
+    for place in range(2):
         for core, ways in ((0, (second_ref, first_ref)), (1, (first_ref, second_ref))):
             pl.when((place_ref[0] == place) & (index_ref[0] % 2 == core))(
-                partial(order, near, far, *ways)
+                partial(order, place, *ways)
             )
 
 
-def layer_kernel(index_ref, own, got_a, got_b, got_c, *out_refs):
+def add_kernel(own, across_out, out_ref):
+    rank = across_out.shape[1]
+    out_ref[:, 0:rank] = own[:, 0:rank]
+    for i in range(own.shape[0]):
+        total = own[i, rank : 2 * rank].astype(F32) + across_out[i].astype(F32)
+        out_ref[i, rank : 2 * rank] = total.astype(BF16)
+
+
+def layer_kernel(index_ref, own, first, across_in, second, *out_refs):
+    rank = across_in.shape[1]
     layer = index_ref[0] // 4
     for k, out_ref in enumerate(out_refs):
         block = layer ^ k
-        total = own[block].astype(F32) + got_a[block].astype(F32)
-        total += got_b[block].astype(F32) + got_c[block].astype(F32)
-        out_ref[...] = total.astype(BF16)
+        total = sum(ref[block].astype(F32) for ref in (own, first, second))
+        out_ref[0:rank] = (total[0:rank] + across_in[block].astype(F32)).astype(BF16)
+        out_ref[rank : 2 * rank] = total[rank : 2 * rank].astype(BF16)
 
 
 def total_kernel(*refs):
@@ -251,8 +283,10 @@
     thin = ((rank, width), BF16)
     gain = ((1, width), F32)
     small = ((rank, tokens), BF16)
-    blocks = ((chips, 2 * rank, share), BF16)
-    quarter = ((layers, 2 * rank, share), BF16)
+    one = ((chips, rank, share), BF16)
+    three = ((3 * chips, rank, share), BF16)
+    quarter = ((layers, rank, share), BF16)
+    double = ((layers, 2 * rank, share), BF16)
     along_x, other_core = (1, 0), (0, 1)
 
     mine = local(
@@ -265,6 +299,7 @@
         place, saved, top, gains, w_in, w_out,
         scratch=[pltpu.VMEM(*wide), pltpu.VMEM(*gain), pltpu.VMEM(*thin), sems((8,))],
     )
+    got_act0 = swapped(act0, along_x)
     xg1, act1, das1, da1, columns = local(
         partial(upper_kernel, share), "upper",
         [wide, small, small, small, ((2, tokens, tokens), F32)],
@@ -273,32 +308,39 @@
     own_half, da1 = lax.optimization_barrier((own_half, da1))
     other_half = swapped(own_half, other_core)
     flow = local(
-        partial(outgoing_kernel, share), "outgoing", [wide], *near(x1, g, gain1, wi1, da1, columns)
-    )
-    send = local(
-        partial(flow_kernel, share), "flow", [((2, rank, tokens), BF16)],
-        index, *near(flow, own_half, other_half, act0), cost=LONG,
-    )
-    got = swapped(send, along_x)
-    keep1, send1 = local(
-        partial(terms_kernel, share), "terms", [blocks, blocks],
-        index, *near(g, xg1, act1, das1, send),
-    )
-    got1 = swapped(send1, other_core)
+        partial(outgoing_kernel, share), "outgoing", [wide], *near(x1, g, gain1, wi1, da1, columns),
+        cost=LONG,
+    )
+    delta = local(
+        partial(flow_kernel, share), "flow", [small], index, *near(flow, own_half, other_half),
+    )
+    got_delta = swapped(delta, along_x)
+    terms1 = local(
+        terms1_kernel, "terms1", [one] * 4, index, *near(g, xg1, act1, das1, delta)
+    )
+    keep, send = local(
+        terms_kernel, "terms", [three, three], index, *near(flow, got_act0, *terms1)
+    )
+    got = swapped(send, other_core)
     keep0, send0 = local(
-        partial(lower_kernel, share), "lower", [blocks, blocks],
-        index, *near(flow, xg0, low, got), cost=LONG,
+        lower_kernel, "lower", [one, one], index, *near(xg0, low, got_delta), cost=LONG
     )
     got0 = swapped(send0, other_core)
-    own, first, second, across = local(
-        plane_kernel, "plane", [quarter] * 4, place, index, *near(keep1, got1, keep0, got0)
+    sums, across_out = local(
+        chip_kernel, "chip", [three, quarter], place, index, *near(keep, got, keep0)
+    )
+    across_out = swapped(across_out, (1, 2))
+    own, first, second, across_in = local(
+        plane_kernel, "plane", [double, double, double, quarter],
+        place, index, *near(sums, keep0, got0),
     )
     first = swapped(first, (0, 2), (1, 0))
+    across_in = swapped(across_in, (1, 2))
     second = swapped(second, (1, 0), (0, 2))
-    across = swapped(across, (1, 2))
+    own = local(add_kernel, "add", [double], *near(own, across_out), cost=LONG)
     mine, *others = local(
         layer_kernel, "layer", [((2 * rank, share), BF16)] * layers,
-        index, *near(own, first, across, second),
+        index, *near(own, first, across_in, second),
     )
     others = [swapped(other, (0, 4 * k)) for k, other in enumerate(others, 1)]
     others = others[1:] + others[:1]

time: 34.5 us -> 34.1 us (0.988)
  waiting for transfers between devices: 13.9 us -> 10.7 us
  starting transfers between devices: 12.8 us -> 15.4 us
    ppermute x11 -> x13, waiting for transfers between devices: 13.9 us -> 10.7 us  [swapped(): return lax.ppermute(array, ('section', 'dp'), pairs)]
    ppermute x11 -> x13, starting transfers between devices: 12.8 us -> 15.4 us  [swapped(): return lax.ppermute(array, ('section', 'dp'), pairs)]
    pallas_call x10 -> x13, Pallas kernels: 6.9 us -> 7.07 us  [local(): pl.pallas_call(kernel, in_specs=[pl.BlockSpec(memory_space=spaces[kind])...]
  transfers between devices with their start and end apart: 11 -> 13, of which waited for: 9 -> 8; matrix products, arithmetic and copies ran while one was open for 0% -> 0% of each run, Pallas kernels for 14% -> 16%
where the time goes in v8:
time: 34.1 us; the launch traced here: 34 us
  starting transfers between devices  15.4 us (45%)
  waiting for transfers between devices  10.7 us (31%)
  Pallas kernels  7.07 us (21%)
  between operations  0.74 us (2%)
    ppermute x13, starting transfers between devices, swapped(): return lax.ppermute(array, ('section', 'dp'), pairs)  15.4 us
    ppermute x13, waiting for transfers between devices, swapped(): return lax.ppermute(array, ('section', 'dp'), pairs)  10.7 us
    pallas_call x13, Pallas kernels, local(): pl.pallas_call(kernel, in_specs=[pl.BlockSpec(memory_space=spaces[kind])...  7.07 us
  transfers between devices with their start and end apart: 13, of which 8 were waited for; matrix products, arithmetic and copies ran while one was open for 0% of the time, Pallas kernels for 16%

profile of v8, /device:TPU:0, one launch (start us, length us, event | category | flops | bytes accessed | tf_op | source)
XLA Modules:
  0.0 34.0 jit_solution(7416168328981533954)
XLA Ops:
  0.6 0.9 %pick.1 = bf16[32,2048]{1,0:T(8,128)(2,1)S(1)} custom-call(s32[1]{0:T(128)} %bitcast.1.place_ref, s32[1]{0:T(128)} %bitcast.index_ref, bf16[1,2,32,4096]{3,2,1,0:T(8,128)(2,1)} %w_out.3), custom_call_target="tpu_custom_call" | custom-call | tf_op jit(solution)/shard_map/pick/pallas_call | solution.py:243
  1.6 3.0 %collective-permute-start = (bf16[32,2048]{1,0:T(8,128)(2,1)S(1)}, bf16[32,2048]{1,0:T(8,128)(2,1)S(1)}, u32[]{:S(2)}, u32[]{:S(2)}) collective-permute-start(bf16[32,2048]{1,0:T(8,128)(2,1)S(1)} %pick.1), channel_id=1, source_target_pairs={{0,16},{1,17},{2,18},{3,19},{4,20},{5,21},{6,22},{7,23},{8,24},{9,... | collective-permute-start | bytes 393224 | tf_op jit(solution)/shard_map/ppermute | solution.py:279
  4.6 2.2 %front.1 = (bf16[32,128]{1,0:T(8,128)(2,1)S(1)}, f32[2,32,128]{2,1,0:T(8,128)S(1)}, bf16[128,4096]{1,0:T(8,128)(2,1)S(1)}, bf16[128,4096]{1,0:T(8,128)(2,1)S(1)}...) custom-call(s32[1]{0:T(128)} %bitcast.1.place_ref, ...), custom_call_target="tpu_custom_call" | custom-call | tf_op jit(solution)/shard_map/front/pallas_call | solution.py:243
  6.8 0.1 collective-permute-start.1
  6.9 0.9 %upper.1 = (bf16[128,4096]{1,0:T(8,128)(2,1)S(1)}, bf16[32,128]{1,0:T(8,128)(2,1)S(1)}, bf16[32,128]{1,0:T(8,128)(2,1)S(1)}, bf16[32,128]{1,0:T(8,128)(2,1)S(1)}, f32[2,128,128]{2,1,0:T(8,128)S(1)}) custom-call(bf16[128,4096]{1,0:T(8,128)(2,1)S(1)} %get-tuple-element.37.x, bf16[128,4096]{1,0:T(8,128)(2,1)S(1)} %get-tuple-element.38.g, ...), custom_call_target="tpu_custom_call" | custom-call | tf_op jit(solution)/shard_map/upper/pallas_call | solution.py:243
  7.8 0.3 collective-permute-done.own_ref
  8.1 0.0 collective-permute-start.2
  8.1 0.7 %outgoing.1.flow_ref = bf16[128,4096]{1,0:T(8,128)(2,1)S(1)} custom-call(bf16[128,4096]{1,0:T(8,128)(2,1)S(1)} %get-tuple-element.37.x, bf16[128,4096]{1,0:T(8,128)(2,1)S(1)} %get-tuple-element.38.g, f32[1,4096]{1,0:T(1,128)S(1)} %get-tuple-element.39.gain, bf16[32,4096]{1,0:T(8,128)(2,1)S(1)} %get-tuple-element.40.wi, ...), custom_call_target="tpu_custom_call" | custom-call | flops 20000000000 | bytes 1048576 | tf_op jit(solution)/shard_map/outgoing/pallas_call | solution.py:243
  8.8 0.6 %collective-permute-done.2.other_ref = bf16[32,2048]{1,0:T(8,128)(2,1)S(1)} collective-permute-done((bf16[32,2048]{1,0:T(8,128)(2,1)S(1)}, bf16[32,2048]{1,0:T(8,128)(2,1)S(1)}, u32[]{:S(2)}, u32[]{:S(2)}) %collective-permute-start.2) | collective-permute-done | bytes 131104 | tf_op jit(solution)/shard_map/ppermute | solution.py:279
  9.4 0.4 %flow.1._ = bf16[32,128]{1,0:T(8,128)(2,1)S(1)} custom-call(s32[1]{0:T(128)} %bitcast.index_ref, bf16[128,4096]{1,0:T(8,128)(2,1)S(1)} %outgoing.1.flow_ref, bf16[32,2048]{1,0:T(8,128)(2,1)S(1)} %collective-permute-done.own_ref, bf16[32,2048]{1,0:T(8,128)(2,1)S(1)} %collective-permute-done.2.other_ref), custom_call_target="tpu_custom_call" | custom-call | tf_op jit(solution)/shard_map/flow/pallas_call | solution.py:243
  9.9 1.8 %collective-permute-start.4 = (bf16[32,128]{1,0:T(8,128)(2,1)S(1)}, bf16[32,128]{1,0:T(8,128)(2,1)S(1)}, u32[]{:S(2)}, u32[]{:S(2)}) collective-permute-start(bf16[32,128]{1,0:T(8,128)(2,1)S(1)} %flow.1._), channel_id=1, source_target_pairs={{0,16},{1,17},{2,18},{3,19},{4,20},{5,21},{6,22},{7,23},{8,24},{9,... | collective-permute-start | bytes 24584 | tf_op jit(solution)/shard_map/ppermute | solution.py:279
  11.7 0.4 %terms1.1 = (bf16[8,32,256]{2,1,0:T(8,128)(2,1)S(1)}, bf16[8,32,256]{2,1,0:T(8,128)(2,1)S(1)}, bf16[8,32,256]{2,1,0:T(8,128)(2,1)S(1)}, bf16[8,32,256]{2,1,0:T(8,128)(2,1)S(1)}) custom-call(s32[1]{0:T(128)} %bitcast.index_ref, bf16[128,4096]{1,0:T(8,128)(2,1)S(1)} %get-tuple-element.38.g, bf16[128,4096]{1,0:T(8,128)(2,1)S(1)} %get-tuple-element.46.xg_ref, ...), custom_call_target="tpu_custom_call" | custom-call | tf_op jit(solution)/shard_map/terms1/pallas_call | solution.py:243
  12.1 0.0 collective-permute-done.1.act0_ref
  12.1 0.3 terms.1
  12.4 0.1 collective-permute-start.3
  12.5 1.0 %collective-permute-done.4.got_ref = bf16[32,128]{1,0:T(8,128)(2,1)S(1)} collective-permute-done((bf16[32,128]{1,0:T(8,128)(2,1)S(1)}, bf16[32,128]{1,0:T(8,128)(2,1)S(1)}, u32[]{:S(2)}, u32[]{:S(2)}) %collective-permute-start.4) | collective-permute-done | bytes 8224 | tf_op jit(solution)/shard_map/ppermute | solution.py:279
  13.5 0.3 lower.1
  13.8 0.1 collective-permute-start.5
  13.9 0.3 collective-permute-done.3.got
  14.2 0.1 chip.1
  14.3 2.5 %collective-permute-start.6 = (bf16[4,32,256]{2,1,0:T(8,128)(2,1)S(1)}, bf16[4,32,256]{2,1,0:T(8,128)(2,1)S(1)}, u32[]{:S(2)}, u32[]{:S(2)}) collective-permute-start(bf16[4,32,256]{2,1,0:T(8,128)(2,1)S(1)} %get-tuple-element.62), channel_id=1, source_target_pairs={{0,18},{1,19},{2,16},{3,17},{4,22},{5,23},{6,20},{7,21},{8,26},{9,... | collective-permute-start | bytes 196616 | tf_op jit(solution)/shard_map/ppermute | solution.py:279
  16.9 0.0 collective-permute-done.5.got0
  16.9 0.1 plane.1
  16.9 1.2 %collective-permute-start.8 = (bf16[4,32,256]{2,1,0:T(8,128)(2,1)S(1)}, bf16[4,32,256]{2,1,0:T(8,128)(2,1)S(1)}, u32[]{:S(2)}, u32[]{:S(2)}) collective-permute-start(bf16[4,32,256]{2,1,0:T(8,128)(2,1)S(1)} %get-tuple-element.64), channel_id=1, source_target_pairs={{0,18},{1,19},{2,16},{3,17},{4,22},{5,23},{6,20},{7,21},{8,26},{9,... | collective-permute-start | bytes 196616 | tf_op jit(solution)/shard_map/ppermute | solution.py:279
  18.1 0.8 %collective-permute-start.7 = (bf16[4,64,256]{2,1,0:T(8,128)(2,1)S(1)}, bf16[4,64,256]{2,1,0:T(8,128)(2,1)S(1)}, u32[]{:S(2)}, u32[]{:S(2)}) collective-permute-start(bf16[4,64,256]{2,1,0:T(8,128)(2,1)S(1)} %get-tuple-element.63), channel_id=1, source_target_pairs={{0,2},{1,17},{2,0},{3,19},{4,6},{5,21},{6,4},{7,23},{8,10},{9,25},... | collective-permute-start | bytes 393224 | tf_op jit(solution)/shard_map/ppermute | solution.py:279
  19.0 1.5 %collective-permute-start.9 = (bf16[4,64,256]{2,1,0:T(8,128)(2,1)S(1)}, bf16[4,64,256]{2,1,0:T(8,128)(2,1)S(1)}, u32[]{:S(2)}, u32[]{:S(2)}) collective-permute-start(bf16[4,64,256]{2,1,0:T(8,128)(2,1)S(1)} %get-tuple-element.65), channel_id=1, source_target_pairs={{0,16},{1,3},{2,18},{3,1},{4,20},{5,7},{6,22},{7,5},{8,24},{9,11},... | collective-permute-start | bytes 393224 | tf_op jit(solution)/shard_map/ppermute | solution.py:279
  20.5 0.0 collective-permute-done.6.across_out
  20.5 2.3 %collective-permute-done.8.across_in = bf16[4,32,256]{2,1,0:T(8,128)(2,1)S(1)} collective-permute-done((bf16[4,32,256]{2,1,0:T(8,128)(2,1)S(1)}, bf16[4,32,256]{2,1,0:T(8,128)(2,1)S(1)}, u32[]{:S(2)}, u32[]{:S(2)}) %collective-permute-start.8) | collective-permute-done | bytes 65568 | tf_op jit(solution)/shard_map/ppermute | solution.py:279
  22.8 2.1 %collective-permute-done.7.first = bf16[4,64,256]{2,1,0:T(8,128)(2,1)S(1)} collective-permute-done((bf16[4,64,256]{2,1,0:T(8,128)(2,1)S(1)}, bf16[4,64,256]{2,1,0:T(8,128)(2,1)S(1)}, u32[]{:S(2)}, u32[]{:S(2)}) %collective-permute-start.7) | collective-permute-done | bytes 131104 | tf_op jit(solution)/shard_map/ppermute | solution.py:279
  24.9 0.0 collective-permute-done.9.second
  24.9 0.1 layer.1
  25.0 2.7 %collective-permute-start.10 = (bf16[64,256]{1,0:T(8,128)(2,1)S(1)}, bf16[64,256]{1,0:T(8,128)(2,1)S(1)}, u32[]{:S(2)}, u32[]{:S(2)}) collective-permute-start(bf16[64,256]{1,0:T(8,128)(2,1)S(1)} %get-tuple-element.67), channel_id=1, source_target_pairs={{0,8},{1,9},{2,10},{3,11},{4,12},{5,13},{6,14},{7,15},{8,0},{9,1},... | collective-permute-start | bytes 98312 | tf_op jit(solution)/shard_map/ppermute | solution.py:279
  27.6 1.3 %collective-permute-start.11 = (bf16[64,256]{1,0:T(8,128)(2,1)S(1)}, bf16[64,256]{1,0:T(8,128)(2,1)S(1)}, u32[]{:S(2)}, u32[]{:S(2)}) collective-permute-start(bf16[64,256]{1,0:T(8,128)(2,1)S(1)} %get-tuple-element.68), channel_id=1, source_target_pairs={{0,12},{1,13},{2,14},{3,15},{4,8},{5,9},{6,10},{7,11},{8,4},{9,5},... | collective-permute-start | bytes 98312 | tf_op jit(solution)/shard_map/ppermute | solution.py:279
  29.0 0.2 collective-permute-start.12
  29.2 1.0 %collective-permute-done.10.refs_1_ = bf16[64,256]{1,0:T(8,128)(2,1)S(1)} collective-permute-done((bf16[64,256]{1,0:T(8,128)(2,1)S(1)}, bf16[64,256]{1,0:T(8,128)(2,1)S(1)}, u32[]{:S(2)}, u32[]{:S(2)}) %collective-permute-start.10) | collective-permute-done | bytes 32800 | tf_op jit(solution)/shard_map/ppermute | solution.py:279
  30.2 3.2 %collective-permute-done.11.refs_2_ = bf16[64,256]{1,0:T(8,128)(2,1)S(1)} collective-permute-done((bf16[64,256]{1,0:T(8,128)(2,1)S(1)}, bf16[64,256]{1,0:T(8,128)(2,1)S(1)}, u32[]{:S(2)}, u32[]{:S(2)}) %collective-permute-start.11) | collective-permute-done | bytes 32800 | tf_op jit(solution)/shard_map/ppermute | solution.py:279
  33.3 0.0 collective-permute-done.12.refs_3_
  33.3 0.6 %total.1 = (f32[1,32,256]{2,1,0:T(8,128)}, f32[1,32,256]{2,1,0:T(8,128)}) custom-call(bf16[64,256]{1,0:T(8,128)(2,1)S(1)} %get-tuple-element.66.refs_0_, bf16[64,256]{1,0:T(8,128)(2,1)S(1)} %collective-permute-done.10.refs_1_, bf16[64,256]{1,0:T(8,128)(2,1)S(1)} %collective-permute-done.11.refs_2_, bf16[64,256]{1,0:T(8,128)(2,1)S(1)} %collective-permute-done.12.refs_3_), custom_call_target="tpu_custom_call" | custom-call | tf_op jit(solution)/shard_map/total/pallas_call | solution.py:243
  (1 shorter events, 0.0 us)
Async XLA Ops:
  1.6 6.5 %collective-permute-start = (bf16[32,2048]{1,0:T(8,128)(2,1)S(1)}, bf16[32,2048]{1,0:T(8,128)(2,1)S(1)}, u32[]{:S(2)}, u32[]{:S(2)}) collective-permute-start(bf16[32,2048]{1,0:T(8,128)(2,1)S(1)} %pick.1), channel_id=1, source_target_pairs={{0,16},{1,17},{2,18},{3,19},{4,20},{5,21},{6,22},{7,23},{8,24},{9,... | collective-permute-start | bytes 393224 | tf_op jit(solution)/shard_map/ppermute | solution.py:279
  6.8 5.3 %collective-permute-start.1 = (bf16[32,128]{1,0:T(8,128)(2,1)S(1)}, bf16[32,128]{1,0:T(8,128)(2,1)S(1)}, u32[]{:S(2)}, u32[]{:S(2)}) collective-permute-start(bf16[32,128]{1,0:T(8,128)(2,1)S(1)} %get-tuple-element.45), channel_id=1, source_target_pairs={{0,16},{1,17},{2,18},{3,19},{4,20},{5,21},{6,22},{7,23},{8,24},{9,... | collective-permute-start | bytes 24584 | tf_op jit(solution)/shard_map/ppermute | solution.py:279
  8.1 1.3 %collective-permute-start.2 = (bf16[32,2048]{1,0:T(8,128)(2,1)S(1)}, bf16[32,2048]{1,0:T(8,128)(2,1)S(1)}, u32[]{:S(2)}, u32[]{:S(2)}) collective-permute-start(bf16[32,2048]{1,0:T(8,128)(2,1)S(1)} %collective-permute-done.own_ref), channel_id=1, source_target_pairs={{0,1},{1,0},{2,3},{3,2},{4,5},{5,4},{6,7},{7,6},{8,9},{9,8},{10,11... | collective-permute-start | bytes 393224 | tf_op jit(solution)/shard_map/ppermute | solution.py:279
  9.9 3.7 %collective-permute-start.4 = (bf16[32,128]{1,0:T(8,128)(2,1)S(1)}, bf16[32,128]{1,0:T(8,128)(2,1)S(1)}, u32[]{:S(2)}, u32[]{:S(2)}) collective-permute-start(bf16[32,128]{1,0:T(8,128)(2,1)S(1)} %flow.1._), channel_id=1, source_target_pairs={{0,16},{1,17},{2,18},{3,19},{4,20},{5,21},{6,22},{7,23},{8,24},{9,... | collective-permute-start | bytes 24584 | tf_op jit(solution)/shard_map/ppermute | solution.py:279
  12.4 1.8 %collective-permute-start.3 = (bf16[24,32,256]{2,1,0:T(8,128)(2,1)S(1)}, bf16[24,32,256]{2,1,0:T(8,128)(2,1)S(1)}, u32[]{:S(2)}, u32[]{:S(2)}) collective-permute-start(bf16[24,32,256]{2,1,0:T(8,128)(2,1)S(1)} %get-tuple-element.55), channel_id=1, source_target_pairs={{0,1},{1,0},{2,3},{3,2},{4,5},{5,4},{6,7},{7,6},{8,9},{9,8},{10,11... | collective-permute-start | bytes 1179656 | tf_op jit(solution)/shard_map/ppermute | solution.py:279
  13.8 3.1 %collective-permute-start.5 = (bf16[8,32,256]{2,1,0:T(8,128)(2,1)S(1)}, bf16[8,32,256]{2,1,0:T(8,128)(2,1)S(1)}, u32[]{:S(2)}, u32[]{:S(2)}) collective-permute-start(bf16[8,32,256]{2,1,0:T(8,128)(2,1)S(1)} %get-tuple-element.60), channel_id=1, source_target_pairs={{0,1},{1,0},{2,3},{3,2},{4,5},{5,4},{6,7},{7,6},{8,9},{9,8},{10,11... | collective-permute-start | bytes 393224 | tf_op jit(solution)/shard_map/ppermute | solution.py:279
  14.3 6.2 %collective-permute-start.6 = (bf16[4,32,256]{2,1,0:T(8,128)(2,1)S(1)}, bf16[4,32,256]{2,1,0:T(8,128)(2,1)S(1)}, u32[]{:S(2)}, u32[]{:S(2)}) collective-permute-start(bf16[4,32,256]{2,1,0:T(8,128)(2,1)S(1)} %get-tuple-element.62), channel_id=1, source_target_pairs={{0,18},{1,19},{2,16},{3,17},{4,22},{5,23},{6,20},{7,21},{8,26},{9,... | collective-permute-start | bytes 196616 | tf_op jit(solution)/shard_map/ppermute | solution.py:279
  16.9 5.9 %collective-permute-start.8 = (bf16[4,32,256]{2,1,0:T(8,128)(2,1)S(1)}, bf16[4,32,256]{2,1,0:T(8,128)(2,1)S(1)}, u32[]{:S(2)}, u32[]{:S(2)}) collective-permute-start(bf16[4,32,256]{2,1,0:T(8,128)(2,1)S(1)} %get-tuple-element.64), channel_id=1, source_target_pairs={{0,18},{1,19},{2,16},{3,17},{4,22},{5,23},{6,20},{7,21},{8,26},{9,... | collective-permute-start | bytes 196616 | tf_op jit(solution)/shard_map/ppermute | solution.py:279
  18.1 6.8 %collective-permute-start.7 = (bf16[4,64,256]{2,1,0:T(8,128)(2,1)S(1)}, bf16[4,64,256]{2,1,0:T(8,128)(2,1)S(1)}, u32[]{:S(2)}, u32[]{:S(2)}) collective-permute-start(bf16[4,64,256]{2,1,0:T(8,128)(2,1)S(1)} %get-tuple-element.63), channel_id=1, source_target_pairs={{0,2},{1,17},{2,0},{3,19},{4,6},{5,21},{6,4},{7,23},{8,10},{9,25},... | collective-permute-start | bytes 393224 | tf_op jit(solution)/shard_map/ppermute | solution.py:279
  19.0 5.9 %collective-permute-start.9 = (bf16[4,64,256]{2,1,0:T(8,128)(2,1)S(1)}, bf16[4,64,256]{2,1,0:T(8,128)(2,1)S(1)}, u32[]{:S(2)}, u32[]{:S(2)}) collective-permute-start(bf16[4,64,256]{2,1,0:T(8,128)(2,1)S(1)} %get-tuple-element.65), channel_id=1, source_target_pairs={{0,16},{1,3},{2,18},{3,1},{4,20},{5,7},{6,22},{7,5},{8,24},{9,11},... | collective-permute-start | bytes 393224 | tf_op jit(solution)/shard_map/ppermute | solution.py:279
  25.0 5.2 %collective-permute-start.10 = (bf16[64,256]{1,0:T(8,128)(2,1)S(1)}, bf16[64,256]{1,0:T(8,128)(2,1)S(1)}, u32[]{:S(2)}, u32[]{:S(2)}) collective-permute-start(bf16[64,256]{1,0:T(8,128)(2,1)S(1)} %get-tuple-element.67), channel_id=1, source_target_pairs={{0,8},{1,9},{2,10},{3,11},{4,12},{5,13},{6,14},{7,15},{8,0},{9,1},... | collective-permute-start | bytes 98312 | tf_op jit(solution)/shard_map/ppermute | solution.py:279
  27.6 5.7 %collective-permute-start.11 = (bf16[64,256]{1,0:T(8,128)(2,1)S(1)}, bf16[64,256]{1,0:T(8,128)(2,1)S(1)}, u32[]{:S(2)}, u32[]{:S(2)}) collective-permute-start(bf16[64,256]{1,0:T(8,128)(2,1)S(1)} %get-tuple-element.68), channel_id=1, source_target_pairs={{0,12},{1,13},{2,14},{3,15},{4,8},{5,9},{6,10},{7,11},{8,4},{9,5},... | collective-permute-start | bytes 98312 | tf_op jit(solution)/shard_map/ppermute | solution.py:279
  29.0 4.4 %collective-permute-start.12 = (bf16[64,256]{1,0:T(8,128)(2,1)S(1)}, bf16[64,256]{1,0:T(8,128)(2,1)S(1)}, u32[]{:S(2)}, u32[]{:S(2)}) collective-permute-start(bf16[64,256]{1,0:T(8,128)(2,1)S(1)} %get-tuple-element.69), channel_id=1, source_target_pairs={{0,4},{1,5},{2,6},{3,7},{4,0},{5,1},{6,2},{7,3},{8,12},{9,13},{10,... | collective-permute-start | bytes 98312 | tf_op jit(solution)/shard_map/ppermute | solution.py:279

commit v9 on v8

--- a/solution.py
+++ b/solution.py
@@ -152,15 +152,22 @@
     copy.wait()
 
 
-def flow_kernel(share, index_ref, flow_ref, own_ref, other_ref, send_ref):
-    half = own_ref.shape[1]
-    core = index_ref[0] % 2
-    delta = jnp.zeros(send_ref.shape, F32)
-    for w_ref, number in ((own_ref, core), (other_ref, 1 - core)):
-        for c in range(0, half, share):
-            cols = pl.ds(pl.multiple_of(number * half + c, share), share)
-            delta += nt(w_ref[:, c : c + share], flow_ref[:, cols])
-    send_ref[...] = delta.astype(BF16)
+def product(step, number, w_ref, flow_ref):
+    half = w_ref.shape[1]
+    delta = jnp.zeros((w_ref.shape[0], flow_ref.shape[0]), F32)
+    for c in range(0, half, step):
+        cols = pl.ds(pl.multiple_of(number * half + c, step), step)
+        delta += nt(w_ref[:, c : c + step], flow_ref[:, cols])
+    return delta
+
+
+def flow_kernel(step, index_ref, flow_ref, own_ref, part_ref):
+    part_ref[...] = product(step, index_ref[0] % 2, own_ref, flow_ref)
+
+
+def flow_rest_kernel(step, index_ref, flow_ref, other_ref, part_ref, send_ref):
+    rest = product(step, 1 - index_ref[0] % 2, other_ref, flow_ref)
+    send_ref[...] = (part_ref[...] + rest).astype(BF16)
 
 
 def lower_kernel(index_ref, xg0_ref, low_ref, got_ref, keep_ref, send_ref):
@@ -229,21 +236,23 @@
 
 
 def total_kernel(*refs):
-    *got, in_ref, out_ref = refs
+    *got, in_far, out_far, in_ref, out_ref, sems = refs
     rank = in_ref.shape[1]
-    total = got[0][...].astype(F32)
-    for ref in got[1:]:
-        total += ref[...].astype(F32)
-    in_ref[0] = total[0:rank]
-    out_ref[0] = total[rank : 2 * rank]
-
-
-def local(kernel, name, out_shapes, *operands, scratch=(), cost=None):
+    copies = []
+    for i, (ref, far) in enumerate(((in_ref, in_far), (out_ref, out_far))):
+        ref[0] = sum(part[i * rank : (i + 1) * rank].astype(F32) for part in got)
+        copies.append(pltpu.make_async_copy(ref, far, sems.at[i]))
+        copies[i].start()
+    for copy in copies:
+        copy.wait()
+
+
+def local(kernel, name, out_shapes, *operands, scratch=(), cost=None, out="near"):
     spaces = {"scalar": pltpu.SMEM, "far": pltpu.HBM, "near": pltpu.VMEM}
     out = pl.pallas_call(
         kernel,
         in_specs=[pl.BlockSpec(memory_space=spaces[kind]) for kind, _ in operands],
-        out_specs=[pl.BlockSpec(memory_space=pltpu.VMEM)] * len(out_shapes),
+        out_specs=[pl.BlockSpec(memory_space=spaces[out])] * len(out_shapes),
         out_shape=[jax.ShapeDtypeStruct(shape, dtype) for shape, dtype in out_shapes],
         scratch_shapes=list(scratch),
         compiler_params=pltpu.CompilerParams(vmem_limit_bytes=VMEM_BYTES),
@@ -311,8 +320,12 @@
         partial(outgoing_kernel, share), "outgoing", [wide], *near(x1, g, gain1, wi1, da1, columns),
         cost=LONG,
     )
+    part = local(
+        partial(flow_kernel, share), "flow", [((rank, tokens), F32)], index, *near(flow, own_half)
+    )
     delta = local(
-        partial(flow_kernel, share), "flow", [small], index, *near(flow, own_half, other_half),
+        partial(flow_rest_kernel, share), "flow_rest", [small],
+        index, *near(flow, other_half, part),
     )
     got_delta = swapped(delta, along_x)
     terms1 = local(
@@ -345,7 +358,10 @@
     others = [swapped(other, (0, 4 * k)) for k, other in enumerate(others, 1)]
     others = others[1:] + others[:1]
     block = ((1, rank, share), F32)
-    total_in, total_out = local(total_kernel, "total", [block, block], *near(mine, *others))
+    total_in, total_out = local(
+        total_kernel, "total", [block, block], *near(mine, *others),
+        scratch=[pltpu.VMEM(*block), pltpu.VMEM(*block), sems((2,))], out="far",
+    )
     return (jnp.swapaxes(total_in, 1, 2), total_out)
 
 

time: 34.1 us -> 34 us (level)
    pallas_call x13 -> x14, Pallas kernels: 7.07 us -> 7.19 us  [local(): pl.pallas_call(kernel, in_specs=[pl.BlockSpec(memory_space=spaces[kind])...]
where the time goes in v9:
time: 34 us; the launch traced here: 33.9 us
  starting transfers between devices  15.5 us (46%)
  waiting for transfers between devices  10.5 us (31%)
  Pallas kernels  7.19 us (21%)
  between operations  0.76 us (2%)
    ppermute x13, starting transfers between devices, swapped(): return lax.ppermute(array, ('section', 'dp'), pairs)  15.5 us
    ppermute x13, waiting for transfers between devices, swapped(): return lax.ppermute(array, ('section', 'dp'), pairs)  10.5 us
    pallas_call x14, Pallas kernels, local(): pl.pallas_call(kernel, in_specs=[pl.BlockSpec(memory_space=spaces[kind])...  7.19 us
  transfers between devices with their start and end apart: 13, of which 8 were waited for; matrix products, arithmetic and copies ran while one was open for 0% of the time, Pallas kernels for 16%

profile of v9, /device:TPU:0, one launch (start us, length us, event | category | flops | bytes accessed | tf_op | source)
XLA Modules:
  0.0 33.9 jit_solution(16504304049013793658)
XLA Ops:
  0.6 0.9 %pick.1 = bf16[32,2048]{1,0:T(8,128)(2,1)S(1)} custom-call(s32[1]{0:T(128)} %bitcast.1.place_ref, s32[1]{0:T(128)} %bitcast.index_ref, bf16[1,2,32,4096]{3,2,1,0:T(8,128)(2,1)} %w_out.3), custom_call_target="tpu_custom_call" | custom-call | tf_op jit(solution)/shard_map/pick/pallas_call | solution.py:252
  1.6 3.0 %collective-permute-start = (bf16[32,2048]{1,0:T(8,128)(2,1)S(1)}, bf16[32,2048]{1,0:T(8,128)(2,1)S(1)}, u32[]{:S(2)}, u32[]{:S(2)}) collective-permute-start(bf16[32,2048]{1,0:T(8,128)(2,1)S(1)} %pick.1), channel_id=1, source_target_pairs={{0,16},{1,17},{2,18},{3,19},{4,20},{5,21},{6,22},{7,23},{8,24},{9,... | collective-permute-start | bytes 393224 | tf_op jit(solution)/shard_map/ppermute | solution.py:288
  4.6 2.2 %front.1 = (bf16[32,128]{1,0:T(8,128)(2,1)S(1)}, f32[2,32,128]{2,1,0:T(8,128)S(1)}, bf16[128,4096]{1,0:T(8,128)(2,1)S(1)}, bf16[128,4096]{1,0:T(8,128)(2,1)S(1)}...) custom-call(s32[1]{0:T(128)} %bitcast.1.place_ref, ...), custom_call_target="tpu_custom_call" | custom-call | tf_op jit(solution)/shard_map/front/pallas_call | solution.py:252
  6.8 0.1 collective-permute-start.1
  6.9 0.9 %upper.1 = (bf16[128,4096]{1,0:T(8,128)(2,1)S(1)}, bf16[32,128]{1,0:T(8,128)(2,1)S(1)}, bf16[32,128]{1,0:T(8,128)(2,1)S(1)}, bf16[32,128]{1,0:T(8,128)(2,1)S(1)}, f32[2,128,128]{2,1,0:T(8,128)S(1)}) custom-call(bf16[128,4096]{1,0:T(8,128)(2,1)S(1)} %get-tuple-element.37.x, bf16[128,4096]{1,0:T(8,128)(2,1)S(1)} %get-tuple-element.38.g, ...), custom_call_target="tpu_custom_call" | custom-call | tf_op jit(solution)/shard_map/upper/pallas_call | solution.py:252
  7.8 0.3 collective-permute-done.own_ref
  8.1 0.0 collective-permute-start.2
  8.1 0.7 %outgoing.1.flow_ref = bf16[128,4096]{1,0:T(8,128)(2,1)S(1)} custom-call(bf16[128,4096]{1,0:T(8,128)(2,1)S(1)} %get-tuple-element.37.x, bf16[128,4096]{1,0:T(8,128)(2,1)S(1)} %get-tuple-element.38.g, f32[1,4096]{1,0:T(1,128)S(1)} %get-tuple-element.39.gain, bf16[32,4096]{1,0:T(8,128)(2,1)S(1)} %get-tuple-element.40.wi, ...), custom_call_target="tpu_custom_call" | custom-call | flops 20000000000 | bytes 1048576 | tf_op jit(solution)/shard_map/outgoing/pallas_call | solution.py:252
  8.8 0.3 flow.1.part_ref
  9.1 0.3 collective-permute-done.2.other_ref
  9.4 0.3 flow_rest.1._
  9.7 1.9 %collective-permute-start.4 = (bf16[32,128]{1,0:T(8,128)(2,1)S(1)}, bf16[32,128]{1,0:T(8,128)(2,1)S(1)}, u32[]{:S(2)}, u32[]{:S(2)}) collective-permute-start(bf16[32,128]{1,0:T(8,128)(2,1)S(1)} %flow_rest.1._), channel_id=1, source_target_pairs={{0,16},{1,17},{2,18},{3,19},{4,20},{5,21},{6,22},{7,23},{8,24},{9,... | collective-permute-start | bytes 24584 | tf_op jit(solution)/shard_map/ppermute | solution.py:288
  11.6 0.4 %terms1.1 = (bf16[8,32,256]{2,1,0:T(8,128)(2,1)S(1)}, bf16[8,32,256]{2,1,0:T(8,128)(2,1)S(1)}, bf16[8,32,256]{2,1,0:T(8,128)(2,1)S(1)}, bf16[8,32,256]{2,1,0:T(8,128)(2,1)S(1)}) custom-call(s32[1]{0:T(128)} %bitcast.index_ref, bf16[128,4096]{1,0:T(8,128)(2,1)S(1)} %get-tuple-element.38.g, bf16[128,4096]{1,0:T(8,128)(2,1)S(1)} %get-tuple-element.46.xg_ref, ...), custom_call_target="tpu_custom_call" | custom-call | tf_op jit(solution)/shard_map/terms1/pallas_call | solution.py:252
  12.0 0.0 collective-permute-done.1.act0_ref
  12.0 0.3 terms.1
  12.3 0.1 collective-permute-start.3
  12.4 1.0 %collective-permute-done.4.got_ref = bf16[32,128]{1,0:T(8,128)(2,1)S(1)} collective-permute-done((bf16[32,128]{1,0:T(8,128)(2,1)S(1)}, bf16[32,128]{1,0:T(8,128)(2,1)S(1)}, u32[]{:S(2)}, u32[]{:S(2)}) %collective-permute-start.4) | collective-permute-done | bytes 8224 | tf_op jit(solution)/shard_map/ppermute | solution.py:288
  13.4 0.3 lower.1
  13.7 0.1 collective-permute-start.5
  13.8 0.3 collective-permute-done.3.got
  14.1 0.1 chip.1
  14.2 2.5 %collective-permute-start.6 = (bf16[4,32,256]{2,1,0:T(8,128)(2,1)S(1)}, bf16[4,32,256]{2,1,0:T(8,128)(2,1)S(1)}, u32[]{:S(2)}, u32[]{:S(2)}) collective-permute-start(bf16[4,32,256]{2,1,0:T(8,128)(2,1)S(1)} %get-tuple-element.62), channel_id=1, source_target_pairs={{0,18},{1,19},{2,16},{3,17},{4,22},{5,23},{6,20},{7,21},{8,26},{9,... | collective-permute-start | bytes 196616 | tf_op jit(solution)/shard_map/ppermute | solution.py:288
  16.7 0.0 collective-permute-done.5.got0
  16.7 0.1 plane.1
  16.8 1.2 %collective-permute-start.8 = (bf16[4,32,256]{2,1,0:T(8,128)(2,1)S(1)}, bf16[4,32,256]{2,1,0:T(8,128)(2,1)S(1)}, u32[]{:S(2)}, u32[]{:S(2)}) collective-permute-start(bf16[4,32,256]{2,1,0:T(8,128)(2,1)S(1)} %get-tuple-element.64), channel_id=1, source_target_pairs={{0,18},{1,19},{2,16},{3,17},{4,22},{5,23},{6,20},{7,21},{8,26},{9,... | collective-permute-start | bytes 196616 | tf_op jit(solution)/shard_map/ppermute | solution.py:288
  18.0 0.8 %collective-permute-start.7 = (bf16[4,64,256]{2,1,0:T(8,128)(2,1)S(1)}, bf16[4,64,256]{2,1,0:T(8,128)(2,1)S(1)}, u32[]{:S(2)}, u32[]{:S(2)}) collective-permute-start(bf16[4,64,256]{2,1,0:T(8,128)(2,1)S(1)} %get-tuple-element.63), channel_id=1, source_target_pairs={{0,2},{1,17},{2,0},{3,19},{4,6},{5,21},{6,4},{7,23},{8,10},{9,25},... | collective-permute-start | bytes 393224 | tf_op jit(solution)/shard_map/ppermute | solution.py:288
  18.8 1.5 %collective-permute-start.9 = (bf16[4,64,256]{2,1,0:T(8,128)(2,1)S(1)}, bf16[4,64,256]{2,1,0:T(8,128)(2,1)S(1)}, u32[]{:S(2)}, u32[]{:S(2)}) collective-permute-start(bf16[4,64,256]{2,1,0:T(8,128)(2,1)S(1)} %get-tuple-element.65), channel_id=1, source_target_pairs={{0,16},{1,3},{2,18},{3,1},{4,20},{5,7},{6,22},{7,5},{8,24},{9,11},... | collective-permute-start | bytes 393224 | tf_op jit(solution)/shard_map/ppermute | solution.py:288
  20.4 0.0 collective-permute-done.6.across_out
  20.4 2.3 %collective-permute-done.8.across_in = bf16[4,32,256]{2,1,0:T(8,128)(2,1)S(1)} collective-permute-done((bf16[4,32,256]{2,1,0:T(8,128)(2,1)S(1)}, bf16[4,32,256]{2,1,0:T(8,128)(2,1)S(1)}, u32[]{:S(2)}, u32[]{:S(2)}) %collective-permute-start.8) | collective-permute-done | bytes 65568 | tf_op jit(solution)/shard_map/ppermute | solution.py:288
  22.7 2.1 %collective-permute-done.7.first = bf16[4,64,256]{2,1,0:T(8,128)(2,1)S(1)} collective-permute-done((bf16[4,64,256]{2,1,0:T(8,128)(2,1)S(1)}, bf16[4,64,256]{2,1,0:T(8,128)(2,1)S(1)}, u32[]{:S(2)}, u32[]{:S(2)}) %collective-permute-start.7) | collective-permute-done | bytes 131104 | tf_op jit(solution)/shard_map/ppermute | solution.py:288
  24.8 0.0 collective-permute-done.9.second
  24.8 0.1 layer.1
  24.8 2.7 %collective-permute-start.10 = (bf16[64,256]{1,0:T(8,128)(2,1)S(1)}, bf16[64,256]{1,0:T(8,128)(2,1)S(1)}, u32[]{:S(2)}, u32[]{:S(2)}) collective-permute-start(bf16[64,256]{1,0:T(8,128)(2,1)S(1)} %get-tuple-element.67), channel_id=1, source_target_pairs={{0,8},{1,9},{2,10},{3,11},{4,12},{5,13},{6,14},{7,15},{8,0},{9,1},... | collective-permute-start | bytes 98312 | tf_op jit(solution)/shard_map/ppermute | solution.py:288
  27.5 1.3 %collective-permute-start.11 = (bf16[64,256]{1,0:T(8,128)(2,1)S(1)}, bf16[64,256]{1,0:T(8,128)(2,1)S(1)}, u32[]{:S(2)}, u32[]{:S(2)}) collective-permute-start(bf16[64,256]{1,0:T(8,128)(2,1)S(1)} %get-tuple-element.68), channel_id=1, source_target_pairs={{0,12},{1,13},{2,14},{3,15},{4,8},{5,9},{6,10},{7,11},{8,4},{9,5},... | collective-permute-start | bytes 98312 | tf_op jit(solution)/shard_map/ppermute | solution.py:288
  28.9 0.2 collective-permute-start.12
  29.1 1.0 %collective-permute-done.10.refs_1_ = bf16[64,256]{1,0:T(8,128)(2,1)S(1)} collective-permute-done((bf16[64,256]{1,0:T(8,128)(2,1)S(1)}, bf16[64,256]{1,0:T(8,128)(2,1)S(1)}, u32[]{:S(2)}, u32[]{:S(2)}) %collective-permute-start.10) | collective-permute-done | bytes 32800 | tf_op jit(solution)/shard_map/ppermute | solution.py:288
  30.1 3.2 %collective-permute-done.11.refs_2_ = bf16[64,256]{1,0:T(8,128)(2,1)S(1)} collective-permute-done((bf16[64,256]{1,0:T(8,128)(2,1)S(1)}, bf16[64,256]{1,0:T(8,128)(2,1)S(1)}, u32[]{:S(2)}, u32[]{:S(2)}) %collective-permute-start.11) | collective-permute-done | bytes 32800 | tf_op jit(solution)/shard_map/ppermute | solution.py:288
  33.2 0.0 collective-permute-done.12.refs_3_
  33.2 0.7 %total.1 = (f32[1,32,256]{2,1,0:T(8,128)}, f32[1,32,256]{2,1,0:T(8,128)}) custom-call(bf16[64,256]{1,0:T(8,128)(2,1)S(1)} %get-tuple-element.66.refs_0_, bf16[64,256]{1,0:T(8,128)(2,1)S(1)} %collective-permute-done.10.refs_1_, bf16[64,256]{1,0:T(8,128)(2,1)S(1)} %collective-permute-done.11.refs_2_, bf16[64,256]{1,0:T(8,128)(2,1)S(1)} %collective-permute-done.12.refs_3_), custom_call_target="tpu_custom_call" | custom-call | tf_op jit(solution)/shard_map/total/pallas_call | solution.py:252
  (1 shorter events, 0.0 us)
Async XLA Ops:
  1.6 6.5 %collective-permute-start = (bf16[32,2048]{1,0:T(8,128)(2,1)S(1)}, bf16[32,2048]{1,0:T(8,128)(2,1)S(1)}, u32[]{:S(2)}, u32[]{:S(2)}) collective-permute-start(bf16[32,2048]{1,0:T(8,128)(2,1)S(1)} %pick.1), channel_id=1, source_target_pairs={{0,16},{1,17},{2,18},{3,19},{4,20},{5,21},{6,22},{7,23},{8,24},{9,... | collective-permute-start | bytes 393224 | tf_op jit(solution)/shard_map/ppermute | solution.py:288
  6.8 5.2 %collective-permute-start.1 = (bf16[32,128]{1,0:T(8,128)(2,1)S(1)}, bf16[32,128]{1,0:T(8,128)(2,1)S(1)}, u32[]{:S(2)}, u32[]{:S(2)}) collective-permute-start(bf16[32,128]{1,0:T(8,128)(2,1)S(1)} %get-tuple-element.45), channel_id=1, source_target_pairs={{0,16},{1,17},{2,18},{3,19},{4,20},{5,21},{6,22},{7,23},{8,24},{9,... | collective-permute-start | bytes 24584 | tf_op jit(solution)/shard_map/ppermute | solution.py:288
  8.1 1.3 %collective-permute-start.2 = (bf16[32,2048]{1,0:T(8,128)(2,1)S(1)}, bf16[32,2048]{1,0:T(8,128)(2,1)S(1)}, u32[]{:S(2)}, u32[]{:S(2)}) collective-permute-start(bf16[32,2048]{1,0:T(8,128)(2,1)S(1)} %collective-permute-done.own_ref), channel_id=1, source_target_pairs={{0,1},{1,0},{2,3},{3,2},{4,5},{5,4},{6,7},{7,6},{8,9},{9,8},{10,11... | collective-permute-start | bytes 393224 | tf_op jit(solution)/shard_map/ppermute | solution.py:288
  9.7 3.7 %collective-permute-start.4 = (bf16[32,128]{1,0:T(8,128)(2,1)S(1)}, bf16[32,128]{1,0:T(8,128)(2,1)S(1)}, u32[]{:S(2)}, u32[]{:S(2)}) collective-permute-start(bf16[32,128]{1,0:T(8,128)(2,1)S(1)} %flow_rest.1._), channel_id=1, source_target_pairs={{0,16},{1,17},{2,18},{3,19},{4,20},{5,21},{6,22},{7,23},{8,24},{9,... | collective-permute-start | bytes 24584 | tf_op jit(solution)/shard_map/ppermute | solution.py:288
  12.3 1.8 %collective-permute-start.3 = (bf16[24,32,256]{2,1,0:T(8,128)(2,1)S(1)}, bf16[24,32,256]{2,1,0:T(8,128)(2,1)S(1)}, u32[]{:S(2)}, u32[]{:S(2)}) collective-permute-start(bf16[24,32,256]{2,1,0:T(8,128)(2,1)S(1)} %get-tuple-element.55), channel_id=1, source_target_pairs={{0,1},{1,0},{2,3},{3,2},{4,5},{5,4},{6,7},{7,6},{8,9},{9,8},{10,11... | collective-permute-start | bytes 1179656 | tf_op jit(solution)/shard_map/ppermute | solution.py:288
  13.7 3.1 %collective-permute-start.5 = (bf16[8,32,256]{2,1,0:T(8,128)(2,1)S(1)}, bf16[8,32,256]{2,1,0:T(8,128)(2,1)S(1)}, u32[]{:S(2)}, u32[]{:S(2)}) collective-permute-start(bf16[8,32,256]{2,1,0:T(8,128)(2,1)S(1)} %get-tuple-element.60), channel_id=1, source_target_pairs={{0,1},{1,0},{2,3},{3,2},{4,5},{5,4},{6,7},{7,6},{8,9},{9,8},{10,11... | collective-permute-start | bytes 393224 | tf_op jit(solution)/shard_map/ppermute | solution.py:288
  14.2 6.2 %collective-permute-start.6 = (bf16[4,32,256]{2,1,0:T(8,128)(2,1)S(1)}, bf16[4,32,256]{2,1,0:T(8,128)(2,1)S(1)}, u32[]{:S(2)}, u32[]{:S(2)}) collective-permute-start(bf16[4,32,256]{2,1,0:T(8,128)(2,1)S(1)} %get-tuple-element.62), channel_id=1, source_target_pairs={{0,18},{1,19},{2,16},{3,17},{4,22},{5,23},{6,20},{7,21},{8,26},{9,... | collective-permute-start | bytes 196616 | tf_op jit(solution)/shard_map/ppermute | solution.py:288
  16.8 5.9 %collective-permute-start.8 = (bf16[4,32,256]{2,1,0:T(8,128)(2,1)S(1)}, bf16[4,32,256]{2,1,0:T(8,128)(2,1)S(1)}, u32[]{:S(2)}, u32[]{:S(2)}) collective-permute-start(bf16[4,32,256]{2,1,0:T(8,128)(2,1)S(1)} %get-tuple-element.64), channel_id=1, source_target_pairs={{0,18},{1,19},{2,16},{3,17},{4,22},{5,23},{6,20},{7,21},{8,26},{9,... | collective-permute-start | bytes 196616 | tf_op jit(solution)/shard_map/ppermute | solution.py:288
  18.0 6.8 %collective-permute-start.7 = (bf16[4,64,256]{2,1,0:T(8,128)(2,1)S(1)}, bf16[4,64,256]{2,1,0:T(8,128)(2,1)S(1)}, u32[]{:S(2)}, u32[]{:S(2)}) collective-permute-start(bf16[4,64,256]{2,1,0:T(8,128)(2,1)S(1)} %get-tuple-element.63), channel_id=1, source_target_pairs={{0,2},{1,17},{2,0},{3,19},{4,6},{5,21},{6,4},{7,23},{8,10},{9,25},... | collective-permute-start | bytes 393224 | tf_op jit(solution)/shard_map/ppermute | solution.py:288
  18.8 5.9 %collective-permute-start.9 = (bf16[4,64,256]{2,1,0:T(8,128)(2,1)S(1)}, bf16[4,64,256]{2,1,0:T(8,128)(2,1)S(1)}, u32[]{:S(2)}, u32[]{:S(2)}) collective-permute-start(bf16[4,64,256]{2,1,0:T(8,128)(2,1)S(1)} %get-tuple-element.65), channel_id=1, source_target_pairs={{0,16},{1,3},{2,18},{3,1},{4,20},{5,7},{6,22},{7,5},{8,24},{9,11},... | collective-permute-start | bytes 393224 | tf_op jit(solution)/shard_map/ppermute | solution.py:288
  24.8 5.2 %collective-permute-start.10 = (bf16[64,256]{1,0:T(8,128)(2,1)S(1)}, bf16[64,256]{1,0:T(8,128)(2,1)S(1)}, u32[]{:S(2)}, u32[]{:S(2)}) collective-permute-start(bf16[64,256]{1,0:T(8,128)(2,1)S(1)} %get-tuple-element.67), channel_id=1, source_target_pairs={{0,8},{1,9},{2,10},{3,11},{4,12},{5,13},{6,14},{7,15},{8,0},{9,1},... | collective-permute-start | bytes 98312 | tf_op jit(solution)/shard_map/ppermute | solution.py:288
  27.5 5.7 %collective-permute-start.11 = (bf16[64,256]{1,0:T(8,128)(2,1)S(1)}, bf16[64,256]{1,0:T(8,128)(2,1)S(1)}, u32[]{:S(2)}, u32[]{:S(2)}) collective-permute-start(bf16[64,256]{1,0:T(8,128)(2,1)S(1)} %get-tuple-element.68), channel_id=1, source_target_pairs={{0,12},{1,13},{2,14},{3,15},{4,8},{5,9},{6,10},{7,11},{8,4},{9,5},... | collective-permute-start | bytes 98312 | tf_op jit(solution)/shard_map/ppermute | solution.py:288
  28.9 4.4 %collective-permute-start.12 = (bf16[64,256]{1,0:T(8,128)(2,1)S(1)}, bf16[64,256]{1,0:T(8,128)(2,1)S(1)}, u32[]{:S(2)}, u32[]{:S(2)}) collective-permute-start(bf16[64,256]{1,0:T(8,128)(2,1)S(1)} %get-tuple-element.69), channel_id=1, source_target_pairs={{0,4},{1,5},{2,6},{3,7},{4,0},{5,1},{6,2},{7,3},{8,12},{9,13},{10,... | collective-permute-start | bytes 98312 | tf_op jit(solution)/shard_map/ppermute | solution.py:288

commit v10 on v9

--- a/solution.py
+++ b/solution.py
@@ -13,6 +13,7 @@
 BF16 = jnp.bfloat16
 
 
+MEDIUM = pl.CostEstimate(flops=10**9, bytes_accessed=2**20, transcendentals=0)
 LONG = pl.CostEstimate(flops=2 * 10**10, bytes_accessed=2**20, transcendentals=0)
 
 
@@ -350,7 +351,7 @@
     first = swapped(first, (0, 2), (1, 0))
     across_in = swapped(across_in, (1, 2))
     second = swapped(second, (1, 0), (0, 2))
-    own = local(add_kernel, "add", [double], *near(own, across_out), cost=LONG)
+    own = local(add_kernel, "add", [double], *near(own, across_out), cost=MEDIUM)
     mine, *others = local(
         layer_kernel, "layer", [((2 * rank, share), BF16)] * layers,
         index, *near(own, first, across_in, second),

time: 34 us -> 33.7 us (level)
  waiting for transfers between devices: 10.5 us -> 10.1 us
  transfers between devices with their start and end apart: 13 -> 13, of which waited for: 8 -> 7; matrix products, arithmetic and copies ran while one was open for 0% -> 0% of each run, Pallas kernels for 16% -> 17%
where the time goes in v10:
time: 33.7 us; the launch traced here: 33.5 us
  starting transfers between devices  15.5 us (46%)
  waiting for transfers between devices  10.1 us (30%)
  Pallas kernels  7.19 us (21%)
  between operations  0.76 us (2%)
    ppermute x13, starting transfers between devices, swapped(): return lax.ppermute(array, ('section', 'dp'), pairs)  15.5 us
    ppermute x13, waiting for transfers between devices, swapped(): return lax.ppermute(array, ('section', 'dp'), pairs)  10.1 us
    pallas_call x14, Pallas kernels, local(): pl.pallas_call(kernel, in_specs=[pl.BlockSpec(memory_space=spaces[kind])...  7.19 us
  transfers between devices with their start and end apart: 13, of which 7 were waited for; matrix products, arithmetic and copies ran while one was open for 0% of the time, Pallas kernels for 17%

profile of v10, /device:TPU:0, one launch (start us, length us, event | category | flops | bytes accessed | tf_op | source)
XLA Modules:
  0.0 33.5 jit_solution(14240335870224431335)
XLA Ops:
  0.6 0.9 %pick.1 = bf16[32,2048]{1,0:T(8,128)(2,1)S(1)} custom-call(s32[1]{0:T(128)} %bitcast.1.place_ref, s32[1]{0:T(128)} %bitcast.index_ref, bf16[1,2,32,4096]{3,2,1,0:T(8,128)(2,1)} %w_out.3), custom_call_target="tpu_custom_call" | custom-call | tf_op jit(solution)/shard_map/pick/pallas_call | solution.py:253
  1.6 3.0 %collective-permute-start = (bf16[32,2048]{1,0:T(8,128)(2,1)S(1)}, bf16[32,2048]{1,0:T(8,128)(2,1)S(1)}, u32[]{:S(2)}, u32[]{:S(2)}) collective-permute-start(bf16[32,2048]{1,0:T(8,128)(2,1)S(1)} %pick.1), channel_id=1, source_target_pairs={{0,16},{1,17},{2,18},{3,19},{4,20},{5,21},{6,22},{7,23},{8,24},{9,... | collective-permute-start | bytes 393224 | tf_op jit(solution)/shard_map/ppermute | solution.py:289
  4.6 2.2 %front.1 = (bf16[32,128]{1,0:T(8,128)(2,1)S(1)}, f32[2,32,128]{2,1,0:T(8,128)S(1)}, bf16[128,4096]{1,0:T(8,128)(2,1)S(1)}, bf16[128,4096]{1,0:T(8,128)(2,1)S(1)}...) custom-call(s32[1]{0:T(128)} %bitcast.1.place_ref, ...), custom_call_target="tpu_custom_call" | custom-call | tf_op jit(solution)/shard_map/front/pallas_call | solution.py:253
  6.8 0.1 collective-permute-start.1
  6.9 0.9 %upper.1 = (bf16[128,4096]{1,0:T(8,128)(2,1)S(1)}, bf16[32,128]{1,0:T(8,128)(2,1)S(1)}, bf16[32,128]{1,0:T(8,128)(2,1)S(1)}, bf16[32,128]{1,0:T(8,128)(2,1)S(1)}, f32[2,128,128]{2,1,0:T(8,128)S(1)}) custom-call(bf16[128,4096]{1,0:T(8,128)(2,1)S(1)} %get-tuple-element.37.x, bf16[128,4096]{1,0:T(8,128)(2,1)S(1)} %get-tuple-element.38.g, ...), custom_call_target="tpu_custom_call" | custom-call | tf_op jit(solution)/shard_map/upper/pallas_call | solution.py:253
  7.8 0.3 collective-permute-done.own_ref
  8.1 0.0 collective-permute-start.2
  8.1 0.7 %outgoing.1.flow_ref = bf16[128,4096]{1,0:T(8,128)(2,1)S(1)} custom-call(bf16[128,4096]{1,0:T(8,128)(2,1)S(1)} %get-tuple-element.37.x, bf16[128,4096]{1,0:T(8,128)(2,1)S(1)} %get-tuple-element.38.g, f32[1,4096]{1,0:T(1,128)S(1)} %get-tuple-element.39.gain, bf16[32,4096]{1,0:T(8,128)(2,1)S(1)} %get-tuple-element.40.wi, ...), custom_call_target="tpu_custom_call" | custom-call | flops 20000000000 | bytes 1048576 | tf_op jit(solution)/shard_map/outgoing/pallas_call | solution.py:253
  8.8 0.3 flow.1.part_ref
  9.1 0.3 collective-permute-done.2.other_ref
  9.4 0.3 flow_rest.1._
  9.7 1.9 %collective-permute-start.4 = (bf16[32,128]{1,0:T(8,128)(2,1)S(1)}, bf16[32,128]{1,0:T(8,128)(2,1)S(1)}, u32[]{:S(2)}, u32[]{:S(2)}) collective-permute-start(bf16[32,128]{1,0:T(8,128)(2,1)S(1)} %flow_rest.1._), channel_id=1, source_target_pairs={{0,16},{1,17},{2,18},{3,19},{4,20},{5,21},{6,22},{7,23},{8,24},{9,... | collective-permute-start | bytes 24584 | tf_op jit(solution)/shard_map/ppermute | solution.py:289
  11.6 0.4 %terms1.1 = (bf16[8,32,256]{2,1,0:T(8,128)(2,1)S(1)}, bf16[8,32,256]{2,1,0:T(8,128)(2,1)S(1)}, bf16[8,32,256]{2,1,0:T(8,128)(2,1)S(1)}, bf16[8,32,256]{2,1,0:T(8,128)(2,1)S(1)}) custom-call(s32[1]{0:T(128)} %bitcast.index_ref, bf16[128,4096]{1,0:T(8,128)(2,1)S(1)} %get-tuple-element.38.g, bf16[128,4096]{1,0:T(8,128)(2,1)S(1)} %get-tuple-element.46.xg_ref, ...), custom_call_target="tpu_custom_call" | custom-call | tf_op jit(solution)/shard_map/terms1/pallas_call | solution.py:253
  12.0 0.0 collective-permute-done.1.act0_ref
  12.0 0.3 terms.1
  12.3 0.1 collective-permute-start.3
  12.4 1.0 %collective-permute-done.4.got_ref = bf16[32,128]{1,0:T(8,128)(2,1)S(1)} collective-permute-done((bf16[32,128]{1,0:T(8,128)(2,1)S(1)}, bf16[32,128]{1,0:T(8,128)(2,1)S(1)}, u32[]{:S(2)}, u32[]{:S(2)}) %collective-permute-start.4) | collective-permute-done | bytes 8224 | tf_op jit(solution)/shard_map/ppermute | solution.py:289
  13.4 0.3 lower.1
  13.7 0.1 collective-permute-start.5
  13.8 0.3 collective-permute-done.3.got
  14.1 0.1 chip.1
  14.2 2.5 %collective-permute-start.6 = (bf16[4,32,256]{2,1,0:T(8,128)(2,1)S(1)}, bf16[4,32,256]{2,1,0:T(8,128)(2,1)S(1)}, u32[]{:S(2)}, u32[]{:S(2)}) collective-permute-start(bf16[4,32,256]{2,1,0:T(8,128)(2,1)S(1)} %get-tuple-element.62), channel_id=1, source_target_pairs={{0,18},{1,19},{2,16},{3,17},{4,22},{5,23},{6,20},{7,21},{8,26},{9,... | collective-permute-start | bytes 196616 | tf_op jit(solution)/shard_map/ppermute | solution.py:289
  16.7 0.0 collective-permute-done.5.got0
  16.7 0.1 plane.1
  16.8 0.6 %collective-permute-start.7 = (bf16[4,64,256]{2,1,0:T(8,128)(2,1)S(1)}, bf16[4,64,256]{2,1,0:T(8,128)(2,1)S(1)}, u32[]{:S(2)}, u32[]{:S(2)}) collective-permute-start(bf16[4,64,256]{2,1,0:T(8,128)(2,1)S(1)} %get-tuple-element.63), channel_id=1, source_target_pairs={{0,2},{1,17},{2,0},{3,19},{4,6},{5,21},{6,4},{7,23},{8,10},{9,25},... | collective-permute-start | bytes 393224 | tf_op jit(solution)/shard_map/ppermute | solution.py:289
  17.4 1.2 %collective-permute-start.9 = (bf16[4,64,256]{2,1,0:T(8,128)(2,1)S(1)}, bf16[4,64,256]{2,1,0:T(8,128)(2,1)S(1)}, u32[]{:S(2)}, u32[]{:S(2)}) collective-permute-start(bf16[4,64,256]{2,1,0:T(8,128)(2,1)S(1)} %get-tuple-element.65), channel_id=1, source_target_pairs={{0,16},{1,3},{2,18},{3,1},{4,20},{5,7},{6,22},{7,5},{8,24},{9,11},... | collective-permute-start | bytes 393224 | tf_op jit(solution)/shard_map/ppermute | solution.py:289
  18.6 1.8 %collective-permute-start.8 = (bf16[4,32,256]{2,1,0:T(8,128)(2,1)S(1)}, bf16[4,32,256]{2,1,0:T(8,128)(2,1)S(1)}, u32[]{:S(2)}, u32[]{:S(2)}) collective-permute-start(bf16[4,32,256]{2,1,0:T(8,128)(2,1)S(1)} %get-tuple-element.64), channel_id=1, source_target_pairs={{0,18},{1,19},{2,16},{3,17},{4,22},{5,23},{6,20},{7,21},{8,26},{9,... | collective-permute-start | bytes 196616 | tf_op jit(solution)/shard_map/ppermute | solution.py:289
  20.4 0.0 collective-permute-done.6.across_out
  20.4 4.0 %collective-permute-done.8.across_in = bf16[4,32,256]{2,1,0:T(8,128)(2,1)S(1)} collective-permute-done((bf16[4,32,256]{2,1,0:T(8,128)(2,1)S(1)}, bf16[4,32,256]{2,1,0:T(8,128)(2,1)S(1)}, u32[]{:S(2)}, u32[]{:S(2)}) %collective-permute-start.8) | collective-permute-done | bytes 65568 | tf_op jit(solution)/shard_map/ppermute | solution.py:289
  24.4 0.0 collective-permute-done.7.first
  24.5 0.0 collective-permute-done.9.second
  24.5 0.1 layer.1
  24.5 2.7 %collective-permute-start.10 = (bf16[64,256]{1,0:T(8,128)(2,1)S(1)}, bf16[64,256]{1,0:T(8,128)(2,1)S(1)}, u32[]{:S(2)}, u32[]{:S(2)}) collective-permute-start(bf16[64,256]{1,0:T(8,128)(2,1)S(1)} %get-tuple-element.67), channel_id=1, source_target_pairs={{0,8},{1,9},{2,10},{3,11},{4,12},{5,13},{6,14},{7,15},{8,0},{9,1},... | collective-permute-start | bytes 98312 | tf_op jit(solution)/shard_map/ppermute | solution.py:289
  27.2 1.3 %collective-permute-start.11 = (bf16[64,256]{1,0:T(8,128)(2,1)S(1)}, bf16[64,256]{1,0:T(8,128)(2,1)S(1)}, u32[]{:S(2)}, u32[]{:S(2)}) collective-permute-start(bf16[64,256]{1,0:T(8,128)(2,1)S(1)} %get-tuple-element.68), channel_id=1, source_target_pairs={{0,12},{1,13},{2,14},{3,15},{4,8},{5,9},{6,10},{7,11},{8,4},{9,5},... | collective-permute-start | bytes 98312 | tf_op jit(solution)/shard_map/ppermute | solution.py:289
  28.5 0.2 collective-permute-start.12
  28.8 0.9 %collective-permute-done.10.refs_1_ = bf16[64,256]{1,0:T(8,128)(2,1)S(1)} collective-permute-done((bf16[64,256]{1,0:T(8,128)(2,1)S(1)}, bf16[64,256]{1,0:T(8,128)(2,1)S(1)}, u32[]{:S(2)}, u32[]{:S(2)}) %collective-permute-start.10) | collective-permute-done | bytes 32800 | tf_op jit(solution)/shard_map/ppermute | solution.py:289
  29.7 3.2 %collective-permute-done.11.refs_2_ = bf16[64,256]{1,0:T(8,128)(2,1)S(1)} collective-permute-done((bf16[64,256]{1,0:T(8,128)(2,1)S(1)}, bf16[64,256]{1,0:T(8,128)(2,1)S(1)}, u32[]{:S(2)}, u32[]{:S(2)}) %collective-permute-start.11) | collective-permute-done | bytes 32800 | tf_op jit(solution)/shard_map/ppermute | solution.py:289
  32.9 0.0 collective-permute-done.12.refs_3_
  32.9 0.7 %total.1 = (f32[1,32,256]{2,1,0:T(8,128)}, f32[1,32,256]{2,1,0:T(8,128)}) custom-call(bf16[64,256]{1,0:T(8,128)(2,1)S(1)} %get-tuple-element.66.refs_0_, bf16[64,256]{1,0:T(8,128)(2,1)S(1)} %collective-permute-done.10.refs_1_, bf16[64,256]{1,0:T(8,128)(2,1)S(1)} %collective-permute-done.11.refs_2_, bf16[64,256]{1,0:T(8,128)(2,1)S(1)} %collective-permute-done.12.refs_3_), custom_call_target="tpu_custom_call" | custom-call | tf_op jit(solution)/shard_map/total/pallas_call | solution.py:253
  (1 shorter events, 0.0 us)
Async XLA Ops:
  1.6 6.5 %collective-permute-start = (bf16[32,2048]{1,0:T(8,128)(2,1)S(1)}, bf16[32,2048]{1,0:T(8,128)(2,1)S(1)}, u32[]{:S(2)}, u32[]{:S(2)}) collective-permute-start(bf16[32,2048]{1,0:T(8,128)(2,1)S(1)} %pick.1), channel_id=1, source_target_pairs={{0,16},{1,17},{2,18},{3,19},{4,20},{5,21},{6,22},{7,23},{8,24},{9,... | collective-permute-start | bytes 393224 | tf_op jit(solution)/shard_map/ppermute | solution.py:289
  6.8 5.2 %collective-permute-start.1 = (bf16[32,128]{1,0:T(8,128)(2,1)S(1)}, bf16[32,128]{1,0:T(8,128)(2,1)S(1)}, u32[]{:S(2)}, u32[]{:S(2)}) collective-permute-start(bf16[32,128]{1,0:T(8,128)(2,1)S(1)} %get-tuple-element.45), channel_id=1, source_target_pairs={{0,16},{1,17},{2,18},{3,19},{4,20},{5,21},{6,22},{7,23},{8,24},{9,... | collective-permute-start | bytes 24584 | tf_op jit(solution)/shard_map/ppermute | solution.py:289
  8.1 1.3 %collective-permute-start.2 = (bf16[32,2048]{1,0:T(8,128)(2,1)S(1)}, bf16[32,2048]{1,0:T(8,128)(2,1)S(1)}, u32[]{:S(2)}, u32[]{:S(2)}) collective-permute-start(bf16[32,2048]{1,0:T(8,128)(2,1)S(1)} %collective-permute-done.own_ref), channel_id=1, source_target_pairs={{0,1},{1,0},{2,3},{3,2},{4,5},{5,4},{6,7},{7,6},{8,9},{9,8},{10,11... | collective-permute-start | bytes 393224 | tf_op jit(solution)/shard_map/ppermute | solution.py:289
  9.7 3.7 %collective-permute-start.4 = (bf16[32,128]{1,0:T(8,128)(2,1)S(1)}, bf16[32,128]{1,0:T(8,128)(2,1)S(1)}, u32[]{:S(2)}, u32[]{:S(2)}) collective-permute-start(bf16[32,128]{1,0:T(8,128)(2,1)S(1)} %flow_rest.1._), channel_id=1, source_target_pairs={{0,16},{1,17},{2,18},{3,19},{4,20},{5,21},{6,22},{7,23},{8,24},{9,... | collective-permute-start | bytes 24584 | tf_op jit(solution)/shard_map/ppermute | solution.py:289
  12.3 1.8 %collective-permute-start.3 = (bf16[24,32,256]{2,1,0:T(8,128)(2,1)S(1)}, bf16[24,32,256]{2,1,0:T(8,128)(2,1)S(1)}, u32[]{:S(2)}, u32[]{:S(2)}) collective-permute-start(bf16[24,32,256]{2,1,0:T(8,128)(2,1)S(1)} %get-tuple-element.55), channel_id=1, source_target_pairs={{0,1},{1,0},{2,3},{3,2},{4,5},{5,4},{6,7},{7,6},{8,9},{9,8},{10,11... | collective-permute-start | bytes 1179656 | tf_op jit(solution)/shard_map/ppermute | solution.py:289
  13.7 3.1 %collective-permute-start.5 = (bf16[8,32,256]{2,1,0:T(8,128)(2,1)S(1)}, bf16[8,32,256]{2,1,0:T(8,128)(2,1)S(1)}, u32[]{:S(2)}, u32[]{:S(2)}) collective-permute-start(bf16[8,32,256]{2,1,0:T(8,128)(2,1)S(1)} %get-tuple-element.60), channel_id=1, source_target_pairs={{0,1},{1,0},{2,3},{3,2},{4,5},{5,4},{6,7},{7,6},{8,9},{9,8},{10,11... | collective-permute-start | bytes 393224 | tf_op jit(solution)/shard_map/ppermute | solution.py:289
  14.2 6.2 %collective-permute-start.6 = (bf16[4,32,256]{2,1,0:T(8,128)(2,1)S(1)}, bf16[4,32,256]{2,1,0:T(8,128)(2,1)S(1)}, u32[]{:S(2)}, u32[]{:S(2)}) collective-permute-start(bf16[4,32,256]{2,1,0:T(8,128)(2,1)S(1)} %get-tuple-element.62), channel_id=1, source_target_pairs={{0,18},{1,19},{2,16},{3,17},{4,22},{5,23},{6,20},{7,21},{8,26},{9,... | collective-permute-start | bytes 196616 | tf_op jit(solution)/shard_map/ppermute | solution.py:289
  16.8 7.6 %collective-permute-start.7 = (bf16[4,64,256]{2,1,0:T(8,128)(2,1)S(1)}, bf16[4,64,256]{2,1,0:T(8,128)(2,1)S(1)}, u32[]{:S(2)}, u32[]{:S(2)}) collective-permute-start(bf16[4,64,256]{2,1,0:T(8,128)(2,1)S(1)} %get-tuple-element.63), channel_id=1, source_target_pairs={{0,2},{1,17},{2,0},{3,19},{4,6},{5,21},{6,4},{7,23},{8,10},{9,25},... | collective-permute-start | bytes 393224 | tf_op jit(solution)/shard_map/ppermute | solution.py:289
  17.4 7.1 %collective-permute-start.9 = (bf16[4,64,256]{2,1,0:T(8,128)(2,1)S(1)}, bf16[4,64,256]{2,1,0:T(8,128)(2,1)S(1)}, u32[]{:S(2)}, u32[]{:S(2)}) collective-permute-start(bf16[4,64,256]{2,1,0:T(8,128)(2,1)S(1)} %get-tuple-element.65), channel_id=1, source_target_pairs={{0,16},{1,3},{2,18},{3,1},{4,20},{5,7},{6,22},{7,5},{8,24},{9,11},... | collective-permute-start | bytes 393224 | tf_op jit(solution)/shard_map/ppermute | solution.py:289
  18.6 5.9 %collective-permute-start.8 = (bf16[4,32,256]{2,1,0:T(8,128)(2,1)S(1)}, bf16[4,32,256]{2,1,0:T(8,128)(2,1)S(1)}, u32[]{:S(2)}, u32[]{:S(2)}) collective-permute-start(bf16[4,32,256]{2,1,0:T(8,128)(2,1)S(1)} %get-tuple-element.64), channel_id=1, source_target_pairs={{0,18},{1,19},{2,16},{3,17},{4,22},{5,23},{6,20},{7,21},{8,26},{9,... | collective-permute-start | bytes 196616 | tf_op jit(solution)/shard_map/ppermute | solution.py:289
  24.5 5.2 %collective-permute-start.10 = (bf16[64,256]{1,0:T(8,128)(2,1)S(1)}, bf16[64,256]{1,0:T(8,128)(2,1)S(1)}, u32[]{:S(2)}, u32[]{:S(2)}) collective-permute-start(bf16[64,256]{1,0:T(8,128)(2,1)S(1)} %get-tuple-element.67), channel_id=1, source_target_pairs={{0,8},{1,9},{2,10},{3,11},{4,12},{5,13},{6,14},{7,15},{8,0},{9,1},... | collective-permute-start | bytes 98312 | tf_op jit(solution)/shard_map/ppermute | solution.py:289
  27.2 5.7 %collective-permute-start.11 = (bf16[64,256]{1,0:T(8,128)(2,1)S(1)}, bf16[64,256]{1,0:T(8,128)(2,1)S(1)}, u32[]{:S(2)}, u32[]{:S(2)}) collective-permute-start(bf16[64,256]{1,0:T(8,128)(2,1)S(1)} %get-tuple-element.68), channel_id=1, source_target_pairs={{0,12},{1,13},{2,14},{3,15},{4,8},{5,9},{6,10},{7,11},{8,4},{9,5},... | collective-permute-start | bytes 98312 | tf_op jit(solution)/shard_map/ppermute | solution.py:289
  28.5 4.4 %collective-permute-start.12 = (bf16[64,256]{1,0:T(8,128)(2,1)S(1)}, bf16[64,256]{1,0:T(8,128)(2,1)S(1)}, u32[]{:S(2)}, u32[]{:S(2)}) collective-permute-start(bf16[64,256]{1,0:T(8,128)(2,1)S(1)} %get-tuple-element.69), channel_id=1, source_target_pairs={{0,4},{1,5},{2,6},{3,7},{4,0},{5,1},{6,2},{7,3},{8,12},{9,13},{10,... | collective-permute-start | bytes 98312 | tf_op jit(solution)/shard_map/ppermute | solution.py:289

commit v11 on v10

--- a/solution.py
+++ b/solution.py
@@ -39,11 +39,27 @@
     return sig, sig * (1.0 + pre * (1.0 - sig))
 
 
-def project(x_ref, gain_ref, w_ref, xg_ref, step):
+PIECES = 4
+
+
+def pieces(source, target, sems, first):
+    step = target.shape[-1] // PIECES
+    copies = []
+    for i in range(PIECES):
+        cols = pl.ds(i * step, step)
+        copies.append(
+            pltpu.make_async_copy(source.at[:, cols], target.at[:, cols], sems.at[first + i])
+        )
+    return copies
+
+
+def project(x_ref, gain_ref, w_ref, xg_ref, step, copies=()):
     tokens, width = x_ref.shape
     squares = jnp.zeros((tokens, 128), F32)
     pre = jnp.zeros((w_ref.shape[0], tokens), F32)
     for c in range(0, width, step):
+        if copies and c % (width // len(copies)) == 0:
+            copies[c * len(copies) // width].wait()
         x = x_ref[:, c : c + step].astype(F32)
         for k in range(0, step, 128):
             part = x[:, k : k + 128]
@@ -75,26 +91,27 @@
     copies = [
         (gains.at[0, pl.ds(lower, 1)], gain0),
         (w_in.at[0, lower], wi0),
-        (saved.at[0, lower], x0),
         (gains.at[0, pl.ds(upper, 1)], gain1),
         (w_in.at[0, upper], wi1),
-        (saved.at[0, upper], x1),
         (w_out.at[0, upper], wo1),
-        (top.at[upper], g),
     ]
     copies = [pltpu.make_async_copy(a, b, sems.at[i]) for i, (a, b) in enumerate(copies)]
-    for copy in copies:
+    first = len(copies)
+    copies_x0 = pieces(saved.at[0, lower], x0, sems, first)
+    others = pieces(saved.at[0, upper], x1, sems, first + PIECES)
+    others += pieces(top.at[upper], g, sems, first + 2 * PIECES)
+    for copy in copies[0:2] + copies_x0 + copies[2:5] + others:
         copy.start()
-    for copy in copies[0:3]:
+    for copy in copies[0:2]:
         copy.wait()
-    scale, raw = project(x0, gain0, wi0, xg0_ref, step)
+    scale, raw = project(x0, gain0, wi0, xg0_ref, step, copies_x0)
     row = as_row(scale)
     pre = raw * row
     sig, slope = silu_slope(pre)
     act0_ref[...] = (pre * sig).astype(BF16)
     low_ref[0] = slope
     low_ref[1] = jnp.broadcast_to(row, raw.shape)
-    for copy in copies[3:8]:
+    for copy in copies[2:5] + others:
         copy.wait()
 
 
@@ -148,9 +165,11 @@
 def pick_kernel(place_ref, index_ref, w_out, out_ref, sems):
     half = out_ref.shape[1]
     cols = pl.ds(pl.multiple_of((index_ref[0] % 2) * half, half), half)
-    copy = pltpu.make_async_copy(w_out.at[0, place_ref[0], :, cols], out_ref, sems.at[0])
-    copy.start()
-    copy.wait()
+    copies = pieces(w_out.at[0, place_ref[0], :, cols], out_ref, sems, 0)
+    for copy in copies:
+        copy.start()
+    for copy in copies:
+        copy.wait()
 
 
 def product(step, number, w_ref, flow_ref):
@@ -300,14 +319,14 @@
     along_x, other_core = (1, 0), (0, 1)
 
     mine = local(
-        pick_kernel, "pick", [((rank, width // 2), BF16)], place, index, w_out, scratch=[sems((1,))]
+        pick_kernel, "pick", [((rank, width // 2), BF16)], place, index, w_out, scratch=[sems((PIECES,))]
     )
     own_half = swapped(mine, along_x)
     act0, low, xg0, x1, g, gain1, wi1, wo1 = local(
         partial(front_kernel, share), "front",
         [small, ((2, rank, tokens), F32), wide, wide, wide, gain, thin, thin],
         place, saved, top, gains, w_in, w_out,
-        scratch=[pltpu.VMEM(*wide), pltpu.VMEM(*gain), pltpu.VMEM(*thin), sems((8,))],
+        scratch=[pltpu.VMEM(*wide), pltpu.VMEM(*gain), pltpu.VMEM(*thin), sems((5 + 3 * PIECES,))],
     )
     got_act0 = swapped(act0, along_x)
     xg1, act1, das1, da1, columns = local(

time: 33.7 us -> 33.7 us (level)
  no operation moved by 1% of the time
where the time goes in v11:
time: 33.7 us; the launch traced here: 33.5 us
  starting transfers between devices  15.5 us (46%)
  waiting for transfers between devices  10.1 us (30%)
  Pallas kernels  7.16 us (21%)
  between operations  0.76 us (2%)
    ppermute x13, starting transfers between devices, swapped(): return lax.ppermute(array, ('section', 'dp'), pairs)  15.5 us
    ppermute x13, waiting for transfers between devices, swapped(): return lax.ppermute(array, ('section', 'dp'), pairs)  10.1 us
    pallas_call x14, Pallas kernels, local(): pl.pallas_call(kernel, in_specs=[pl.BlockSpec(memory_space=spaces[kind])...  7.16 us
  transfers between devices with their start and end apart: 13, of which 7 were waited for; matrix products, arithmetic and copies ran while one was open for 0% of the time, Pallas kernels for 17%

profile of v11, /device:TPU:0, one launch (start us, length us, event | category | flops | bytes accessed | tf_op | source)
XLA Modules:
  0.0 33.5 jit_solution(12114103287506985774)
XLA Ops:
  0.6 0.8 %pick.1 = bf16[32,2048]{1,0:T(8,128)(2,1)S(1)} custom-call(s32[1]{0:T(128)} %bitcast.1.place_ref, s32[1]{0:T(128)} %bitcast.index_ref, bf16[1,2,32,4096]{3,2,1,0:T(8,128)(2,1)} %w_out.3), custom_call_target="tpu_custom_call" | custom-call | tf_op jit(solution)/shard_map/pick/pallas_call | solution.py:272
  1.5 3.0 %collective-permute-start = (bf16[32,2048]{1,0:T(8,128)(2,1)S(1)}, bf16[32,2048]{1,0:T(8,128)(2,1)S(1)}, u32[]{:S(2)}, u32[]{:S(2)}) collective-permute-start(bf16[32,2048]{1,0:T(8,128)(2,1)S(1)} %pick.1), channel_id=1, source_target_pairs={{0,16},{1,17},{2,18},{3,19},{4,20},{5,21},{6,22},{7,23},{8,24},{9,... | collective-permute-start | bytes 393224 | tf_op jit(solution)/shard_map/ppermute | solution.py:308
  4.5 2.2 %front.1 = (bf16[32,128]{1,0:T(8,128)(2,1)S(1)}, f32[2,32,128]{2,1,0:T(8,128)S(1)}, bf16[128,4096]{1,0:T(8,128)(2,1)S(1)}, bf16[128,4096]{1,0:T(8,128)(2,1)S(1)}...) custom-call(s32[1]{0:T(128)} %bitcast.1.place_ref, ...), custom_call_target="tpu_custom_call" | custom-call | tf_op jit(solution)/shard_map/front/pallas_call | solution.py:272
  6.7 0.1 collective-permute-start.1
  6.8 0.9 %upper.1 = (bf16[128,4096]{1,0:T(8,128)(2,1)S(1)}, bf16[32,128]{1,0:T(8,128)(2,1)S(1)}, bf16[32,128]{1,0:T(8,128)(2,1)S(1)}, bf16[32,128]{1,0:T(8,128)(2,1)S(1)}, f32[2,128,128]{2,1,0:T(8,128)S(1)}) custom-call(bf16[128,4096]{1,0:T(8,128)(2,1)S(1)} %get-tuple-element.37.x, bf16[128,4096]{1,0:T(8,128)(2,1)S(1)} %get-tuple-element.38.g, ...), custom_call_target="tpu_custom_call" | custom-call | tf_op jit(solution)/shard_map/upper/pallas_call | solution.py:272
  7.8 0.2 collective-permute-done.own_ref
  8.0 0.0 collective-permute-start.2
  8.0 0.7 %outgoing.1.flow_ref = bf16[128,4096]{1,0:T(8,128)(2,1)S(1)} custom-call(bf16[128,4096]{1,0:T(8,128)(2,1)S(1)} %get-tuple-element.37.x, bf16[128,4096]{1,0:T(8,128)(2,1)S(1)} %get-tuple-element.38.g, f32[1,4096]{1,0:T(1,128)S(1)} %get-tuple-element.39.gain, bf16[32,4096]{1,0:T(8,128)(2,1)S(1)} %get-tuple-element.40.wi, ...), custom_call_target="tpu_custom_call" | custom-call | flops 20000000000 | bytes 1048576 | tf_op jit(solution)/shard_map/outgoing/pallas_call | solution.py:272
  8.7 0.3 flow.1.part_ref
  9.0 0.3 collective-permute-done.2.other_ref
  9.3 0.3 flow_rest.1._
  9.6 1.9 %collective-permute-start.4 = (bf16[32,128]{1,0:T(8,128)(2,1)S(1)}, bf16[32,128]{1,0:T(8,128)(2,1)S(1)}, u32[]{:S(2)}, u32[]{:S(2)}) collective-permute-start(bf16[32,128]{1,0:T(8,128)(2,1)S(1)} %flow_rest.1._), channel_id=1, source_target_pairs={{0,16},{1,17},{2,18},{3,19},{4,20},{5,21},{6,22},{7,23},{8,24},{9,... | collective-permute-start | bytes 24584 | tf_op jit(solution)/shard_map/ppermute | solution.py:308
  11.5 0.4 %terms1.1 = (bf16[8,32,256]{2,1,0:T(8,128)(2,1)S(1)}, bf16[8,32,256]{2,1,0:T(8,128)(2,1)S(1)}, bf16[8,32,256]{2,1,0:T(8,128)(2,1)S(1)}, bf16[8,32,256]{2,1,0:T(8,128)(2,1)S(1)}) custom-call(s32[1]{0:T(128)} %bitcast.index_ref, bf16[128,4096]{1,0:T(8,128)(2,1)S(1)} %get-tuple-element.38.g, bf16[128,4096]{1,0:T(8,128)(2,1)S(1)} %get-tuple-element.46.xg_ref, ...), custom_call_target="tpu_custom_call" | custom-call | tf_op jit(solution)/shard_map/terms1/pallas_call | solution.py:272
  12.0 0.0 collective-permute-done.1.act0_ref
  12.0 0.3 terms.1
  12.3 0.1 collective-permute-start.3
  12.3 1.0 %collective-permute-done.4.got_ref = bf16[32,128]{1,0:T(8,128)(2,1)S(1)} collective-permute-done((bf16[32,128]{1,0:T(8,128)(2,1)S(1)}, bf16[32,128]{1,0:T(8,128)(2,1)S(1)}, u32[]{:S(2)}, u32[]{:S(2)}) %collective-permute-start.4) | collective-permute-done | bytes 8224 | tf_op jit(solution)/shard_map/ppermute | solution.py:308
  13.3 0.3 lower.1
  13.6 0.1 collective-permute-start.5
  13.7 0.3 %collective-permute-done.3.got = bf16[24,32,256]{2,1,0:T(8,128)(2,1)S(1)} collective-permute-done((bf16[24,32,256]{2,1,0:T(8,128)(2,1)S(1)}, bf16[24,32,256]{2,1,0:T(8,128)(2,1)S(1)}, u32[]{:S(2)}, u32[]{:S(2)}) %collective-permute-start.3) | collective-permute-done | bytes 393248 | tf_op jit(solution)/shard_map/ppermute | solution.py:308
  14.0 0.1 chip.1
  14.1 2.5 %collective-permute-start.6 = (bf16[4,32,256]{2,1,0:T(8,128)(2,1)S(1)}, bf16[4,32,256]{2,1,0:T(8,128)(2,1)S(1)}, u32[]{:S(2)}, u32[]{:S(2)}) collective-permute-start(bf16[4,32,256]{2,1,0:T(8,128)(2,1)S(1)} %get-tuple-element.62), channel_id=1, source_target_pairs={{0,18},{1,19},{2,16},{3,17},{4,22},{5,23},{6,20},{7,21},{8,26},{9,... | collective-permute-start | bytes 196616 | tf_op jit(solution)/shard_map/ppermute | solution.py:308
  16.7 0.0 collective-permute-done.5.got0
  16.7 0.1 plane.1
  16.8 0.6 %collective-permute-start.7 = (bf16[4,64,256]{2,1,0:T(8,128)(2,1)S(1)}, bf16[4,64,256]{2,1,0:T(8,128)(2,1)S(1)}, u32[]{:S(2)}, u32[]{:S(2)}) collective-permute-start(bf16[4,64,256]{2,1,0:T(8,128)(2,1)S(1)} %get-tuple-element.63), channel_id=1, source_target_pairs={{0,2},{1,17},{2,0},{3,19},{4,6},{5,21},{6,4},{7,23},{8,10},{9,25},... | collective-permute-start | bytes 393224 | tf_op jit(solution)/shard_map/ppermute | solution.py:308
  17.4 1.2 %collective-permute-start.9 = (bf16[4,64,256]{2,1,0:T(8,128)(2,1)S(1)}, bf16[4,64,256]{2,1,0:T(8,128)(2,1)S(1)}, u32[]{:S(2)}, u32[]{:S(2)}) collective-permute-start(bf16[4,64,256]{2,1,0:T(8,128)(2,1)S(1)} %get-tuple-element.65), channel_id=1, source_target_pairs={{0,16},{1,3},{2,18},{3,1},{4,20},{5,7},{6,22},{7,5},{8,24},{9,11},... | collective-permute-start | bytes 393224 | tf_op jit(solution)/shard_map/ppermute | solution.py:308
  18.5 1.8 %collective-permute-start.8 = (bf16[4,32,256]{2,1,0:T(8,128)(2,1)S(1)}, bf16[4,32,256]{2,1,0:T(8,128)(2,1)S(1)}, u32[]{:S(2)}, u32[]{:S(2)}) collective-permute-start(bf16[4,32,256]{2,1,0:T(8,128)(2,1)S(1)} %get-tuple-element.64), channel_id=1, source_target_pairs={{0,18},{1,19},{2,16},{3,17},{4,22},{5,23},{6,20},{7,21},{8,26},{9,... | collective-permute-start | bytes 196616 | tf_op jit(solution)/shard_map/ppermute | solution.py:308
  20.3 0.0 collective-permute-done.6.across_out
  20.4 4.0 %collective-permute-done.8.across_in = bf16[4,32,256]{2,1,0:T(8,128)(2,1)S(1)} collective-permute-done((bf16[4,32,256]{2,1,0:T(8,128)(2,1)S(1)}, bf16[4,32,256]{2,1,0:T(8,128)(2,1)S(1)}, u32[]{:S(2)}, u32[]{:S(2)}) %collective-permute-start.8) | collective-permute-done | bytes 65568 | tf_op jit(solution)/shard_map/ppermute | solution.py:308
  24.4 0.0 collective-permute-done.7.first
  24.4 0.0 collective-permute-done.9.second
  24.4 0.1 layer.1
  24.5 2.7 %collective-permute-start.10 = (bf16[64,256]{1,0:T(8,128)(2,1)S(1)}, bf16[64,256]{1,0:T(8,128)(2,1)S(1)}, u32[]{:S(2)}, u32[]{:S(2)}) collective-permute-start(bf16[64,256]{1,0:T(8,128)(2,1)S(1)} %get-tuple-element.67), channel_id=1, source_target_pairs={{0,8},{1,9},{2,10},{3,11},{4,12},{5,13},{6,14},{7,15},{8,0},{9,1},... | collective-permute-start | bytes 98312 | tf_op jit(solution)/shard_map/ppermute | solution.py:308
  27.1 1.4 %collective-permute-start.11 = (bf16[64,256]{1,0:T(8,128)(2,1)S(1)}, bf16[64,256]{1,0:T(8,128)(2,1)S(1)}, u32[]{:S(2)}, u32[]{:S(2)}) collective-permute-start(bf16[64,256]{1,0:T(8,128)(2,1)S(1)} %get-tuple-element.68), channel_id=1, source_target_pairs={{0,12},{1,13},{2,14},{3,15},{4,8},{5,9},{6,10},{7,11},{8,4},{9,5},... | collective-permute-start | bytes 98312 | tf_op jit(solution)/shard_map/ppermute | solution.py:308
  28.5 0.2 collective-permute-start.12
  28.7 0.9 %collective-permute-done.10.refs_1_ = bf16[64,256]{1,0:T(8,128)(2,1)S(1)} collective-permute-done((bf16[64,256]{1,0:T(8,128)(2,1)S(1)}, bf16[64,256]{1,0:T(8,128)(2,1)S(1)}, u32[]{:S(2)}, u32[]{:S(2)}) %collective-permute-start.10) | collective-permute-done | bytes 32800 | tf_op jit(solution)/shard_map/ppermute | solution.py:308
  29.6 3.2 %collective-permute-done.11.refs_2_ = bf16[64,256]{1,0:T(8,128)(2,1)S(1)} collective-permute-done((bf16[64,256]{1,0:T(8,128)(2,1)S(1)}, bf16[64,256]{1,0:T(8,128)(2,1)S(1)}, u32[]{:S(2)}, u32[]{:S(2)}) %collective-permute-start.11) | collective-permute-done | bytes 32800 | tf_op jit(solution)/shard_map/ppermute | solution.py:308
  32.8 0.0 collective-permute-done.12.refs_3_
  32.8 0.7 %total.1 = (f32[1,32,256]{2,1,0:T(8,128)}, f32[1,32,256]{2,1,0:T(8,128)}) custom-call(bf16[64,256]{1,0:T(8,128)(2,1)S(1)} %get-tuple-element.66.refs_0_, bf16[64,256]{1,0:T(8,128)(2,1)S(1)} %collective-permute-done.10.refs_1_, bf16[64,256]{1,0:T(8,128)(2,1)S(1)} %collective-permute-done.11.refs_2_, bf16[64,256]{1,0:T(8,128)(2,1)S(1)} %collective-permute-done.12.refs_3_), custom_call_target="tpu_custom_call" | custom-call | tf_op jit(solution)/shard_map/total/pallas_call | solution.py:272
  (1 shorter events, 0.0 us)
Async XLA Ops:
  1.5 6.5 %collective-permute-start = (bf16[32,2048]{1,0:T(8,128)(2,1)S(1)}, bf16[32,2048]{1,0:T(8,128)(2,1)S(1)}, u32[]{:S(2)}, u32[]{:S(2)}) collective-permute-start(bf16[32,2048]{1,0:T(8,128)(2,1)S(1)} %pick.1), channel_id=1, source_target_pairs={{0,16},{1,17},{2,18},{3,19},{4,20},{5,21},{6,22},{7,23},{8,24},{9,... | collective-permute-start | bytes 393224 | tf_op jit(solution)/shard_map/ppermute | solution.py:308
  6.7 5.2 %collective-permute-start.1 = (bf16[32,128]{1,0:T(8,128)(2,1)S(1)}, bf16[32,128]{1,0:T(8,128)(2,1)S(1)}, u32[]{:S(2)}, u32[]{:S(2)}) collective-permute-start(bf16[32,128]{1,0:T(8,128)(2,1)S(1)} %get-tuple-element.45), channel_id=1, source_target_pairs={{0,16},{1,17},{2,18},{3,19},{4,20},{5,21},{6,22},{7,23},{8,24},{9,... | collective-permute-start | bytes 24584 | tf_op jit(solution)/shard_map/ppermute | solution.py:308
  8.0 1.3 %collective-permute-start.2 = (bf16[32,2048]{1,0:T(8,128)(2,1)S(1)}, bf16[32,2048]{1,0:T(8,128)(2,1)S(1)}, u32[]{:S(2)}, u32[]{:S(2)}) collective-permute-start(bf16[32,2048]{1,0:T(8,128)(2,1)S(1)} %collective-permute-done.own_ref), channel_id=1, source_target_pairs={{0,1},{1,0},{2,3},{3,2},{4,5},{5,4},{6,7},{7,6},{8,9},{9,8},{10,11... | collective-permute-start | bytes 393224 | tf_op jit(solution)/shard_map/ppermute | solution.py:308
  9.6 3.7 %collective-permute-start.4 = (bf16[32,128]{1,0:T(8,128)(2,1)S(1)}, bf16[32,128]{1,0:T(8,128)(2,1)S(1)}, u32[]{:S(2)}, u32[]{:S(2)}) collective-permute-start(bf16[32,128]{1,0:T(8,128)(2,1)S(1)} %flow_rest.1._), channel_id=1, source_target_pairs={{0,16},{1,17},{2,18},{3,19},{4,20},{5,21},{6,22},{7,23},{8,24},{9,... | collective-permute-start | bytes 24584 | tf_op jit(solution)/shard_map/ppermute | solution.py:308
  12.3 1.8 %collective-permute-start.3 = (bf16[24,32,256]{2,1,0:T(8,128)(2,1)S(1)}, bf16[24,32,256]{2,1,0:T(8,128)(2,1)S(1)}, u32[]{:S(2)}, u32[]{:S(2)}) collective-permute-start(bf16[24,32,256]{2,1,0:T(8,128)(2,1)S(1)} %get-tuple-element.55), channel_id=1, source_target_pairs={{0,1},{1,0},{2,3},{3,2},{4,5},{5,4},{6,7},{7,6},{8,9},{9,8},{10,11... | collective-permute-start | bytes 1179656 | tf_op jit(solution)/shard_map/ppermute | solution.py:308
  13.6 3.1 %collective-permute-start.5 = (bf16[8,32,256]{2,1,0:T(8,128)(2,1)S(1)}, bf16[8,32,256]{2,1,0:T(8,128)(2,1)S(1)}, u32[]{:S(2)}, u32[]{:S(2)}) collective-permute-start(bf16[8,32,256]{2,1,0:T(8,128)(2,1)S(1)} %get-tuple-element.60), channel_id=1, source_target_pairs={{0,1},{1,0},{2,3},{3,2},{4,5},{5,4},{6,7},{7,6},{8,9},{9,8},{10,11... | collective-permute-start | bytes 393224 | tf_op jit(solution)/shard_map/ppermute | solution.py:308
  14.1 6.2 %collective-permute-start.6 = (bf16[4,32,256]{2,1,0:T(8,128)(2,1)S(1)}, bf16[4,32,256]{2,1,0:T(8,128)(2,1)S(1)}, u32[]{:S(2)}, u32[]{:S(2)}) collective-permute-start(bf16[4,32,256]{2,1,0:T(8,128)(2,1)S(1)} %get-tuple-element.62), channel_id=1, source_target_pairs={{0,18},{1,19},{2,16},{3,17},{4,22},{5,23},{6,20},{7,21},{8,26},{9,... | collective-permute-start | bytes 196616 | tf_op jit(solution)/shard_map/ppermute | solution.py:308
  16.8 7.6 %collective-permute-start.7 = (bf16[4,64,256]{2,1,0:T(8,128)(2,1)S(1)}, bf16[4,64,256]{2,1,0:T(8,128)(2,1)S(1)}, u32[]{:S(2)}, u32[]{:S(2)}) collective-permute-start(bf16[4,64,256]{2,1,0:T(8,128)(2,1)S(1)} %get-tuple-element.63), channel_id=1, source_target_pairs={{0,2},{1,17},{2,0},{3,19},{4,6},{5,21},{6,4},{7,23},{8,10},{9,25},... | collective-permute-start | bytes 393224 | tf_op jit(solution)/shard_map/ppermute | solution.py:308
  17.4 7.1 %collective-permute-start.9 = (bf16[4,64,256]{2,1,0:T(8,128)(2,1)S(1)}, bf16[4,64,256]{2,1,0:T(8,128)(2,1)S(1)}, u32[]{:S(2)}, u32[]{:S(2)}) collective-permute-start(bf16[4,64,256]{2,1,0:T(8,128)(2,1)S(1)} %get-tuple-element.65), channel_id=1, source_target_pairs={{0,16},{1,3},{2,18},{3,1},{4,20},{5,7},{6,22},{7,5},{8,24},{9,11},... | collective-permute-start | bytes 393224 | tf_op jit(solution)/shard_map/ppermute | solution.py:308
  18.5 5.9 %collective-permute-start.8 = (bf16[4,32,256]{2,1,0:T(8,128)(2,1)S(1)}, bf16[4,32,256]{2,1,0:T(8,128)(2,1)S(1)}, u32[]{:S(2)}, u32[]{:S(2)}) collective-permute-start(bf16[4,32,256]{2,1,0:T(8,128)(2,1)S(1)} %get-tuple-element.64), channel_id=1, source_target_pairs={{0,18},{1,19},{2,16},{3,17},{4,22},{5,23},{6,20},{7,21},{8,26},{9,... | collective-permute-start | bytes 196616 | tf_op jit(solution)/shard_map/ppermute | solution.py:308
  24.5 5.2 %collective-permute-start.10 = (bf16[64,256]{1,0:T(8,128)(2,1)S(1)}, bf16[64,256]{1,0:T(8,128)(2,1)S(1)}, u32[]{:S(2)}, u32[]{:S(2)}) collective-permute-start(bf16[64,256]{1,0:T(8,128)(2,1)S(1)} %get-tuple-element.67), channel_id=1, source_target_pairs={{0,8},{1,9},{2,10},{3,11},{4,12},{5,13},{6,14},{7,15},{8,0},{9,1},... | collective-permute-start | bytes 98312 | tf_op jit(solution)/shard_map/ppermute | solution.py:308
  27.1 5.7 %collective-permute-start.11 = (bf16[64,256]{1,0:T(8,128)(2,1)S(1)}, bf16[64,256]{1,0:T(8,128)(2,1)S(1)}, u32[]{:S(2)}, u32[]{:S(2)}) collective-permute-start(bf16[64,256]{1,0:T(8,128)(2,1)S(1)} %get-tuple-element.68), channel_id=1, source_target_pairs={{0,12},{1,13},{2,14},{3,15},{4,8},{5,9},{6,10},{7,11},{8,4},{9,5},... | collective-permute-start | bytes 98312 | tf_op jit(solution)/shard_map/ppermute | solution.py:308
  28.5 4.4 %collective-permute-start.12 = (bf16[64,256]{1,0:T(8,128)(2,1)S(1)}, bf16[64,256]{1,0:T(8,128)(2,1)S(1)}, u32[]{:S(2)}, u32[]{:S(2)}) collective-permute-start(bf16[64,256]{1,0:T(8,128)(2,1)S(1)} %get-tuple-element.69), channel_id=1, source_target_pairs={{0,4},{1,5},{2,6},{3,7},{4,0},{5,1},{6,2},{7,3},{8,12},{9,13},{10,... | collective-permute-start | bytes 98312 | tf_op jit(solution)/shard_map/ppermute | solution.py:308

commit v12 on v11

--- a/solution.py
+++ b/solution.py
@@ -82,8 +82,8 @@
 
 
 def front_kernel(
-    step, place_ref, saved, top, gains, w_in, w_out,
-    act0_ref, low_ref, xg0_ref, x1, g, gain1, wi1, wo1,
+    step, place_ref, saved, gains, w_in,
+    act0_ref, low_ref, xg0_ref, x1, gain1, wi1,
     x0, gain0, wi0, sems,
 ):
     lower = place_ref[0]
@@ -93,14 +93,12 @@
         (w_in.at[0, lower], wi0),
         (gains.at[0, pl.ds(upper, 1)], gain1),
         (w_in.at[0, upper], wi1),
-        (w_out.at[0, upper], wo1),
     ]
     copies = [pltpu.make_async_copy(a, b, sems.at[i]) for i, (a, b) in enumerate(copies)]
     first = len(copies)
     copies_x0 = pieces(saved.at[0, lower], x0, sems, first)
     others = pieces(saved.at[0, upper], x1, sems, first + PIECES)
-    others += pieces(top.at[upper], g, sems, first + 2 * PIECES)
-    for copy in copies[0:2] + copies_x0 + copies[2:5] + others:
+    for copy in copies[0:2] + copies_x0 + copies[2:4] + others:
         copy.start()
     for copy in copies[0:2]:
         copy.wait()
@@ -111,15 +109,28 @@
     act0_ref[...] = (pre * sig).astype(BF16)
     low_ref[0] = slope
     low_ref[1] = jnp.broadcast_to(row, raw.shape)
-    for copy in copies[2:5] + others:
+    for copy in copies[2:4] + others:
         copy.wait()
 
 
-def upper_kernel(step, x, g, gain, wi, wo, xg_ref, act_ref, das_ref, da_ref, columns_ref):
+def upper_kernel(
+    step, place_ref, x, gain, wi, top, w_out,
+    xg_ref, act_ref, das_ref, da_ref, columns_ref, g,
+    wo, sems,
+):
     width = x.shape[1]
+    upper = 1 - place_ref[0]
+    copies = pieces(w_out.at[0, upper], wo, sems, 0)
+    copies_g = pieces(top.at[upper], g, sems, PIECES)
+    for copy in copies + copies_g:
+        copy.start()
     scale, raw = project(x, gain, wi, xg_ref, step)
     delta = jnp.zeros(raw.shape, F32)
+    for copy in copies:
+        copy.wait()
     for c in range(0, width, step):
+        if c % (width // PIECES) == 0:
+            copies_g[c * PIECES // width].wait()
         delta += nt(wo[:, c : c + step], g[:, c : c + step])
     row = as_row(scale)
     pre = raw * row
@@ -322,17 +333,18 @@
         pick_kernel, "pick", [((rank, width // 2), BF16)], place, index, w_out, scratch=[sems((PIECES,))]
     )
     own_half = swapped(mine, along_x)
-    act0, low, xg0, x1, g, gain1, wi1, wo1 = local(
+    act0, low, xg0, x1, gain1, wi1 = local(
         partial(front_kernel, share), "front",
-        [small, ((2, rank, tokens), F32), wide, wide, wide, gain, thin, thin],
-        place, saved, top, gains, w_in, w_out,
-        scratch=[pltpu.VMEM(*wide), pltpu.VMEM(*gain), pltpu.VMEM(*thin), sems((5 + 3 * PIECES,))],
+        [small, ((2, rank, tokens), F32), wide, wide, gain, thin],
+        place, saved, gains, w_in,
+        scratch=[pltpu.VMEM(*wide), pltpu.VMEM(*gain), pltpu.VMEM(*thin), sems((4 + 2 * PIECES,))],
     )
     got_act0 = swapped(act0, along_x)
-    xg1, act1, das1, da1, columns = local(
+    xg1, act1, das1, da1, columns, g = local(
         partial(upper_kernel, share), "upper",
-        [wide, small, small, small, ((2, tokens, tokens), F32)],
-        *near(x1, g, gain1, wi1, wo1),
+        [wide, small, small, small, ((2, tokens, tokens), F32), wide],
+        place, *near(x1, gain1, wi1), top, w_out,
+        scratch=[pltpu.VMEM(*thin), sems((2 * PIECES,))],
     )
     own_half, da1 = lax.optimization_barrier((own_half, da1))
     other_half = swapped(own_half, other_core)

time: 33.7 us -> 34.9 us (1.036)
  Pallas kernels: 7.16 us -> 8.34 us
    pallas_call x14, Pallas kernels: 7.16 us -> 8.34 us  [local(): pl.pallas_call(kernel, in_specs=[pl.BlockSpec(memory_space=spaces[kind])...]
  transfers between devices with their start and end apart: 13 -> 13, of which waited for: 7 -> 6; matrix products, arithmetic and copies ran while one was open for 0% -> 0% of each run, Pallas kernels for 17% -> 20%
where the time goes in v12:
time: 34.9 us; the launch traced here: 34.7 us
  starting transfers between devices  15.7 us (45%)
  waiting for transfers between devices  9.86 us (28%)
  Pallas kernels  8.34 us (24%)
  between operations  0.77 us (2%)
    ppermute x13, starting transfers between devices, swapped(): return lax.ppermute(array, ('section', 'dp'), pairs)  15.7 us
    ppermute x13, waiting for transfers between devices, swapped(): return lax.ppermute(array, ('section', 'dp'), pairs)  9.86 us
    pallas_call x14, Pallas kernels, local(): pl.pallas_call(kernel, in_specs=[pl.BlockSpec(memory_space=spaces[kind])...  8.34 us
  transfers between devices with their start and end apart: 13, of which 6 were waited for; matrix products, arithmetic and copies ran while one was open for 0% of the time, Pallas kernels for 20%

profile of v12, /device:TPU:0, one launch (start us, length us, event | category | flops | bytes accessed | tf_op | source)
XLA Modules:
  0.0 34.7 jit_solution(6682882321202006536)
XLA Ops:
  0.6 0.8 %pick.1 = bf16[32,2048]{1,0:T(8,128)(2,1)S(1)} custom-call(s32[1]{0:T(128)} %bitcast.1.place_ref, s32[1]{0:T(128)} %bitcast.index_ref, bf16[1,2,32,4096]{3,2,1,0:T(8,128)(2,1)} %w_out.3), custom_call_target="tpu_custom_call" | custom-call | tf_op jit(solution)/shard_map/pick/pallas_call | solution.py:283
  1.5 3.0 %collective-permute-start = (bf16[32,2048]{1,0:T(8,128)(2,1)S(1)}, bf16[32,2048]{1,0:T(8,128)(2,1)S(1)}, u32[]{:S(2)}, u32[]{:S(2)}) collective-permute-start(bf16[32,2048]{1,0:T(8,128)(2,1)S(1)} %pick.1), channel_id=1, source_target_pairs={{0,16},{1,17},{2,18},{3,19},{4,20},{5,21},{6,22},{7,23},{8,24},{9,... | collective-permute-start | bytes 393224 | tf_op jit(solution)/shard_map/ppermute | solution.py:319
  4.5 2.0 %front.1 = (bf16[32,128]{1,0:T(8,128)(2,1)S(1)}, f32[2,32,128]{2,1,0:T(8,128)S(1)}, bf16[128,4096]{1,0:T(8,128)(2,1)S(1)}, bf16[128,4096]{1,0:T(8,128)(2,1)S(1)}...) custom-call(s32[1]{0:T(128)} %bitcast.1.place_ref, bf16[1,2,128,4096]{3,2,1,0:T(8,128)(2,1)} %saved.1, ...), custom_call_target="tpu_custom_call" | custom-call | tf_op jit(solution)/shard_map/front/pallas_call | solution.py:283
  6.5 0.1 collective-permute-start.1
  6.6 2.4 %upper.1 = (bf16[128,4096]{1,0:T(8,128)(2,1)S(1)}, bf16[32,128]{1,0:T(8,128)(2,1)S(1)}, bf16[32,128]{1,0:T(8,128)(2,1)S(1)}, bf16[32,128]{1,0:T(8,128)(2,1)S(1)}...) custom-call(s32[1]{0:T(128)} %bitcast.1.place_ref, bf16[128,4096]{1,0:T(8,128)(2,1)S(1)} %get-tuple-element.36.x, ...), custom_call_target="tpu_custom_call" | custom-call | tf_op jit(solution)/shard_map/upper/pallas_call | solution.py:283
  8.9 0.0 collective-permute-done.own_ref
  9.0 0.1 collective-permute-start.2
  9.0 0.7 %outgoing.1.flow_ref = bf16[128,4096]{1,0:T(8,128)(2,1)S(1)} custom-call(bf16[128,4096]{1,0:T(8,128)(2,1)S(1)} %get-tuple-element.36.x, bf16[128,4096]{1,0:T(8,128)(2,1)S(1)} %get-tuple-element.39.g, f32[1,4096]{1,0:T(1,128)S(1)} %get-tuple-element.37.gain, bf16[32,4096]{1,0:T(8,128)(2,1)S(1)} %get-tuple-element.38.wi, ...), custom_call_target="tpu_custom_call" | custom-call | flops 20000000000 | bytes 1048576 | tf_op jit(solution)/shard_map/outgoing/pallas_call | solution.py:283
  9.8 0.3 flow.1.part_ref
  10.1 0.3 collective-permute-done.2.other_ref
  10.4 0.3 flow_rest.1._
  10.7 2.1 %collective-permute-start.4 = (bf16[32,128]{1,0:T(8,128)(2,1)S(1)}, bf16[32,128]{1,0:T(8,128)(2,1)S(1)}, u32[]{:S(2)}, u32[]{:S(2)}) collective-permute-start(bf16[32,128]{1,0:T(8,128)(2,1)S(1)} %flow_rest.1._), channel_id=1, source_target_pairs={{0,16},{1,17},{2,18},{3,19},{4,20},{5,21},{6,22},{7,23},{8,24},{9,... | collective-permute-start | bytes 24584 | tf_op jit(solution)/shard_map/ppermute | solution.py:319
  12.7 0.4 %terms1.1 = (bf16[8,32,256]{2,1,0:T(8,128)(2,1)S(1)}, bf16[8,32,256]{2,1,0:T(8,128)(2,1)S(1)}, bf16[8,32,256]{2,1,0:T(8,128)(2,1)S(1)}, bf16[8,32,256]{2,1,0:T(8,128)(2,1)S(1)}) custom-call(s32[1]{0:T(128)} %bitcast.index_ref, bf16[128,4096]{1,0:T(8,128)(2,1)S(1)} %get-tuple-element.39.g, bf16[128,4096]{1,0:T(8,128)(2,1)S(1)} %get-tuple-element.44.xg_ref, ...), custom_call_target="tpu_custom_call" | custom-call | tf_op jit(solution)/shard_map/terms1/pallas_call | solution.py:283
  13.1 0.0 collective-permute-done.1.act0_ref
  13.1 0.3 terms.1
  13.4 0.1 collective-permute-start.3
  13.5 0.9 %collective-permute-done.4.got_ref = bf16[32,128]{1,0:T(8,128)(2,1)S(1)} collective-permute-done((bf16[32,128]{1,0:T(8,128)(2,1)S(1)}, bf16[32,128]{1,0:T(8,128)(2,1)S(1)}, u32[]{:S(2)}, u32[]{:S(2)}) %collective-permute-start.4) | collective-permute-done | bytes 8224 | tf_op jit(solution)/shard_map/ppermute | solution.py:319
  14.4 0.3 lower.1
  14.6 0.1 collective-permute-start.5
  14.7 0.5 %collective-permute-done.3.got = bf16[24,32,256]{2,1,0:T(8,128)(2,1)S(1)} collective-permute-done((bf16[24,32,256]{2,1,0:T(8,128)(2,1)S(1)}, bf16[24,32,256]{2,1,0:T(8,128)(2,1)S(1)}, u32[]{:S(2)}, u32[]{:S(2)}) %collective-permute-start.3) | collective-permute-done | bytes 393248 | tf_op jit(solution)/shard_map/ppermute | solution.py:319
  15.2 0.1 chip.1
  15.3 2.5 %collective-permute-start.6 = (bf16[4,32,256]{2,1,0:T(8,128)(2,1)S(1)}, bf16[4,32,256]{2,1,0:T(8,128)(2,1)S(1)}, u32[]{:S(2)}, u32[]{:S(2)}) collective-permute-start(bf16[4,32,256]{2,1,0:T(8,128)(2,1)S(1)} %get-tuple-element.60), channel_id=1, source_target_pairs={{0,18},{1,19},{2,16},{3,17},{4,22},{5,23},{6,20},{7,21},{8,26},{9,... | collective-permute-start | bytes 196616 | tf_op jit(solution)/shard_map/ppermute | solution.py:319
  17.9 0.0 collective-permute-done.5.got0
  17.9 0.1 plane.1
  18.0 0.6 %collective-permute-start.7 = (bf16[4,64,256]{2,1,0:T(8,128)(2,1)S(1)}, bf16[4,64,256]{2,1,0:T(8,128)(2,1)S(1)}, u32[]{:S(2)}, u32[]{:S(2)}) collective-permute-start(bf16[4,64,256]{2,1,0:T(8,128)(2,1)S(1)} %get-tuple-element.61), channel_id=1, source_target_pairs={{0,2},{1,17},{2,0},{3,19},{4,6},{5,21},{6,4},{7,23},{8,10},{9,25},... | collective-permute-start | bytes 393224 | tf_op jit(solution)/shard_map/ppermute | solution.py:319
  18.5 1.2 %collective-permute-start.9 = (bf16[4,64,256]{2,1,0:T(8,128)(2,1)S(1)}, bf16[4,64,256]{2,1,0:T(8,128)(2,1)S(1)}, u32[]{:S(2)}, u32[]{:S(2)}) collective-permute-start(bf16[4,64,256]{2,1,0:T(8,128)(2,1)S(1)} %get-tuple-element.63), channel_id=1, source_target_pairs={{0,16},{1,3},{2,18},{3,1},{4,20},{5,7},{6,22},{7,5},{8,24},{9,11},... | collective-permute-start | bytes 393224 | tf_op jit(solution)/shard_map/ppermute | solution.py:319
  19.7 1.8 %collective-permute-start.8 = (bf16[4,32,256]{2,1,0:T(8,128)(2,1)S(1)}, bf16[4,32,256]{2,1,0:T(8,128)(2,1)S(1)}, u32[]{:S(2)}, u32[]{:S(2)}) collective-permute-start(bf16[4,32,256]{2,1,0:T(8,128)(2,1)S(1)} %get-tuple-element.62), channel_id=1, source_target_pairs={{0,18},{1,19},{2,16},{3,17},{4,22},{5,23},{6,20},{7,21},{8,26},{9,... | collective-permute-start | bytes 196616 | tf_op jit(solution)/shard_map/ppermute | solution.py:319
  21.5 0.0 collective-permute-done.6.across_out
  21.5 4.0 %collective-permute-done.8.across_in = bf16[4,32,256]{2,1,0:T(8,128)(2,1)S(1)} collective-permute-done((bf16[4,32,256]{2,1,0:T(8,128)(2,1)S(1)}, bf16[4,32,256]{2,1,0:T(8,128)(2,1)S(1)}, u32[]{:S(2)}, u32[]{:S(2)}) %collective-permute-start.8) | collective-permute-done | bytes 65568 | tf_op jit(solution)/shard_map/ppermute | solution.py:319
  25.6 0.0 collective-permute-done.7.first
  25.6 0.0 collective-permute-done.9.second
  25.6 0.1 layer.1
  25.7 2.7 %collective-permute-start.10 = (bf16[64,256]{1,0:T(8,128)(2,1)S(1)}, bf16[64,256]{1,0:T(8,128)(2,1)S(1)}, u32[]{:S(2)}, u32[]{:S(2)}) collective-permute-start(bf16[64,256]{1,0:T(8,128)(2,1)S(1)} %get-tuple-element.65), channel_id=1, source_target_pairs={{0,8},{1,9},{2,10},{3,11},{4,12},{5,13},{6,14},{7,15},{8,0},{9,1},... | collective-permute-start | bytes 98312 | tf_op jit(solution)/shard_map/ppermute | solution.py:319
  28.3 1.3 %collective-permute-start.11 = (bf16[64,256]{1,0:T(8,128)(2,1)S(1)}, bf16[64,256]{1,0:T(8,128)(2,1)S(1)}, u32[]{:S(2)}, u32[]{:S(2)}) collective-permute-start(bf16[64,256]{1,0:T(8,128)(2,1)S(1)} %get-tuple-element.66), channel_id=1, source_target_pairs={{0,12},{1,13},{2,14},{3,15},{4,8},{5,9},{6,10},{7,11},{8,4},{9,5},... | collective-permute-start | bytes 98312 | tf_op jit(solution)/shard_map/ppermute | solution.py:319
  29.7 0.2 collective-permute-start.12
  29.9 0.9 %collective-permute-done.10.refs_1_ = bf16[64,256]{1,0:T(8,128)(2,1)S(1)} collective-permute-done((bf16[64,256]{1,0:T(8,128)(2,1)S(1)}, bf16[64,256]{1,0:T(8,128)(2,1)S(1)}, u32[]{:S(2)}, u32[]{:S(2)}) %collective-permute-start.10) | collective-permute-done | bytes 32800 | tf_op jit(solution)/shard_map/ppermute | solution.py:319
  30.8 3.2 %collective-permute-done.11.refs_2_ = bf16[64,256]{1,0:T(8,128)(2,1)S(1)} collective-permute-done((bf16[64,256]{1,0:T(8,128)(2,1)S(1)}, bf16[64,256]{1,0:T(8,128)(2,1)S(1)}, u32[]{:S(2)}, u32[]{:S(2)}) %collective-permute-start.11) | collective-permute-done | bytes 32800 | tf_op jit(solution)/shard_map/ppermute | solution.py:319
  34.0 0.0 collective-permute-done.12.refs_3_
  34.0 0.7 %total.1 = (f32[1,32,256]{2,1,0:T(8,128)}, f32[1,32,256]{2,1,0:T(8,128)}) custom-call(bf16[64,256]{1,0:T(8,128)(2,1)S(1)} %get-tuple-element.64.refs_0_, bf16[64,256]{1,0:T(8,128)(2,1)S(1)} %collective-permute-done.10.refs_1_, bf16[64,256]{1,0:T(8,128)(2,1)S(1)} %collective-permute-done.11.refs_2_, bf16[64,256]{1,0:T(8,128)(2,1)S(1)} %collective-permute-done.12.refs_3_), custom_call_target="tpu_custom_call" | custom-call | tf_op jit(solution)/shard_map/total/pallas_call | solution.py:283
  (1 shorter events, 0.0 us)
Async XLA Ops:
  1.5 7.5 %collective-permute-start = (bf16[32,2048]{1,0:T(8,128)(2,1)S(1)}, bf16[32,2048]{1,0:T(8,128)(2,1)S(1)}, u32[]{:S(2)}, u32[]{:S(2)}) collective-permute-start(bf16[32,2048]{1,0:T(8,128)(2,1)S(1)} %pick.1), channel_id=1, source_target_pairs={{0,16},{1,17},{2,18},{3,19},{4,20},{5,21},{6,22},{7,23},{8,24},{9,... | collective-permute-start | bytes 393224 | tf_op jit(solution)/shard_map/ppermute | solution.py:319
  6.5 6.7 %collective-permute-start.1 = (bf16[32,128]{1,0:T(8,128)(2,1)S(1)}, bf16[32,128]{1,0:T(8,128)(2,1)S(1)}, u32[]{:S(2)}, u32[]{:S(2)}) collective-permute-start(bf16[32,128]{1,0:T(8,128)(2,1)S(1)} %get-tuple-element.43), channel_id=1, source_target_pairs={{0,16},{1,17},{2,18},{3,19},{4,20},{5,21},{6,22},{7,23},{8,24},{9,... | collective-permute-start | bytes 24584 | tf_op jit(solution)/shard_map/ppermute | solution.py:319
  9.0 1.4 %collective-permute-start.2 = (bf16[32,2048]{1,0:T(8,128)(2,1)S(1)}, bf16[32,2048]{1,0:T(8,128)(2,1)S(1)}, u32[]{:S(2)}, u32[]{:S(2)}) collective-permute-start(bf16[32,2048]{1,0:T(8,128)(2,1)S(1)} %collective-permute-done.own_ref), channel_id=1, source_target_pairs={{0,1},{1,0},{2,3},{3,2},{4,5},{5,4},{6,7},{7,6},{8,9},{9,8},{10,11... | collective-permute-start | bytes 393224 | tf_op jit(solution)/shard_map/ppermute | solution.py:319
  10.7 3.7 %collective-permute-start.4 = (bf16[32,128]{1,0:T(8,128)(2,1)S(1)}, bf16[32,128]{1,0:T(8,128)(2,1)S(1)}, u32[]{:S(2)}, u32[]{:S(2)}) collective-permute-start(bf16[32,128]{1,0:T(8,128)(2,1)S(1)} %flow_rest.1._), channel_id=1, source_target_pairs={{0,16},{1,17},{2,18},{3,19},{4,20},{5,21},{6,22},{7,23},{8,24},{9,... | collective-permute-start | bytes 24584 | tf_op jit(solution)/shard_map/ppermute | solution.py:319
  13.4 1.8 %collective-permute-start.3 = (bf16[24,32,256]{2,1,0:T(8,128)(2,1)S(1)}, bf16[24,32,256]{2,1,0:T(8,128)(2,1)S(1)}, u32[]{:S(2)}, u32[]{:S(2)}) collective-permute-start(bf16[24,32,256]{2,1,0:T(8,128)(2,1)S(1)} %get-tuple-element.53), channel_id=1, source_target_pairs={{0,1},{1,0},{2,3},{3,2},{4,5},{5,4},{6,7},{7,6},{8,9},{9,8},{10,11... | collective-permute-start | bytes 1179656 | tf_op jit(solution)/shard_map/ppermute | solution.py:319
  14.6 3.2 %collective-permute-start.5 = (bf16[8,32,256]{2,1,0:T(8,128)(2,1)S(1)}, bf16[8,32,256]{2,1,0:T(8,128)(2,1)S(1)}, u32[]{:S(2)}, u32[]{:S(2)}) collective-permute-start(bf16[8,32,256]{2,1,0:T(8,128)(2,1)S(1)} %get-tuple-element.58), channel_id=1, source_target_pairs={{0,1},{1,0},{2,3},{3,2},{4,5},{5,4},{6,7},{7,6},{8,9},{9,8},{10,11... | collective-permute-start | bytes 393224 | tf_op jit(solution)/shard_map/ppermute | solution.py:319
  15.3 6.2 %collective-permute-start.6 = (bf16[4,32,256]{2,1,0:T(8,128)(2,1)S(1)}, bf16[4,32,256]{2,1,0:T(8,128)(2,1)S(1)}, u32[]{:S(2)}, u32[]{:S(2)}) collective-permute-start(bf16[4,32,256]{2,1,0:T(8,128)(2,1)S(1)} %get-tuple-element.60), channel_id=1, source_target_pairs={{0,18},{1,19},{2,16},{3,17},{4,22},{5,23},{6,20},{7,21},{8,26},{9,... | collective-permute-start | bytes 196616 | tf_op jit(solution)/shard_map/ppermute | solution.py:319
  18.0 7.6 %collective-permute-start.7 = (bf16[4,64,256]{2,1,0:T(8,128)(2,1)S(1)}, bf16[4,64,256]{2,1,0:T(8,128)(2,1)S(1)}, u32[]{:S(2)}, u32[]{:S(2)}) collective-permute-start(bf16[4,64,256]{2,1,0:T(8,128)(2,1)S(1)} %get-tuple-element.61), channel_id=1, source_target_pairs={{0,2},{1,17},{2,0},{3,19},{4,6},{5,21},{6,4},{7,23},{8,10},{9,25},... | collective-permute-start | bytes 393224 | tf_op jit(solution)/shard_map/ppermute | solution.py:319
  18.5 7.1 %collective-permute-start.9 = (bf16[4,64,256]{2,1,0:T(8,128)(2,1)S(1)}, bf16[4,64,256]{2,1,0:T(8,128)(2,1)S(1)}, u32[]{:S(2)}, u32[]{:S(2)}) collective-permute-start(bf16[4,64,256]{2,1,0:T(8,128)(2,1)S(1)} %get-tuple-element.63), channel_id=1, source_target_pairs={{0,16},{1,3},{2,18},{3,1},{4,20},{5,7},{6,22},{7,5},{8,24},{9,11},... | collective-permute-start | bytes 393224 | tf_op jit(solution)/shard_map/ppermute | solution.py:319
  19.7 5.9 %collective-permute-start.8 = (bf16[4,32,256]{2,1,0:T(8,128)(2,1)S(1)}, bf16[4,32,256]{2,1,0:T(8,128)(2,1)S(1)}, u32[]{:S(2)}, u32[]{:S(2)}) collective-permute-start(bf16[4,32,256]{2,1,0:T(8,128)(2,1)S(1)} %get-tuple-element.62), channel_id=1, source_target_pairs={{0,18},{1,19},{2,16},{3,17},{4,22},{5,23},{6,20},{7,21},{8,26},{9,... | collective-permute-start | bytes 196616 | tf_op jit(solution)/shard_map/ppermute | solution.py:319
  25.7 5.2 %collective-permute-start.10 = (bf16[64,256]{1,0:T(8,128)(2,1)S(1)}, bf16[64,256]{1,0:T(8,128)(2,1)S(1)}, u32[]{:S(2)}, u32[]{:S(2)}) collective-permute-start(bf16[64,256]{1,0:T(8,128)(2,1)S(1)} %get-tuple-element.65), channel_id=1, source_target_pairs={{0,8},{1,9},{2,10},{3,11},{4,12},{5,13},{6,14},{7,15},{8,0},{9,1},... | collective-permute-start | bytes 98312 | tf_op jit(solution)/shard_map/ppermute | solution.py:319
  28.3 5.7 %collective-permute-start.11 = (bf16[64,256]{1,0:T(8,128)(2,1)S(1)}, bf16[64,256]{1,0:T(8,128)(2,1)S(1)}, u32[]{:S(2)}, u32[]{:S(2)}) collective-permute-start(bf16[64,256]{1,0:T(8,128)(2,1)S(1)} %get-tuple-element.66), channel_id=1, source_target_pairs={{0,12},{1,13},{2,14},{3,15},{4,8},{5,9},{6,10},{7,11},{8,4},{9,5},... | collective-permute-start | bytes 98312 | tf_op jit(solution)/shard_map/ppermute | solution.py:319
  29.7 4.4 %collective-permute-start.12 = (bf16[64,256]{1,0:T(8,128)(2,1)S(1)}, bf16[64,256]{1,0:T(8,128)(2,1)S(1)}, u32[]{:S(2)}, u32[]{:S(2)}) collective-permute-start(bf16[64,256]{1,0:T(8,128)(2,1)S(1)} %get-tuple-element.67), channel_id=1, source_target_pairs={{0,4},{1,5},{2,6},{3,7},{4,0},{5,1},{6,2},{7,3},{8,12},{9,13},{10,... | collective-permute-start | bytes 98312 | tf_op jit(solution)/shard_map/ppermute | solution.py:319

commit v13 on v11

--- a/solution.py
+++ b/solution.py
@@ -245,11 +245,17 @@
         out_ref[i, rank : 2 * rank] = total.astype(BF16)
 
 
-def layer_kernel(index_ref, own, first, across_in, second, *out_refs):
+def layer_routes(layers):
+    if layers == 4:
+        return [[1, 3, 0, 2], [3, 2, 1, 0], [2, 0, 3, 1]]
+    return [[i ^ k for i in range(layers)] for k in range(1, layers)]
+
+
+def layer_kernel(routes, index_ref, own, first, across_in, second, *out_refs):
     rank = across_in.shape[1]
     layer = index_ref[0] // 4
-    for k, out_ref in enumerate(out_refs):
-        block = layer ^ k
+    for route, out_ref in zip([range(len(out_refs)), *routes], out_refs):
+        block = sum(jnp.where(layer == i, target, 0) for i, target in enumerate(route))
         total = sum(ref[block].astype(F32) for ref in (own, first, second))
         out_ref[0:rank] = (total[0:rank] + across_in[block].astype(F32)).astype(BF16)
         out_ref[rank : 2 * rank] = total[rank : 2 * rank].astype(BF16)
@@ -371,12 +377,23 @@
     across_in = swapped(across_in, (1, 2))
     second = swapped(second, (1, 0), (0, 2))
     own = local(add_kernel, "add", [double], *near(own, across_out), cost=MEDIUM)
+    routes = layer_routes(layers)
     mine, *others = local(
-        layer_kernel, "layer", [((2 * rank, share), BF16)] * layers,
+        partial(layer_kernel, routes), "layer", [((2 * rank, share), BF16)] * layers,
         index, *near(own, first, across_in, second),
     )
-    others = [swapped(other, (0, 4 * k)) for k, other in enumerate(others, 1)]
-    others = others[1:] + others[:1]
+    others = [
+        lax.ppermute(
+            other,
+            ("section", "dp"),
+            [
+                (s * count + d, s * count + 4 * route[d // 4] + d % 4)
+                for s in range(2)
+                for d in range(count)
+            ],
+        )
+        for route, other in zip(routes, others)
+    ]
     block = ((1, rank, share), F32)
     total_in, total_out = local(
         total_kernel, "total", [block, block], *near(mine, *others),

time: 33.7 us -> 33.3 us (0.988)
  waiting for transfers between devices: 10.1 us -> 8.29 us
  starting transfers between devices: 15.5 us -> 16.9 us
    ppermute x0 -> x3, starting transfers between devices: none -> 5.68 us  [pair_on_device(): lax.ppermute(other, ('section', 'dp'), [(s * count + d, s * count + 4 * r...]
    ppermute x13 -> x10, starting transfers between devices: 15.5 us -> 11.3 us  [swapped(): return lax.ppermute(array, ('section', 'dp'), pairs)]
    ppermute x13 -> x10, waiting for transfers between devices: 10.1 us -> 5.95 us  [swapped(): return lax.ppermute(array, ('section', 'dp'), pairs)]
    ppermute x0 -> x3, waiting for transfers between devices: none -> 2.34 us  [pair_on_device(): lax.ppermute(other, ('section', 'dp'), [(s * count + d, s * count + 4 * r...]
where the time goes in v13:
time: 33.3 us; the launch traced here: 33.1 us
  starting transfers between devices  16.9 us (51%)
  waiting for transfers between devices  8.29 us (25%)
  Pallas kernels  7.16 us (22%)
  between operations  0.76 us (2%)
    ppermute x10, starting transfers between devices, swapped(): return lax.ppermute(array, ('section', 'dp'), pairs)  11.3 us
    pallas_call x14, Pallas kernels, local(): pl.pallas_call(kernel, in_specs=[pl.BlockSpec(memory_space=spaces[kind])...  7.16 us
    ppermute x10, waiting for transfers between devices, swapped(): return lax.ppermute(array, ('section', 'dp'), pairs)  5.95 us
    ppermute x3, starting transfers between devices, pair_on_device(): lax.ppermute(other, ('section', 'dp'), [(s * count + d, s * count + 4 * r...  5.68 us
    ppermute x3, waiting for transfers between devices, pair_on_device(): lax.ppermute(other, ('section', 'dp'), [(s * count + d, s * count + 4 * r...  2.34 us
  transfers between devices with their start and end apart: 13, of which 7 were waited for; matrix products, arithmetic and copies ran while one was open for 0% of the time, Pallas kernels for 17%

profile of v13, /device:TPU:0, one launch (start us, length us, event | category | flops | bytes accessed | tf_op | source)
XLA Modules:
  0.0 33.1 jit_solution(4618921632046847969)
XLA Ops:
  0.6 0.8 %pick.1 = bf16[32,2048]{1,0:T(8,128)(2,1)S(1)} custom-call(s32[1]{0:T(128)} %bitcast.1.place_ref, s32[1]{0:T(128)} %bitcast.index_ref, bf16[1,2,32,4096]{3,2,1,0:T(8,128)(2,1)} %w_out.3), custom_call_target="tpu_custom_call" | custom-call | tf_op jit(solution)/shard_map/pick/pallas_call | solution.py:278
  1.5 3.0 %collective-permute-start = (bf16[32,2048]{1,0:T(8,128)(2,1)S(1)}, bf16[32,2048]{1,0:T(8,128)(2,1)S(1)}, u32[]{:S(2)}, u32[]{:S(2)}) collective-permute-start(bf16[32,2048]{1,0:T(8,128)(2,1)S(1)} %pick.1), channel_id=1, source_target_pairs={{0,16},{1,17},{2,18},{3,19},{4,20},{5,21},{6,22},{7,23},{8,24},{9,... | collective-permute-start | bytes 393224 | tf_op jit(solution)/shard_map/ppermute | solution.py:314
  4.5 2.2 %front.1 = (bf16[32,128]{1,0:T(8,128)(2,1)S(1)}, f32[2,32,128]{2,1,0:T(8,128)S(1)}, bf16[128,4096]{1,0:T(8,128)(2,1)S(1)}, bf16[128,4096]{1,0:T(8,128)(2,1)S(1)}...) custom-call(s32[1]{0:T(128)} %bitcast.1.place_ref, ...), custom_call_target="tpu_custom_call" | custom-call | tf_op jit(solution)/shard_map/front/pallas_call | solution.py:278
  6.7 0.1 collective-permute-start.1
  6.8 0.9 %upper.1 = (bf16[128,4096]{1,0:T(8,128)(2,1)S(1)}, bf16[32,128]{1,0:T(8,128)(2,1)S(1)}, bf16[32,128]{1,0:T(8,128)(2,1)S(1)}, bf16[32,128]{1,0:T(8,128)(2,1)S(1)}, f32[2,128,128]{2,1,0:T(8,128)S(1)}) custom-call(bf16[128,4096]{1,0:T(8,128)(2,1)S(1)} %get-tuple-element.37.x, bf16[128,4096]{1,0:T(8,128)(2,1)S(1)} %get-tuple-element.38.g, ...), custom_call_target="tpu_custom_call" | custom-call | tf_op jit(solution)/shard_map/upper/pallas_call | solution.py:278
  7.8 0.2 collective-permute-done.own_ref
  8.0 0.0 collective-permute-start.2
  8.0 0.7 %outgoing.1.flow_ref = bf16[128,4096]{1,0:T(8,128)(2,1)S(1)} custom-call(bf16[128,4096]{1,0:T(8,128)(2,1)S(1)} %get-tuple-element.37.x, bf16[128,4096]{1,0:T(8,128)(2,1)S(1)} %get-tuple-element.38.g, f32[1,4096]{1,0:T(1,128)S(1)} %get-tuple-element.39.gain, bf16[32,4096]{1,0:T(8,128)(2,1)S(1)} %get-tuple-element.40.wi, ...), custom_call_target="tpu_custom_call" | custom-call | flops 20000000000 | bytes 1048576 | tf_op jit(solution)/shard_map/outgoing/pallas_call | solution.py:278
  8.7 0.3 flow.1.part_ref
  9.0 0.3 collective-permute-done.2.other_ref
  9.3 0.3 flow_rest.1._
  9.6 1.9 %collective-permute-start.4 = (bf16[32,128]{1,0:T(8,128)(2,1)S(1)}, bf16[32,128]{1,0:T(8,128)(2,1)S(1)}, u32[]{:S(2)}, u32[]{:S(2)}) collective-permute-start(bf16[32,128]{1,0:T(8,128)(2,1)S(1)} %flow_rest.1._), channel_id=1, source_target_pairs={{0,16},{1,17},{2,18},{3,19},{4,20},{5,21},{6,22},{7,23},{8,24},{9,... | collective-permute-start | bytes 24584 | tf_op jit(solution)/shard_map/ppermute | solution.py:314
  11.5 0.4 %terms1.1 = (bf16[8,32,256]{2,1,0:T(8,128)(2,1)S(1)}, bf16[8,32,256]{2,1,0:T(8,128)(2,1)S(1)}, bf16[8,32,256]{2,1,0:T(8,128)(2,1)S(1)}, bf16[8,32,256]{2,1,0:T(8,128)(2,1)S(1)}) custom-call(s32[1]{0:T(128)} %bitcast.index_ref, bf16[128,4096]{1,0:T(8,128)(2,1)S(1)} %get-tuple-element.38.g, bf16[128,4096]{1,0:T(8,128)(2,1)S(1)} %get-tuple-element.46.xg_ref, ...), custom_call_target="tpu_custom_call" | custom-call | tf_op jit(solution)/shard_map/terms1/pallas_call | solution.py:278
  12.0 0.0 collective-permute-done.1.act0_ref
  12.0 0.3 terms.1
  12.3 0.1 collective-permute-start.3
  12.3 1.0 %collective-permute-done.4.got_ref = bf16[32,128]{1,0:T(8,128)(2,1)S(1)} collective-permute-done((bf16[32,128]{1,0:T(8,128)(2,1)S(1)}, bf16[32,128]{1,0:T(8,128)(2,1)S(1)}, u32[]{:S(2)}, u32[]{:S(2)}) %collective-permute-start.4) | collective-permute-done | bytes 8224 | tf_op jit(solution)/shard_map/ppermute | solution.py:314
  13.3 0.3 lower.1
  13.6 0.1 collective-permute-start.5
  13.7 0.3 %collective-permute-done.3.got = bf16[24,32,256]{2,1,0:T(8,128)(2,1)S(1)} collective-permute-done((bf16[24,32,256]{2,1,0:T(8,128)(2,1)S(1)}, bf16[24,32,256]{2,1,0:T(8,128)(2,1)S(1)}, u32[]{:S(2)}, u32[]{:S(2)}) %collective-permute-start.3) | collective-permute-done | bytes 393248 | tf_op jit(solution)/shard_map/ppermute | solution.py:314
  14.0 0.1 chip.1
  14.1 2.5 %collective-permute-start.6 = (bf16[4,32,256]{2,1,0:T(8,128)(2,1)S(1)}, bf16[4,32,256]{2,1,0:T(8,128)(2,1)S(1)}, u32[]{:S(2)}, u32[]{:S(2)}) collective-permute-start(bf16[4,32,256]{2,1,0:T(8,128)(2,1)S(1)} %get-tuple-element.62), channel_id=1, source_target_pairs={{0,18},{1,19},{2,16},{3,17},{4,22},{5,23},{6,20},{7,21},{8,26},{9,... | collective-permute-start | bytes 196616 | tf_op jit(solution)/shard_map/ppermute | solution.py:314
  16.7 0.0 collective-permute-done.5.got0
  16.7 0.1 plane.1
  16.8 0.6 %collective-permute-start.7 = (bf16[4,64,256]{2,1,0:T(8,128)(2,1)S(1)}, bf16[4,64,256]{2,1,0:T(8,128)(2,1)S(1)}, u32[]{:S(2)}, u32[]{:S(2)}) collective-permute-start(bf16[4,64,256]{2,1,0:T(8,128)(2,1)S(1)} %get-tuple-element.63), channel_id=1, source_target_pairs={{0,2},{1,17},{2,0},{3,19},{4,6},{5,21},{6,4},{7,23},{8,10},{9,25},... | collective-permute-start | bytes 393224 | tf_op jit(solution)/shard_map/ppermute | solution.py:314
  17.4 1.2 %collective-permute-start.9 = (bf16[4,64,256]{2,1,0:T(8,128)(2,1)S(1)}, bf16[4,64,256]{2,1,0:T(8,128)(2,1)S(1)}, u32[]{:S(2)}, u32[]{:S(2)}) collective-permute-start(bf16[4,64,256]{2,1,0:T(8,128)(2,1)S(1)} %get-tuple-element.65), channel_id=1, source_target_pairs={{0,16},{1,3},{2,18},{3,1},{4,20},{5,7},{6,22},{7,5},{8,24},{9,11},... | collective-permute-start | bytes 393224 | tf_op jit(solution)/shard_map/ppermute | solution.py:314
  18.5 1.8 %collective-permute-start.8 = (bf16[4,32,256]{2,1,0:T(8,128)(2,1)S(1)}, bf16[4,32,256]{2,1,0:T(8,128)(2,1)S(1)}, u32[]{:S(2)}, u32[]{:S(2)}) collective-permute-start(bf16[4,32,256]{2,1,0:T(8,128)(2,1)S(1)} %get-tuple-element.64), channel_id=1, source_target_pairs={{0,18},{1,19},{2,16},{3,17},{4,22},{5,23},{6,20},{7,21},{8,26},{9,... | collective-permute-start | bytes 196616 | tf_op jit(solution)/shard_map/ppermute | solution.py:314
  20.3 0.0 collective-permute-done.6.across_out
  20.4 4.0 %collective-permute-done.8.across_in = bf16[4,32,256]{2,1,0:T(8,128)(2,1)S(1)} collective-permute-done((bf16[4,32,256]{2,1,0:T(8,128)(2,1)S(1)}, bf16[4,32,256]{2,1,0:T(8,128)(2,1)S(1)}, u32[]{:S(2)}, u32[]{:S(2)}) %collective-permute-start.8) | collective-permute-done | bytes 65568 | tf_op jit(solution)/shard_map/ppermute | solution.py:314
  24.4 0.0 collective-permute-done.7.first
  24.4 0.0 collective-permute-done.9.second
  24.4 0.1 layer.1
  24.5 1.6 %collective-permute-start.10 = (bf16[64,256]{1,0:T(8,128)(2,1)S(1)}, bf16[64,256]{1,0:T(8,128)(2,1)S(1)}, u32[]{:S(2)}, u32[]{:S(2)}) collective-permute-start(bf16[64,256]{1,0:T(8,128)(2,1)S(1)} %get-tuple-element.67), channel_id=1, source_target_pairs={{0,4},{1,5},{2,6},{3,7},{4,12},{5,13},{6,14},{7,15},{8,0},{9,1},{1... | collective-permute-start | bytes 98312 | tf_op jit(solution)/shard_map/ppermute | solution.py:386
  26.1 2.5 %collective-permute-start.11 = (bf16[64,256]{1,0:T(8,128)(2,1)S(1)}, bf16[64,256]{1,0:T(8,128)(2,1)S(1)}, u32[]{:S(2)}, u32[]{:S(2)}) collective-permute-start(bf16[64,256]{1,0:T(8,128)(2,1)S(1)} %get-tuple-element.68), channel_id=1, source_target_pairs={{0,12},{1,13},{2,14},{3,15},{4,8},{5,9},{6,10},{7,11},{8,4},{9,5},... | collective-permute-start | bytes 98312 | tf_op jit(solution)/shard_map/ppermute | solution.py:386
  28.6 1.6 %collective-permute-start.12 = (bf16[64,256]{1,0:T(8,128)(2,1)S(1)}, bf16[64,256]{1,0:T(8,128)(2,1)S(1)}, u32[]{:S(2)}, u32[]{:S(2)}) collective-permute-start(bf16[64,256]{1,0:T(8,128)(2,1)S(1)} %get-tuple-element.69), channel_id=1, source_target_pairs={{0,8},{1,9},{2,10},{3,11},{4,0},{5,1},{6,2},{7,3},{8,12},{9,13},{1... | collective-permute-start | bytes 98312 | tf_op jit(solution)/shard_map/ppermute | solution.py:386
  30.2 0.0 collective-permute-done.10.refs_1_
  30.2 1.7 %collective-permute-done.11.refs_2_ = bf16[64,256]{1,0:T(8,128)(2,1)S(1)} collective-permute-done((bf16[64,256]{1,0:T(8,128)(2,1)S(1)}, bf16[64,256]{1,0:T(8,128)(2,1)S(1)}, u32[]{:S(2)}, u32[]{:S(2)}) %collective-permute-start.11) | collective-permute-done | bytes 32800 | tf_op jit(solution)/shard_map/ppermute | solution.py:386
  31.8 0.7 %collective-permute-done.12.refs_3_ = bf16[64,256]{1,0:T(8,128)(2,1)S(1)} collective-permute-done((bf16[64,256]{1,0:T(8,128)(2,1)S(1)}, bf16[64,256]{1,0:T(8,128)(2,1)S(1)}, u32[]{:S(2)}, u32[]{:S(2)}) %collective-permute-start.12) | collective-permute-done | bytes 32800 | tf_op jit(solution)/shard_map/ppermute | solution.py:386
  32.5 0.7 %total.1 = (f32[1,32,256]{2,1,0:T(8,128)}, f32[1,32,256]{2,1,0:T(8,128)}) custom-call(bf16[64,256]{1,0:T(8,128)(2,1)S(1)} %get-tuple-element.66.refs_0_, bf16[64,256]{1,0:T(8,128)(2,1)S(1)} %collective-permute-done.10.refs_1_, bf16[64,256]{1,0:T(8,128)(2,1)S(1)} %collective-permute-done.11.refs_2_, bf16[64,256]{1,0:T(8,128)(2,1)S(1)} %collective-permute-done.12.refs_3_), custom_call_target="tpu_custom_call" | custom-call | tf_op jit(solution)/shard_map/total/pallas_call | solution.py:278
  (1 shorter events, 0.0 us)
Async XLA Ops:
  1.5 6.5 %collective-permute-start = (bf16[32,2048]{1,0:T(8,128)(2,1)S(1)}, bf16[32,2048]{1,0:T(8,128)(2,1)S(1)}, u32[]{:S(2)}, u32[]{:S(2)}) collective-permute-start(bf16[32,2048]{1,0:T(8,128)(2,1)S(1)} %pick.1), channel_id=1, source_target_pairs={{0,16},{1,17},{2,18},{3,19},{4,20},{5,21},{6,22},{7,23},{8,24},{9,... | collective-permute-start | bytes 393224 | tf_op jit(solution)/shard_map/ppermute | solution.py:314
  6.7 5.2 %collective-permute-start.1 = (bf16[32,128]{1,0:T(8,128)(2,1)S(1)}, bf16[32,128]{1,0:T(8,128)(2,1)S(1)}, u32[]{:S(2)}, u32[]{:S(2)}) collective-permute-start(bf16[32,128]{1,0:T(8,128)(2,1)S(1)} %get-tuple-element.45), channel_id=1, source_target_pairs={{0,16},{1,17},{2,18},{3,19},{4,20},{5,21},{6,22},{7,23},{8,24},{9,... | collective-permute-start | bytes 24584 | tf_op jit(solution)/shard_map/ppermute | solution.py:314
  8.0 1.3 %collective-permute-start.2 = (bf16[32,2048]{1,0:T(8,128)(2,1)S(1)}, bf16[32,2048]{1,0:T(8,128)(2,1)S(1)}, u32[]{:S(2)}, u32[]{:S(2)}) collective-permute-start(bf16[32,2048]{1,0:T(8,128)(2,1)S(1)} %collective-permute-done.own_ref), channel_id=1, source_target_pairs={{0,1},{1,0},{2,3},{3,2},{4,5},{5,4},{6,7},{7,6},{8,9},{9,8},{10,11... | collective-permute-start | bytes 393224 | tf_op jit(solution)/shard_map/ppermute | solution.py:314
  9.6 3.7 %collective-permute-start.4 = (bf16[32,128]{1,0:T(8,128)(2,1)S(1)}, bf16[32,128]{1,0:T(8,128)(2,1)S(1)}, u32[]{:S(2)}, u32[]{:S(2)}) collective-permute-start(bf16[32,128]{1,0:T(8,128)(2,1)S(1)} %flow_rest.1._), channel_id=1, source_target_pairs={{0,16},{1,17},{2,18},{3,19},{4,20},{5,21},{6,22},{7,23},{8,24},{9,... | collective-permute-start | bytes 24584 | tf_op jit(solution)/shard_map/ppermute | solution.py:314
  12.3 1.8 %collective-permute-start.3 = (bf16[24,32,256]{2,1,0:T(8,128)(2,1)S(1)}, bf16[24,32,256]{2,1,0:T(8,128)(2,1)S(1)}, u32[]{:S(2)}, u32[]{:S(2)}) collective-permute-start(bf16[24,32,256]{2,1,0:T(8,128)(2,1)S(1)} %get-tuple-element.55), channel_id=1, source_target_pairs={{0,1},{1,0},{2,3},{3,2},{4,5},{5,4},{6,7},{7,6},{8,9},{9,8},{10,11... | collective-permute-start | bytes 1179656 | tf_op jit(solution)/shard_map/ppermute | solution.py:314
  13.6 3.1 %collective-permute-start.5 = (bf16[8,32,256]{2,1,0:T(8,128)(2,1)S(1)}, bf16[8,32,256]{2,1,0:T(8,128)(2,1)S(1)}, u32[]{:S(2)}, u32[]{:S(2)}) collective-permute-start(bf16[8,32,256]{2,1,0:T(8,128)(2,1)S(1)} %get-tuple-element.60), channel_id=1, source_target_pairs={{0,1},{1,0},{2,3},{3,2},{4,5},{5,4},{6,7},{7,6},{8,9},{9,8},{10,11... | collective-permute-start | bytes 393224 | tf_op jit(solution)/shard_map/ppermute | solution.py:314
  14.1 6.2 %collective-permute-start.6 = (bf16[4,32,256]{2,1,0:T(8,128)(2,1)S(1)}, bf16[4,32,256]{2,1,0:T(8,128)(2,1)S(1)}, u32[]{:S(2)}, u32[]{:S(2)}) collective-permute-start(bf16[4,32,256]{2,1,0:T(8,128)(2,1)S(1)} %get-tuple-element.62), channel_id=1, source_target_pairs={{0,18},{1,19},{2,16},{3,17},{4,22},{5,23},{6,20},{7,21},{8,26},{9,... | collective-permute-start | bytes 196616 | tf_op jit(solution)/shard_map/ppermute | solution.py:314
  16.8 7.6 %collective-permute-start.7 = (bf16[4,64,256]{2,1,0:T(8,128)(2,1)S(1)}, bf16[4,64,256]{2,1,0:T(8,128)(2,1)S(1)}, u32[]{:S(2)}, u32[]{:S(2)}) collective-permute-start(bf16[4,64,256]{2,1,0:T(8,128)(2,1)S(1)} %get-tuple-element.63), channel_id=1, source_target_pairs={{0,2},{1,17},{2,0},{3,19},{4,6},{5,21},{6,4},{7,23},{8,10},{9,25},... | collective-permute-start | bytes 393224 | tf_op jit(solution)/shard_map/ppermute | solution.py:314
  17.4 7.1 %collective-permute-start.9 = (bf16[4,64,256]{2,1,0:T(8,128)(2,1)S(1)}, bf16[4,64,256]{2,1,0:T(8,128)(2,1)S(1)}, u32[]{:S(2)}, u32[]{:S(2)}) collective-permute-start(bf16[4,64,256]{2,1,0:T(8,128)(2,1)S(1)} %get-tuple-element.65), channel_id=1, source_target_pairs={{0,16},{1,3},{2,18},{3,1},{4,20},{5,7},{6,22},{7,5},{8,24},{9,11},... | collective-permute-start | bytes 393224 | tf_op jit(solution)/shard_map/ppermute | solution.py:314
  18.5 5.9 %collective-permute-start.8 = (bf16[4,32,256]{2,1,0:T(8,128)(2,1)S(1)}, bf16[4,32,256]{2,1,0:T(8,128)(2,1)S(1)}, u32[]{:S(2)}, u32[]{:S(2)}) collective-permute-start(bf16[4,32,256]{2,1,0:T(8,128)(2,1)S(1)} %get-tuple-element.64), channel_id=1, source_target_pairs={{0,18},{1,19},{2,16},{3,17},{4,22},{5,23},{6,20},{7,21},{8,26},{9,... | collective-permute-start | bytes 196616 | tf_op jit(solution)/shard_map/ppermute | solution.py:314
  24.5 5.7 %collective-permute-start.10 = (bf16[64,256]{1,0:T(8,128)(2,1)S(1)}, bf16[64,256]{1,0:T(8,128)(2,1)S(1)}, u32[]{:S(2)}, u32[]{:S(2)}) collective-permute-start(bf16[64,256]{1,0:T(8,128)(2,1)S(1)} %get-tuple-element.67), channel_id=1, source_target_pairs={{0,4},{1,5},{2,6},{3,7},{4,12},{5,13},{6,14},{7,15},{8,0},{9,1},{1... | collective-permute-start | bytes 98312 | tf_op jit(solution)/shard_map/ppermute | solution.py:386
  26.1 5.7 %collective-permute-start.11 = (bf16[64,256]{1,0:T(8,128)(2,1)S(1)}, bf16[64,256]{1,0:T(8,128)(2,1)S(1)}, u32[]{:S(2)}, u32[]{:S(2)}) collective-permute-start(bf16[64,256]{1,0:T(8,128)(2,1)S(1)} %get-tuple-element.68), channel_id=1, source_target_pairs={{0,12},{1,13},{2,14},{3,15},{4,8},{5,9},{6,10},{7,11},{8,4},{9,5},... | collective-permute-start | bytes 98312 | tf_op jit(solution)/shard_map/ppermute | solution.py:386
  28.6 3.9 %collective-permute-start.12 = (bf16[64,256]{1,0:T(8,128)(2,1)S(1)}, bf16[64,256]{1,0:T(8,128)(2,1)S(1)}, u32[]{:S(2)}, u32[]{:S(2)}) collective-permute-start(bf16[64,256]{1,0:T(8,128)(2,1)S(1)} %get-tuple-element.69), channel_id=1, source_target_pairs={{0,8},{1,9},{2,10},{3,11},{4,0},{5,1},{6,2},{7,3},{8,12},{9,13},{1... | collective-permute-start | bytes 98312 | tf_op jit(solution)/shard_map/ppermute | solution.py:386

commit v14 on v13

--- a/solution.py
+++ b/solution.py
@@ -205,6 +205,10 @@
         across[i] = sum_ref[first + 2 * i]
 
 
+def x_first(section, index):
+    return (index % 2 == 0) | (section == (index // 2) % 2)
+
+
 def plane_kernel(
     place_ref, index_ref, sums, keep0, got0, own_ref, first_ref, second_ref, across
 ):
@@ -230,9 +234,10 @@
                 to_ref[i, 0:rank] = terms_in(section, block)
                 to_ref[i, rank : 2 * rank] = sums[section * chips + block]
 
+    along_x = x_first(place_ref[0], index_ref[0])
     for place in range(2):
-        for core, ways in ((0, (second_ref, first_ref)), (1, (first_ref, second_ref))):
-            pl.when((place_ref[0] == place) & (index_ref[0] % 2 == core))(
+        for x_is_first, ways in ((True, (first_ref, second_ref)), (False, (second_ref, first_ref))):
+            pl.when((place_ref[0] == place) & (along_x == x_is_first))(
                 partial(order, place, *ways)
             )
 
@@ -305,13 +310,19 @@
         for a in (saved, top_grad, gains, jnp.swapaxes(adapter_in, 2, 3), adapter_out)
     ]
 
-    def swapped(array, *ways):
+    def swapped(array, way):
         pairs = []
         for s in range(2):
             for d in range(count):
-                over_section, bits = ways[d % len(ways)]
+                over_section, bits = way(s, d) if callable(way) else way
                 pairs.append((s * count + d, (s ^ over_section) * count + (d ^ bits)))
         return lax.ppermute(array, ("section", "dp"), pairs)
+
+    def first_way(s, d):
+        return (1, 0) if x_first(s, d) else (0, 2)
+
+    def second_way(s, d):
+        return (0, 2) if x_first(s, d) else (1, 0)
 
     sems = pltpu.SemaphoreType.DMA
     wide = ((tokens, width), BF16)
@@ -373,9 +384,9 @@
         plane_kernel, "plane", [double, double, double, quarter],
         place, index, *near(sums, keep0, got0),
     )
-    first = swapped(first, (0, 2), (1, 0))
+    first = swapped(first, first_way)
     across_in = swapped(across_in, (1, 2))
-    second = swapped(second, (1, 0), (0, 2))
+    second = swapped(second, second_way)
     own = local(add_kernel, "add", [double], *near(own, across_out), cost=MEDIUM)
     routes = layer_routes(layers)
     mine, *others = local(

time: 33.3 us -> 32.8 us (0.985)
  waiting for transfers between devices: 8.29 us -> 7.74 us
    ppermute x10, waiting for transfers between devices: 5.95 us -> 5.4 us  [swapped(): return lax.ppermute(array, ('section', 'dp'), pairs)]
where the time goes in v14:
time: 32.8 us; the launch traced here: 32.6 us
  starting transfers between devices  17 us (52%)
  waiting for transfers between devices  7.74 us (24%)
  Pallas kernels  7.15 us (22%)
  between operations  0.76 us (2%)
    ppermute x10, starting transfers between devices, swapped(): return lax.ppermute(array, ('section', 'dp'), pairs)  11.2 us
    pallas_call x14, Pallas kernels, local(): pl.pallas_call(kernel, in_specs=[pl.BlockSpec(memory_space=spaces[kind])...  7.15 us
    ppermute x3, starting transfers between devices, pair_on_device(): lax.ppermute(other, ('section', 'dp'), [(s * count + d, s * count + 4 * r...  5.74 us
    ppermute x10, waiting for transfers between devices, swapped(): return lax.ppermute(array, ('section', 'dp'), pairs)  5.4 us
    ppermute x3, waiting for transfers between devices, pair_on_device(): lax.ppermute(other, ('section', 'dp'), [(s * count + d, s * count + 4 * r...  2.34 us
  transfers between devices with their start and end apart: 13, of which 7 were waited for; matrix products, arithmetic and copies ran while one was open for 0% of the time, Pallas kernels for 17%

profile of v14, /device:TPU:0, one launch (start us, length us, event | category | flops | bytes accessed | tf_op | source)
XLA Modules:
  0.0 32.6 jit_solution(11567417205405288207)
XLA Ops:
  0.6 0.8 %pick.1 = bf16[32,2048]{1,0:T(8,128)(2,1)S(1)} custom-call(s32[1]{0:T(128)} %bitcast.1.place_ref, s32[1]{0:T(128)} %bitcast.index_ref, bf16[1,2,32,4096]{3,2,1,0:T(8,128)(2,1)} %w_out.3), custom_call_target="tpu_custom_call" | custom-call | tf_op jit(solution)/shard_map/pick/pallas_call | solution.py:283
  1.5 3.0 %collective-permute-start = (bf16[32,2048]{1,0:T(8,128)(2,1)S(1)}, bf16[32,2048]{1,0:T(8,128)(2,1)S(1)}, u32[]{:S(2)}, u32[]{:S(2)}) collective-permute-start(bf16[32,2048]{1,0:T(8,128)(2,1)S(1)} %pick.1), channel_id=1, source_target_pairs={{0,16},{1,17},{2,18},{3,19},{4,20},{5,21},{6,22},{7,23},{8,24},{9,... | collective-permute-start | bytes 393224 | tf_op jit(solution)/shard_map/ppermute | solution.py:319
  4.5 2.2 %front.1 = (bf16[32,128]{1,0:T(8,128)(2,1)S(1)}, f32[2,32,128]{2,1,0:T(8,128)S(1)}, bf16[128,4096]{1,0:T(8,128)(2,1)S(1)}, bf16[128,4096]{1,0:T(8,128)(2,1)S(1)}...) custom-call(s32[1]{0:T(128)} %bitcast.1.place_ref, ...), custom_call_target="tpu_custom_call" | custom-call | tf_op jit(solution)/shard_map/front/pallas_call | solution.py:283
  6.7 0.1 collective-permute-start.1
  6.8 0.9 %upper.1 = (bf16[128,4096]{1,0:T(8,128)(2,1)S(1)}, bf16[32,128]{1,0:T(8,128)(2,1)S(1)}, bf16[32,128]{1,0:T(8,128)(2,1)S(1)}, bf16[32,128]{1,0:T(8,128)(2,1)S(1)}, f32[2,128,128]{2,1,0:T(8,128)S(1)}) custom-call(bf16[128,4096]{1,0:T(8,128)(2,1)S(1)} %get-tuple-element.37.x, bf16[128,4096]{1,0:T(8,128)(2,1)S(1)} %get-tuple-element.38.g, ...), custom_call_target="tpu_custom_call" | custom-call | tf_op jit(solution)/shard_map/upper/pallas_call | solution.py:283
  7.8 0.2 collective-permute-done.own_ref
  8.0 0.0 collective-permute-start.2
  8.0 0.7 %outgoing.1.flow_ref = bf16[128,4096]{1,0:T(8,128)(2,1)S(1)} custom-call(bf16[128,4096]{1,0:T(8,128)(2,1)S(1)} %get-tuple-element.37.x, bf16[128,4096]{1,0:T(8,128)(2,1)S(1)} %get-tuple-element.38.g, f32[1,4096]{1,0:T(1,128)S(1)} %get-tuple-element.39.gain, bf16[32,4096]{1,0:T(8,128)(2,1)S(1)} %get-tuple-element.40.wi, ...), custom_call_target="tpu_custom_call" | custom-call | flops 20000000000 | bytes 1048576 | tf_op jit(solution)/shard_map/outgoing/pallas_call | solution.py:283
  8.7 0.3 flow.1.part_ref
  9.0 0.3 collective-permute-done.2.other_ref
  9.3 0.3 flow_rest.1._
  9.6 1.9 %collective-permute-start.4 = (bf16[32,128]{1,0:T(8,128)(2,1)S(1)}, bf16[32,128]{1,0:T(8,128)(2,1)S(1)}, u32[]{:S(2)}, u32[]{:S(2)}) collective-permute-start(bf16[32,128]{1,0:T(8,128)(2,1)S(1)} %flow_rest.1._), channel_id=1, source_target_pairs={{0,16},{1,17},{2,18},{3,19},{4,20},{5,21},{6,22},{7,23},{8,24},{9,... | collective-permute-start | bytes 24584 | tf_op jit(solution)/shard_map/ppermute | solution.py:319
  11.5 0.4 %terms1.1 = (bf16[8,32,256]{2,1,0:T(8,128)(2,1)S(1)}, bf16[8,32,256]{2,1,0:T(8,128)(2,1)S(1)}, bf16[8,32,256]{2,1,0:T(8,128)(2,1)S(1)}, bf16[8,32,256]{2,1,0:T(8,128)(2,1)S(1)}) custom-call(s32[1]{0:T(128)} %bitcast.index_ref, bf16[128,4096]{1,0:T(8,128)(2,1)S(1)} %get-tuple-element.38.g, bf16[128,4096]{1,0:T(8,128)(2,1)S(1)} %get-tuple-element.46.xg_ref, ...), custom_call_target="tpu_custom_call" | custom-call | tf_op jit(solution)/shard_map/terms1/pallas_call | solution.py:283
  12.0 0.0 collective-permute-done.1.act0_ref
  12.0 0.3 terms.1
  12.3 0.1 collective-permute-start.3
  12.3 1.0 %collective-permute-done.4.got_ref = bf16[32,128]{1,0:T(8,128)(2,1)S(1)} collective-permute-done((bf16[32,128]{1,0:T(8,128)(2,1)S(1)}, bf16[32,128]{1,0:T(8,128)(2,1)S(1)}, u32[]{:S(2)}, u32[]{:S(2)}) %collective-permute-start.4) | collective-permute-done | bytes 8224 | tf_op jit(solution)/shard_map/ppermute | solution.py:319
  13.3 0.3 lower.1
  13.6 0.1 collective-permute-start.5
  13.7 0.3 %collective-permute-done.3.got = bf16[24,32,256]{2,1,0:T(8,128)(2,1)S(1)} collective-permute-done((bf16[24,32,256]{2,1,0:T(8,128)(2,1)S(1)}, bf16[24,32,256]{2,1,0:T(8,128)(2,1)S(1)}, u32[]{:S(2)}, u32[]{:S(2)}) %collective-permute-start.3) | collective-permute-done | bytes 393248 | tf_op jit(solution)/shard_map/ppermute | solution.py:319
  14.0 0.1 chip.1
  14.1 2.5 %collective-permute-start.6 = (bf16[4,32,256]{2,1,0:T(8,128)(2,1)S(1)}, bf16[4,32,256]{2,1,0:T(8,128)(2,1)S(1)}, u32[]{:S(2)}, u32[]{:S(2)}) collective-permute-start(bf16[4,32,256]{2,1,0:T(8,128)(2,1)S(1)} %get-tuple-element.62), channel_id=1, source_target_pairs={{0,18},{1,19},{2,16},{3,17},{4,22},{5,23},{6,20},{7,21},{8,26},{9,... | collective-permute-start | bytes 196616 | tf_op jit(solution)/shard_map/ppermute | solution.py:319
  16.7 0.0 collective-permute-done.5.got0
  16.7 0.1 plane.1
  16.8 0.6 %collective-permute-start.7 = (bf16[4,64,256]{2,1,0:T(8,128)(2,1)S(1)}, bf16[4,64,256]{2,1,0:T(8,128)(2,1)S(1)}, u32[]{:S(2)}, u32[]{:S(2)}) collective-permute-start(bf16[4,64,256]{2,1,0:T(8,128)(2,1)S(1)} %get-tuple-element.63), channel_id=1, source_target_pairs={{0,16},{1,17},{2,18},{3,1},{4,20},{5,21},{6,22},{7,5},{8,24},{9,25... | collective-permute-start | bytes 393224 | tf_op jit(solution)/shard_map/ppermute | solution.py:319
  17.3 1.2 %collective-permute-start.9 = (bf16[4,64,256]{2,1,0:T(8,128)(2,1)S(1)}, bf16[4,64,256]{2,1,0:T(8,128)(2,1)S(1)}, u32[]{:S(2)}, u32[]{:S(2)}) collective-permute-start(bf16[4,64,256]{2,1,0:T(8,128)(2,1)S(1)} %get-tuple-element.65), channel_id=1, source_target_pairs={{0,2},{1,3},{2,0},{3,19},{4,6},{5,7},{6,4},{7,23},{8,10},{9,11},{1... | collective-permute-start | bytes 393224 | tf_op jit(solution)/shard_map/ppermute | solution.py:319
  18.5 1.8 %collective-permute-start.8 = (bf16[4,32,256]{2,1,0:T(8,128)(2,1)S(1)}, bf16[4,32,256]{2,1,0:T(8,128)(2,1)S(1)}, u32[]{:S(2)}, u32[]{:S(2)}) collective-permute-start(bf16[4,32,256]{2,1,0:T(8,128)(2,1)S(1)} %get-tuple-element.64), channel_id=1, source_target_pairs={{0,18},{1,19},{2,16},{3,17},{4,22},{5,23},{6,20},{7,21},{8,26},{9,... | collective-permute-start | bytes 196616 | tf_op jit(solution)/shard_map/ppermute | solution.py:319
  20.3 0.0 collective-permute-done.6.across_out
  20.3 3.5 %collective-permute-done.8.across_in = bf16[4,32,256]{2,1,0:T(8,128)(2,1)S(1)} collective-permute-done((bf16[4,32,256]{2,1,0:T(8,128)(2,1)S(1)}, bf16[4,32,256]{2,1,0:T(8,128)(2,1)S(1)}, u32[]{:S(2)}, u32[]{:S(2)}) %collective-permute-start.8) | collective-permute-done | bytes 65568 | tf_op jit(solution)/shard_map/ppermute | solution.py:319
  23.8 0.0 collective-permute-done.7.first
  23.8 0.0 collective-permute-done.9.second
  23.8 0.1 layer.1
  23.9 1.7 %collective-permute-start.10 = (bf16[64,256]{1,0:T(8,128)(2,1)S(1)}, bf16[64,256]{1,0:T(8,128)(2,1)S(1)}, u32[]{:S(2)}, u32[]{:S(2)}) collective-permute-start(bf16[64,256]{1,0:T(8,128)(2,1)S(1)} %get-tuple-element.67), channel_id=1, source_target_pairs={{0,4},{1,5},{2,6},{3,7},{4,12},{5,13},{6,14},{7,15},{8,0},{9,1},{1... | collective-permute-start | bytes 98312 | tf_op jit(solution)/shard_map/ppermute | solution.py:397
  25.6 2.5 %collective-permute-start.11 = (bf16[64,256]{1,0:T(8,128)(2,1)S(1)}, bf16[64,256]{1,0:T(8,128)(2,1)S(1)}, u32[]{:S(2)}, u32[]{:S(2)}) collective-permute-start(bf16[64,256]{1,0:T(8,128)(2,1)S(1)} %get-tuple-element.68), channel_id=1, source_target_pairs={{0,12},{1,13},{2,14},{3,15},{4,8},{5,9},{6,10},{7,11},{8,4},{9,5},... | collective-permute-start | bytes 98312 | tf_op jit(solution)/shard_map/ppermute | solution.py:397
  28.1 1.6 %collective-permute-start.12 = (bf16[64,256]{1,0:T(8,128)(2,1)S(1)}, bf16[64,256]{1,0:T(8,128)(2,1)S(1)}, u32[]{:S(2)}, u32[]{:S(2)}) collective-permute-start(bf16[64,256]{1,0:T(8,128)(2,1)S(1)} %get-tuple-element.69), channel_id=1, source_target_pairs={{0,8},{1,9},{2,10},{3,11},{4,0},{5,1},{6,2},{7,3},{8,12},{9,13},{1... | collective-permute-start | bytes 98312 | tf_op jit(solution)/shard_map/ppermute | solution.py:397
  29.6 0.0 collective-permute-done.10.refs_1_
  29.6 1.7 %collective-permute-done.11.refs_2_ = bf16[64,256]{1,0:T(8,128)(2,1)S(1)} collective-permute-done((bf16[64,256]{1,0:T(8,128)(2,1)S(1)}, bf16[64,256]{1,0:T(8,128)(2,1)S(1)}, u32[]{:S(2)}, u32[]{:S(2)}) %collective-permute-start.11) | collective-permute-done | bytes 32800 | tf_op jit(solution)/shard_map/ppermute | solution.py:397
  31.3 0.7 %collective-permute-done.12.refs_3_ = bf16[64,256]{1,0:T(8,128)(2,1)S(1)} collective-permute-done((bf16[64,256]{1,0:T(8,128)(2,1)S(1)}, bf16[64,256]{1,0:T(8,128)(2,1)S(1)}, u32[]{:S(2)}, u32[]{:S(2)}) %collective-permute-start.12) | collective-permute-done | bytes 32800 | tf_op jit(solution)/shard_map/ppermute | solution.py:397
  32.0 0.7 %total.1 = (f32[1,32,256]{2,1,0:T(8,128)}, f32[1,32,256]{2,1,0:T(8,128)}) custom-call(bf16[64,256]{1,0:T(8,128)(2,1)S(1)} %get-tuple-element.66.refs_0_, bf16[64,256]{1,0:T(8,128)(2,1)S(1)} %collective-permute-done.10.refs_1_, bf16[64,256]{1,0:T(8,128)(2,1)S(1)} %collective-permute-done.11.refs_2_, bf16[64,256]{1,0:T(8,128)(2,1)S(1)} %collective-permute-done.12.refs_3_), custom_call_target="tpu_custom_call" | custom-call | tf_op jit(solution)/shard_map/total/pallas_call | solution.py:283
  (1 shorter events, 0.0 us)
Async XLA Ops:
  1.5 6.5 %collective-permute-start = (bf16[32,2048]{1,0:T(8,128)(2,1)S(1)}, bf16[32,2048]{1,0:T(8,128)(2,1)S(1)}, u32[]{:S(2)}, u32[]{:S(2)}) collective-permute-start(bf16[32,2048]{1,0:T(8,128)(2,1)S(1)} %pick.1), channel_id=1, source_target_pairs={{0,16},{1,17},{2,18},{3,19},{4,20},{5,21},{6,22},{7,23},{8,24},{9,... | collective-permute-start | bytes 393224 | tf_op jit(solution)/shard_map/ppermute | solution.py:319
  6.7 5.2 %collective-permute-start.1 = (bf16[32,128]{1,0:T(8,128)(2,1)S(1)}, bf16[32,128]{1,0:T(8,128)(2,1)S(1)}, u32[]{:S(2)}, u32[]{:S(2)}) collective-permute-start(bf16[32,128]{1,0:T(8,128)(2,1)S(1)} %get-tuple-element.45), channel_id=1, source_target_pairs={{0,16},{1,17},{2,18},{3,19},{4,20},{5,21},{6,22},{7,23},{8,24},{9,... | collective-permute-start | bytes 24584 | tf_op jit(solution)/shard_map/ppermute | solution.py:319
  8.0 1.3 %collective-permute-start.2 = (bf16[32,2048]{1,0:T(8,128)(2,1)S(1)}, bf16[32,2048]{1,0:T(8,128)(2,1)S(1)}, u32[]{:S(2)}, u32[]{:S(2)}) collective-permute-start(bf16[32,2048]{1,0:T(8,128)(2,1)S(1)} %collective-permute-done.own_ref), channel_id=1, source_target_pairs={{0,1},{1,0},{2,3},{3,2},{4,5},{5,4},{6,7},{7,6},{8,9},{9,8},{10,11... | collective-permute-start | bytes 393224 | tf_op jit(solution)/shard_map/ppermute | solution.py:319
  9.6 3.7 %collective-permute-start.4 = (bf16[32,128]{1,0:T(8,128)(2,1)S(1)}, bf16[32,128]{1,0:T(8,128)(2,1)S(1)}, u32[]{:S(2)}, u32[]{:S(2)}) collective-permute-start(bf16[32,128]{1,0:T(8,128)(2,1)S(1)} %flow_rest.1._), channel_id=1, source_target_pairs={{0,16},{1,17},{2,18},{3,19},{4,20},{5,21},{6,22},{7,23},{8,24},{9,... | collective-permute-start | bytes 24584 | tf_op jit(solution)/shard_map/ppermute | solution.py:319
  12.3 1.8 %collective-permute-start.3 = (bf16[24,32,256]{2,1,0:T(8,128)(2,1)S(1)}, bf16[24,32,256]{2,1,0:T(8,128)(2,1)S(1)}, u32[]{:S(2)}, u32[]{:S(2)}) collective-permute-start(bf16[24,32,256]{2,1,0:T(8,128)(2,1)S(1)} %get-tuple-element.55), channel_id=1, source_target_pairs={{0,1},{1,0},{2,3},{3,2},{4,5},{5,4},{6,7},{7,6},{8,9},{9,8},{10,11... | collective-permute-start | bytes 1179656 | tf_op jit(solution)/shard_map/ppermute | solution.py:319
  13.6 3.1 %collective-permute-start.5 = (bf16[8,32,256]{2,1,0:T(8,128)(2,1)S(1)}, bf16[8,32,256]{2,1,0:T(8,128)(2,1)S(1)}, u32[]{:S(2)}, u32[]{:S(2)}) collective-permute-start(bf16[8,32,256]{2,1,0:T(8,128)(2,1)S(1)} %get-tuple-element.60), channel_id=1, source_target_pairs={{0,1},{1,0},{2,3},{3,2},{4,5},{5,4},{6,7},{7,6},{8,9},{9,8},{10,11... | collective-permute-start | bytes 393224 | tf_op jit(solution)/shard_map/ppermute | solution.py:319
  14.1 6.2 %collective-permute-start.6 = (bf16[4,32,256]{2,1,0:T(8,128)(2,1)S(1)}, bf16[4,32,256]{2,1,0:T(8,128)(2,1)S(1)}, u32[]{:S(2)}, u32[]{:S(2)}) collective-permute-start(bf16[4,32,256]{2,1,0:T(8,128)(2,1)S(1)} %get-tuple-element.62), channel_id=1, source_target_pairs={{0,18},{1,19},{2,16},{3,17},{4,22},{5,23},{6,20},{7,21},{8,26},{9,... | collective-permute-start | bytes 196616 | tf_op jit(solution)/shard_map/ppermute | solution.py:319
  16.8 7.1 %collective-permute-start.7 = (bf16[4,64,256]{2,1,0:T(8,128)(2,1)S(1)}, bf16[4,64,256]{2,1,0:T(8,128)(2,1)S(1)}, u32[]{:S(2)}, u32[]{:S(2)}) collective-permute-start(bf16[4,64,256]{2,1,0:T(8,128)(2,1)S(1)} %get-tuple-element.63), channel_id=1, source_target_pairs={{0,16},{1,17},{2,18},{3,1},{4,20},{5,21},{6,22},{7,5},{8,24},{9,25... | collective-permute-start | bytes 393224 | tf_op jit(solution)/shard_map/ppermute | solution.py:319
  17.3 6.5 %collective-permute-start.9 = (bf16[4,64,256]{2,1,0:T(8,128)(2,1)S(1)}, bf16[4,64,256]{2,1,0:T(8,128)(2,1)S(1)}, u32[]{:S(2)}, u32[]{:S(2)}) collective-permute-start(bf16[4,64,256]{2,1,0:T(8,128)(2,1)S(1)} %get-tuple-element.65), channel_id=1, source_target_pairs={{0,2},{1,3},{2,0},{3,19},{4,6},{5,7},{6,4},{7,23},{8,10},{9,11},{1... | collective-permute-start | bytes 393224 | tf_op jit(solution)/shard_map/ppermute | solution.py:319
  18.5 5.3 %collective-permute-start.8 = (bf16[4,32,256]{2,1,0:T(8,128)(2,1)S(1)}, bf16[4,32,256]{2,1,0:T(8,128)(2,1)S(1)}, u32[]{:S(2)}, u32[]{:S(2)}) collective-permute-start(bf16[4,32,256]{2,1,0:T(8,128)(2,1)S(1)} %get-tuple-element.64), channel_id=1, source_target_pairs={{0,18},{1,19},{2,16},{3,17},{4,22},{5,23},{6,20},{7,21},{8,26},{9,... | collective-permute-start | bytes 196616 | tf_op jit(solution)/shard_map/ppermute | solution.py:319
  23.9 5.7 %collective-permute-start.10 = (bf16[64,256]{1,0:T(8,128)(2,1)S(1)}, bf16[64,256]{1,0:T(8,128)(2,1)S(1)}, u32[]{:S(2)}, u32[]{:S(2)}) collective-permute-start(bf16[64,256]{1,0:T(8,128)(2,1)S(1)} %get-tuple-element.67), channel_id=1, source_target_pairs={{0,4},{1,5},{2,6},{3,7},{4,12},{5,13},{6,14},{7,15},{8,0},{9,1},{1... | collective-permute-start | bytes 98312 | tf_op jit(solution)/shard_map/ppermute | solution.py:397
  25.6 5.7 %collective-permute-start.11 = (bf16[64,256]{1,0:T(8,128)(2,1)S(1)}, bf16[64,256]{1,0:T(8,128)(2,1)S(1)}, u32[]{:S(2)}, u32[]{:S(2)}) collective-permute-start(bf16[64,256]{1,0:T(8,128)(2,1)S(1)} %get-tuple-element.68), channel_id=1, source_target_pairs={{0,12},{1,13},{2,14},{3,15},{4,8},{5,9},{6,10},{7,11},{8,4},{9,5},... | collective-permute-start | bytes 98312 | tf_op jit(solution)/shard_map/ppermute | solution.py:397
  28.1 3.9 %collective-permute-start.12 = (bf16[64,256]{1,0:T(8,128)(2,1)S(1)}, bf16[64,256]{1,0:T(8,128)(2,1)S(1)}, u32[]{:S(2)}, u32[]{:S(2)}) collective-permute-start(bf16[64,256]{1,0:T(8,128)(2,1)S(1)} %get-tuple-element.69), channel_id=1, source_target_pairs={{0,8},{1,9},{2,10},{3,11},{4,0},{5,1},{6,2},{7,3},{8,12},{9,13},{1... | collective-permute-start | bytes 98312 | tf_op jit(solution)/shard_map/ppermute | solution.py:397

commit v15 on v14

--- a/solution.py
+++ b/solution.py
@@ -252,7 +252,7 @@
 
 def layer_routes(layers):
     if layers == 4:
-        return [[1, 3, 0, 2], [3, 2, 1, 0], [2, 0, 3, 1]]
+        return [[2, 3, 1, 0], [3, 2, 0, 1], [1, 0, 3, 2]]
     return [[i ^ k for i in range(layers)] for k in range(1, layers)]
 
 

time: 32.8 us -> 32.6 us (level)
  starting transfers between devices: 17 us -> 15.5 us
  waiting for transfers between devices: 7.74 us -> 8.98 us
    ppermute x3, starting transfers between devices: 5.74 us -> 4.28 us  [pair_on_device(): lax.ppermute(other, ('section', 'dp'), [(s * count + d, s * count + 4 * r...]
    ppermute x3, waiting for transfers between devices: 2.34 us -> 3.58 us  [pair_on_device(): lax.ppermute(other, ('section', 'dp'), [(s * count + d, s * count + 4 * r...]
  transfers between devices with their start and end apart: 13 -> 13, of which waited for: 7 -> 8; matrix products, arithmetic and copies ran while one was open for 0% -> 0% of each run, Pallas kernels for 17% -> 17%
where the time goes in v15:
time: 32.6 us; the launch traced here: 32.4 us
  starting transfers between devices  15.5 us (48%)
  waiting for transfers between devices  8.98 us (28%)
  Pallas kernels  7.15 us (22%)
  between operations  0.76 us (2%)
    ppermute x10, starting transfers between devices, swapped(): return lax.ppermute(array, ('section', 'dp'), pairs)  11.2 us
    pallas_call x14, Pallas kernels, local(): pl.pallas_call(kernel, in_specs=[pl.BlockSpec(memory_space=spaces[kind])...  7.15 us
    ppermute x10, waiting for transfers between devices, swapped(): return lax.ppermute(array, ('section', 'dp'), pairs)  5.4 us
    ppermute x3, starting transfers between devices, pair_on_device(): lax.ppermute(other, ('section', 'dp'), [(s * count + d, s * count + 4 * r...  4.28 us
    ppermute x3, waiting for transfers between devices, pair_on_device(): lax.ppermute(other, ('section', 'dp'), [(s * count + d, s * count + 4 * r...  3.58 us
  transfers between devices with their start and end apart: 13, of which 8 were waited for; matrix products, arithmetic and copies ran while one was open for 0% of the time, Pallas kernels for 17%

profile of v15, /device:TPU:0, one launch (start us, length us, event | category | flops | bytes accessed | tf_op | source)
XLA Modules:
  0.0 32.4 jit_solution(8420858033819676631)
XLA Ops:
  0.6 0.8 %pick.1 = bf16[32,2048]{1,0:T(8,128)(2,1)S(1)} custom-call(s32[1]{0:T(128)} %bitcast.1.place_ref, s32[1]{0:T(128)} %bitcast.index_ref, bf16[1,2,32,4096]{3,2,1,0:T(8,128)(2,1)} %w_out.3), custom_call_target="tpu_custom_call" | custom-call | tf_op jit(solution)/shard_map/pick/pallas_call | solution.py:283
  1.5 3.0 %collective-permute-start = (bf16[32,2048]{1,0:T(8,128)(2,1)S(1)}, bf16[32,2048]{1,0:T(8,128)(2,1)S(1)}, u32[]{:S(2)}, u32[]{:S(2)}) collective-permute-start(bf16[32,2048]{1,0:T(8,128)(2,1)S(1)} %pick.1), channel_id=1, source_target_pairs={{0,16},{1,17},{2,18},{3,19},{4,20},{5,21},{6,22},{7,23},{8,24},{9,... | collective-permute-start | bytes 393224 | tf_op jit(solution)/shard_map/ppermute | solution.py:319
  4.5 2.2 %front.1 = (bf16[32,128]{1,0:T(8,128)(2,1)S(1)}, f32[2,32,128]{2,1,0:T(8,128)S(1)}, bf16[128,4096]{1,0:T(8,128)(2,1)S(1)}, bf16[128,4096]{1,0:T(8,128)(2,1)S(1)}...) custom-call(s32[1]{0:T(128)} %bitcast.1.place_ref, ...), custom_call_target="tpu_custom_call" | custom-call | tf_op jit(solution)/shard_map/front/pallas_call | solution.py:283
  6.7 0.1 collective-permute-start.1
  6.8 0.9 %upper.1 = (bf16[128,4096]{1,0:T(8,128)(2,1)S(1)}, bf16[32,128]{1,0:T(8,128)(2,1)S(1)}, bf16[32,128]{1,0:T(8,128)(2,1)S(1)}, bf16[32,128]{1,0:T(8,128)(2,1)S(1)}, f32[2,128,128]{2,1,0:T(8,128)S(1)}) custom-call(bf16[128,4096]{1,0:T(8,128)(2,1)S(1)} %get-tuple-element.37.x, bf16[128,4096]{1,0:T(8,128)(2,1)S(1)} %get-tuple-element.38.g, ...), custom_call_target="tpu_custom_call" | custom-call | tf_op jit(solution)/shard_map/upper/pallas_call | solution.py:283
  7.8 0.2 collective-permute-done.own_ref
  8.0 0.0 collective-permute-start.2
  8.0 0.7 %outgoing.1.flow_ref = bf16[128,4096]{1,0:T(8,128)(2,1)S(1)} custom-call(bf16[128,4096]{1,0:T(8,128)(2,1)S(1)} %get-tuple-element.37.x, bf16[128,4096]{1,0:T(8,128)(2,1)S(1)} %get-tuple-element.38.g, f32[1,4096]{1,0:T(1,128)S(1)} %get-tuple-element.39.gain, bf16[32,4096]{1,0:T(8,128)(2,1)S(1)} %get-tuple-element.40.wi, ...), custom_call_target="tpu_custom_call" | custom-call | flops 20000000000 | bytes 1048576 | tf_op jit(solution)/shard_map/outgoing/pallas_call | solution.py:283
  8.7 0.3 flow.1.part_ref
  9.0 0.3 collective-permute-done.2.other_ref
  9.3 0.3 flow_rest.1._
  9.6 1.9 %collective-permute-start.4 = (bf16[32,128]{1,0:T(8,128)(2,1)S(1)}, bf16[32,128]{1,0:T(8,128)(2,1)S(1)}, u32[]{:S(2)}, u32[]{:S(2)}) collective-permute-start(bf16[32,128]{1,0:T(8,128)(2,1)S(1)} %flow_rest.1._), channel_id=1, source_target_pairs={{0,16},{1,17},{2,18},{3,19},{4,20},{5,21},{6,22},{7,23},{8,24},{9,... | collective-permute-start | bytes 24584 | tf_op jit(solution)/shard_map/ppermute | solution.py:319
  11.5 0.4 %terms1.1 = (bf16[8,32,256]{2,1,0:T(8,128)(2,1)S(1)}, bf16[8,32,256]{2,1,0:T(8,128)(2,1)S(1)}, bf16[8,32,256]{2,1,0:T(8,128)(2,1)S(1)}, bf16[8,32,256]{2,1,0:T(8,128)(2,1)S(1)}) custom-call(s32[1]{0:T(128)} %bitcast.index_ref, bf16[128,4096]{1,0:T(8,128)(2,1)S(1)} %get-tuple-element.38.g, bf16[128,4096]{1,0:T(8,128)(2,1)S(1)} %get-tuple-element.46.xg_ref, ...), custom_call_target="tpu_custom_call" | custom-call | tf_op jit(solution)/shard_map/terms1/pallas_call | solution.py:283
  12.0 0.0 collective-permute-done.1.act0_ref
  12.0 0.3 terms.1
  12.3 0.1 collective-permute-start.3
  12.3 1.0 %collective-permute-done.4.got_ref = bf16[32,128]{1,0:T(8,128)(2,1)S(1)} collective-permute-done((bf16[32,128]{1,0:T(8,128)(2,1)S(1)}, bf16[32,128]{1,0:T(8,128)(2,1)S(1)}, u32[]{:S(2)}, u32[]{:S(2)}) %collective-permute-start.4) | collective-permute-done | bytes 8224 | tf_op jit(solution)/shard_map/ppermute | solution.py:319
  13.3 0.3 lower.1
  13.6 0.1 collective-permute-start.5
  13.7 0.3 %collective-permute-done.3.got = bf16[24,32,256]{2,1,0:T(8,128)(2,1)S(1)} collective-permute-done((bf16[24,32,256]{2,1,0:T(8,128)(2,1)S(1)}, bf16[24,32,256]{2,1,0:T(8,128)(2,1)S(1)}, u32[]{:S(2)}, u32[]{:S(2)}) %collective-permute-start.3) | collective-permute-done | bytes 393248 | tf_op jit(solution)/shard_map/ppermute | solution.py:319
  14.0 0.1 chip.1
  14.1 2.5 %collective-permute-start.6 = (bf16[4,32,256]{2,1,0:T(8,128)(2,1)S(1)}, bf16[4,32,256]{2,1,0:T(8,128)(2,1)S(1)}, u32[]{:S(2)}, u32[]{:S(2)}) collective-permute-start(bf16[4,32,256]{2,1,0:T(8,128)(2,1)S(1)} %get-tuple-element.62), channel_id=1, source_target_pairs={{0,18},{1,19},{2,16},{3,17},{4,22},{5,23},{6,20},{7,21},{8,26},{9,... | collective-permute-start | bytes 196616 | tf_op jit(solution)/shard_map/ppermute | solution.py:319
  16.7 0.0 collective-permute-done.5.got0
  16.7 0.1 plane.1
  16.8 0.6 %collective-permute-start.7 = (bf16[4,64,256]{2,1,0:T(8,128)(2,1)S(1)}, bf16[4,64,256]{2,1,0:T(8,128)(2,1)S(1)}, u32[]{:S(2)}, u32[]{:S(2)}) collective-permute-start(bf16[4,64,256]{2,1,0:T(8,128)(2,1)S(1)} %get-tuple-element.63), channel_id=1, source_target_pairs={{0,16},{1,17},{2,18},{3,1},{4,20},{5,21},{6,22},{7,5},{8,24},{9,25... | collective-permute-start | bytes 393224 | tf_op jit(solution)/shard_map/ppermute | solution.py:319
  17.3 1.2 %collective-permute-start.9 = (bf16[4,64,256]{2,1,0:T(8,128)(2,1)S(1)}, bf16[4,64,256]{2,1,0:T(8,128)(2,1)S(1)}, u32[]{:S(2)}, u32[]{:S(2)}) collective-permute-start(bf16[4,64,256]{2,1,0:T(8,128)(2,1)S(1)} %get-tuple-element.65), channel_id=1, source_target_pairs={{0,2},{1,3},{2,0},{3,19},{4,6},{5,7},{6,4},{7,23},{8,10},{9,11},{1... | collective-permute-start | bytes 393224 | tf_op jit(solution)/shard_map/ppermute | solution.py:319
  18.5 1.8 %collective-permute-start.8 = (bf16[4,32,256]{2,1,0:T(8,128)(2,1)S(1)}, bf16[4,32,256]{2,1,0:T(8,128)(2,1)S(1)}, u32[]{:S(2)}, u32[]{:S(2)}) collective-permute-start(bf16[4,32,256]{2,1,0:T(8,128)(2,1)S(1)} %get-tuple-element.64), channel_id=1, source_target_pairs={{0,18},{1,19},{2,16},{3,17},{4,22},{5,23},{6,20},{7,21},{8,26},{9,... | collective-permute-start | bytes 196616 | tf_op jit(solution)/shard_map/ppermute | solution.py:319
  20.3 0.0 collective-permute-done.6.across_out
  20.3 3.5 %collective-permute-done.8.across_in = bf16[4,32,256]{2,1,0:T(8,128)(2,1)S(1)} collective-permute-done((bf16[4,32,256]{2,1,0:T(8,128)(2,1)S(1)}, bf16[4,32,256]{2,1,0:T(8,128)(2,1)S(1)}, u32[]{:S(2)}, u32[]{:S(2)}) %collective-permute-start.8) | collective-permute-done | bytes 65568 | tf_op jit(solution)/shard_map/ppermute | solution.py:319
  23.8 0.0 collective-permute-done.7.first
  23.8 0.0 collective-permute-done.9.second
  23.8 0.1 layer.1
  23.9 2.7 %collective-permute-start.10 = (bf16[64,256]{1,0:T(8,128)(2,1)S(1)}, bf16[64,256]{1,0:T(8,128)(2,1)S(1)}, u32[]{:S(2)}, u32[]{:S(2)}) collective-permute-start(bf16[64,256]{1,0:T(8,128)(2,1)S(1)} %get-tuple-element.67), channel_id=1, source_target_pairs={{0,8},{1,9},{2,10},{3,11},{4,12},{5,13},{6,14},{7,15},{8,4},{9,5},... | collective-permute-start | bytes 98312 | tf_op jit(solution)/shard_map/ppermute | solution.py:397
  26.6 1.2 %collective-permute-start.11 = (bf16[64,256]{1,0:T(8,128)(2,1)S(1)}, bf16[64,256]{1,0:T(8,128)(2,1)S(1)}, u32[]{:S(2)}, u32[]{:S(2)}) collective-permute-start(bf16[64,256]{1,0:T(8,128)(2,1)S(1)} %get-tuple-element.68), channel_id=1, source_target_pairs={{0,12},{1,13},{2,14},{3,15},{4,8},{5,9},{6,10},{7,11},{8,0},{9,1},... | collective-permute-start | bytes 98312 | tf_op jit(solution)/shard_map/ppermute | solution.py:397
  27.8 0.4 %collective-permute-start.12 = (bf16[64,256]{1,0:T(8,128)(2,1)S(1)}, bf16[64,256]{1,0:T(8,128)(2,1)S(1)}, u32[]{:S(2)}, u32[]{:S(2)}) collective-permute-start(bf16[64,256]{1,0:T(8,128)(2,1)S(1)} %get-tuple-element.69), channel_id=1, source_target_pairs={{0,4},{1,5},{2,6},{3,7},{4,0},{5,1},{6,2},{7,3},{8,12},{9,13},{10,... | collective-permute-start | bytes 98312 | tf_op jit(solution)/shard_map/ppermute | solution.py:397
  28.2 1.5 %collective-permute-done.10.refs_1_ = bf16[64,256]{1,0:T(8,128)(2,1)S(1)} collective-permute-done((bf16[64,256]{1,0:T(8,128)(2,1)S(1)}, bf16[64,256]{1,0:T(8,128)(2,1)S(1)}, u32[]{:S(2)}, u32[]{:S(2)}) %collective-permute-start.10) | collective-permute-done | bytes 32800 | tf_op jit(solution)/shard_map/ppermute | solution.py:397
  29.7 1.7 %collective-permute-done.11.refs_2_ = bf16[64,256]{1,0:T(8,128)(2,1)S(1)} collective-permute-done((bf16[64,256]{1,0:T(8,128)(2,1)S(1)}, bf16[64,256]{1,0:T(8,128)(2,1)S(1)}, u32[]{:S(2)}, u32[]{:S(2)}) %collective-permute-start.11) | collective-permute-done | bytes 32800 | tf_op jit(solution)/shard_map/ppermute | solution.py:397
  31.4 0.3 %collective-permute-done.12.refs_3_ = bf16[64,256]{1,0:T(8,128)(2,1)S(1)} collective-permute-done((bf16[64,256]{1,0:T(8,128)(2,1)S(1)}, bf16[64,256]{1,0:T(8,128)(2,1)S(1)}, u32[]{:S(2)}, u32[]{:S(2)}) %collective-permute-start.12) | collective-permute-done | bytes 32800 | tf_op jit(solution)/shard_map/ppermute | solution.py:397
  31.8 0.7 %total.1 = (f32[1,32,256]{2,1,0:T(8,128)}, f32[1,32,256]{2,1,0:T(8,128)}) custom-call(bf16[64,256]{1,0:T(8,128)(2,1)S(1)} %get-tuple-element.66.refs_0_, bf16[64,256]{1,0:T(8,128)(2,1)S(1)} %collective-permute-done.10.refs_1_, bf16[64,256]{1,0:T(8,128)(2,1)S(1)} %collective-permute-done.11.refs_2_, bf16[64,256]{1,0:T(8,128)(2,1)S(1)} %collective-permute-done.12.refs_3_), custom_call_target="tpu_custom_call" | custom-call | tf_op jit(solution)/shard_map/total/pallas_call | solution.py:283
  (1 shorter events, 0.0 us)
Async XLA Ops:
  1.5 6.5 %collective-permute-start = (bf16[32,2048]{1,0:T(8,128)(2,1)S(1)}, bf16[32,2048]{1,0:T(8,128)(2,1)S(1)}, u32[]{:S(2)}, u32[]{:S(2)}) collective-permute-start(bf16[32,2048]{1,0:T(8,128)(2,1)S(1)} %pick.1), channel_id=1, source_target_pairs={{0,16},{1,17},{2,18},{3,19},{4,20},{5,21},{6,22},{7,23},{8,24},{9,... | collective-permute-start | bytes 393224 | tf_op jit(solution)/shard_map/ppermute | solution.py:319
  6.7 5.2 %collective-permute-start.1 = (bf16[32,128]{1,0:T(8,128)(2,1)S(1)}, bf16[32,128]{1,0:T(8,128)(2,1)S(1)}, u32[]{:S(2)}, u32[]{:S(2)}) collective-permute-start(bf16[32,128]{1,0:T(8,128)(2,1)S(1)} %get-tuple-element.45), channel_id=1, source_target_pairs={{0,16},{1,17},{2,18},{3,19},{4,20},{5,21},{6,22},{7,23},{8,24},{9,... | collective-permute-start | bytes 24584 | tf_op jit(solution)/shard_map/ppermute | solution.py:319
  8.0 1.3 %collective-permute-start.2 = (bf16[32,2048]{1,0:T(8,128)(2,1)S(1)}, bf16[32,2048]{1,0:T(8,128)(2,1)S(1)}, u32[]{:S(2)}, u32[]{:S(2)}) collective-permute-start(bf16[32,2048]{1,0:T(8,128)(2,1)S(1)} %collective-permute-done.own_ref), channel_id=1, source_target_pairs={{0,1},{1,0},{2,3},{3,2},{4,5},{5,4},{6,7},{7,6},{8,9},{9,8},{10,11... | collective-permute-start | bytes 393224 | tf_op jit(solution)/shard_map/ppermute | solution.py:319
  9.6 3.7 %collective-permute-start.4 = (bf16[32,128]{1,0:T(8,128)(2,1)S(1)}, bf16[32,128]{1,0:T(8,128)(2,1)S(1)}, u32[]{:S(2)}, u32[]{:S(2)}) collective-permute-start(bf16[32,128]{1,0:T(8,128)(2,1)S(1)} %flow_rest.1._), channel_id=1, source_target_pairs={{0,16},{1,17},{2,18},{3,19},{4,20},{5,21},{6,22},{7,23},{8,24},{9,... | collective-permute-start | bytes 24584 | tf_op jit(solution)/shard_map/ppermute | solution.py:319
  12.3 1.8 %collective-permute-start.3 = (bf16[24,32,256]{2,1,0:T(8,128)(2,1)S(1)}, bf16[24,32,256]{2,1,0:T(8,128)(2,1)S(1)}, u32[]{:S(2)}, u32[]{:S(2)}) collective-permute-start(bf16[24,32,256]{2,1,0:T(8,128)(2,1)S(1)} %get-tuple-element.55), channel_id=1, source_target_pairs={{0,1},{1,0},{2,3},{3,2},{4,5},{5,4},{6,7},{7,6},{8,9},{9,8},{10,11... | collective-permute-start | bytes 1179656 | tf_op jit(solution)/shard_map/ppermute | solution.py:319
  13.6 3.1 %collective-permute-start.5 = (bf16[8,32,256]{2,1,0:T(8,128)(2,1)S(1)}, bf16[8,32,256]{2,1,0:T(8,128)(2,1)S(1)}, u32[]{:S(2)}, u32[]{:S(2)}) collective-permute-start(bf16[8,32,256]{2,1,0:T(8,128)(2,1)S(1)} %get-tuple-element.60), channel_id=1, source_target_pairs={{0,1},{1,0},{2,3},{3,2},{4,5},{5,4},{6,7},{7,6},{8,9},{9,8},{10,11... | collective-permute-start | bytes 393224 | tf_op jit(solution)/shard_map/ppermute | solution.py:319
  14.1 6.2 %collective-permute-start.6 = (bf16[4,32,256]{2,1,0:T(8,128)(2,1)S(1)}, bf16[4,32,256]{2,1,0:T(8,128)(2,1)S(1)}, u32[]{:S(2)}, u32[]{:S(2)}) collective-permute-start(bf16[4,32,256]{2,1,0:T(8,128)(2,1)S(1)} %get-tuple-element.62), channel_id=1, source_target_pairs={{0,18},{1,19},{2,16},{3,17},{4,22},{5,23},{6,20},{7,21},{8,26},{9,... | collective-permute-start | bytes 196616 | tf_op jit(solution)/shard_map/ppermute | solution.py:319
  16.8 7.1 %collective-permute-start.7 = (bf16[4,64,256]{2,1,0:T(8,128)(2,1)S(1)}, bf16[4,64,256]{2,1,0:T(8,128)(2,1)S(1)}, u32[]{:S(2)}, u32[]{:S(2)}) collective-permute-start(bf16[4,64,256]{2,1,0:T(8,128)(2,1)S(1)} %get-tuple-element.63), channel_id=1, source_target_pairs={{0,16},{1,17},{2,18},{3,1},{4,20},{5,21},{6,22},{7,5},{8,24},{9,25... | collective-permute-start | bytes 393224 | tf_op jit(solution)/shard_map/ppermute | solution.py:319
  17.3 6.5 %collective-permute-start.9 = (bf16[4,64,256]{2,1,0:T(8,128)(2,1)S(1)}, bf16[4,64,256]{2,1,0:T(8,128)(2,1)S(1)}, u32[]{:S(2)}, u32[]{:S(2)}) collective-permute-start(bf16[4,64,256]{2,1,0:T(8,128)(2,1)S(1)} %get-tuple-element.65), channel_id=1, source_target_pairs={{0,2},{1,3},{2,0},{3,19},{4,6},{5,7},{6,4},{7,23},{8,10},{9,11},{1... | collective-permute-start | bytes 393224 | tf_op jit(solution)/shard_map/ppermute | solution.py:319
  18.5 5.3 %collective-permute-start.8 = (bf16[4,32,256]{2,1,0:T(8,128)(2,1)S(1)}, bf16[4,32,256]{2,1,0:T(8,128)(2,1)S(1)}, u32[]{:S(2)}, u32[]{:S(2)}) collective-permute-start(bf16[4,32,256]{2,1,0:T(8,128)(2,1)S(1)} %get-tuple-element.64), channel_id=1, source_target_pairs={{0,18},{1,19},{2,16},{3,17},{4,22},{5,23},{6,20},{7,21},{8,26},{9,... | collective-permute-start | bytes 196616 | tf_op jit(solution)/shard_map/ppermute | solution.py:319
  23.9 5.8 %collective-permute-start.10 = (bf16[64,256]{1,0:T(8,128)(2,1)S(1)}, bf16[64,256]{1,0:T(8,128)(2,1)S(1)}, u32[]{:S(2)}, u32[]{:S(2)}) collective-permute-start(bf16[64,256]{1,0:T(8,128)(2,1)S(1)} %get-tuple-element.67), channel_id=1, source_target_pairs={{0,8},{1,9},{2,10},{3,11},{4,12},{5,13},{6,14},{7,15},{8,4},{9,5},... | collective-permute-start | bytes 98312 | tf_op jit(solution)/shard_map/ppermute | solution.py:397
  26.6 4.8 %collective-permute-start.11 = (bf16[64,256]{1,0:T(8,128)(2,1)S(1)}, bf16[64,256]{1,0:T(8,128)(2,1)S(1)}, u32[]{:S(2)}, u32[]{:S(2)}) collective-permute-start(bf16[64,256]{1,0:T(8,128)(2,1)S(1)} %get-tuple-element.68), channel_id=1, source_target_pairs={{0,12},{1,13},{2,14},{3,15},{4,8},{5,9},{6,10},{7,11},{8,0},{9,1},... | collective-permute-start | bytes 98312 | tf_op jit(solution)/shard_map/ppermute | solution.py:397
  27.8 4.0 %collective-permute-start.12 = (bf16[64,256]{1,0:T(8,128)(2,1)S(1)}, bf16[64,256]{1,0:T(8,128)(2,1)S(1)}, u32[]{:S(2)}, u32[]{:S(2)}) collective-permute-start(bf16[64,256]{1,0:T(8,128)(2,1)S(1)} %get-tuple-element.69), channel_id=1, source_target_pairs={{0,4},{1,5},{2,6},{3,7},{4,0},{5,1},{6,2},{7,3},{8,12},{9,13},{10,... | collective-permute-start | bytes 98312 | tf_op jit(solution)/shard_map/ppermute | solution.py:397

commit v16 on v15

--- a/solution.py
+++ b/solution.py
@@ -206,7 +206,7 @@
 
 
 def x_first(section, index):
-    return (index % 2 == 0) | (section == (index // 2) % 2)
+    return section == (index // 2) % 2
 
 
 def plane_kernel(

time: 32.6 us -> 32.7 us (level)
  waiting for transfers between devices: 8.98 us -> 9.5 us
  starting transfers between devices: 15.5 us -> 15.1 us
    ppermute x10, waiting for transfers between devices: 5.4 us -> 5.91 us  [swapped(): return lax.ppermute(array, ('section', 'dp'), pairs)]
    ppermute x10, starting transfers between devices: 11.2 us -> 10.9 us  [swapped(): return lax.ppermute(array, ('section', 'dp'), pairs)]
where the time goes in v16:
time: 32.7 us; the launch traced here: 32.5 us
  starting transfers between devices  15.1 us (46%)
  waiting for transfers between devices  9.5 us (29%)
  Pallas kernels  7.15 us (22%)
  between operations  0.76 us (2%)
    ppermute x10, starting transfers between devices, swapped(): return lax.ppermute(array, ('section', 'dp'), pairs)  10.9 us
    pallas_call x14, Pallas kernels, local(): pl.pallas_call(kernel, in_specs=[pl.BlockSpec(memory_space=spaces[kind])...  7.15 us
    ppermute x10, waiting for transfers between devices, swapped(): return lax.ppermute(array, ('section', 'dp'), pairs)  5.91 us
    ppermute x3, starting transfers between devices, pair_on_device(): lax.ppermute(other, ('section', 'dp'), [(s * count + d, s * count + 4 * r...  4.22 us
    ppermute x3, waiting for transfers between devices, pair_on_device(): lax.ppermute(other, ('section', 'dp'), [(s * count + d, s * count + 4 * r...  3.58 us
  transfers between devices with their start and end apart: 13, of which 8 were waited for; matrix products, arithmetic and copies ran while one was open for 0% of the time, Pallas kernels for 17%

profile of v16, /device:TPU:0, one launch (start us, length us, event | category | flops | bytes accessed | tf_op | source)
XLA Modules:
  0.0 32.5 jit_solution(18185965459081865244)
XLA Ops:
  0.6 0.8 %pick.1 = bf16[32,2048]{1,0:T(8,128)(2,1)S(1)} custom-call(s32[1]{0:T(128)} %bitcast.1.place_ref, s32[1]{0:T(128)} %bitcast.index_ref, bf16[1,2,32,4096]{3,2,1,0:T(8,128)(2,1)} %w_out.3), custom_call_target="tpu_custom_call" | custom-call | tf_op jit(solution)/shard_map/pick/pallas_call | solution.py:283
  1.5 3.0 %collective-permute-start = (bf16[32,2048]{1,0:T(8,128)(2,1)S(1)}, bf16[32,2048]{1,0:T(8,128)(2,1)S(1)}, u32[]{:S(2)}, u32[]{:S(2)}) collective-permute-start(bf16[32,2048]{1,0:T(8,128)(2,1)S(1)} %pick.1), channel_id=1, source_target_pairs={{0,16},{1,17},{2,18},{3,19},{4,20},{5,21},{6,22},{7,23},{8,24},{9,... | collective-permute-start | bytes 393224 | tf_op jit(solution)/shard_map/ppermute | solution.py:319
  4.5 2.2 %front.1 = (bf16[32,128]{1,0:T(8,128)(2,1)S(1)}, f32[2,32,128]{2,1,0:T(8,128)S(1)}, bf16[128,4096]{1,0:T(8,128)(2,1)S(1)}, bf16[128,4096]{1,0:T(8,128)(2,1)S(1)}...) custom-call(s32[1]{0:T(128)} %bitcast.1.place_ref, ...), custom_call_target="tpu_custom_call" | custom-call | tf_op jit(solution)/shard_map/front/pallas_call | solution.py:283
  6.7 0.1 collective-permute-start.1
  6.8 0.9 %upper.1 = (bf16[128,4096]{1,0:T(8,128)(2,1)S(1)}, bf16[32,128]{1,0:T(8,128)(2,1)S(1)}, bf16[32,128]{1,0:T(8,128)(2,1)S(1)}, bf16[32,128]{1,0:T(8,128)(2,1)S(1)}, f32[2,128,128]{2,1,0:T(8,128)S(1)}) custom-call(bf16[128,4096]{1,0:T(8,128)(2,1)S(1)} %get-tuple-element.37.x, bf16[128,4096]{1,0:T(8,128)(2,1)S(1)} %get-tuple-element.38.g, ...), custom_call_target="tpu_custom_call" | custom-call | tf_op jit(solution)/shard_map/upper/pallas_call | solution.py:283
  7.8 0.2 collective-permute-done.own_ref
  8.0 0.0 collective-permute-start.2
  8.0 0.7 %outgoing.1.flow_ref = bf16[128,4096]{1,0:T(8,128)(2,1)S(1)} custom-call(bf16[128,4096]{1,0:T(8,128)(2,1)S(1)} %get-tuple-element.37.x, bf16[128,4096]{1,0:T(8,128)(2,1)S(1)} %get-tuple-element.38.g, f32[1,4096]{1,0:T(1,128)S(1)} %get-tuple-element.39.gain, bf16[32,4096]{1,0:T(8,128)(2,1)S(1)} %get-tuple-element.40.wi, ...), custom_call_target="tpu_custom_call" | custom-call | flops 20000000000 | bytes 1048576 | tf_op jit(solution)/shard_map/outgoing/pallas_call | solution.py:283
  8.7 0.3 flow.1.part_ref
  9.0 0.3 collective-permute-done.2.other_ref
  9.3 0.3 flow_rest.1._
  9.6 1.9 %collective-permute-start.4 = (bf16[32,128]{1,0:T(8,128)(2,1)S(1)}, bf16[32,128]{1,0:T(8,128)(2,1)S(1)}, u32[]{:S(2)}, u32[]{:S(2)}) collective-permute-start(bf16[32,128]{1,0:T(8,128)(2,1)S(1)} %flow_rest.1._), channel_id=1, source_target_pairs={{0,16},{1,17},{2,18},{3,19},{4,20},{5,21},{6,22},{7,23},{8,24},{9,... | collective-permute-start | bytes 24584 | tf_op jit(solution)/shard_map/ppermute | solution.py:319
  11.5 0.4 %terms1.1 = (bf16[8,32,256]{2,1,0:T(8,128)(2,1)S(1)}, bf16[8,32,256]{2,1,0:T(8,128)(2,1)S(1)}, bf16[8,32,256]{2,1,0:T(8,128)(2,1)S(1)}, bf16[8,32,256]{2,1,0:T(8,128)(2,1)S(1)}) custom-call(s32[1]{0:T(128)} %bitcast.index_ref, bf16[128,4096]{1,0:T(8,128)(2,1)S(1)} %get-tuple-element.38.g, bf16[128,4096]{1,0:T(8,128)(2,1)S(1)} %get-tuple-element.46.xg_ref, ...), custom_call_target="tpu_custom_call" | custom-call | tf_op jit(solution)/shard_map/terms1/pallas_call | solution.py:283
  12.0 0.0 collective-permute-done.1.act0_ref
  12.0 0.3 terms.1
  12.3 0.1 collective-permute-start.3
  12.3 1.0 %collective-permute-done.4.got_ref = bf16[32,128]{1,0:T(8,128)(2,1)S(1)} collective-permute-done((bf16[32,128]{1,0:T(8,128)(2,1)S(1)}, bf16[32,128]{1,0:T(8,128)(2,1)S(1)}, u32[]{:S(2)}, u32[]{:S(2)}) %collective-permute-start.4) | collective-permute-done | bytes 8224 | tf_op jit(solution)/shard_map/ppermute | solution.py:319
  13.3 0.3 lower.1
  13.6 0.1 collective-permute-start.5
  13.7 0.3 %collective-permute-done.3.got = bf16[24,32,256]{2,1,0:T(8,128)(2,1)S(1)} collective-permute-done((bf16[24,32,256]{2,1,0:T(8,128)(2,1)S(1)}, bf16[24,32,256]{2,1,0:T(8,128)(2,1)S(1)}, u32[]{:S(2)}, u32[]{:S(2)}) %collective-permute-start.3) | collective-permute-done | bytes 393248 | tf_op jit(solution)/shard_map/ppermute | solution.py:319
  14.0 0.1 chip.1
  14.1 2.5 %collective-permute-start.6 = (bf16[4,32,256]{2,1,0:T(8,128)(2,1)S(1)}, bf16[4,32,256]{2,1,0:T(8,128)(2,1)S(1)}, u32[]{:S(2)}, u32[]{:S(2)}) collective-permute-start(bf16[4,32,256]{2,1,0:T(8,128)(2,1)S(1)} %get-tuple-element.62), channel_id=1, source_target_pairs={{0,18},{1,19},{2,16},{3,17},{4,22},{5,23},{6,20},{7,21},{8,26},{9,... | collective-permute-start | bytes 196616 | tf_op jit(solution)/shard_map/ppermute | solution.py:319
  16.7 0.0 collective-permute-done.5.got0
  16.7 0.1 plane.1
  16.8 0.6 %collective-permute-start.7 = (bf16[4,64,256]{2,1,0:T(8,128)(2,1)S(1)}, bf16[4,64,256]{2,1,0:T(8,128)(2,1)S(1)}, u32[]{:S(2)}, u32[]{:S(2)}) collective-permute-start(bf16[4,64,256]{2,1,0:T(8,128)(2,1)S(1)} %get-tuple-element.63), channel_id=1, source_target_pairs={{0,16},{1,17},{2,0},{3,1},{4,20},{5,21},{6,4},{7,5},{8,24},{9,25},... | collective-permute-start | bytes 393224 | tf_op jit(solution)/shard_map/ppermute | solution.py:319
  17.3 1.5 %collective-permute-start.9 = (bf16[4,64,256]{2,1,0:T(8,128)(2,1)S(1)}, bf16[4,64,256]{2,1,0:T(8,128)(2,1)S(1)}, u32[]{:S(2)}, u32[]{:S(2)}) collective-permute-start(bf16[4,64,256]{2,1,0:T(8,128)(2,1)S(1)} %get-tuple-element.65), channel_id=1, source_target_pairs={{0,2},{1,3},{2,18},{3,19},{4,6},{5,7},{6,22},{7,23},{8,10},{9,11},... | collective-permute-start | bytes 393224 | tf_op jit(solution)/shard_map/ppermute | solution.py:319
  18.8 1.1 %collective-permute-start.8 = (bf16[4,32,256]{2,1,0:T(8,128)(2,1)S(1)}, bf16[4,32,256]{2,1,0:T(8,128)(2,1)S(1)}, u32[]{:S(2)}, u32[]{:S(2)}) collective-permute-start(bf16[4,32,256]{2,1,0:T(8,128)(2,1)S(1)} %get-tuple-element.64), channel_id=1, source_target_pairs={{0,18},{1,19},{2,16},{3,17},{4,22},{5,23},{6,20},{7,21},{8,26},{9,... | collective-permute-start | bytes 196616 | tf_op jit(solution)/shard_map/ppermute | solution.py:319
  20.0 0.0 collective-permute-done.6.across_out
  20.0 4.0 %collective-permute-done.8.across_in = bf16[4,32,256]{2,1,0:T(8,128)(2,1)S(1)} collective-permute-done((bf16[4,32,256]{2,1,0:T(8,128)(2,1)S(1)}, bf16[4,32,256]{2,1,0:T(8,128)(2,1)S(1)}, u32[]{:S(2)}, u32[]{:S(2)}) %collective-permute-start.8) | collective-permute-done | bytes 65568 | tf_op jit(solution)/shard_map/ppermute | solution.py:319
  24.0 0.0 collective-permute-done.7.first
  24.0 0.0 collective-permute-done.9.second
  24.0 0.1 layer.1
  24.1 2.6 %collective-permute-start.10 = (bf16[64,256]{1,0:T(8,128)(2,1)S(1)}, bf16[64,256]{1,0:T(8,128)(2,1)S(1)}, u32[]{:S(2)}, u32[]{:S(2)}) collective-permute-start(bf16[64,256]{1,0:T(8,128)(2,1)S(1)} %get-tuple-element.67), channel_id=1, source_target_pairs={{0,8},{1,9},{2,10},{3,11},{4,12},{5,13},{6,14},{7,15},{8,4},{9,5},... | collective-permute-start | bytes 98312 | tf_op jit(solution)/shard_map/ppermute | solution.py:397
  26.7 1.2 %collective-permute-start.11 = (bf16[64,256]{1,0:T(8,128)(2,1)S(1)}, bf16[64,256]{1,0:T(8,128)(2,1)S(1)}, u32[]{:S(2)}, u32[]{:S(2)}) collective-permute-start(bf16[64,256]{1,0:T(8,128)(2,1)S(1)} %get-tuple-element.68), channel_id=1, source_target_pairs={{0,12},{1,13},{2,14},{3,15},{4,8},{5,9},{6,10},{7,11},{8,0},{9,1},... | collective-permute-start | bytes 98312 | tf_op jit(solution)/shard_map/ppermute | solution.py:397
  28.0 0.3 %collective-permute-start.12 = (bf16[64,256]{1,0:T(8,128)(2,1)S(1)}, bf16[64,256]{1,0:T(8,128)(2,1)S(1)}, u32[]{:S(2)}, u32[]{:S(2)}) collective-permute-start(bf16[64,256]{1,0:T(8,128)(2,1)S(1)} %get-tuple-element.69), channel_id=1, source_target_pairs={{0,4},{1,5},{2,6},{3,7},{4,0},{5,1},{6,2},{7,3},{8,12},{9,13},{10,... | collective-permute-start | bytes 98312 | tf_op jit(solution)/shard_map/ppermute | solution.py:397
  28.3 1.6 %collective-permute-done.10.refs_1_ = bf16[64,256]{1,0:T(8,128)(2,1)S(1)} collective-permute-done((bf16[64,256]{1,0:T(8,128)(2,1)S(1)}, bf16[64,256]{1,0:T(8,128)(2,1)S(1)}, u32[]{:S(2)}, u32[]{:S(2)}) %collective-permute-start.10) | collective-permute-done | bytes 32800 | tf_op jit(solution)/shard_map/ppermute | solution.py:397
  29.9 1.6 %collective-permute-done.11.refs_2_ = bf16[64,256]{1,0:T(8,128)(2,1)S(1)} collective-permute-done((bf16[64,256]{1,0:T(8,128)(2,1)S(1)}, bf16[64,256]{1,0:T(8,128)(2,1)S(1)}, u32[]{:S(2)}, u32[]{:S(2)}) %collective-permute-start.11) | collective-permute-done | bytes 32800 | tf_op jit(solution)/shard_map/ppermute | solution.py:397
  31.5 0.4 %collective-permute-done.12.refs_3_ = bf16[64,256]{1,0:T(8,128)(2,1)S(1)} collective-permute-done((bf16[64,256]{1,0:T(8,128)(2,1)S(1)}, bf16[64,256]{1,0:T(8,128)(2,1)S(1)}, u32[]{:S(2)}, u32[]{:S(2)}) %collective-permute-start.12) | collective-permute-done | bytes 32800 | tf_op jit(solution)/shard_map/ppermute | solution.py:397
  31.9 0.7 %total.1 = (f32[1,32,256]{2,1,0:T(8,128)}, f32[1,32,256]{2,1,0:T(8,128)}) custom-call(bf16[64,256]{1,0:T(8,128)(2,1)S(1)} %get-tuple-element.66.refs_0_, bf16[64,256]{1,0:T(8,128)(2,1)S(1)} %collective-permute-done.10.refs_1_, bf16[64,256]{1,0:T(8,128)(2,1)S(1)} %collective-permute-done.11.refs_2_, bf16[64,256]{1,0:T(8,128)(2,1)S(1)} %collective-permute-done.12.refs_3_), custom_call_target="tpu_custom_call" | custom-call | tf_op jit(solution)/shard_map/total/pallas_call | solution.py:283
  (1 shorter events, 0.0 us)
Async XLA Ops:
  1.5 6.5 %collective-permute-start = (bf16[32,2048]{1,0:T(8,128)(2,1)S(1)}, bf16[32,2048]{1,0:T(8,128)(2,1)S(1)}, u32[]{:S(2)}, u32[]{:S(2)}) collective-permute-start(bf16[32,2048]{1,0:T(8,128)(2,1)S(1)} %pick.1), channel_id=1, source_target_pairs={{0,16},{1,17},{2,18},{3,19},{4,20},{5,21},{6,22},{7,23},{8,24},{9,... | collective-permute-start | bytes 393224 | tf_op jit(solution)/shard_map/ppermute | solution.py:319
  6.7 5.2 %collective-permute-start.1 = (bf16[32,128]{1,0:T(8,128)(2,1)S(1)}, bf16[32,128]{1,0:T(8,128)(2,1)S(1)}, u32[]{:S(2)}, u32[]{:S(2)}) collective-permute-start(bf16[32,128]{1,0:T(8,128)(2,1)S(1)} %get-tuple-element.45), channel_id=1, source_target_pairs={{0,16},{1,17},{2,18},{3,19},{4,20},{5,21},{6,22},{7,23},{8,24},{9,... | collective-permute-start | bytes 24584 | tf_op jit(solution)/shard_map/ppermute | solution.py:319
  8.0 1.3 %collective-permute-start.2 = (bf16[32,2048]{1,0:T(8,128)(2,1)S(1)}, bf16[32,2048]{1,0:T(8,128)(2,1)S(1)}, u32[]{:S(2)}, u32[]{:S(2)}) collective-permute-start(bf16[32,2048]{1,0:T(8,128)(2,1)S(1)} %collective-permute-done.own_ref), channel_id=1, source_target_pairs={{0,1},{1,0},{2,3},{3,2},{4,5},{5,4},{6,7},{7,6},{8,9},{9,8},{10,11... | collective-permute-start | bytes 393224 | tf_op jit(solution)/shard_map/ppermute | solution.py:319
  9.6 3.7 %collective-permute-start.4 = (bf16[32,128]{1,0:T(8,128)(2,1)S(1)}, bf16[32,128]{1,0:T(8,128)(2,1)S(1)}, u32[]{:S(2)}, u32[]{:S(2)}) collective-permute-start(bf16[32,128]{1,0:T(8,128)(2,1)S(1)} %flow_rest.1._), channel_id=1, source_target_pairs={{0,16},{1,17},{2,18},{3,19},{4,20},{5,21},{6,22},{7,23},{8,24},{9,... | collective-permute-start | bytes 24584 | tf_op jit(solution)/shard_map/ppermute | solution.py:319
  12.3 1.8 %collective-permute-start.3 = (bf16[24,32,256]{2,1,0:T(8,128)(2,1)S(1)}, bf16[24,32,256]{2,1,0:T(8,128)(2,1)S(1)}, u32[]{:S(2)}, u32[]{:S(2)}) collective-permute-start(bf16[24,32,256]{2,1,0:T(8,128)(2,1)S(1)} %get-tuple-element.55), channel_id=1, source_target_pairs={{0,1},{1,0},{2,3},{3,2},{4,5},{5,4},{6,7},{7,6},{8,9},{9,8},{10,11... | collective-permute-start | bytes 1179656 | tf_op jit(solution)/shard_map/ppermute | solution.py:319
  13.6 3.1 %collective-permute-start.5 = (bf16[8,32,256]{2,1,0:T(8,128)(2,1)S(1)}, bf16[8,32,256]{2,1,0:T(8,128)(2,1)S(1)}, u32[]{:S(2)}, u32[]{:S(2)}) collective-permute-start(bf16[8,32,256]{2,1,0:T(8,128)(2,1)S(1)} %get-tuple-element.60), channel_id=1, source_target_pairs={{0,1},{1,0},{2,3},{3,2},{4,5},{5,4},{6,7},{7,6},{8,9},{9,8},{10,11... | collective-permute-start | bytes 393224 | tf_op jit(solution)/shard_map/ppermute | solution.py:319
  14.1 5.8 %collective-permute-start.6 = (bf16[4,32,256]{2,1,0:T(8,128)(2,1)S(1)}, bf16[4,32,256]{2,1,0:T(8,128)(2,1)S(1)}, u32[]{:S(2)}, u32[]{:S(2)}) collective-permute-start(bf16[4,32,256]{2,1,0:T(8,128)(2,1)S(1)} %get-tuple-element.62), channel_id=1, source_target_pairs={{0,18},{1,19},{2,16},{3,17},{4,22},{5,23},{6,20},{7,21},{8,26},{9,... | collective-permute-start | bytes 196616 | tf_op jit(solution)/shard_map/ppermute | solution.py:319
  16.8 7.2 %collective-permute-start.7 = (bf16[4,64,256]{2,1,0:T(8,128)(2,1)S(1)}, bf16[4,64,256]{2,1,0:T(8,128)(2,1)S(1)}, u32[]{:S(2)}, u32[]{:S(2)}) collective-permute-start(bf16[4,64,256]{2,1,0:T(8,128)(2,1)S(1)} %get-tuple-element.63), channel_id=1, source_target_pairs={{0,16},{1,17},{2,0},{3,1},{4,20},{5,21},{6,4},{7,5},{8,24},{9,25},... | collective-permute-start | bytes 393224 | tf_op jit(solution)/shard_map/ppermute | solution.py:319
  17.3 6.7 %collective-permute-start.9 = (bf16[4,64,256]{2,1,0:T(8,128)(2,1)S(1)}, bf16[4,64,256]{2,1,0:T(8,128)(2,1)S(1)}, u32[]{:S(2)}, u32[]{:S(2)}) collective-permute-start(bf16[4,64,256]{2,1,0:T(8,128)(2,1)S(1)} %get-tuple-element.65), channel_id=1, source_target_pairs={{0,2},{1,3},{2,18},{3,19},{4,6},{5,7},{6,22},{7,23},{8,10},{9,11},... | collective-permute-start | bytes 393224 | tf_op jit(solution)/shard_map/ppermute | solution.py:319
  18.8 5.2 %collective-permute-start.8 = (bf16[4,32,256]{2,1,0:T(8,128)(2,1)S(1)}, bf16[4,32,256]{2,1,0:T(8,128)(2,1)S(1)}, u32[]{:S(2)}, u32[]{:S(2)}) collective-permute-start(bf16[4,32,256]{2,1,0:T(8,128)(2,1)S(1)} %get-tuple-element.64), channel_id=1, source_target_pairs={{0,18},{1,19},{2,16},{3,17},{4,22},{5,23},{6,20},{7,21},{8,26},{9,... | collective-permute-start | bytes 196616 | tf_op jit(solution)/shard_map/ppermute | solution.py:319
  24.1 5.8 %collective-permute-start.10 = (bf16[64,256]{1,0:T(8,128)(2,1)S(1)}, bf16[64,256]{1,0:T(8,128)(2,1)S(1)}, u32[]{:S(2)}, u32[]{:S(2)}) collective-permute-start(bf16[64,256]{1,0:T(8,128)(2,1)S(1)} %get-tuple-element.67), channel_id=1, source_target_pairs={{0,8},{1,9},{2,10},{3,11},{4,12},{5,13},{6,14},{7,15},{8,4},{9,5},... | collective-permute-start | bytes 98312 | tf_op jit(solution)/shard_map/ppermute | solution.py:397
  26.7 4.8 %collective-permute-start.11 = (bf16[64,256]{1,0:T(8,128)(2,1)S(1)}, bf16[64,256]{1,0:T(8,128)(2,1)S(1)}, u32[]{:S(2)}, u32[]{:S(2)}) collective-permute-start(bf16[64,256]{1,0:T(8,128)(2,1)S(1)} %get-tuple-element.68), channel_id=1, source_target_pairs={{0,12},{1,13},{2,14},{3,15},{4,8},{5,9},{6,10},{7,11},{8,0},{9,1},... | collective-permute-start | bytes 98312 | tf_op jit(solution)/shard_map/ppermute | solution.py:397
  28.0 3.9 %collective-permute-start.12 = (bf16[64,256]{1,0:T(8,128)(2,1)S(1)}, bf16[64,256]{1,0:T(8,128)(2,1)S(1)}, u32[]{:S(2)}, u32[]{:S(2)}) collective-permute-start(bf16[64,256]{1,0:T(8,128)(2,1)S(1)} %get-tuple-element.69), channel_id=1, source_target_pairs={{0,4},{1,5},{2,6},{3,7},{4,0},{5,1},{6,2},{7,3},{8,12},{9,13},{10,... | collective-permute-start | bytes 98312 | tf_op jit(solution)/shard_map/ppermute | solution.py:397

commit v17 on v15

--- a/solution.py
+++ b/solution.py
@@ -252,15 +252,15 @@
 
 def layer_routes(layers):
     if layers == 4:
-        return [[2, 3, 1, 0], [3, 2, 0, 1], [1, 0, 3, 2]]
+        return [[None, None, None, 0], [1, 0, 3, 2], [2, 3, 0, 1], [3, 2, 1, None]]
     return [[i ^ k for i in range(layers)] for k in range(1, layers)]
 
 
 def layer_kernel(routes, index_ref, own, first, across_in, second, *out_refs):
     rank = across_in.shape[1]
     layer = index_ref[0] // 4
-    for route, out_ref in zip([range(len(out_refs)), *routes], out_refs):
-        block = sum(jnp.where(layer == i, target, 0) for i, target in enumerate(route))
+    for route, out_ref in zip([range(own.shape[0]), *routes], out_refs):
+        block = sum(jnp.where(layer == i, target or 0, 0) for i, target in enumerate(route))
         total = sum(ref[block].astype(F32) for ref in (own, first, second))
         out_ref[0:rank] = (total[0:rank] + across_in[block].astype(F32)).astype(BF16)
         out_ref[rank : 2 * rank] = total[rank : 2 * rank].astype(BF16)
@@ -390,7 +390,7 @@
     own = local(add_kernel, "add", [double], *near(own, across_out), cost=MEDIUM)
     routes = layer_routes(layers)
     mine, *others = local(
-        partial(layer_kernel, routes), "layer", [((2 * rank, share), BF16)] * layers,
+        partial(layer_kernel, routes), "layer", [((2 * rank, share), BF16)] * (1 + len(routes)),
         index, *near(own, first, across_in, second),
     )
     others = [
@@ -401,6 +401,7 @@
                 (s * count + d, s * count + 4 * route[d // 4] + d % 4)
                 for s in range(2)
                 for d in range(count)
+                if route[d // 4] is not None
             ],
         )
         for route, other in zip(routes, others)

time: 32.6 us -> 34.2 us (1.049)
  starting transfers between devices: 15.5 us -> 19 us
  waiting for transfers between devices: 8.98 us -> 6.96 us
    ppermute x3 -> x4, starting transfers between devices: 4.28 us -> 7.79 us  [pair_on_device(): lax.ppermute(other, ('section', 'dp'), [(s * count + d, s * count + 4 * r...]
    ppermute x3 -> x4, waiting for transfers between devices: 3.58 us -> 1.56 us  [pair_on_device(): lax.ppermute(other, ('section', 'dp'), [(s * count + d, s * count + 4 * r...]
  transfers between devices with their start and end apart: 13 -> 14, of which waited for: 8 -> 7; matrix products, arithmetic and copies ran while one was open for 0% -> 0% of each run, Pallas kernels for 17% -> 16%
where the time goes in v17:
time: 34.2 us; the launch traced here: 34 us
  starting transfers between devices  19 us (56%)
  Pallas kernels  7.16 us (21%)
  waiting for transfers between devices  6.96 us (20%)
  between operations  0.79 us (2%)
    ppermute x10, starting transfers between devices, swapped(): return lax.ppermute(array, ('section', 'dp'), pairs)  11.2 us
    ppermute x4, starting transfers between devices, pair_on_device(): lax.ppermute(other, ('section', 'dp'), [(s * count + d, s * count + 4 * r...  7.79 us
    pallas_call x14, Pallas kernels, local(): pl.pallas_call(kernel, in_specs=[pl.BlockSpec(memory_space=spaces[kind])...  7.16 us
    ppermute x10, waiting for transfers between devices, swapped(): return lax.ppermute(array, ('section', 'dp'), pairs)  5.4 us
    ppermute x4, waiting for transfers between devices, pair_on_device(): lax.ppermute(other, ('section', 'dp'), [(s * count + d, s * count + 4 * r...  1.56 us
  transfers between devices with their start and end apart: 14, of which 7 were waited for; matrix products, arithmetic and copies ran while one was open for 0% of the time, Pallas kernels for 16%

profile of v17, /device:TPU:0, one launch (start us, length us, event | category | flops | bytes accessed | tf_op | source)
XLA Modules:
  0.0 34.0 jit_solution(6691081637534140904)
XLA Ops:
  0.6 0.8 %pick.1 = bf16[32,2048]{1,0:T(8,128)(2,1)S(1)} custom-call(s32[1]{0:T(128)} %bitcast.1.place_ref, s32[1]{0:T(128)} %bitcast.index_ref, bf16[1,2,32,4096]{3,2,1,0:T(8,128)(2,1)} %w_out.3), custom_call_target="tpu_custom_call" | custom-call | tf_op jit(solution)/shard_map/pick/pallas_call | solution.py:283
  1.5 3.0 %collective-permute-start = (bf16[32,2048]{1,0:T(8,128)(2,1)S(1)}, bf16[32,2048]{1,0:T(8,128)(2,1)S(1)}, u32[]{:S(2)}, u32[]{:S(2)}) collective-permute-start(bf16[32,2048]{1,0:T(8,128)(2,1)S(1)} %pick.1), channel_id=1, source_target_pairs={{0,16},{1,17},{2,18},{3,19},{4,20},{5,21},{6,22},{7,23},{8,24},{9,... | collective-permute-start | bytes 393224 | tf_op jit(solution)/shard_map/ppermute | solution.py:319
  4.5 2.2 %front.1 = (bf16[32,128]{1,0:T(8,128)(2,1)S(1)}, f32[2,32,128]{2,1,0:T(8,128)S(1)}, bf16[128,4096]{1,0:T(8,128)(2,1)S(1)}, bf16[128,4096]{1,0:T(8,128)(2,1)S(1)}...) custom-call(s32[1]{0:T(128)} %bitcast.1.place_ref, ...), custom_call_target="tpu_custom_call" | custom-call | tf_op jit(solution)/shard_map/front/pallas_call | solution.py:283
  6.7 0.1 collective-permute-start.1
  6.8 0.9 %upper.1 = (bf16[128,4096]{1,0:T(8,128)(2,1)S(1)}, bf16[32,128]{1,0:T(8,128)(2,1)S(1)}, bf16[32,128]{1,0:T(8,128)(2,1)S(1)}, bf16[32,128]{1,0:T(8,128)(2,1)S(1)}, f32[2,128,128]{2,1,0:T(8,128)S(1)}) custom-call(bf16[128,4096]{1,0:T(8,128)(2,1)S(1)} %get-tuple-element.38.x, bf16[128,4096]{1,0:T(8,128)(2,1)S(1)} %get-tuple-element.39.g, ...), custom_call_target="tpu_custom_call" | custom-call | tf_op jit(solution)/shard_map/upper/pallas_call | solution.py:283
  7.8 0.2 collective-permute-done.own_ref
  8.0 0.0 collective-permute-start.2
  8.0 0.7 %outgoing.1.flow_ref = bf16[128,4096]{1,0:T(8,128)(2,1)S(1)} custom-call(bf16[128,4096]{1,0:T(8,128)(2,1)S(1)} %get-tuple-element.38.x, bf16[128,4096]{1,0:T(8,128)(2,1)S(1)} %get-tuple-element.39.g, f32[1,4096]{1,0:T(1,128)S(1)} %get-tuple-element.40.gain, bf16[32,4096]{1,0:T(8,128)(2,1)S(1)} %get-tuple-element.41.wi, ...), custom_call_target="tpu_custom_call" | custom-call | flops 20000000000 | bytes 1048576 | tf_op jit(solution)/shard_map/outgoing/pallas_call | solution.py:283
  8.7 0.3 flow.1.part_ref
  9.0 0.3 collective-permute-done.2.other_ref
  9.3 0.3 flow_rest.1._
  9.6 1.9 %collective-permute-start.4 = (bf16[32,128]{1,0:T(8,128)(2,1)S(1)}, bf16[32,128]{1,0:T(8,128)(2,1)S(1)}, u32[]{:S(2)}, u32[]{:S(2)}) collective-permute-start(bf16[32,128]{1,0:T(8,128)(2,1)S(1)} %flow_rest.1._), channel_id=1, source_target_pairs={{0,16},{1,17},{2,18},{3,19},{4,20},{5,21},{6,22},{7,23},{8,24},{9,... | collective-permute-start | bytes 24584 | tf_op jit(solution)/shard_map/ppermute | solution.py:319
  11.5 0.4 %terms1.1 = (bf16[8,32,256]{2,1,0:T(8,128)(2,1)S(1)}, bf16[8,32,256]{2,1,0:T(8,128)(2,1)S(1)}, bf16[8,32,256]{2,1,0:T(8,128)(2,1)S(1)}, bf16[8,32,256]{2,1,0:T(8,128)(2,1)S(1)}) custom-call(s32[1]{0:T(128)} %bitcast.index_ref, bf16[128,4096]{1,0:T(8,128)(2,1)S(1)} %get-tuple-element.39.g, bf16[128,4096]{1,0:T(8,128)(2,1)S(1)} %get-tuple-element.47.xg_ref, ...), custom_call_target="tpu_custom_call" | custom-call | tf_op jit(solution)/shard_map/terms1/pallas_call | solution.py:283
  12.0 0.0 collective-permute-done.1.act0_ref
  12.0 0.3 terms.1
  12.3 0.1 collective-permute-start.3
  12.3 1.0 %collective-permute-done.4.got_ref = bf16[32,128]{1,0:T(8,128)(2,1)S(1)} collective-permute-done((bf16[32,128]{1,0:T(8,128)(2,1)S(1)}, bf16[32,128]{1,0:T(8,128)(2,1)S(1)}, u32[]{:S(2)}, u32[]{:S(2)}) %collective-permute-start.4) | collective-permute-done | bytes 8224 | tf_op jit(solution)/shard_map/ppermute | solution.py:319
  13.3 0.3 lower.1
  13.6 0.1 collective-permute-start.5
  13.7 0.3 %collective-permute-done.3.got = bf16[24,32,256]{2,1,0:T(8,128)(2,1)S(1)} collective-permute-done((bf16[24,32,256]{2,1,0:T(8,128)(2,1)S(1)}, bf16[24,32,256]{2,1,0:T(8,128)(2,1)S(1)}, u32[]{:S(2)}, u32[]{:S(2)}) %collective-permute-start.3) | collective-permute-done | bytes 393248 | tf_op jit(solution)/shard_map/ppermute | solution.py:319
  14.0 0.1 chip.1
  14.1 2.5 %collective-permute-start.6 = (bf16[4,32,256]{2,1,0:T(8,128)(2,1)S(1)}, bf16[4,32,256]{2,1,0:T(8,128)(2,1)S(1)}, u32[]{:S(2)}, u32[]{:S(2)}) collective-permute-start(bf16[4,32,256]{2,1,0:T(8,128)(2,1)S(1)} %get-tuple-element.63), channel_id=1, source_target_pairs={{0,18},{1,19},{2,16},{3,17},{4,22},{5,23},{6,20},{7,21},{8,26},{9,... | collective-permute-start | bytes 196616 | tf_op jit(solution)/shard_map/ppermute | solution.py:319
  16.7 0.0 collective-permute-done.5.got0
  16.7 0.1 plane.1
  16.8 0.6 %collective-permute-start.7 = (bf16[4,64,256]{2,1,0:T(8,128)(2,1)S(1)}, bf16[4,64,256]{2,1,0:T(8,128)(2,1)S(1)}, u32[]{:S(2)}, u32[]{:S(2)}) collective-permute-start(bf16[4,64,256]{2,1,0:T(8,128)(2,1)S(1)} %get-tuple-element.64), channel_id=1, source_target_pairs={{0,16},{1,17},{2,18},{3,1},{4,20},{5,21},{6,22},{7,5},{8,24},{9,25... | collective-permute-start | bytes 393224 | tf_op jit(solution)/shard_map/ppermute | solution.py:319
  17.3 1.2 %collective-permute-start.9 = (bf16[4,64,256]{2,1,0:T(8,128)(2,1)S(1)}, bf16[4,64,256]{2,1,0:T(8,128)(2,1)S(1)}, u32[]{:S(2)}, u32[]{:S(2)}) collective-permute-start(bf16[4,64,256]{2,1,0:T(8,128)(2,1)S(1)} %get-tuple-element.66), channel_id=1, source_target_pairs={{0,2},{1,3},{2,0},{3,19},{4,6},{5,7},{6,4},{7,23},{8,10},{9,11},{1... | collective-permute-start | bytes 393224 | tf_op jit(solution)/shard_map/ppermute | solution.py:319
  18.5 1.8 %collective-permute-start.8 = (bf16[4,32,256]{2,1,0:T(8,128)(2,1)S(1)}, bf16[4,32,256]{2,1,0:T(8,128)(2,1)S(1)}, u32[]{:S(2)}, u32[]{:S(2)}) collective-permute-start(bf16[4,32,256]{2,1,0:T(8,128)(2,1)S(1)} %get-tuple-element.65), channel_id=1, source_target_pairs={{0,18},{1,19},{2,16},{3,17},{4,22},{5,23},{6,20},{7,21},{8,26},{9,... | collective-permute-start | bytes 196616 | tf_op jit(solution)/shard_map/ppermute | solution.py:319
  20.3 0.0 collective-permute-done.6.across_out
  20.3 3.5 %collective-permute-done.8.across_in = bf16[4,32,256]{2,1,0:T(8,128)(2,1)S(1)} collective-permute-done((bf16[4,32,256]{2,1,0:T(8,128)(2,1)S(1)}, bf16[4,32,256]{2,1,0:T(8,128)(2,1)S(1)}, u32[]{:S(2)}, u32[]{:S(2)}) %collective-permute-start.8) | collective-permute-done | bytes 65568 | tf_op jit(solution)/shard_map/ppermute | solution.py:319
  23.8 0.0 collective-permute-done.7.first
  23.8 0.0 collective-permute-done.9.second
  23.8 0.1 layer.1
  23.9 1.3 %collective-permute-start.10 = (bf16[64,256]{1,0:T(8,128)(2,1)S(1)}, bf16[64,256]{1,0:T(8,128)(2,1)S(1)}, u32[]{:S(2)}, u32[]{:S(2)}) collective-permute-start(bf16[64,256]{1,0:T(8,128)(2,1)S(1)} %get-tuple-element.68), channel_id=1, source_target_pairs={{12,0},{13,1},{14,2},{15,3},{28,16},{29,17},{30,18},{31,19}} | collective-permute-start | bytes 98312 | tf_op jit(solution)/shard_map/ppermute | solution.py:397
  25.2 1.1 %collective-permute-start.11 = (bf16[64,256]{1,0:T(8,128)(2,1)S(1)}, bf16[64,256]{1,0:T(8,128)(2,1)S(1)}, u32[]{:S(2)}, u32[]{:S(2)}) collective-permute-start(bf16[64,256]{1,0:T(8,128)(2,1)S(1)} %get-tuple-element.69), channel_id=1, source_target_pairs={{0,4},{1,5},{2,6},{3,7},{4,0},{5,1},{6,2},{7,3},{8,12},{9,13},{10,... | collective-permute-start | bytes 98312 | tf_op jit(solution)/shard_map/ppermute | solution.py:397
  26.3 4.0 %collective-permute-start.12 = (bf16[64,256]{1,0:T(8,128)(2,1)S(1)}, bf16[64,256]{1,0:T(8,128)(2,1)S(1)}, u32[]{:S(2)}, u32[]{:S(2)}) collective-permute-start(bf16[64,256]{1,0:T(8,128)(2,1)S(1)} %get-tuple-element.70), channel_id=1, source_target_pairs={{0,8},{1,9},{2,10},{3,11},{4,12},{5,13},{6,14},{7,15},{8,0},{9,1},... | collective-permute-start | bytes 98312 | tf_op jit(solution)/shard_map/ppermute | solution.py:397
  30.3 1.4 %collective-permute-start.13 = (bf16[64,256]{1,0:T(8,128)(2,1)S(1)}, bf16[64,256]{1,0:T(8,128)(2,1)S(1)}, u32[]{:S(2)}, u32[]{:S(2)}) collective-permute-start(bf16[64,256]{1,0:T(8,128)(2,1)S(1)} %get-tuple-element.71), channel_id=1, source_target_pairs={{0,12},{1,13},{2,14},{3,15},{4,8},{5,9},{6,10},{7,11},{8,4},{9,5},... | collective-permute-start | bytes 98312 | tf_op jit(solution)/shard_map/ppermute | solution.py:397
  31.7 0.0 collective-permute-done.10.refs_1_
  31.7 0.0 collective-permute-done.11.refs_2_
  31.7 0.8 %collective-permute-done.12.refs_3_ = bf16[64,256]{1,0:T(8,128)(2,1)S(1)} collective-permute-done((bf16[64,256]{1,0:T(8,128)(2,1)S(1)}, bf16[64,256]{1,0:T(8,128)(2,1)S(1)}, u32[]{:S(2)}, u32[]{:S(2)}) %collective-permute-start.12) | collective-permute-done | bytes 32800 | tf_op jit(solution)/shard_map/ppermute | solution.py:397
  32.5 0.8 %collective-permute-done.13.refs_4_ = bf16[64,256]{1,0:T(8,128)(2,1)S(1)} collective-permute-done((bf16[64,256]{1,0:T(8,128)(2,1)S(1)}, bf16[64,256]{1,0:T(8,128)(2,1)S(1)}, u32[]{:S(2)}, u32[]{:S(2)}) %collective-permute-start.13) | collective-permute-done | bytes 32800 | tf_op jit(solution)/shard_map/ppermute | solution.py:397
  33.3 0.7 %total.1 = (f32[1,32,256]{2,1,0:T(8,128)}, f32[1,32,256]{2,1,0:T(8,128)}) custom-call(bf16[64,256]{1,0:T(8,128)(2,1)S(1)} %get-tuple-element.67.refs_0_, bf16[64,256]{1,0:T(8,128)(2,1)S(1)} %collective-permute-done.10.refs_1_, bf16[64,256]{1,0:T(8,128)(2,1)S(1)} %collective-permute-done.11.refs_2_, bf16[64,256]{1,0:T(8,128)(2,1)S(1)} %collective-permute-done.12.refs_3_, ...), custom_call_target="tpu_custom_call" | custom-call | tf_op jit(solution)/shard_map/total/pallas_call | solution.py:283
  (1 shorter events, 0.0 us)
Async XLA Ops:
  1.5 6.5 %collective-permute-start = (bf16[32,2048]{1,0:T(8,128)(2,1)S(1)}, bf16[32,2048]{1,0:T(8,128)(2,1)S(1)}, u32[]{:S(2)}, u32[]{:S(2)}) collective-permute-start(bf16[32,2048]{1,0:T(8,128)(2,1)S(1)} %pick.1), channel_id=1, source_target_pairs={{0,16},{1,17},{2,18},{3,19},{4,20},{5,21},{6,22},{7,23},{8,24},{9,... | collective-permute-start | bytes 393224 | tf_op jit(solution)/shard_map/ppermute | solution.py:319
  6.7 5.2 %collective-permute-start.1 = (bf16[32,128]{1,0:T(8,128)(2,1)S(1)}, bf16[32,128]{1,0:T(8,128)(2,1)S(1)}, u32[]{:S(2)}, u32[]{:S(2)}) collective-permute-start(bf16[32,128]{1,0:T(8,128)(2,1)S(1)} %get-tuple-element.46), channel_id=1, source_target_pairs={{0,16},{1,17},{2,18},{3,19},{4,20},{5,21},{6,22},{7,23},{8,24},{9,... | collective-permute-start | bytes 24584 | tf_op jit(solution)/shard_map/ppermute | solution.py:319
  8.0 1.3 %collective-permute-start.2 = (bf16[32,2048]{1,0:T(8,128)(2,1)S(1)}, bf16[32,2048]{1,0:T(8,128)(2,1)S(1)}, u32[]{:S(2)}, u32[]{:S(2)}) collective-permute-start(bf16[32,2048]{1,0:T(8,128)(2,1)S(1)} %collective-permute-done.own_ref), channel_id=1, source_target_pairs={{0,1},{1,0},{2,3},{3,2},{4,5},{5,4},{6,7},{7,6},{8,9},{9,8},{10,11... | collective-permute-start | bytes 393224 | tf_op jit(solution)/shard_map/ppermute | solution.py:319
  9.6 3.7 %collective-permute-start.4 = (bf16[32,128]{1,0:T(8,128)(2,1)S(1)}, bf16[32,128]{1,0:T(8,128)(2,1)S(1)}, u32[]{:S(2)}, u32[]{:S(2)}) collective-permute-start(bf16[32,128]{1,0:T(8,128)(2,1)S(1)} %flow_rest.1._), channel_id=1, source_target_pairs={{0,16},{1,17},{2,18},{3,19},{4,20},{5,21},{6,22},{7,23},{8,24},{9,... | collective-permute-start | bytes 24584 | tf_op jit(solution)/shard_map/ppermute | solution.py:319
  12.3 1.8 %collective-permute-start.3 = (bf16[24,32,256]{2,1,0:T(8,128)(2,1)S(1)}, bf16[24,32,256]{2,1,0:T(8,128)(2,1)S(1)}, u32[]{:S(2)}, u32[]{:S(2)}) collective-permute-start(bf16[24,32,256]{2,1,0:T(8,128)(2,1)S(1)} %get-tuple-element.56), channel_id=1, source_target_pairs={{0,1},{1,0},{2,3},{3,2},{4,5},{5,4},{6,7},{7,6},{8,9},{9,8},{10,11... | collective-permute-start | bytes 1179656 | tf_op jit(solution)/shard_map/ppermute | solution.py:319
  13.6 3.1 %collective-permute-start.5 = (bf16[8,32,256]{2,1,0:T(8,128)(2,1)S(1)}, bf16[8,32,256]{2,1,0:T(8,128)(2,1)S(1)}, u32[]{:S(2)}, u32[]{:S(2)}) collective-permute-start(bf16[8,32,256]{2,1,0:T(8,128)(2,1)S(1)} %get-tuple-element.61), channel_id=1, source_target_pairs={{0,1},{1,0},{2,3},{3,2},{4,5},{5,4},{6,7},{7,6},{8,9},{9,8},{10,11... | collective-permute-start | bytes 393224 | tf_op jit(solution)/shard_map/ppermute | solution.py:319
  14.1 6.2 %collective-permute-start.6 = (bf16[4,32,256]{2,1,0:T(8,128)(2,1)S(1)}, bf16[4,32,256]{2,1,0:T(8,128)(2,1)S(1)}, u32[]{:S(2)}, u32[]{:S(2)}) collective-permute-start(bf16[4,32,256]{2,1,0:T(8,128)(2,1)S(1)} %get-tuple-element.63), channel_id=1, source_target_pairs={{0,18},{1,19},{2,16},{3,17},{4,22},{5,23},{6,20},{7,21},{8,26},{9,... | collective-permute-start | bytes 196616 | tf_op jit(solution)/shard_map/ppermute | solution.py:319
  16.8 7.1 %collective-permute-start.7 = (bf16[4,64,256]{2,1,0:T(8,128)(2,1)S(1)}, bf16[4,64,256]{2,1,0:T(8,128)(2,1)S(1)}, u32[]{:S(2)}, u32[]{:S(2)}) collective-permute-start(bf16[4,64,256]{2,1,0:T(8,128)(2,1)S(1)} %get-tuple-element.64), channel_id=1, source_target_pairs={{0,16},{1,17},{2,18},{3,1},{4,20},{5,21},{6,22},{7,5},{8,24},{9,25... | collective-permute-start | bytes 393224 | tf_op jit(solution)/shard_map/ppermute | solution.py:319
  17.3 6.5 %collective-permute-start.9 = (bf16[4,64,256]{2,1,0:T(8,128)(2,1)S(1)}, bf16[4,64,256]{2,1,0:T(8,128)(2,1)S(1)}, u32[]{:S(2)}, u32[]{:S(2)}) collective-permute-start(bf16[4,64,256]{2,1,0:T(8,128)(2,1)S(1)} %get-tuple-element.66), channel_id=1, source_target_pairs={{0,2},{1,3},{2,0},{3,19},{4,6},{5,7},{6,4},{7,23},{8,10},{9,11},{1... | collective-permute-start | bytes 393224 | tf_op jit(solution)/shard_map/ppermute | solution.py:319
  18.5 5.3 %collective-permute-start.8 = (bf16[4,32,256]{2,1,0:T(8,128)(2,1)S(1)}, bf16[4,32,256]{2,1,0:T(8,128)(2,1)S(1)}, u32[]{:S(2)}, u32[]{:S(2)}) collective-permute-start(bf16[4,32,256]{2,1,0:T(8,128)(2,1)S(1)} %get-tuple-element.65), channel_id=1, source_target_pairs={{0,18},{1,19},{2,16},{3,17},{4,22},{5,23},{6,20},{7,21},{8,26},{9,... | collective-permute-start | bytes 196616 | tf_op jit(solution)/shard_map/ppermute | solution.py:319
  23.9 7.8 %collective-permute-start.10 = (bf16[64,256]{1,0:T(8,128)(2,1)S(1)}, bf16[64,256]{1,0:T(8,128)(2,1)S(1)}, u32[]{:S(2)}, u32[]{:S(2)}) collective-permute-start(bf16[64,256]{1,0:T(8,128)(2,1)S(1)} %get-tuple-element.68), channel_id=1, source_target_pairs={{12,0},{13,1},{14,2},{15,3},{28,16},{29,17},{30,18},{31,19}} | collective-permute-start | bytes 98312 | tf_op jit(solution)/shard_map/ppermute | solution.py:397
  25.2 6.5 %collective-permute-start.11 = (bf16[64,256]{1,0:T(8,128)(2,1)S(1)}, bf16[64,256]{1,0:T(8,128)(2,1)S(1)}, u32[]{:S(2)}, u32[]{:S(2)}) collective-permute-start(bf16[64,256]{1,0:T(8,128)(2,1)S(1)} %get-tuple-element.69), channel_id=1, source_target_pairs={{0,4},{1,5},{2,6},{3,7},{4,0},{5,1},{6,2},{7,3},{8,12},{9,13},{10,... | collective-permute-start | bytes 98312 | tf_op jit(solution)/shard_map/ppermute | solution.py:397
  26.3 6.2 %collective-permute-start.12 = (bf16[64,256]{1,0:T(8,128)(2,1)S(1)}, bf16[64,256]{1,0:T(8,128)(2,1)S(1)}, u32[]{:S(2)}, u32[]{:S(2)}) collective-permute-start(bf16[64,256]{1,0:T(8,128)(2,1)S(1)} %get-tuple-element.70), channel_id=1, source_target_pairs={{0,8},{1,9},{2,10},{3,11},{4,12},{5,13},{6,14},{7,15},{8,0},{9,1},... | collective-permute-start | bytes 98312 | tf_op jit(solution)/shard_map/ppermute | solution.py:397
  30.3 3.0 %collective-permute-start.13 = (bf16[64,256]{1,0:T(8,128)(2,1)S(1)}, bf16[64,256]{1,0:T(8,128)(2,1)S(1)}, u32[]{:S(2)}, u32[]{:S(2)}) collective-permute-start(bf16[64,256]{1,0:T(8,128)(2,1)S(1)} %get-tuple-element.71), channel_id=1, source_target_pairs={{0,12},{1,13},{2,14},{3,15},{4,8},{5,9},{6,10},{7,11},{8,4},{9,5},... | collective-permute-start | bytes 98312 | tf_op jit(solution)/shard_map/ppermute | solution.py:397

commit v18 on v16

--- a/solution.py
+++ b/solution.py
@@ -252,15 +252,24 @@
 
 def layer_routes(layers):
     if layers == 4:
-        return [[2, 3, 1, 0], [3, 2, 0, 1], [1, 0, 3, 2]]
-    return [[i ^ k for i in range(layers)] for k in range(1, layers)]
+        even = [[2, 3, 1, 0], [3, 2, 0, 1], [1, 0, 3, 2]]
+        odd = [[1, 3, 0, 2], [3, 2, 1, 0], [2, 0, 3, 1]]
+    else:
+        even = odd = [[i ^ k for i in range(layers)] for k in range(1, layers)]
+    return list(zip(even, odd))
 
 
 def layer_kernel(routes, index_ref, own, first, across_in, second, *out_refs):
     rank = across_in.shape[1]
     layer = index_ref[0] // 4
-    for route, out_ref in zip([range(len(out_refs)), *routes], out_refs):
-        block = sum(jnp.where(layer == i, target, 0) for i, target in enumerate(route))
+    core = index_ref[0] % 2
+    own_way = range(len(out_refs))
+    for ways, out_ref in zip([(own_way, own_way), *routes], out_refs):
+        block = sum(
+            jnp.where((layer == i) & (core == k), target, 0)
+            for k, route in enumerate(ways)
+            for i, target in enumerate(route)
+        )
         total = sum(ref[block].astype(F32) for ref in (own, first, second))
         out_ref[0:rank] = (total[0:rank] + across_in[block].astype(F32)).astype(BF16)
         out_ref[rank : 2 * rank] = total[rank : 2 * rank].astype(BF16)
@@ -398,12 +407,12 @@
             other,
             ("section", "dp"),
             [
-                (s * count + d, s * count + 4 * route[d // 4] + d % 4)
+                (s * count + d, s * count + 4 * ways[d % 2][d // 4] + d % 4)
                 for s in range(2)
                 for d in range(count)
             ],
         )
-        for route, other in zip(routes, others)
+        for ways, other in zip(routes, others)
     ]
     block = ((1, rank, share), F32)
     total_in, total_out = local(

time: 32.7 us -> 32.7 us (level)
  no operation moved by 1% of the time
where the time goes in v18:
time: 32.7 us; the launch traced here: 32.5 us
  starting transfers between devices  15.1 us (46%)
  waiting for transfers between devices  9.5 us (29%)
  Pallas kernels  7.15 us (22%)
  between operations  0.76 us (2%)
    ppermute x10, starting transfers between devices, swapped(): return lax.ppermute(array, ('section', 'dp'), pairs)  10.9 us
    pallas_call x14, Pallas kernels, local(): pl.pallas_call(kernel, in_specs=[pl.BlockSpec(memory_space=spaces[kind])...  7.15 us
    ppermute x10, waiting for transfers between devices, swapped(): return lax.ppermute(array, ('section', 'dp'), pairs)  5.91 us
    ppermute x3, starting transfers between devices, pair_on_device(): lax.ppermute(other, ('section', 'dp'), [(s * count + d, s * count + 4 * w...  4.22 us
    ppermute x3, waiting for transfers between devices, pair_on_device(): lax.ppermute(other, ('section', 'dp'), [(s * count + d, s * count + 4 * w...  3.58 us
  transfers between devices with their start and end apart: 13, of which 8 were waited for; matrix products, arithmetic and copies ran while one was open for 0% of the time, Pallas kernels for 17%

profile of v18, /device:TPU:0, one launch (start us, length us, event | category | flops | bytes accessed | tf_op | source)
XLA Modules:
  0.0 32.5 jit_solution(1141082698945436919)
XLA Ops:
  0.6 0.8 %pick.1 = bf16[32,2048]{1,0:T(8,128)(2,1)S(1)} custom-call(s32[1]{0:T(128)} %bitcast.1.place_ref, s32[1]{0:T(128)} %bitcast.index_ref, bf16[1,2,32,4096]{3,2,1,0:T(8,128)(2,1)} %w_out.3), custom_call_target="tpu_custom_call" | custom-call | tf_op jit(solution)/shard_map/pick/pallas_call | solution.py:292
  1.5 3.0 %collective-permute-start = (bf16[32,2048]{1,0:T(8,128)(2,1)S(1)}, bf16[32,2048]{1,0:T(8,128)(2,1)S(1)}, u32[]{:S(2)}, u32[]{:S(2)}) collective-permute-start(bf16[32,2048]{1,0:T(8,128)(2,1)S(1)} %pick.1), channel_id=1, source_target_pairs={{0,16},{1,17},{2,18},{3,19},{4,20},{5,21},{6,22},{7,23},{8,24},{9,... | collective-permute-start | bytes 393224 | tf_op jit(solution)/shard_map/ppermute | solution.py:328
  4.5 2.2 %front.1 = (bf16[32,128]{1,0:T(8,128)(2,1)S(1)}, f32[2,32,128]{2,1,0:T(8,128)S(1)}, bf16[128,4096]{1,0:T(8,128)(2,1)S(1)}, bf16[128,4096]{1,0:T(8,128)(2,1)S(1)}...) custom-call(s32[1]{0:T(128)} %bitcast.1.place_ref, ...), custom_call_target="tpu_custom_call" | custom-call | tf_op jit(solution)/shard_map/front/pallas_call | solution.py:292
  6.7 0.1 collective-permute-start.1
  6.8 0.9 %upper.1 = (bf16[128,4096]{1,0:T(8,128)(2,1)S(1)}, bf16[32,128]{1,0:T(8,128)(2,1)S(1)}, bf16[32,128]{1,0:T(8,128)(2,1)S(1)}, bf16[32,128]{1,0:T(8,128)(2,1)S(1)}, f32[2,128,128]{2,1,0:T(8,128)S(1)}) custom-call(bf16[128,4096]{1,0:T(8,128)(2,1)S(1)} %get-tuple-element.37.x, bf16[128,4096]{1,0:T(8,128)(2,1)S(1)} %get-tuple-element.38.g, ...), custom_call_target="tpu_custom_call" | custom-call | tf_op jit(solution)/shard_map/upper/pallas_call | solution.py:292
  7.8 0.2 collective-permute-done.own_ref
  8.0 0.0 collective-permute-start.2
  8.0 0.7 %outgoing.1.flow_ref = bf16[128,4096]{1,0:T(8,128)(2,1)S(1)} custom-call(bf16[128,4096]{1,0:T(8,128)(2,1)S(1)} %get-tuple-element.37.x, bf16[128,4096]{1,0:T(8,128)(2,1)S(1)} %get-tuple-element.38.g, f32[1,4096]{1,0:T(1,128)S(1)} %get-tuple-element.39.gain, bf16[32,4096]{1,0:T(8,128)(2,1)S(1)} %get-tuple-element.40.wi, ...), custom_call_target="tpu_custom_call" | custom-call | flops 20000000000 | bytes 1048576 | tf_op jit(solution)/shard_map/outgoing/pallas_call | solution.py:292
  8.7 0.3 flow.1.part_ref
  9.0 0.3 collective-permute-done.2.other_ref
  9.3 0.3 flow_rest.1._
  9.6 1.9 %collective-permute-start.4 = (bf16[32,128]{1,0:T(8,128)(2,1)S(1)}, bf16[32,128]{1,0:T(8,128)(2,1)S(1)}, u32[]{:S(2)}, u32[]{:S(2)}) collective-permute-start(bf16[32,128]{1,0:T(8,128)(2,1)S(1)} %flow_rest.1._), channel_id=1, source_target_pairs={{0,16},{1,17},{2,18},{3,19},{4,20},{5,21},{6,22},{7,23},{8,24},{9,... | collective-permute-start | bytes 24584 | tf_op jit(solution)/shard_map/ppermute | solution.py:328
  11.5 0.4 %terms1.1 = (bf16[8,32,256]{2,1,0:T(8,128)(2,1)S(1)}, bf16[8,32,256]{2,1,0:T(8,128)(2,1)S(1)}, bf16[8,32,256]{2,1,0:T(8,128)(2,1)S(1)}, bf16[8,32,256]{2,1,0:T(8,128)(2,1)S(1)}) custom-call(s32[1]{0:T(128)} %bitcast.index_ref, bf16[128,4096]{1,0:T(8,128)(2,1)S(1)} %get-tuple-element.38.g, bf16[128,4096]{1,0:T(8,128)(2,1)S(1)} %get-tuple-element.46.xg_ref, ...), custom_call_target="tpu_custom_call" | custom-call | tf_op jit(solution)/shard_map/terms1/pallas_call | solution.py:292
  12.0 0.0 collective-permute-done.1.act0_ref
  12.0 0.3 terms.1
  12.3 0.1 collective-permute-start.3
  12.3 1.0 %collective-permute-done.4.got_ref = bf16[32,128]{1,0:T(8,128)(2,1)S(1)} collective-permute-done((bf16[32,128]{1,0:T(8,128)(2,1)S(1)}, bf16[32,128]{1,0:T(8,128)(2,1)S(1)}, u32[]{:S(2)}, u32[]{:S(2)}) %collective-permute-start.4) | collective-permute-done | bytes 8224 | tf_op jit(solution)/shard_map/ppermute | solution.py:328
  13.3 0.3 lower.1
  13.6 0.1 collective-permute-start.5
  13.7 0.3 %collective-permute-done.3.got = bf16[24,32,256]{2,1,0:T(8,128)(2,1)S(1)} collective-permute-done((bf16[24,32,256]{2,1,0:T(8,128)(2,1)S(1)}, bf16[24,32,256]{2,1,0:T(8,128)(2,1)S(1)}, u32[]{:S(2)}, u32[]{:S(2)}) %collective-permute-start.3) | collective-permute-done | bytes 393248 | tf_op jit(solution)/shard_map/ppermute | solution.py:328
  14.0 0.1 chip.1
  14.1 2.5 %collective-permute-start.6 = (bf16[4,32,256]{2,1,0:T(8,128)(2,1)S(1)}, bf16[4,32,256]{2,1,0:T(8,128)(2,1)S(1)}, u32[]{:S(2)}, u32[]{:S(2)}) collective-permute-start(bf16[4,32,256]{2,1,0:T(8,128)(2,1)S(1)} %get-tuple-element.62), channel_id=1, source_target_pairs={{0,18},{1,19},{2,16},{3,17},{4,22},{5,23},{6,20},{7,21},{8,26},{9,... | collective-permute-start | bytes 196616 | tf_op jit(solution)/shard_map/ppermute | solution.py:328
  16.7 0.0 collective-permute-done.5.got0
  16.7 0.1 plane.1
  16.8 0.6 %collective-permute-start.7 = (bf16[4,64,256]{2,1,0:T(8,128)(2,1)S(1)}, bf16[4,64,256]{2,1,0:T(8,128)(2,1)S(1)}, u32[]{:S(2)}, u32[]{:S(2)}) collective-permute-start(bf16[4,64,256]{2,1,0:T(8,128)(2,1)S(1)} %get-tuple-element.63), channel_id=1, source_target_pairs={{0,16},{1,17},{2,0},{3,1},{4,20},{5,21},{6,4},{7,5},{8,24},{9,25},... | collective-permute-start | bytes 393224 | tf_op jit(solution)/shard_map/ppermute | solution.py:328
  17.3 1.5 %collective-permute-start.9 = (bf16[4,64,256]{2,1,0:T(8,128)(2,1)S(1)}, bf16[4,64,256]{2,1,0:T(8,128)(2,1)S(1)}, u32[]{:S(2)}, u32[]{:S(2)}) collective-permute-start(bf16[4,64,256]{2,1,0:T(8,128)(2,1)S(1)} %get-tuple-element.65), channel_id=1, source_target_pairs={{0,2},{1,3},{2,18},{3,19},{4,6},{5,7},{6,22},{7,23},{8,10},{9,11},... | collective-permute-start | bytes 393224 | tf_op jit(solution)/shard_map/ppermute | solution.py:328
  18.8 1.1 %collective-permute-start.8 = (bf16[4,32,256]{2,1,0:T(8,128)(2,1)S(1)}, bf16[4,32,256]{2,1,0:T(8,128)(2,1)S(1)}, u32[]{:S(2)}, u32[]{:S(2)}) collective-permute-start(bf16[4,32,256]{2,1,0:T(8,128)(2,1)S(1)} %get-tuple-element.64), channel_id=1, source_target_pairs={{0,18},{1,19},{2,16},{3,17},{4,22},{5,23},{6,20},{7,21},{8,26},{9,... | collective-permute-start | bytes 196616 | tf_op jit(solution)/shard_map/ppermute | solution.py:328
  20.0 0.0 collective-permute-done.6.across_out
  20.0 4.0 %collective-permute-done.8.across_in = bf16[4,32,256]{2,1,0:T(8,128)(2,1)S(1)} collective-permute-done((bf16[4,32,256]{2,1,0:T(8,128)(2,1)S(1)}, bf16[4,32,256]{2,1,0:T(8,128)(2,1)S(1)}, u32[]{:S(2)}, u32[]{:S(2)}) %collective-permute-start.8) | collective-permute-done | bytes 65568 | tf_op jit(solution)/shard_map/ppermute | solution.py:328
  24.0 0.0 collective-permute-done.7.first
  24.0 0.0 collective-permute-done.9.second
  24.0 0.1 layer.1
  24.1 2.6 %collective-permute-start.10 = (bf16[64,256]{1,0:T(8,128)(2,1)S(1)}, bf16[64,256]{1,0:T(8,128)(2,1)S(1)}, u32[]{:S(2)}, u32[]{:S(2)}) collective-permute-start(bf16[64,256]{1,0:T(8,128)(2,1)S(1)} %get-tuple-element.67), channel_id=1, source_target_pairs={{0,8},{1,5},{2,10},{3,7},{4,12},{5,13},{6,14},{7,15},{8,4},{9,1},{... | collective-permute-start | bytes 98312 | tf_op jit(solution)/shard_map/ppermute | solution.py:406
  26.7 1.2 %collective-permute-start.11 = (bf16[64,256]{1,0:T(8,128)(2,1)S(1)}, bf16[64,256]{1,0:T(8,128)(2,1)S(1)}, u32[]{:S(2)}, u32[]{:S(2)}) collective-permute-start(bf16[64,256]{1,0:T(8,128)(2,1)S(1)} %get-tuple-element.68), channel_id=1, source_target_pairs={{0,12},{1,13},{2,14},{3,15},{4,8},{5,9},{6,10},{7,11},{8,0},{9,5},... | collective-permute-start | bytes 98312 | tf_op jit(solution)/shard_map/ppermute | solution.py:406
  28.0 0.3 %collective-permute-start.12 = (bf16[64,256]{1,0:T(8,128)(2,1)S(1)}, bf16[64,256]{1,0:T(8,128)(2,1)S(1)}, u32[]{:S(2)}, u32[]{:S(2)}) collective-permute-start(bf16[64,256]{1,0:T(8,128)(2,1)S(1)} %get-tuple-element.69), channel_id=1, source_target_pairs={{0,4},{1,9},{2,6},{3,11},{4,0},{5,1},{6,2},{7,3},{8,12},{9,13},{10... | collective-permute-start | bytes 98312 | tf_op jit(solution)/shard_map/ppermute | solution.py:406
  28.3 1.6 %collective-permute-done.10.refs_1_ = bf16[64,256]{1,0:T(8,128)(2,1)S(1)} collective-permute-done((bf16[64,256]{1,0:T(8,128)(2,1)S(1)}, bf16[64,256]{1,0:T(8,128)(2,1)S(1)}, u32[]{:S(2)}, u32[]{:S(2)}) %collective-permute-start.10) | collective-permute-done | bytes 32800 | tf_op jit(solution)/shard_map/ppermute | solution.py:406
  29.9 1.7 %collective-permute-done.11.refs_2_ = bf16[64,256]{1,0:T(8,128)(2,1)S(1)} collective-permute-done((bf16[64,256]{1,0:T(8,128)(2,1)S(1)}, bf16[64,256]{1,0:T(8,128)(2,1)S(1)}, u32[]{:S(2)}, u32[]{:S(2)}) %collective-permute-start.11) | collective-permute-done | bytes 32800 | tf_op jit(solution)/shard_map/ppermute | solution.py:406
  31.5 0.4 %collective-permute-done.12.refs_3_ = bf16[64,256]{1,0:T(8,128)(2,1)S(1)} collective-permute-done((bf16[64,256]{1,0:T(8,128)(2,1)S(1)}, bf16[64,256]{1,0:T(8,128)(2,1)S(1)}, u32[]{:S(2)}, u32[]{:S(2)}) %collective-permute-start.12) | collective-permute-done | bytes 32800 | tf_op jit(solution)/shard_map/ppermute | solution.py:406
  31.9 0.7 %total.1 = (f32[1,32,256]{2,1,0:T(8,128)}, f32[1,32,256]{2,1,0:T(8,128)}) custom-call(bf16[64,256]{1,0:T(8,128)(2,1)S(1)} %get-tuple-element.66.refs_0_, bf16[64,256]{1,0:T(8,128)(2,1)S(1)} %collective-permute-done.10.refs_1_, bf16[64,256]{1,0:T(8,128)(2,1)S(1)} %collective-permute-done.11.refs_2_, bf16[64,256]{1,0:T(8,128)(2,1)S(1)} %collective-permute-done.12.refs_3_), custom_call_target="tpu_custom_call" | custom-call | tf_op jit(solution)/shard_map/total/pallas_call | solution.py:292
  (1 shorter events, 0.0 us)
Async XLA Ops:
  1.5 6.5 %collective-permute-start = (bf16[32,2048]{1,0:T(8,128)(2,1)S(1)}, bf16[32,2048]{1,0:T(8,128)(2,1)S(1)}, u32[]{:S(2)}, u32[]{:S(2)}) collective-permute-start(bf16[32,2048]{1,0:T(8,128)(2,1)S(1)} %pick.1), channel_id=1, source_target_pairs={{0,16},{1,17},{2,18},{3,19},{4,20},{5,21},{6,22},{7,23},{8,24},{9,... | collective-permute-start | bytes 393224 | tf_op jit(solution)/shard_map/ppermute | solution.py:328
  6.7 5.2 %collective-permute-start.1 = (bf16[32,128]{1,0:T(8,128)(2,1)S(1)}, bf16[32,128]{1,0:T(8,128)(2,1)S(1)}, u32[]{:S(2)}, u32[]{:S(2)}) collective-permute-start(bf16[32,128]{1,0:T(8,128)(2,1)S(1)} %get-tuple-element.45), channel_id=1, source_target_pairs={{0,16},{1,17},{2,18},{3,19},{4,20},{5,21},{6,22},{7,23},{8,24},{9,... | collective-permute-start | bytes 24584 | tf_op jit(solution)/shard_map/ppermute | solution.py:328
  8.0 1.3 %collective-permute-start.2 = (bf16[32,2048]{1,0:T(8,128)(2,1)S(1)}, bf16[32,2048]{1,0:T(8,128)(2,1)S(1)}, u32[]{:S(2)}, u32[]{:S(2)}) collective-permute-start(bf16[32,2048]{1,0:T(8,128)(2,1)S(1)} %collective-permute-done.own_ref), channel_id=1, source_target_pairs={{0,1},{1,0},{2,3},{3,2},{4,5},{5,4},{6,7},{7,6},{8,9},{9,8},{10,11... | collective-permute-start | bytes 393224 | tf_op jit(solution)/shard_map/ppermute | solution.py:328
  9.6 3.7 %collective-permute-start.4 = (bf16[32,128]{1,0:T(8,128)(2,1)S(1)}, bf16[32,128]{1,0:T(8,128)(2,1)S(1)}, u32[]{:S(2)}, u32[]{:S(2)}) collective-permute-start(bf16[32,128]{1,0:T(8,128)(2,1)S(1)} %flow_rest.1._), channel_id=1, source_target_pairs={{0,16},{1,17},{2,18},{3,19},{4,20},{5,21},{6,22},{7,23},{8,24},{9,... | collective-permute-start | bytes 24584 | tf_op jit(solution)/shard_map/ppermute | solution.py:328
  12.3 1.8 %collective-permute-start.3 = (bf16[24,32,256]{2,1,0:T(8,128)(2,1)S(1)}, bf16[24,32,256]{2,1,0:T(8,128)(2,1)S(1)}, u32[]{:S(2)}, u32[]{:S(2)}) collective-permute-start(bf16[24,32,256]{2,1,0:T(8,128)(2,1)S(1)} %get-tuple-element.55), channel_id=1, source_target_pairs={{0,1},{1,0},{2,3},{3,2},{4,5},{5,4},{6,7},{7,6},{8,9},{9,8},{10,11... | collective-permute-start | bytes 1179656 | tf_op jit(solution)/shard_map/ppermute | solution.py:328
  13.6 3.1 %collective-permute-start.5 = (bf16[8,32,256]{2,1,0:T(8,128)(2,1)S(1)}, bf16[8,32,256]{2,1,0:T(8,128)(2,1)S(1)}, u32[]{:S(2)}, u32[]{:S(2)}) collective-permute-start(bf16[8,32,256]{2,1,0:T(8,128)(2,1)S(1)} %get-tuple-element.60), channel_id=1, source_target_pairs={{0,1},{1,0},{2,3},{3,2},{4,5},{5,4},{6,7},{7,6},{8,9},{9,8},{10,11... | collective-permute-start | bytes 393224 | tf_op jit(solution)/shard_map/ppermute | solution.py:328
  14.1 5.8 %collective-permute-start.6 = (bf16[4,32,256]{2,1,0:T(8,128)(2,1)S(1)}, bf16[4,32,256]{2,1,0:T(8,128)(2,1)S(1)}, u32[]{:S(2)}, u32[]{:S(2)}) collective-permute-start(bf16[4,32,256]{2,1,0:T(8,128)(2,1)S(1)} %get-tuple-element.62), channel_id=1, source_target_pairs={{0,18},{1,19},{2,16},{3,17},{4,22},{5,23},{6,20},{7,21},{8,26},{9,... | collective-permute-start | bytes 196616 | tf_op jit(solution)/shard_map/ppermute | solution.py:328
  16.8 7.2 %collective-permute-start.7 = (bf16[4,64,256]{2,1,0:T(8,128)(2,1)S(1)}, bf16[4,64,256]{2,1,0:T(8,128)(2,1)S(1)}, u32[]{:S(2)}, u32[]{:S(2)}) collective-permute-start(bf16[4,64,256]{2,1,0:T(8,128)(2,1)S(1)} %get-tuple-element.63), channel_id=1, source_target_pairs={{0,16},{1,17},{2,0},{3,1},{4,20},{5,21},{6,4},{7,5},{8,24},{9,25},... | collective-permute-start | bytes 393224 | tf_op jit(solution)/shard_map/ppermute | solution.py:328
  17.3 6.7 %collective-permute-start.9 = (bf16[4,64,256]{2,1,0:T(8,128)(2,1)S(1)}, bf16[4,64,256]{2,1,0:T(8,128)(2,1)S(1)}, u32[]{:S(2)}, u32[]{:S(2)}) collective-permute-start(bf16[4,64,256]{2,1,0:T(8,128)(2,1)S(1)} %get-tuple-element.65), channel_id=1, source_target_pairs={{0,2},{1,3},{2,18},{3,19},{4,6},{5,7},{6,22},{7,23},{8,10},{9,11},... | collective-permute-start | bytes 393224 | tf_op jit(solution)/shard_map/ppermute | solution.py:328
  18.8 5.2 %collective-permute-start.8 = (bf16[4,32,256]{2,1,0:T(8,128)(2,1)S(1)}, bf16[4,32,256]{2,1,0:T(8,128)(2,1)S(1)}, u32[]{:S(2)}, u32[]{:S(2)}) collective-permute-start(bf16[4,32,256]{2,1,0:T(8,128)(2,1)S(1)} %get-tuple-element.64), channel_id=1, source_target_pairs={{0,18},{1,19},{2,16},{3,17},{4,22},{5,23},{6,20},{7,21},{8,26},{9,... | collective-permute-start | bytes 196616 | tf_op jit(solution)/shard_map/ppermute | solution.py:328
  24.1 5.8 %collective-permute-start.10 = (bf16[64,256]{1,0:T(8,128)(2,1)S(1)}, bf16[64,256]{1,0:T(8,128)(2,1)S(1)}, u32[]{:S(2)}, u32[]{:S(2)}) collective-permute-start(bf16[64,256]{1,0:T(8,128)(2,1)S(1)} %get-tuple-element.67), channel_id=1, source_target_pairs={{0,8},{1,5},{2,10},{3,7},{4,12},{5,13},{6,14},{7,15},{8,4},{9,1},{... | collective-permute-start | bytes 98312 | tf_op jit(solution)/shard_map/ppermute | solution.py:406
  26.7 4.8 %collective-permute-start.11 = (bf16[64,256]{1,0:T(8,128)(2,1)S(1)}, bf16[64,256]{1,0:T(8,128)(2,1)S(1)}, u32[]{:S(2)}, u32[]{:S(2)}) collective-permute-start(bf16[64,256]{1,0:T(8,128)(2,1)S(1)} %get-tuple-element.68), channel_id=1, source_target_pairs={{0,12},{1,13},{2,14},{3,15},{4,8},{5,9},{6,10},{7,11},{8,0},{9,5},... | collective-permute-start | bytes 98312 | tf_op jit(solution)/shard_map/ppermute | solution.py:406
  28.0 3.9 %collective-permute-start.12 = (bf16[64,256]{1,0:T(8,128)(2,1)S(1)}, bf16[64,256]{1,0:T(8,128)(2,1)S(1)}, u32[]{:S(2)}, u32[]{:S(2)}) collective-permute-start(bf16[64,256]{1,0:T(8,128)(2,1)S(1)} %get-tuple-element.69), channel_id=1, source_target_pairs={{0,4},{1,9},{2,6},{3,11},{4,0},{5,1},{6,2},{7,3},{8,12},{9,13},{10... | collective-permute-start | bytes 98312 | tf_op jit(solution)/shard_map/ppermute | solution.py:406

commit v19 on v16

--- a/solution.py
+++ b/solution.py
@@ -39,7 +39,7 @@
     return sig, sig * (1.0 + pre * (1.0 - sig))
 
 
-PIECES = 4
+PIECES = 8
 
 
 def pieces(source, target, sems, first):

time: 32.7 us -> 32.9 us (level)
  transfers between devices with their start and end apart: 13 -> 13, of which waited for: 8 -> 8; matrix products, arithmetic and copies ran while one was open for 0% -> 0% of each run, Pallas kernels for 17% -> 18%
where the time goes in v19:
time: 32.9 us; the launch traced here: 32.7 us
  starting transfers between devices  15.3 us (47%)
  waiting for transfers between devices  9.34 us (28%)
  Pallas kernels  7.36 us (22%)
  between operations  0.77 us (2%)
    ppermute x10, starting transfers between devices, swapped(): return lax.ppermute(array, ('section', 'dp'), pairs)  11.1 us
    pallas_call x14, Pallas kernels, local(): pl.pallas_call(kernel, in_specs=[pl.BlockSpec(memory_space=spaces[kind])...  7.36 us
    ppermute x10, waiting for transfers between devices, swapped(): return lax.ppermute(array, ('section', 'dp'), pairs)  5.76 us
    ppermute x3, starting transfers between devices, pair_on_device(): lax.ppermute(other, ('section', 'dp'), [(s * count + d, s * count + 4 * r...  4.22 us
    ppermute x3, waiting for transfers between devices, pair_on_device(): lax.ppermute(other, ('section', 'dp'), [(s * count + d, s * count + 4 * r...  3.58 us
  transfers between devices with their start and end apart: 13, of which 8 were waited for; matrix products, arithmetic and copies ran while one was open for 0% of the time, Pallas kernels for 18%

profile of v19, /device:TPU:0, one launch (start us, length us, event | category | flops | bytes accessed | tf_op | source)
XLA Modules:
  0.0 32.7 jit_solution(16005808606383751314)
XLA Ops:
  0.6 0.9 %pick.1 = bf16[32,2048]{1,0:T(8,128)(2,1)S(1)} custom-call(s32[1]{0:T(128)} %bitcast.1.place_ref, s32[1]{0:T(128)} %bitcast.index_ref, bf16[1,2,32,4096]{3,2,1,0:T(8,128)(2,1)} %w_out.3), custom_call_target="tpu_custom_call" | custom-call | tf_op jit(solution)/shard_map/pick/pallas_call | solution.py:283
  1.6 3.0 %collective-permute-start = (bf16[32,2048]{1,0:T(8,128)(2,1)S(1)}, bf16[32,2048]{1,0:T(8,128)(2,1)S(1)}, u32[]{:S(2)}, u32[]{:S(2)}) collective-permute-start(bf16[32,2048]{1,0:T(8,128)(2,1)S(1)} %pick.1), channel_id=1, source_target_pairs={{0,16},{1,17},{2,18},{3,19},{4,20},{5,21},{6,22},{7,23},{8,24},{9,... | collective-permute-start | bytes 393224 | tf_op jit(solution)/shard_map/ppermute | solution.py:319
  4.6 2.4 %front.1 = (bf16[32,128]{1,0:T(8,128)(2,1)S(1)}, f32[2,32,128]{2,1,0:T(8,128)S(1)}, bf16[128,4096]{1,0:T(8,128)(2,1)S(1)}, bf16[128,4096]{1,0:T(8,128)(2,1)S(1)}...) custom-call(s32[1]{0:T(128)} %bitcast.1.place_ref, ...), custom_call_target="tpu_custom_call" | custom-call | tf_op jit(solution)/shard_map/front/pallas_call | solution.py:283
  7.0 0.1 collective-permute-start.1
  7.0 0.9 %upper.1 = (bf16[128,4096]{1,0:T(8,128)(2,1)S(1)}, bf16[32,128]{1,0:T(8,128)(2,1)S(1)}, bf16[32,128]{1,0:T(8,128)(2,1)S(1)}, bf16[32,128]{1,0:T(8,128)(2,1)S(1)}, f32[2,128,128]{2,1,0:T(8,128)S(1)}) custom-call(bf16[128,4096]{1,0:T(8,128)(2,1)S(1)} %get-tuple-element.37.x, bf16[128,4096]{1,0:T(8,128)(2,1)S(1)} %get-tuple-element.38.g, ...), custom_call_target="tpu_custom_call" | custom-call | tf_op jit(solution)/shard_map/upper/pallas_call | solution.py:283
  8.0 0.1 collective-permute-done.own_ref
  8.1 0.0 collective-permute-start.2
  8.1 0.7 %outgoing.1.flow_ref = bf16[128,4096]{1,0:T(8,128)(2,1)S(1)} custom-call(bf16[128,4096]{1,0:T(8,128)(2,1)S(1)} %get-tuple-element.37.x, bf16[128,4096]{1,0:T(8,128)(2,1)S(1)} %get-tuple-element.38.g, f32[1,4096]{1,0:T(1,128)S(1)} %get-tuple-element.39.gain, bf16[32,4096]{1,0:T(8,128)(2,1)S(1)} %get-tuple-element.40.wi, ...), custom_call_target="tpu_custom_call" | custom-call | flops 20000000000 | bytes 1048576 | tf_op jit(solution)/shard_map/outgoing/pallas_call | solution.py:283
  8.8 0.3 flow.1.part_ref
  9.1 0.3 collective-permute-done.2.other_ref
  9.4 0.3 flow_rest.1._
  9.7 2.1 %collective-permute-start.4 = (bf16[32,128]{1,0:T(8,128)(2,1)S(1)}, bf16[32,128]{1,0:T(8,128)(2,1)S(1)}, u32[]{:S(2)}, u32[]{:S(2)}) collective-permute-start(bf16[32,128]{1,0:T(8,128)(2,1)S(1)} %flow_rest.1._), channel_id=1, source_target_pairs={{0,16},{1,17},{2,18},{3,19},{4,20},{5,21},{6,22},{7,23},{8,24},{9,... | collective-permute-start | bytes 24584 | tf_op jit(solution)/shard_map/ppermute | solution.py:319
  11.8 0.4 %terms1.1 = (bf16[8,32,256]{2,1,0:T(8,128)(2,1)S(1)}, bf16[8,32,256]{2,1,0:T(8,128)(2,1)S(1)}, bf16[8,32,256]{2,1,0:T(8,128)(2,1)S(1)}, bf16[8,32,256]{2,1,0:T(8,128)(2,1)S(1)}) custom-call(s32[1]{0:T(128)} %bitcast.index_ref, bf16[128,4096]{1,0:T(8,128)(2,1)S(1)} %get-tuple-element.38.g, bf16[128,4096]{1,0:T(8,128)(2,1)S(1)} %get-tuple-element.46.xg_ref, ...), custom_call_target="tpu_custom_call" | custom-call | tf_op jit(solution)/shard_map/terms1/pallas_call | solution.py:283
  12.2 0.0 collective-permute-done.1.act0_ref
  12.2 0.3 terms.1
  12.5 0.1 collective-permute-start.3
  12.5 0.9 %collective-permute-done.4.got_ref = bf16[32,128]{1,0:T(8,128)(2,1)S(1)} collective-permute-done((bf16[32,128]{1,0:T(8,128)(2,1)S(1)}, bf16[32,128]{1,0:T(8,128)(2,1)S(1)}, u32[]{:S(2)}, u32[]{:S(2)}) %collective-permute-start.4) | collective-permute-done | bytes 8224 | tf_op jit(solution)/shard_map/ppermute | solution.py:319
  13.4 0.3 lower.1
  13.7 0.1 collective-permute-start.5
  13.8 0.5 %collective-permute-done.3.got = bf16[24,32,256]{2,1,0:T(8,128)(2,1)S(1)} collective-permute-done((bf16[24,32,256]{2,1,0:T(8,128)(2,1)S(1)}, bf16[24,32,256]{2,1,0:T(8,128)(2,1)S(1)}, u32[]{:S(2)}, u32[]{:S(2)}) %collective-permute-start.3) | collective-permute-done | bytes 393248 | tf_op jit(solution)/shard_map/ppermute | solution.py:319
  14.3 0.1 chip.1
  14.4 2.5 %collective-permute-start.6 = (bf16[4,32,256]{2,1,0:T(8,128)(2,1)S(1)}, bf16[4,32,256]{2,1,0:T(8,128)(2,1)S(1)}, u32[]{:S(2)}, u32[]{:S(2)}) collective-permute-start(bf16[4,32,256]{2,1,0:T(8,128)(2,1)S(1)} %get-tuple-element.62), channel_id=1, source_target_pairs={{0,18},{1,19},{2,16},{3,17},{4,22},{5,23},{6,20},{7,21},{8,26},{9,... | collective-permute-start | bytes 196616 | tf_op jit(solution)/shard_map/ppermute | solution.py:319
  16.9 0.0 collective-permute-done.5.got0
  16.9 0.1 plane.1
  17.0 0.6 %collective-permute-start.7 = (bf16[4,64,256]{2,1,0:T(8,128)(2,1)S(1)}, bf16[4,64,256]{2,1,0:T(8,128)(2,1)S(1)}, u32[]{:S(2)}, u32[]{:S(2)}) collective-permute-start(bf16[4,64,256]{2,1,0:T(8,128)(2,1)S(1)} %get-tuple-element.63), channel_id=1, source_target_pairs={{0,16},{1,17},{2,0},{3,1},{4,20},{5,21},{6,4},{7,5},{8,24},{9,25},... | collective-permute-start | bytes 393224 | tf_op jit(solution)/shard_map/ppermute | solution.py:319
  17.5 1.5 %collective-permute-start.9 = (bf16[4,64,256]{2,1,0:T(8,128)(2,1)S(1)}, bf16[4,64,256]{2,1,0:T(8,128)(2,1)S(1)}, u32[]{:S(2)}, u32[]{:S(2)}) collective-permute-start(bf16[4,64,256]{2,1,0:T(8,128)(2,1)S(1)} %get-tuple-element.65), channel_id=1, source_target_pairs={{0,2},{1,3},{2,18},{3,19},{4,6},{5,7},{6,22},{7,23},{8,10},{9,11},... | collective-permute-start | bytes 393224 | tf_op jit(solution)/shard_map/ppermute | solution.py:319
  19.1 1.1 %collective-permute-start.8 = (bf16[4,32,256]{2,1,0:T(8,128)(2,1)S(1)}, bf16[4,32,256]{2,1,0:T(8,128)(2,1)S(1)}, u32[]{:S(2)}, u32[]{:S(2)}) collective-permute-start(bf16[4,32,256]{2,1,0:T(8,128)(2,1)S(1)} %get-tuple-element.64), channel_id=1, source_target_pairs={{0,18},{1,19},{2,16},{3,17},{4,22},{5,23},{6,20},{7,21},{8,26},{9,... | collective-permute-start | bytes 196616 | tf_op jit(solution)/shard_map/ppermute | solution.py:319
  20.2 0.0 collective-permute-done.6.across_out
  20.2 4.0 %collective-permute-done.8.across_in = bf16[4,32,256]{2,1,0:T(8,128)(2,1)S(1)} collective-permute-done((bf16[4,32,256]{2,1,0:T(8,128)(2,1)S(1)}, bf16[4,32,256]{2,1,0:T(8,128)(2,1)S(1)}, u32[]{:S(2)}, u32[]{:S(2)}) %collective-permute-start.8) | collective-permute-done | bytes 65568 | tf_op jit(solution)/shard_map/ppermute | solution.py:319
  24.2 0.0 collective-permute-done.7.first
  24.2 0.0 collective-permute-done.9.second
  24.2 0.1 layer.1
  24.3 2.6 %collective-permute-start.10 = (bf16[64,256]{1,0:T(8,128)(2,1)S(1)}, bf16[64,256]{1,0:T(8,128)(2,1)S(1)}, u32[]{:S(2)}, u32[]{:S(2)}) collective-permute-start(bf16[64,256]{1,0:T(8,128)(2,1)S(1)} %get-tuple-element.67), channel_id=1, source_target_pairs={{0,8},{1,9},{2,10},{3,11},{4,12},{5,13},{6,14},{7,15},{8,4},{9,5},... | collective-permute-start | bytes 98312 | tf_op jit(solution)/shard_map/ppermute | solution.py:397
  26.9 1.2 %collective-permute-start.11 = (bf16[64,256]{1,0:T(8,128)(2,1)S(1)}, bf16[64,256]{1,0:T(8,128)(2,1)S(1)}, u32[]{:S(2)}, u32[]{:S(2)}) collective-permute-start(bf16[64,256]{1,0:T(8,128)(2,1)S(1)} %get-tuple-element.68), channel_id=1, source_target_pairs={{0,12},{1,13},{2,14},{3,15},{4,8},{5,9},{6,10},{7,11},{8,0},{9,1},... | collective-permute-start | bytes 98312 | tf_op jit(solution)/shard_map/ppermute | solution.py:397
  28.2 0.3 %collective-permute-start.12 = (bf16[64,256]{1,0:T(8,128)(2,1)S(1)}, bf16[64,256]{1,0:T(8,128)(2,1)S(1)}, u32[]{:S(2)}, u32[]{:S(2)}) collective-permute-start(bf16[64,256]{1,0:T(8,128)(2,1)S(1)} %get-tuple-element.69), channel_id=1, source_target_pairs={{0,4},{1,5},{2,6},{3,7},{4,0},{5,1},{6,2},{7,3},{8,12},{9,13},{10,... | collective-permute-start | bytes 98312 | tf_op jit(solution)/shard_map/ppermute | solution.py:397
  28.5 1.6 %collective-permute-done.10.refs_1_ = bf16[64,256]{1,0:T(8,128)(2,1)S(1)} collective-permute-done((bf16[64,256]{1,0:T(8,128)(2,1)S(1)}, bf16[64,256]{1,0:T(8,128)(2,1)S(1)}, u32[]{:S(2)}, u32[]{:S(2)}) %collective-permute-start.10) | collective-permute-done | bytes 32800 | tf_op jit(solution)/shard_map/ppermute | solution.py:397
  30.1 1.6 %collective-permute-done.11.refs_2_ = bf16[64,256]{1,0:T(8,128)(2,1)S(1)} collective-permute-done((bf16[64,256]{1,0:T(8,128)(2,1)S(1)}, bf16[64,256]{1,0:T(8,128)(2,1)S(1)}, u32[]{:S(2)}, u32[]{:S(2)}) %collective-permute-start.11) | collective-permute-done | bytes 32800 | tf_op jit(solution)/shard_map/ppermute | solution.py:397
  31.7 0.4 %collective-permute-done.12.refs_3_ = bf16[64,256]{1,0:T(8,128)(2,1)S(1)} collective-permute-done((bf16[64,256]{1,0:T(8,128)(2,1)S(1)}, bf16[64,256]{1,0:T(8,128)(2,1)S(1)}, u32[]{:S(2)}, u32[]{:S(2)}) %collective-permute-start.12) | collective-permute-done | bytes 32800 | tf_op jit(solution)/shard_map/ppermute | solution.py:397
  32.1 0.7 %total.1 = (f32[1,32,256]{2,1,0:T(8,128)}, f32[1,32,256]{2,1,0:T(8,128)}) custom-call(bf16[64,256]{1,0:T(8,128)(2,1)S(1)} %get-tuple-element.66.refs_0_, bf16[64,256]{1,0:T(8,128)(2,1)S(1)} %collective-permute-done.10.refs_1_, bf16[64,256]{1,0:T(8,128)(2,1)S(1)} %collective-permute-done.11.refs_2_, bf16[64,256]{1,0:T(8,128)(2,1)S(1)} %collective-permute-done.12.refs_3_), custom_call_target="tpu_custom_call" | custom-call | tf_op jit(solution)/shard_map/total/pallas_call | solution.py:283
  (1 shorter events, 0.0 us)
Async XLA Ops:
  1.6 6.5 %collective-permute-start = (bf16[32,2048]{1,0:T(8,128)(2,1)S(1)}, bf16[32,2048]{1,0:T(8,128)(2,1)S(1)}, u32[]{:S(2)}, u32[]{:S(2)}) collective-permute-start(bf16[32,2048]{1,0:T(8,128)(2,1)S(1)} %pick.1), channel_id=1, source_target_pairs={{0,16},{1,17},{2,18},{3,19},{4,20},{5,21},{6,22},{7,23},{8,24},{9,... | collective-permute-start | bytes 393224 | tf_op jit(solution)/shard_map/ppermute | solution.py:319
  7.0 5.2 %collective-permute-start.1 = (bf16[32,128]{1,0:T(8,128)(2,1)S(1)}, bf16[32,128]{1,0:T(8,128)(2,1)S(1)}, u32[]{:S(2)}, u32[]{:S(2)}) collective-permute-start(bf16[32,128]{1,0:T(8,128)(2,1)S(1)} %get-tuple-element.45), channel_id=1, source_target_pairs={{0,16},{1,17},{2,18},{3,19},{4,20},{5,21},{6,22},{7,23},{8,24},{9,... | collective-permute-start | bytes 24584 | tf_op jit(solution)/shard_map/ppermute | solution.py:319
  8.1 1.4 %collective-permute-start.2 = (bf16[32,2048]{1,0:T(8,128)(2,1)S(1)}, bf16[32,2048]{1,0:T(8,128)(2,1)S(1)}, u32[]{:S(2)}, u32[]{:S(2)}) collective-permute-start(bf16[32,2048]{1,0:T(8,128)(2,1)S(1)} %collective-permute-done.own_ref), channel_id=1, source_target_pairs={{0,1},{1,0},{2,3},{3,2},{4,5},{5,4},{6,7},{7,6},{8,9},{9,8},{10,11... | collective-permute-start | bytes 393224 | tf_op jit(solution)/shard_map/ppermute | solution.py:319
  9.7 3.7 %collective-permute-start.4 = (bf16[32,128]{1,0:T(8,128)(2,1)S(1)}, bf16[32,128]{1,0:T(8,128)(2,1)S(1)}, u32[]{:S(2)}, u32[]{:S(2)}) collective-permute-start(bf16[32,128]{1,0:T(8,128)(2,1)S(1)} %flow_rest.1._), channel_id=1, source_target_pairs={{0,16},{1,17},{2,18},{3,19},{4,20},{5,21},{6,22},{7,23},{8,24},{9,... | collective-permute-start | bytes 24584 | tf_op jit(solution)/shard_map/ppermute | solution.py:319
  12.5 1.8 %collective-permute-start.3 = (bf16[24,32,256]{2,1,0:T(8,128)(2,1)S(1)}, bf16[24,32,256]{2,1,0:T(8,128)(2,1)S(1)}, u32[]{:S(2)}, u32[]{:S(2)}) collective-permute-start(bf16[24,32,256]{2,1,0:T(8,128)(2,1)S(1)} %get-tuple-element.55), channel_id=1, source_target_pairs={{0,1},{1,0},{2,3},{3,2},{4,5},{5,4},{6,7},{7,6},{8,9},{9,8},{10,11... | collective-permute-start | bytes 1179656 | tf_op jit(solution)/shard_map/ppermute | solution.py:319
  13.7 3.2 %collective-permute-start.5 = (bf16[8,32,256]{2,1,0:T(8,128)(2,1)S(1)}, bf16[8,32,256]{2,1,0:T(8,128)(2,1)S(1)}, u32[]{:S(2)}, u32[]{:S(2)}) collective-permute-start(bf16[8,32,256]{2,1,0:T(8,128)(2,1)S(1)} %get-tuple-element.60), channel_id=1, source_target_pairs={{0,1},{1,0},{2,3},{3,2},{4,5},{5,4},{6,7},{7,6},{8,9},{9,8},{10,11... | collective-permute-start | bytes 393224 | tf_op jit(solution)/shard_map/ppermute | solution.py:319
  14.4 5.8 %collective-permute-start.6 = (bf16[4,32,256]{2,1,0:T(8,128)(2,1)S(1)}, bf16[4,32,256]{2,1,0:T(8,128)(2,1)S(1)}, u32[]{:S(2)}, u32[]{:S(2)}) collective-permute-start(bf16[4,32,256]{2,1,0:T(8,128)(2,1)S(1)} %get-tuple-element.62), channel_id=1, source_target_pairs={{0,18},{1,19},{2,16},{3,17},{4,22},{5,23},{6,20},{7,21},{8,26},{9,... | collective-permute-start | bytes 196616 | tf_op jit(solution)/shard_map/ppermute | solution.py:319
  17.0 7.2 %collective-permute-start.7 = (bf16[4,64,256]{2,1,0:T(8,128)(2,1)S(1)}, bf16[4,64,256]{2,1,0:T(8,128)(2,1)S(1)}, u32[]{:S(2)}, u32[]{:S(2)}) collective-permute-start(bf16[4,64,256]{2,1,0:T(8,128)(2,1)S(1)} %get-tuple-element.63), channel_id=1, source_target_pairs={{0,16},{1,17},{2,0},{3,1},{4,20},{5,21},{6,4},{7,5},{8,24},{9,25},... | collective-permute-start | bytes 393224 | tf_op jit(solution)/shard_map/ppermute | solution.py:319
  17.5 6.7 %collective-permute-start.9 = (bf16[4,64,256]{2,1,0:T(8,128)(2,1)S(1)}, bf16[4,64,256]{2,1,0:T(8,128)(2,1)S(1)}, u32[]{:S(2)}, u32[]{:S(2)}) collective-permute-start(bf16[4,64,256]{2,1,0:T(8,128)(2,1)S(1)} %get-tuple-element.65), channel_id=1, source_target_pairs={{0,2},{1,3},{2,18},{3,19},{4,6},{5,7},{6,22},{7,23},{8,10},{9,11},... | collective-permute-start | bytes 393224 | tf_op jit(solution)/shard_map/ppermute | solution.py:319
  19.1 5.2 %collective-permute-start.8 = (bf16[4,32,256]{2,1,0:T(8,128)(2,1)S(1)}, bf16[4,32,256]{2,1,0:T(8,128)(2,1)S(1)}, u32[]{:S(2)}, u32[]{:S(2)}) collective-permute-start(bf16[4,32,256]{2,1,0:T(8,128)(2,1)S(1)} %get-tuple-element.64), channel_id=1, source_target_pairs={{0,18},{1,19},{2,16},{3,17},{4,22},{5,23},{6,20},{7,21},{8,26},{9,... | collective-permute-start | bytes 196616 | tf_op jit(solution)/shard_map/ppermute | solution.py:319
  24.3 5.8 %collective-permute-start.10 = (bf16[64,256]{1,0:T(8,128)(2,1)S(1)}, bf16[64,256]{1,0:T(8,128)(2,1)S(1)}, u32[]{:S(2)}, u32[]{:S(2)}) collective-permute-start(bf16[64,256]{1,0:T(8,128)(2,1)S(1)} %get-tuple-element.67), channel_id=1, source_target_pairs={{0,8},{1,9},{2,10},{3,11},{4,12},{5,13},{6,14},{7,15},{8,4},{9,5},... | collective-permute-start | bytes 98312 | tf_op jit(solution)/shard_map/ppermute | solution.py:397
  26.9 4.8 %collective-permute-start.11 = (bf16[64,256]{1,0:T(8,128)(2,1)S(1)}, bf16[64,256]{1,0:T(8,128)(2,1)S(1)}, u32[]{:S(2)}, u32[]{:S(2)}) collective-permute-start(bf16[64,256]{1,0:T(8,128)(2,1)S(1)} %get-tuple-element.68), channel_id=1, source_target_pairs={{0,12},{1,13},{2,14},{3,15},{4,8},{5,9},{6,10},{7,11},{8,0},{9,1},... | collective-permute-start | bytes 98312 | tf_op jit(solution)/shard_map/ppermute | solution.py:397
  28.2 3.9 %collective-permute-start.12 = (bf16[64,256]{1,0:T(8,128)(2,1)S(1)}, bf16[64,256]{1,0:T(8,128)(2,1)S(1)}, u32[]{:S(2)}, u32[]{:S(2)}) collective-permute-start(bf16[64,256]{1,0:T(8,128)(2,1)S(1)} %get-tuple-element.69), channel_id=1, source_target_pairs={{0,4},{1,5},{2,6},{3,7},{4,0},{5,1},{6,2},{7,3},{8,12},{9,13},{10,... | collective-permute-start | bytes 98312 | tf_op jit(solution)/shard_map/ppermute | solution.py:397
